TPU v7x, 256 devices: a whole 4x4x8 slice. The times are simulated.
256 devices in a mesh: group: 8 (over x, y_hi), loop: 32 (over z, y_lo, core).
Axes of the slice: x: 4, y: 4 (y_hi: 2, y_lo: 2; y = y_hi * 2 + y_lo), z: 8, core: 2. Of those that a mesh axis runs over, the one named last changes fastest.
Arguments:
- tile_values: bfloat16 [32, 8, 4, 128, 128], P('loop', 'group'), may hold values from 0 to 20, as said below
- tile_coords: int32 [32, 8, 4], P('loop', 'group'), may hold values from 0 to 15, as said below
- tile_counts: int32 [32, 8], P('loop', 'group'), may hold values from 2 to 4, as said below
- result_coords: int32 [32, 8, 8], P('loop', 'group'), may hold values from 0 to 15, as said below
- result_counts: int32 [32, 8], P('loop', 'group'), may hold values from 4 to 8, as said below
Outputs:
- result_tiles: float32 [32, 8, 8, 128, 128], P('loop', 'group')
Inputs may be any that keep to these rules, and one draw needn't show every extreme that they name: `tile_coords`: in each block the first tile_counts slots name distinct positions, and every tile on the matrix's diagonal lying in that block is among them; the other slots name further distinct positions of the block. `tile_counts`: 4 is reached by some block. `result_coords`: in each block the first result_counts slots name distinct positions, and every tile on the matrix's diagonal lying in that block is among them; the other slots name further distinct positions of the block. `result_counts`: 8 is reached by some block. `tile_values`: entries are nonnegative; a diagonal tile's own diagonal entries are 1 or more.
All inputs are finite; a program needn't handle non-finite values.
Results may differ from a plain program's by a relative error of at most 0.0003.
Values may be sent and summed in bfloat16 or wider, within the bound.
No kernel may reach another device: no remote copies, remote signals or barrier semaphores. Data moves between devices by JAX's collectives and lax.ppermute only.
A program may use at most 128 MiB of HBM per device.

v0:
```python
import jax
import jax.numpy as jnp
from jax import lax
from jax.sharding import PartitionSpec as P

BROWS = 2


def densify(tile_values, tile_coords, tile_counts, positions):
    slot_index = jnp.arange(tile_coords.shape[-1], dtype=jnp.int32)
    in_pattern = slot_index[None, :] < tile_counts[:, None]
    position_index = jnp.arange(positions, dtype=jnp.int32)
    selector = (
        (tile_coords[:, None, :] == position_index[None, :, None]) & in_pattern[:, None, :]
    ).astype(jnp.bfloat16)
    densified = jnp.einsum(
        "bps,bsij->bpij", selector, tile_values, preferred_element_type=jnp.float32
    )
    return densified.astype(jnp.bfloat16)


def shards(tile_values, tile_coords, tile_counts, result_coords, result_counts):
    tile_size = tile_values.shape[-1]
    loop_count = lax.axis_size("loop")
    group_count = lax.axis_size("group")
    tile_rows = BROWS
    tile_cols = tile_rows * loop_count // group_count
    positions = tile_rows * tile_cols
    gathered = (
        lax.all_gather(tile_values, "loop", axis=0, tiled=True),
        lax.all_gather(tile_coords, "loop", axis=0, tiled=True),
        lax.all_gather(tile_counts, "loop", axis=0, tiled=True),
    )
    right_dense = densify(gathered[0][:, 0], gathered[1][:, 0], gathered[2][:, 0], positions)
    right_dense = right_dense.reshape(loop_count * tile_rows, tile_cols, tile_size, tile_size)
    portion = (
        lax.all_gather(tile_values, "group", axis=1, tiled=True),
        lax.all_gather(tile_coords, "group", axis=1, tiled=True),
        lax.all_gather(tile_counts, "group", axis=1, tiled=True),
    )
    amount = portion[0].shape[1]
    left_dense = densify(portion[0][0], portion[1][0], portion[2][0], positions)
    left_dense = left_dense.reshape(amount, tile_rows, tile_cols, tile_size, tile_size)

    def right_slice(offset):
        return lax.dynamic_slice_in_dim(right_dense, offset * tile_cols, tile_cols, 0)

    slices = jax.vmap(right_slice)(jnp.arange(amount, dtype=jnp.int32))
    product = jnp.einsum(
        "qrcia,qcdaj->rdij", left_dense, slices, preferred_element_type=jnp.float32
    )
    flattened = product.reshape(positions, tile_size, tile_size)
    chosen = jnp.take(flattened, result_coords[0, 0], axis=0)
    in_result = jnp.arange(result_coords.shape[-1], dtype=jnp.int32) < result_counts[0, 0]
    squared = jnp.where(in_result[:, None, None], chosen * chosen, jnp.float32(0.0))
    column_pick = (
        (result_coords[0, 0] % tile_cols)[:, None]
        == jnp.arange(tile_cols, dtype=jnp.int32)[None, :]
    ).astype(jnp.float32)
    partial_sums = jnp.einsum(
        "sc,sj->cj", column_pick, jnp.sum(squared, axis=1), precision=lax.Precision.HIGHEST
    )
    totals = lax.psum(partial_sums, "loop")
    column_total = jnp.einsum("sc,cj->sj", column_pick, totals, precision=lax.Precision.HIGHEST)
    row_total = tile_rows * loop_count * tile_size
    output_tiles = squared * (row_total / column_total)[:, None, :]
    return output_tiles[None, None]


def solution(mesh):
    placed = (
        P("loop", "group", None, None, None),
        P("loop", "group", None),
        P("loop", "group"),
        P("loop", "group", None),
        P("loop", "group"),
    )
    return jax.shard_map(
        shards,
        mesh=mesh,
        in_specs=placed,
        out_specs=P("loop", "group", None, None, None),
        check_vma=False,
    )
```

profile of v0, /device:TPU:1, one launch (start us, length us, event | category | flops | bytes accessed | tf_op | source)
XLA Modules:
  0.0 272.0 jit_solution(16980727169920347949)
XLA Ops:
  6.5 0.0 all-gather.5.cloned.1.call-start
  6.5 0.7 all-gather.5.cloned.1.call-update
  7.3 0.0 all-gather.3.cloned.1.call-start
  7.3 0.7 all-gather.3.cloned.1.call-update
  8.7 1.3 dynamic-slice.5
  9.9 0.7 bitcast_dynamic-update-slice_fusion.1
  10.6 11.1 %all-reduce.1 = s32[8]{0:T(128)S(1)} all-reduce(s32[8]{0:T(128)S(1)} %bitcast_dynamic-update-slice_fusion.1), channel_id=1, replica_groups=mesh['group'=8,'loop'=32] {'group'}, use_global_device_ids=true, to_apply=%add.1 | all-reduce | flops 8 | bytes 64
  21.7 1.3 dynamic-slice.4
  23.0 0.1 pad.4.clone
  23.8 0.7 bitcast_dynamic-update-slice_fusion.2
  24.4 17.7 %all_gather.21 = s32[1,8,4]{2,0,1:T(1,128)S(1)} all-gather(s32[1,1,4]{2,0,1:T(1,128)} %bitcast.70), channel_id=1, replica_groups=mesh['group'=8,'loop'=32] {'group'}, dimensions={1}, use_global_device_ids=true | all-gather | bytes 144 | tf_op jit(solution)/shard_map/all_gather | solution.py:38
  42.1 23.0 %all-reduce = s32[32]{0:T(128)S(1)} all-reduce(s32[32]{0:T(128)S(1)} %bitcast_dynamic-update-slice_fusion.2), channel_id=1, replica_groups=mesh['group'=8,'loop'=32] {'loop'}, use_global_device_ids=true, to_apply=%add | all-reduce | flops 32 | bytes 256
  65.1 34.3 %all_gather.18 = s32[32,1,4]{2,1,0:T(1,128)S(1)} all-gather(s32[1,1,4]{2,1,0:T(1,128)} %param.6), channel_id=1, replica_groups=mesh['group'=8,'loop'=32] {'loop'}, dimensions={0}, use_global_device_ids=true | all-gather | bytes 528 | tf_op jit(solution)/shard_map/all_gather | solution.py:31
  99.4 0.7 fusion.29
  100.1 0.7 and_select_fusion
  100.8 0.1 iota_compare_fusion.6
  100.8 0.7 compare_and_fusion
  101.5 0.1 add_add_fusion
  101.6 0.1 iota_compare_fusion.2
  101.7 0.0 all-gather.5.cloned.1.call-done
  101.7 5.4 %convert_bitcast_fusion = bf16[8,2,8,128,128,1]{4,2,1,3,0,5:T(8,128)(2,1)} fusion(bf16[1,8,4,128,128]{4,3,2,0,1:T(8,128)(2,1)} %all-gather.5.cloned.1.call-done, s32[8,4]{1,0:T(8,128)S(1)} %bitcast.69, pred[8,4]{1,0:T(8,128)(4,1)S(1)} %iota_compare_fusion.6), kind=kOutput, calls=%fused_computation.9 | convolution fusion | flops 18875392 | bytes 5243040 | tf_op jit(solution)/shard_map/bps,bsij->bpij/dot_general | solution.py:16
  107.1 27.4 %all-gather.3.cloned.1.call-done = bf16[32,1,4,128,128]{4,3,2,1,0:T(8,128)(2,1)} async-done(((bf16[1,1,4,128,128]{4,3,2,1,0:T(8,128)(2,1)}), bf16[32,1,4,128,128]{4,3,2,1,0:T(8,128)(2,1)}) %all-gather.3.cloned.1.call-update) | async-done | bytes 4194320 | tf_op jit(solution)/shard_map/all_gather | solution.py:30
  134.4 13.0 %convolution_convert_fusion = bf16[32,16,128,128]{3,1,2,0:T(8,128)(2,1)} fusion(bf16[32,1,4,128,128]{4,3,2,1,0:T(8,128)(2,1)} %all-gather.3.cloned.1.call-done, s32[32,4]{1,0:T(8,128)S(1)} %bitcast.68, pred[32,4]{1,0:T(8,128)(4,1)S(1)} %iota_compare_fusion.2), kind=kOutput, calls=%fused_computation.5 | convolution fusion | flops 75501568 | bytes 20972160 | tf_op jit(solution)/shard_map/bps,bsij->bpij/dot_general | solution.py:16
  147.4 16.6 %copy.27 = bf16[32,16,128,128]{3,2,1,0:T(8,128)(2,1)} copy(bf16[32,16,128,128]{3,1,2,0:T(8,128)(2,1)} %convolution_convert_fusion) | data formatting | bytes 33554432 | tf_op jit(solution)/shard_map/convert_element_type | solution.py:19
  164.1 36.0 %while.1 = (s32[]{:T(128)}, bf16[64,8,128,128]{3,2,1,0:T(8,128)(2,1)}, s32[8,4]{0,1:T(4,128)S(1)}, bf16[8,8,8,128,128]{4,3,2,1,0:T(8,128)(2,1)}, s32[]{:T(128)}) while((s32[]{:T(128)}, bf16[64,8,128,128]{3,2,1,0:T(8,128)(2,1)}, s32[8,4]{0,1:T(4,128)S(1)}, bf16[8,8,8,128,128]{4,3,2,1,0:T(8,128)(2,1)}, s32[]{:T(128)}) %tuple.24), condition=%wide.while_cond, body=%wide.while_body.sunk | while | flops 2 | bytes 4195433 | solution.py:46
  164.1 0.1 constant_dynamic-slice_fusion.2
  164.2 0.6 slice.22
  164.7 3.9 %bitcast_dynamic-update-slice_fusion.4 = bf16[8,8,8,128,128]{4,3,2,1,0:T(8,128)(2,1)} fusion(bf16[8,8,8,128,128]{4,3,2,1,0:T(8,128)(2,1)} %get-tuple-element.56, s32[]{:T(128)} %get-tuple-element.53, bf16[64,8,128,128]{3,2,1,0:T(8,128)(2,1)} %get-tuple-element.59, s32[]{:T(128)} %bitcast.63), kind=kLoop, calls=%fused_computation.1.clone.1 | loop fusion | bytes 4195328 | tf_op jit(solution)/shard_map/vmap()/gather
  168.6 0.1 constant_dynamic-slice_fusion.2
  168.7 0.6 slice.22
  169.3 3.8 %bitcast_dynamic-update-slice_fusion.4 = bf16[8,8,8,128,128]{4,3,2,1,0:T(8,128)(2,1)} fusion(bf16[8,8,8,128,128]{4,3,2,1,0:T(8,128)(2,1)} %get-tuple-element.56, s32[]{:T(128)} %get-tuple-element.53, bf16[64,8,128,128]{3,2,1,0:T(8,128)(2,1)} %get-tuple-element.59, s32[]{:T(128)} %bitcast.63), kind=kLoop, calls=%fused_computation.1.clone.1 | loop fusion | bytes 4195328 | tf_op jit(solution)/shard_map/vmap()/gather
  173.1 0.1 constant_dynamic-slice_fusion.2
  173.1 0.6 slice.22
  173.7 3.8 %bitcast_dynamic-update-slice_fusion.4 = bf16[8,8,8,128,128]{4,3,2,1,0:T(8,128)(2,1)} fusion(bf16[8,8,8,128,128]{4,3,2,1,0:T(8,128)(2,1)} %get-tuple-element.56, s32[]{:T(128)} %get-tuple-element.53, bf16[64,8,128,128]{3,2,1,0:T(8,128)(2,1)} %get-tuple-element.59, s32[]{:T(128)} %bitcast.63), kind=kLoop, calls=%fused_computation.1.clone.1 | loop fusion | bytes 4195328 | tf_op jit(solution)/shard_map/vmap()/gather
  177.6 0.1 constant_dynamic-slice_fusion.2
  177.6 0.6 slice.22
  178.2 3.9 %bitcast_dynamic-update-slice_fusion.4 = bf16[8,8,8,128,128]{4,3,2,1,0:T(8,128)(2,1)} fusion(bf16[8,8,8,128,128]{4,3,2,1,0:T(8,128)(2,1)} %get-tuple-element.56, s32[]{:T(128)} %get-tuple-element.53, bf16[64,8,128,128]{3,2,1,0:T(8,128)(2,1)} %get-tuple-element.59, s32[]{:T(128)} %bitcast.63), kind=kLoop, calls=%fused_computation.1.clone.1 | loop fusion | bytes 4195328 | tf_op jit(solution)/shard_map/vmap()/gather
  182.1 0.1 constant_dynamic-slice_fusion.2
  182.1 0.6 slice.22
  182.7 3.9 %bitcast_dynamic-update-slice_fusion.4 = bf16[8,8,8,128,128]{4,3,2,1,0:T(8,128)(2,1)} fusion(bf16[8,8,8,128,128]{4,3,2,1,0:T(8,128)(2,1)} %get-tuple-element.56, s32[]{:T(128)} %get-tuple-element.53, bf16[64,8,128,128]{3,2,1,0:T(8,128)(2,1)} %get-tuple-element.59, s32[]{:T(128)} %bitcast.63), kind=kLoop, calls=%fused_computation.1.clone.1 | loop fusion | bytes 4195328 | tf_op jit(solution)/shard_map/vmap()/gather
  186.6 0.1 constant_dynamic-slice_fusion.2
  186.7 0.6 slice.22
  187.3 3.8 %bitcast_dynamic-update-slice_fusion.4 = bf16[8,8,8,128,128]{4,3,2,1,0:T(8,128)(2,1)} fusion(bf16[8,8,8,128,128]{4,3,2,1,0:T(8,128)(2,1)} %get-tuple-element.56, s32[]{:T(128)} %get-tuple-element.53, bf16[64,8,128,128]{3,2,1,0:T(8,128)(2,1)} %get-tuple-element.59, s32[]{:T(128)} %bitcast.63), kind=kLoop, calls=%fused_computation.1.clone.1 | loop fusion | bytes 4195328 | tf_op jit(solution)/shard_map/vmap()/gather
  191.1 0.1 constant_dynamic-slice_fusion.2
  191.2 0.6 slice.22
  191.7 3.9 %bitcast_dynamic-update-slice_fusion.4 = bf16[8,8,8,128,128]{4,3,2,1,0:T(8,128)(2,1)} fusion(bf16[8,8,8,128,128]{4,3,2,1,0:T(8,128)(2,1)} %get-tuple-element.56, s32[]{:T(128)} %get-tuple-element.53, bf16[64,8,128,128]{3,2,1,0:T(8,128)(2,1)} %get-tuple-element.59, s32[]{:T(128)} %bitcast.63), kind=kLoop, calls=%fused_computation.1.clone.1 | loop fusion | bytes 4195328 | tf_op jit(solution)/shard_map/vmap()/gather
  195.6 0.1 constant_dynamic-slice_fusion.2
  195.7 0.6 slice.22
  196.3 3.8 %bitcast_dynamic-update-slice_fusion.4 = bf16[8,8,8,128,128]{4,3,2,1,0:T(8,128)(2,1)} fusion(bf16[8,8,8,128,128]{4,3,2,1,0:T(8,128)(2,1)} %get-tuple-element.56, s32[]{:T(128)} %get-tuple-element.53, bf16[64,8,128,128]{3,2,1,0:T(8,128)(2,1)} %get-tuple-element.59, s32[]{:T(128)} %bitcast.63), kind=kLoop, calls=%fused_computation.1.clone.1 | loop fusion | bytes 4195328 | tf_op jit(solution)/shard_map/vmap()/gather
  200.1 10.0 %fusion.5 = f32[2,8,128,128]{2,3,0,1:T(8,128)S(1)} fusion(bf16[8,2,8,128,128,1]{4,2,1,3,0,5:T(8,128)(2,1)} %convert_bitcast_fusion, bf16[8,8,8,128,128]{4,3,2,1,0:T(8,128)(2,1)} %get-tuple-element.12), kind=kOutput, calls=%fused_computation.10 | convolution fusion | flops 4294967296 | bytes 22020096 | tf_op jit(solution)/shard_map/qrcia,qcdaj->rdij/dot_general | solution.py:49
  210.1 0.3 copy.35
  210.4 0.6 gather_fusion
  211.0 0.2 select_reduce_fusion
  211.2 0.3 fusion.25
  211.4 52.6 %psum.7 = f32[8,128]{1,0:T(8,128)S(1)} all-reduce(f32[8,128]{1,0:T(8,128)S(1)} %fusion.25), channel_id=1, replica_groups=mesh['group'=8,'loop'=32] {'loop'}, use_global_device_ids=true, to_apply=%region_1.2 | all-reduce | flops 1024 | bytes 8192 | tf_op jit(solution)/shard_map/psum | solution.py:63
  264.0 0.2 convolution_divide_fusion
  264.2 0.9 fusion.14
  (7 shorter events, 0.0 us)
Async XLA Ops:
  6.5 95.1 %all-gather.5.cloned.1.call-start = ((), (), s32[]{:S(2)}) async-start(), calls=%async_computation.1 | async-start | bytes 1179648 | tf_op jit(solution)/shard_map/all_gather | solution.py:37
  7.3 127.2 %all-gather.3.cloned.1.call-start = ((), (), s32[]{:S(2)}) async-start(), calls=%async_computation | async-start | bytes 4325376 | tf_op jit(solution)/shard_map/all_gather | solution.py:30
Sparse Core Ops, SparseCore 0:
  10.0 55.3 all-gather.4
  67.2 67.1 all-gather.2
where the time goes:
time: 273 us; the launch traced here: 272 us
  blocking collectives  139 us (51%)
  local copies, waits for them, and re-layouts  57.5 us (21%)
  waiting for transfers between devices  28.8 us (11%)
  matrix products  28.8 us (11%)
  between operations  14.8 us (5%)
  other arithmetic  3.32 us (1%)
    psum x1, blocking collectives, shards(): totals = lax.psum(partial_sums, 'loop')  52.6 us
    gather x24, local copies, waits for them, and re-layouts  36 us
    all_gather x1, blocking collectives, shards(): lax.all_gather(tile_coords, 'loop', axis=0, tiled=True)  34.3 us
    unnamed x2, blocking collectives  34.1 us
    all_gather x1, waiting for transfers between devices, shards(): lax.all_gather(tile_values, 'loop', axis=0, tiled=True)  27.4 us
    dot_general x2, matrix products, densify(): jnp.einsum('bps,bsij->bpij', selector, tile_values, preferred_element_typ...  18.4 us
    all_gather x1, blocking collectives, shards(): lax.all_gather(tile_coords, 'group', axis=1, tiled=True)  17.7 us
    convert_element_type x1, local copies, waits for them, and re-layouts, densify(): return densified.astype(jnp.bfloat16)  16.6 us
  transfers between devices with their start and end apart: 2, of which 1 were waited for; matrix products, arithmetic and copies ran while one was open for 4% of the time, Pallas kernels for 0%

commit v1 on v0

v1 whole, which is shorter than its diff:
```python
import jax
import jax.numpy as jnp
from jax import lax
from jax.experimental import pallas as pl
from jax.experimental.pallas import tpu as pltpu
from jax.sharding import PartitionSpec as P

TILE = 128
SLOTS = 4
BODY = SLOTS * TILE
UNIT = BODY + 16
WIDE = 9 * TILE
F32, BF16 = jnp.float32, jnp.bfloat16


def loop_perm(f):
    pairs = []
    for i in range(32):
        z, y, c = f(i >> 2, (i >> 1) & 1, i & 1)
        pairs.append((i, (z % 8) * 4 + y * 2 + c))
    return pairs


def group_perm(f):
    pairs = []
    for i in range(8):
        x, y = f(i >> 1, i & 1)
        pairs.append((i, (x % 4) * 2 + y))
    return pairs


CORE = loop_perm(lambda z, y, c: (z, y, 1 - c))
YLO = loop_perm(lambda z, y, c: (z, 1 - y, c))
RING = loop_perm(lambda z, y, c: (z + 1 - 2 * c, y, c))
YHI = group_perm(lambda x, y: (x, 1 - y))
XUP = group_perm(lambda x, y: (x + 1, y))
XDOWN = group_perm(lambda x, y: (x - 1, y))
XFAR = group_perm(lambda x, y: (x + 2, y))


def place(dst, ref, base, row):
    marks = ref[base + BODY : base + UNIT, :].astype(F32)
    for s in range(SLOTS):
        code = jnp.max(marks[s : s + 1, :]).astype(jnp.int32)
        r = (code >= 9).astype(jnp.int32)
        c = code - 9 * r
        rows = pl.ds(pl.multiple_of(row + r * TILE, TILE), TILE)
        cols = pl.ds(pl.multiple_of(c * TILE, TILE), TILE)
        dst[rows, cols] = ref[base + s * TILE : base + (s + 1) * TILE, :]


def where_am_i():
    i = lax.axis_index("loop")
    j = lax.axis_index("group")
    return i >> 2, (i >> 1) & 1, i & 1, j >> 1, j & 1


def expand(coords, counts, *refs):
    right, left = refs[:16], refs[16:20]
    squares, sums, dense_left, dense_right, product = refs[20:]
    z, y, c, x, h = where_am_i()
    dense_left[...] = jnp.zeros_like(dense_left)
    for k, step in enumerate((0, 3, 1, 2)):
        for half in range(2):
            j = ((x + step) & 3) * 2 + (h ^ half)
            place(dense_left.at[j], left[k], half * UNIT, 0)
    product[...] = jnp.zeros_like(product)

    def chunk(first, second, j, y_first, y_second, c_first, c_second):
        dense_right[...] = jnp.zeros_like(dense_right)
        for ref, yy, cc in ((first, y_first, c_first), (second, y_second, c_second)):
            place(dense_right, ref, 0, (yy * 2 + cc) * 256)
            place(dense_right, ref, UNIT, (yy * 2 + 1 - cc) * 256)
        product[...] += jnp.dot(
            dense_left[j, :, : 8 * TILE], dense_right[:, : 8 * TILE], preferred_element_type=F32
        )

    near = y ^ c
    sign = 1 - 2 * c
    chunk(right[0], right[1], z, near, 1 - near, c, c)
    for r in range(1, 4):
        a, b, d, e = right[4 * r - 2 : 4 * r + 2]
        chunk(a, b, (z - sign * r) & 7, near, 1 - near, c, c)
        chunk(d, e, (z + sign * r) & 7, 1 - near, near, 1 - c, 1 - c)
    chunk(right[14], right[15], (z + 4) & 7, near, 1 - near, c, 1 - c)

    column = lax.broadcasted_iota(jnp.int32, (8, TILE), 0)
    total = jnp.zeros((8, TILE), F32)
    for s in range(8):
        p = coords[s]
        rows = pl.ds(pl.multiple_of((p >> 3) * TILE, TILE), TILE)
        cols = pl.ds(pl.multiple_of((p & 7) * TILE, TILE), TILE)
        tile = product[rows, cols]
        tile = jnp.where(s < counts[0], tile * tile, 0.0)
        squares[s] = tile
        part = jnp.sum(tile, axis=0, keepdims=True)
        total += jnp.where(column == (p & 7), part, 0.0)
    for k in range(32):
        sums[k] = total


def rescale(coords, squares, sums, out):
    factor = 8192.0 / jnp.sum(sums[...], axis=0)
    column = lax.broadcasted_iota(jnp.int32, (8, TILE), 0)
    for s in range(8):
        pick = jnp.where(column == (coords[s] & 7), factor, 0.0)
        out[s] = squares[s] * jnp.sum(pick, axis=0, keepdims=True)


def shards(tile_values, tile_coords, tile_counts, result_coords, result_counts):
    slot = jnp.arange(16, dtype=jnp.int32)
    at = jnp.pad(tile_coords[0, 0], (0, 12))
    code = jnp.where(slot < tile_counts[0, 0], at + (at >> 3), 8).astype(BF16)
    unit = jnp.concatenate(
        [tile_values.reshape(BODY, TILE), jnp.broadcast_to(code[:, None], (16, TILE))]
    )
    core = lax.axis_index("loop") & 1

    def along(perm, v):
        return lax.ppermute(v, "loop", perm)

    def across(perm, v):
        return lax.ppermute(v, "group", perm)

    pair = along(CORE, unit)
    beside = along(YLO, unit)
    beside_pair = along(CORE, beside)
    mine = jnp.concatenate([unit, pair])
    theirs = jnp.concatenate([beside, beside_pair])
    first = jnp.where(core == 0, mine, theirs)
    second = jnp.where(core == 0, theirs, mine)
    right = [first, second]
    for r in range(1, 4):
        first, second = along(RING, first), along(RING, second)
        right += [first, second, along(CORE, first), along(CORE, second)]
    first = along(RING, first)
    right += [first, along(CORE, first)]

    row = jnp.concatenate([unit, across(YHI, unit)])
    left = [row, across(XUP, row), across(XDOWN, row), across(XFAR, row)]

    coords, counts = result_coords.reshape(8), result_counts.reshape(1)
    whole = pl.BlockSpec(memory_space=pltpu.VMEM)
    squares, sums = pl.pallas_call(
        expand,
        grid_spec=pltpu.PrefetchScalarGridSpec(
            num_scalar_prefetch=2,
            grid=(),
            in_specs=[whole] * 20,
            out_specs=[whole] * 2,
            scratch_shapes=[
                pltpu.VMEM((8, 256, WIDE), BF16),
                pltpu.VMEM((1024, WIDE), BF16),
                pltpu.VMEM((256, 1024), F32),
            ],
        ),
        out_shape=[
            jax.ShapeDtypeStruct((8, TILE, TILE), F32),
            jax.ShapeDtypeStruct((32, 8, TILE), F32),
        ],
        compiler_params=pltpu.CompilerParams(vmem_limit_bytes=48 * 2**20),
    )(coords, counts, *right, *left)
    sums = lax.all_to_all(sums, "loop", 0, 0, tiled=True)
    out = pl.pallas_call(
        rescale,
        grid_spec=pltpu.PrefetchScalarGridSpec(
            num_scalar_prefetch=1,
            grid=(),
            in_specs=[whole] * 2,
            out_specs=whole,
        ),
        out_shape=jax.ShapeDtypeStruct((8, TILE, TILE), F32),
    )(coords, squares, sums)
    return out[None, None]


def solution(mesh):
    placed = (
        P("loop", "group", None, None, None),
        P("loop", "group", None),
        P("loop", "group"),
        P("loop", "group", None),
        P("loop", "group"),
    )
    return jax.shard_map(
        shards,
        mesh=mesh,
        in_specs=placed,
        out_specs=P("loop", "group", None, None, None),
        check_vma=False,
    )
```

time: 273 us -> 82 us (0.30)
  blocking collectives: 139 us -> 14 us
  local copies, waits for them, and re-layouts: 57.5 us -> 2.21 us
  starting transfers between devices: 0.04 us -> 31.1 us
  matrix products: 28.8 us -> 0 us
  between operations: 14.8 us -> 1.42 us
  Pallas kernels: 0 us -> 10.4 us
  waiting for transfers between devices: 28.8 us -> 21.6 us
    psum x1 -> x0, blocking collectives: 52.6 us -> none  [shards(): totals = lax.psum(partial_sums, 'loop')]
    all_gather x2 -> x0, blocking collectives: 52 us -> none  [the longest x1 34.3 us: shards(): lax.all_gather(tile_coords, 'loop', axis=0, tiled=True)]
    gather x25 -> x0, local copies, waits for them, and re-layouts: 36.6 us -> none
    unnamed x2 -> x0, blocking collectives: 34.1 us -> none
    ppermute x0 -> x21, starting transfers between devices: none -> 31.1 us  [the longest x17 25.1 us: along(): return lax.ppermute(v, 'loop', perm)]
    dot_general x5 -> x0, matrix products: 28.8 us -> none  [the longest x2 18.4 us: densify(): jnp.einsum('bps,bsij->bpij', selector, tile_values, preferred_element_typ...]
    all_gather x2 -> x0, waiting for transfers between devices: 27.4 us -> none  [the longest x1 27.4 us: shards(): lax.all_gather(tile_values, 'loop', axis=0, tiled=True)]
    ppermute x0 -> x21, waiting for transfers between devices: none -> 21.6 us  [the longest x4 12.3 us: across(): return lax.ppermute(v, 'group', perm)]
  transfers between devices with their start and end apart: 2 -> 21, of which waited for: 1 -> 8; matrix products, arithmetic and copies ran while one was open for 4% -> 0% of each run, Pallas kernels for 0% -> 0%
where the time goes in v1:
time: 82 us; the launch traced here: 81.8 us
  starting transfers between devices  31.1 us (38%)
  waiting for transfers between devices  21.6 us (26%)
  blocking collectives  14 us (17%)
  Pallas kernels  10.4 us (13%)
  local copies, waits for them, and re-layouts  2.21 us (3%)
  between operations  1.42 us (2%)
  other arithmetic  1.04 us (1%)
    ppermute x17, starting transfers between devices, along(): return lax.ppermute(v, 'loop', perm)  25.1 us
    all_to_all x1, blocking collectives, shards(): sums = lax.all_to_all(sums, 'loop', 0, 0, tiled=True)  14 us
    ppermute x4, waiting for transfers between devices, across(): return lax.ppermute(v, 'group', perm)  12.3 us
    ppermute x17, waiting for transfers between devices, along(): return lax.ppermute(v, 'loop', perm)  9.23 us
    pallas_call x1, Pallas kernels, shards(): pl.pallas_call(expand, grid_spec=pltpu.PrefetchScalarGridSpec(num_scalar_...  7.81 us
    ppermute x4, starting transfers between devices, across(): return lax.ppermute(v, 'group', perm)  6.01 us
    pallas_call x1, Pallas kernels, shards(): pl.pallas_call(rescale, grid_spec=pltpu.PrefetchScalarGridSpec(num_scalar...  2.6 us
    unnamed x9, local copies, waits for them, and re-layouts  2.11 us
  transfers between devices with their start and end apart: 21, of which 8 were waited for; matrix products, arithmetic and copies ran while one was open for 0% of the time, Pallas kernels for 0%

profile of v1, /device:TPU:1, one launch (start us, length us, event | category | flops | bytes accessed | tf_op | source)
XLA Modules:
  0.0 81.8 jit_solution(114373390108573419)
XLA Ops:
  0.7 0.0 copy-start.3
  0.7 0.6 copy-done.3
  1.3 0.1 broadcast_in_dim.14
  1.4 0.9 %pad_maximum_fusion.3 = bf16[528,128]{1,0:T(8,128)(2,1)S(1)} fusion(bf16[16,128]{1,0:T(8,128)(2,1)S(1)} %broadcast_in_dim.14, bf16[512,128]{1,0:T(8,128)(2,1)} %bitcast.10), kind=kLoop, calls=%fused_computation.5 | loop fusion | flops 270336 | bytes 270336 | tf_op jit(solution)/shard_map/concatenate | solution.py:114
  2.3 2.2 %collective-permute-start.1 = (bf16[528,128]{1,0:T(8,128)(2,1)S(1)}, bf16[528,128]{1,0:T(8,128)(2,1)S(1)}, u32[]{:S(2)}, u32[]{:S(2)}) collective-permute-start(bf16[528,128]{1,0:T(8,128)(2,1)S(1)} %pad_maximum_fusion.3), channel_id=1, source_target_pairs={{0,2},{1,3},{2,0},{3,1},{4,6},{5,7},{6,4},{7,5},{8,10},{9,11},{10,... | collective-permute-start | bytes 405512 | tf_op jit(solution)/shard_map/ppermute | solution.py:120
  4.5 2.4 %collective-permute-done.1 = bf16[528,128]{1,0:T(8,128)(2,1)S(1)} collective-permute-done((bf16[528,128]{1,0:T(8,128)(2,1)S(1)}, bf16[528,128]{1,0:T(8,128)(2,1)S(1)}, u32[]{:S(2)}, u32[]{:S(2)}) %collective-permute-start.1) | collective-permute-done | bytes 135200 | tf_op jit(solution)/shard_map/ppermute | solution.py:120
  6.9 3.7 %collective-permute-start.2 = (bf16[528,128]{1,0:T(8,128)(2,1)S(1)}, bf16[528,128]{1,0:T(8,128)(2,1)S(1)}, u32[]{:S(2)}, u32[]{:S(2)}) collective-permute-start(bf16[528,128]{1,0:T(8,128)(2,1)S(1)} %collective-permute-done.1), channel_id=1, source_target_pairs={{0,1},{1,0},{2,3},{3,2},{4,5},{5,4},{6,7},{7,6},{8,9},{9,8},{10,11... | collective-permute-start | bytes 405512 | tf_op jit(solution)/shard_map/ppermute | solution.py:120
  10.7 1.5 %collective-permute-start.17 = (bf16[528,128]{1,0:T(8,128)(2,1)S(1)}, bf16[528,128]{1,0:T(8,128)(2,1)S(1)}, u32[]{:S(2)}, u32[]{:S(2)}) collective-permute-start(bf16[528,128]{1,0:T(8,128)(2,1)S(1)} %pad_maximum_fusion.3), channel_id=1, source_target_pairs={{0,32},{32,0},{64,96},{96,64},{128,160},{160,128},{192,224},{224,1... | collective-permute-start | bytes 405512 | tf_op jit(solution)/shard_map/ppermute | solution.py:123
  12.1 0.3 collective-permute-start
  12.4 0.0 copy-start.2
  12.5 0.0 collective-permute-done.2
  12.5 4.9 %collective-permute-done.17 = bf16[528,128]{1,0:T(8,128)(2,1)S(1)} collective-permute-done((bf16[528,128]{1,0:T(8,128)(2,1)S(1)}, bf16[528,128]{1,0:T(8,128)(2,1)S(1)}, u32[]{:S(2)}, u32[]{:S(2)}) %collective-permute-start.17) | collective-permute-done | bytes 135200 | tf_op jit(solution)/shard_map/ppermute | solution.py:123
  17.4 0.0 collective-permute-done
  17.4 0.0 copy-done.2
  17.4 0.1 broadcast_select_fusion
  17.5 4.2 %collective-permute-start.3 = (bf16[1056,128]{1,0:T(8,128)(2,1)S(1)}, bf16[1056,128]{1,0:T(8,128)(2,1)S(1)}, u32[]{:S(2)}, u32[]{:S(2)}) collective-permute-start(bf16[1056,128]{1,0:T(8,128)(2,1)S(1)} %get-tuple-element.10.refs_0_), channel_id=1, source_target_pairs={{0,4},{1,29},{2,6},{3,31},{4,8},{5,1},{6,10},{7,3},{8,12},{9,5},{1... | collective-permute-start | bytes 811016 | tf_op jit(solution)/shard_map/ppermute | solution.py:120
  21.7 0.7 collective-permute-start.4
  22.5 2.7 %collective-permute-done.3.refs_2_ = bf16[1056,128]{1,0:T(8,128)(2,1)S(1)} collective-permute-done((bf16[1056,128]{1,0:T(8,128)(2,1)S(1)}, bf16[1056,128]{1,0:T(8,128)(2,1)S(1)}, u32[]{:S(2)}, u32[]{:S(2)}) %collective-permute-start.3) | collective-permute-done | bytes 270368 | tf_op jit(solution)/shard_map/ppermute | solution.py:120
  25.1 3.1 %collective-permute-start.7 = (bf16[1056,128]{1,0:T(8,128)(2,1)S(1)}, bf16[1056,128]{1,0:T(8,128)(2,1)S(1)}, u32[]{:S(2)}, u32[]{:S(2)}) collective-permute-start(bf16[1056,128]{1,0:T(8,128)(2,1)S(1)} %collective-permute-done.3.refs_2_), channel_id=1, source_target_pairs={{0,4},{1,29},{2,6},{3,31},{4,8},{5,1},{6,10},{7,3},{8,12},{9,5},{1... | collective-permute-start | bytes 811016 | tf_op jit(solution)/shard_map/ppermute | solution.py:120
  28.3 2.7 %collective-permute-start.20 = (bf16[1056,128]{1,0:T(8,128)(2,1)S(1)}, bf16[1056,128]{1,0:T(8,128)(2,1)S(1)}, u32[]{:S(2)}, u32[]{:S(2)}) collective-permute-start(bf16[1056,128]{1,0:T(8,128)(2,1)S(1)} %get-tuple-element.11.refs_16_), channel_id=1, source_target_pairs={{0,128},{32,160},{64,192},{96,224},{128,0},{160,32},{192,64},{224,... | collective-permute-start | bytes 811016 | tf_op jit(solution)/shard_map/ppermute | solution.py:123
  31.0 0.9 %collective-permute-start.19 = (bf16[1056,128]{1,0:T(8,128)(2,1)S(1)}, bf16[1056,128]{1,0:T(8,128)(2,1)S(1)}, u32[]{:S(2)}, u32[]{:S(2)}) collective-permute-start(bf16[1056,128]{1,0:T(8,128)(2,1)S(1)} %get-tuple-element.11.refs_16_), channel_id=1, source_target_pairs={{0,192},{32,224},{64,0},{96,32},{128,64},{160,96},{192,128},{224,1... | collective-permute-start | bytes 811016 | tf_op jit(solution)/shard_map/ppermute | solution.py:123
  31.9 0.0 collective-permute-done.4.refs_3_
  31.9 0.0 collective-permute-start.8
  31.9 0.0 collective-permute-done.7.refs_6_
  31.9 3.2 %collective-permute-start.11 = (bf16[1056,128]{1,0:T(8,128)(2,1)S(1)}, bf16[1056,128]{1,0:T(8,128)(2,1)S(1)}, u32[]{:S(2)}, u32[]{:S(2)}) collective-permute-start(bf16[1056,128]{1,0:T(8,128)(2,1)S(1)} %collective-permute-done.7.refs_6_), channel_id=1, source_target_pairs={{0,4},{1,29},{2,6},{3,31},{4,8},{5,1},{6,10},{7,3},{8,12},{9,5},{1... | collective-permute-start | bytes 811016 | tf_op jit(solution)/shard_map/ppermute | solution.py:120
  35.1 0.9 %collective-permute-start.18 = (bf16[1056,128]{1,0:T(8,128)(2,1)S(1)}, bf16[1056,128]{1,0:T(8,128)(2,1)S(1)}, u32[]{:S(2)}, u32[]{:S(2)}) collective-permute-start(bf16[1056,128]{1,0:T(8,128)(2,1)S(1)} %get-tuple-element.11.refs_16_), channel_id=1, source_target_pairs={{0,64},{32,96},{64,128},{96,160},{128,192},{160,224},{192,0},{224,... | collective-permute-start | bytes 811016 | tf_op jit(solution)/shard_map/ppermute | solution.py:123
  36.0 1.4 %collective-permute-done.20.refs_19_ = bf16[1056,128]{1,0:T(8,128)(2,1)S(1)} collective-permute-done((bf16[1056,128]{1,0:T(8,128)(2,1)S(1)}, bf16[1056,128]{1,0:T(8,128)(2,1)S(1)}, u32[]{:S(2)}, u32[]{:S(2)}) %collective-permute-start.20) | collective-permute-done | bytes 270368 | tf_op jit(solution)/shard_map/ppermute | solution.py:123
  37.4 0.2 collective-permute-start.6
  37.6 6.0 %collective-permute-done.19.refs_18_ = bf16[1056,128]{1,0:T(8,128)(2,1)S(1)} collective-permute-done((bf16[1056,128]{1,0:T(8,128)(2,1)S(1)}, bf16[1056,128]{1,0:T(8,128)(2,1)S(1)}, u32[]{:S(2)}, u32[]{:S(2)}) %collective-permute-start.19) | collective-permute-done | bytes 270368 | tf_op jit(solution)/shard_map/ppermute | solution.py:123
  43.6 0.0 collective-permute-start.5
  43.6 0.0 collective-permute-done.8.refs_7_
  43.6 0.9 %collective-permute-start.12 = (bf16[1056,128]{1,0:T(8,128)(2,1)S(1)}, bf16[1056,128]{1,0:T(8,128)(2,1)S(1)}, u32[]{:S(2)}, u32[]{:S(2)}) collective-permute-start(bf16[1056,128]{1,0:T(8,128)(2,1)S(1)} %collective-permute-done.8.refs_7_), channel_id=1, source_target_pairs={{0,4},{1,29},{2,6},{3,31},{4,8},{5,1},{6,10},{7,3},{8,12},{9,5},{1... | collective-permute-start | bytes 811016 | tf_op jit(solution)/shard_map/ppermute | solution.py:120
  44.6 0.0 collective-permute-done.11.refs_10_
  44.6 0.5 collective-permute-start.15
  45.1 0.0 collective-permute-done.18.refs_17_
  45.1 0.0 collective-permute-start.10
  45.2 0.0 collective-permute-done.6.refs_5_
  45.2 0.5 collective-permute-start.9
  45.6 0.0 collective-permute-done.5.refs_4_
  45.6 0.3 collective-permute-start.13
  45.9 3.3 %collective-permute-done.12.refs_11_ = bf16[1056,128]{1,0:T(8,128)(2,1)S(1)} collective-permute-done((bf16[1056,128]{1,0:T(8,128)(2,1)S(1)}, bf16[1056,128]{1,0:T(8,128)(2,1)S(1)}, u32[]{:S(2)}, u32[]{:S(2)}) %collective-permute-start.12) | collective-permute-done | bytes 270368 | tf_op jit(solution)/shard_map/ppermute | solution.py:120
  49.2 2.6 %collective-permute-start.14 = (bf16[1056,128]{1,0:T(8,128)(2,1)S(1)}, bf16[1056,128]{1,0:T(8,128)(2,1)S(1)}, u32[]{:S(2)}, u32[]{:S(2)}) collective-permute-start(bf16[1056,128]{1,0:T(8,128)(2,1)S(1)} %collective-permute-done.12.refs_11_), channel_id=1, source_target_pairs={{0,1},{1,0},{2,3},{3,2},{4,5},{5,4},{6,7},{7,6},{8,9},{9,8},{10,11... | collective-permute-start | bytes 811016 | tf_op jit(solution)/shard_map/ppermute | solution.py:120
  51.8 0.3 collective-permute-done.15.refs_14_
  52.1 2.6 %collective-permute-start.16 = (bf16[1056,128]{1,0:T(8,128)(2,1)S(1)}, bf16[1056,128]{1,0:T(8,128)(2,1)S(1)}, u32[]{:S(2)}, u32[]{:S(2)}) collective-permute-start(bf16[1056,128]{1,0:T(8,128)(2,1)S(1)} %collective-permute-done.15.refs_14_), channel_id=1, source_target_pairs={{0,1},{1,0},{2,3},{3,2},{4,5},{5,4},{6,7},{7,6},{8,9},{9,8},{10,11... | collective-permute-start | bytes 811016 | tf_op jit(solution)/shard_map/ppermute | solution.py:120
  55.4 0.0 collective-permute-done.10.refs_9_
  55.4 0.0 collective-permute-done.9.refs_8_
  55.4 0.0 collective-permute-done.14.refs_13_
  55.4 0.0 collective-permute-done.13.refs_12_
  55.4 0.5 collective-permute-done.16.refs_15_
  55.9 0.0 copy-start.1
  55.9 0.7 copy-done.1
  56.5 7.8 %shard_map.55 = (f32[8,128,128]{2,1,0:T(8,128)S(1)}, f32[32,8,128]{2,1,0:T(8,128)S(1)}) custom-call(s32[8]{0:T(128)S(1)} %bitcast.9, s32[1]{0:T(128)} %bitcast.7.counts, bf16[1056,128]{1,0:T(8,128)(2,1)S(1)} %get-tuple-element.10.refs_0_, bf16[1056,128]{1,0:T(8,128)(2,1)S(1)} %get-tuple-element.9.refs_1_, ...), custom_call_target="tpu_custom_call" | custom-call | tf_op jit(solution)/shard_map/pallas_call | solution.py:144
  64.4 0.0 copy-start
  64.4 0.8 copy-done
  65.2 14.0 %all_to_all.5.sums = f32[32,8,128]{2,1,0:T(8,128)} all-to-all(f32[32,8,128]{2,1,0:T(8,128)S(1)} %get-tuple-element.8), channel_id=1, replica_groups=mesh['group'=8,'loop'=32] {'loop'}, dimensions={0} | all-to-all | bytes 262144 | tf_op jit(solution)/shard_map/all_to_all | solution.py:163
  79.2 2.6 %shard_map.56 = f32[8,128,128]{2,1,0:T(8,128)} custom-call(s32[8]{0:T(128)} %bitcast.8, f32[8,128,128]{2,1,0:T(8,128)} %copy-done, f32[32,8,128]{2,1,0:T(8,128)} %all_to_all.5.sums), custom_call_target="tpu_custom_call" | custom-call | tf_op jit(solution)/shard_map/pallas_call | solution.py:164
  (3 shorter events, 0.0 us)
Async XLA Ops:
  0.7 0.7 copy-start.3
  2.3 4.6 %collective-permute-start.1 = (bf16[528,128]{1,0:T(8,128)(2,1)S(1)}, bf16[528,128]{1,0:T(8,128)(2,1)S(1)}, u32[]{:S(2)}, u32[]{:S(2)}) collective-permute-start(bf16[528,128]{1,0:T(8,128)(2,1)S(1)} %pad_maximum_fusion.3), channel_id=1, source_target_pairs={{0,2},{1,3},{2,0},{3,1},{4,6},{5,7},{6,4},{7,5},{8,10},{9,11},{10,... | collective-permute-start | bytes 405512 | tf_op jit(solution)/shard_map/ppermute | solution.py:120
  6.9 5.5 %collective-permute-start.2 = (bf16[528,128]{1,0:T(8,128)(2,1)S(1)}, bf16[528,128]{1,0:T(8,128)(2,1)S(1)}, u32[]{:S(2)}, u32[]{:S(2)}) collective-permute-start(bf16[528,128]{1,0:T(8,128)(2,1)S(1)} %collective-permute-done.1), channel_id=1, source_target_pairs={{0,1},{1,0},{2,3},{3,2},{4,5},{5,4},{6,7},{7,6},{8,9},{9,8},{10,11... | collective-permute-start | bytes 405512 | tf_op jit(solution)/shard_map/ppermute | solution.py:120
  10.7 6.7 %collective-permute-start.17 = (bf16[528,128]{1,0:T(8,128)(2,1)S(1)}, bf16[528,128]{1,0:T(8,128)(2,1)S(1)}, u32[]{:S(2)}, u32[]{:S(2)}) collective-permute-start(bf16[528,128]{1,0:T(8,128)(2,1)S(1)} %pad_maximum_fusion.3), channel_id=1, source_target_pairs={{0,32},{32,0},{64,96},{96,64},{128,160},{160,128},{192,224},{224,1... | collective-permute-start | bytes 405512 | tf_op jit(solution)/shard_map/ppermute | solution.py:123
  12.1 5.2 %collective-permute-start = (bf16[528,128]{1,0:T(8,128)(2,1)S(1)}, bf16[528,128]{1,0:T(8,128)(2,1)S(1)}, u32[]{:S(2)}, u32[]{:S(2)}) collective-permute-start(bf16[528,128]{1,0:T(8,128)(2,1)S(1)} %pad_maximum_fusion.3), channel_id=1, source_target_pairs={{0,1},{1,0},{2,3},{3,2},{4,5},{5,4},{6,7},{7,6},{8,9},{9,8},{10,11... | collective-permute-start | bytes 405512 | tf_op jit(solution)/shard_map/ppermute | solution.py:120
  12.4 4.9 %copy-start.2 = (bf16[1,1,4,128,128]{4,3,2,1,0:T(8,128)(2,1)S(1)}, bf16[1,1,4,128,128]{4,3,2,1,0:T(8,128)(2,1)}, u32[]{:S(2)}) copy-start(bf16[1,1,4,128,128]{4,3,2,1,0:T(8,128)(2,1)} %param.5) | copy-start | bytes 393220
  17.5 7.6 %collective-permute-start.3 = (bf16[1056,128]{1,0:T(8,128)(2,1)S(1)}, bf16[1056,128]{1,0:T(8,128)(2,1)S(1)}, u32[]{:S(2)}, u32[]{:S(2)}) collective-permute-start(bf16[1056,128]{1,0:T(8,128)(2,1)S(1)} %get-tuple-element.10.refs_0_), channel_id=1, source_target_pairs={{0,4},{1,29},{2,6},{3,31},{4,8},{5,1},{6,10},{7,3},{8,12},{9,5},{1... | collective-permute-start | bytes 811016 | tf_op jit(solution)/shard_map/ppermute | solution.py:120
  21.7 10.1 %collective-permute-start.4 = (bf16[1056,128]{1,0:T(8,128)(2,1)S(1)}, bf16[1056,128]{1,0:T(8,128)(2,1)S(1)}, u32[]{:S(2)}, u32[]{:S(2)}) collective-permute-start(bf16[1056,128]{1,0:T(8,128)(2,1)S(1)} %get-tuple-element.9.refs_1_), channel_id=1, source_target_pairs={{0,4},{1,29},{2,6},{3,31},{4,8},{5,1},{6,10},{7,3},{8,12},{9,5},{1... | collective-permute-start | bytes 811016 | tf_op jit(solution)/shard_map/ppermute | solution.py:120
  25.1 6.7 %collective-permute-start.7 = (bf16[1056,128]{1,0:T(8,128)(2,1)S(1)}, bf16[1056,128]{1,0:T(8,128)(2,1)S(1)}, u32[]{:S(2)}, u32[]{:S(2)}) collective-permute-start(bf16[1056,128]{1,0:T(8,128)(2,1)S(1)} %collective-permute-done.3.refs_2_), channel_id=1, source_target_pairs={{0,4},{1,29},{2,6},{3,31},{4,8},{5,1},{6,10},{7,3},{8,12},{9,5},{1... | collective-permute-start | bytes 811016 | tf_op jit(solution)/shard_map/ppermute | solution.py:120
  28.3 9.2 %collective-permute-start.20 = (bf16[1056,128]{1,0:T(8,128)(2,1)S(1)}, bf16[1056,128]{1,0:T(8,128)(2,1)S(1)}, u32[]{:S(2)}, u32[]{:S(2)}) collective-permute-start(bf16[1056,128]{1,0:T(8,128)(2,1)S(1)} %get-tuple-element.11.refs_16_), channel_id=1, source_target_pairs={{0,128},{32,160},{64,192},{96,224},{128,0},{160,32},{192,64},{224,... | collective-permute-start | bytes 811016 | tf_op jit(solution)/shard_map/ppermute | solution.py:123
  31.0 12.6 %collective-permute-start.19 = (bf16[1056,128]{1,0:T(8,128)(2,1)S(1)}, bf16[1056,128]{1,0:T(8,128)(2,1)S(1)}, u32[]{:S(2)}, u32[]{:S(2)}) collective-permute-start(bf16[1056,128]{1,0:T(8,128)(2,1)S(1)} %get-tuple-element.11.refs_16_), channel_id=1, source_target_pairs={{0,192},{32,224},{64,0},{96,32},{128,64},{160,96},{192,128},{224,1... | collective-permute-start | bytes 811016 | tf_op jit(solution)/shard_map/ppermute | solution.py:123
  31.9 11.8 %collective-permute-start.8 = (bf16[1056,128]{1,0:T(8,128)(2,1)S(1)}, bf16[1056,128]{1,0:T(8,128)(2,1)S(1)}, u32[]{:S(2)}, u32[]{:S(2)}) collective-permute-start(bf16[1056,128]{1,0:T(8,128)(2,1)S(1)} %collective-permute-done.4.refs_3_), channel_id=1, source_target_pairs={{0,4},{1,29},{2,6},{3,31},{4,8},{5,1},{6,10},{7,3},{8,12},{9,5},{1... | collective-permute-start | bytes 811016 | tf_op jit(solution)/shard_map/ppermute | solution.py:120
  31.9 12.7 %collective-permute-start.11 = (bf16[1056,128]{1,0:T(8,128)(2,1)S(1)}, bf16[1056,128]{1,0:T(8,128)(2,1)S(1)}, u32[]{:S(2)}, u32[]{:S(2)}) collective-permute-start(bf16[1056,128]{1,0:T(8,128)(2,1)S(1)} %collective-permute-done.7.refs_6_), channel_id=1, source_target_pairs={{0,4},{1,29},{2,6},{3,31},{4,8},{5,1},{6,10},{7,3},{8,12},{9,5},{1... | collective-permute-start | bytes 811016 | tf_op jit(solution)/shard_map/ppermute | solution.py:120
  35.1 10.1 %collective-permute-start.18 = (bf16[1056,128]{1,0:T(8,128)(2,1)S(1)}, bf16[1056,128]{1,0:T(8,128)(2,1)S(1)}, u32[]{:S(2)}, u32[]{:S(2)}) collective-permute-start(bf16[1056,128]{1,0:T(8,128)(2,1)S(1)} %get-tuple-element.11.refs_16_), channel_id=1, source_target_pairs={{0,64},{32,96},{64,128},{96,160},{128,192},{160,224},{192,0},{224,... | collective-permute-start | bytes 811016 | tf_op jit(solution)/shard_map/ppermute | solution.py:123
  37.4 7.8 %collective-permute-start.6 = (bf16[1056,128]{1,0:T(8,128)(2,1)S(1)}, bf16[1056,128]{1,0:T(8,128)(2,1)S(1)}, u32[]{:S(2)}, u32[]{:S(2)}) collective-permute-start(bf16[1056,128]{1,0:T(8,128)(2,1)S(1)} %collective-permute-done.4.refs_3_), channel_id=1, source_target_pairs={{0,1},{1,0},{2,3},{3,2},{4,5},{5,4},{6,7},{7,6},{8,9},{9,8},{10,11... | collective-permute-start | bytes 811016 | tf_op jit(solution)/shard_map/ppermute | solution.py:120
  43.6 2.0 %collective-permute-start.5 = (bf16[1056,128]{1,0:T(8,128)(2,1)S(1)}, bf16[1056,128]{1,0:T(8,128)(2,1)S(1)}, u32[]{:S(2)}, u32[]{:S(2)}) collective-permute-start(bf16[1056,128]{1,0:T(8,128)(2,1)S(1)} %collective-permute-done.3.refs_2_), channel_id=1, source_target_pairs={{0,1},{1,0},{2,3},{3,2},{4,5},{5,4},{6,7},{7,6},{8,9},{9,8},{10,11... | collective-permute-start | bytes 811016 | tf_op jit(solution)/shard_map/ppermute | solution.py:120
  43.6 5.6 %collective-permute-start.12 = (bf16[1056,128]{1,0:T(8,128)(2,1)S(1)}, bf16[1056,128]{1,0:T(8,128)(2,1)S(1)}, u32[]{:S(2)}, u32[]{:S(2)}) collective-permute-start(bf16[1056,128]{1,0:T(8,128)(2,1)S(1)} %collective-permute-done.8.refs_7_), channel_id=1, source_target_pairs={{0,4},{1,29},{2,6},{3,31},{4,8},{5,1},{6,10},{7,3},{8,12},{9,5},{1... | collective-permute-start | bytes 811016 | tf_op jit(solution)/shard_map/ppermute | solution.py:120
  44.6 7.6 %collective-permute-start.15 = (bf16[1056,128]{1,0:T(8,128)(2,1)S(1)}, bf16[1056,128]{1,0:T(8,128)(2,1)S(1)}, u32[]{:S(2)}, u32[]{:S(2)}) collective-permute-start(bf16[1056,128]{1,0:T(8,128)(2,1)S(1)} %collective-permute-done.11.refs_10_), channel_id=1, source_target_pairs={{0,4},{1,29},{2,6},{3,31},{4,8},{5,1},{6,10},{7,3},{8,12},{9,5},{1... | collective-permute-start | bytes 811016 | tf_op jit(solution)/shard_map/ppermute | solution.py:120
  45.1 10.2 %collective-permute-start.10 = (bf16[1056,128]{1,0:T(8,128)(2,1)S(1)}, bf16[1056,128]{1,0:T(8,128)(2,1)S(1)}, u32[]{:S(2)}, u32[]{:S(2)}) collective-permute-start(bf16[1056,128]{1,0:T(8,128)(2,1)S(1)} %collective-permute-done.8.refs_7_), channel_id=1, source_target_pairs={{0,1},{1,0},{2,3},{3,2},{4,5},{5,4},{6,7},{7,6},{8,9},{9,8},{10,11... | collective-permute-start | bytes 811016 | tf_op jit(solution)/shard_map/ppermute | solution.py:120
  45.2 10.2 %collective-permute-start.9 = (bf16[1056,128]{1,0:T(8,128)(2,1)S(1)}, bf16[1056,128]{1,0:T(8,128)(2,1)S(1)}, u32[]{:S(2)}, u32[]{:S(2)}) collective-permute-start(bf16[1056,128]{1,0:T(8,128)(2,1)S(1)} %collective-permute-done.7.refs_6_), channel_id=1, source_target_pairs={{0,1},{1,0},{2,3},{3,2},{4,5},{5,4},{6,7},{7,6},{8,9},{9,8},{10,11... | collective-permute-start | bytes 811016 | tf_op jit(solution)/shard_map/ppermute | solution.py:120
  45.6 9.7 %collective-permute-start.13 = (bf16[1056,128]{1,0:T(8,128)(2,1)S(1)}, bf16[1056,128]{1,0:T(8,128)(2,1)S(1)}, u32[]{:S(2)}, u32[]{:S(2)}) collective-permute-start(bf16[1056,128]{1,0:T(8,128)(2,1)S(1)} %collective-permute-done.11.refs_10_), channel_id=1, source_target_pairs={{0,1},{1,0},{2,3},{3,2},{4,5},{5,4},{6,7},{7,6},{8,9},{9,8},{10,11... | collective-permute-start | bytes 811016 | tf_op jit(solution)/shard_map/ppermute | solution.py:120
  49.2 6.1 %collective-permute-start.14 = (bf16[1056,128]{1,0:T(8,128)(2,1)S(1)}, bf16[1056,128]{1,0:T(8,128)(2,1)S(1)}, u32[]{:S(2)}, u32[]{:S(2)}) collective-permute-start(bf16[1056,128]{1,0:T(8,128)(2,1)S(1)} %collective-permute-done.12.refs_11_), channel_id=1, source_target_pairs={{0,1},{1,0},{2,3},{3,2},{4,5},{5,4},{6,7},{7,6},{8,9},{9,8},{10,11... | collective-permute-start | bytes 811016 | tf_op jit(solution)/shard_map/ppermute | solution.py:120
  52.1 3.7 %collective-permute-start.16 = (bf16[1056,128]{1,0:T(8,128)(2,1)S(1)}, bf16[1056,128]{1,0:T(8,128)(2,1)S(1)}, u32[]{:S(2)}, u32[]{:S(2)}) collective-permute-start(bf16[1056,128]{1,0:T(8,128)(2,1)S(1)} %collective-permute-done.15.refs_14_), channel_id=1, source_target_pairs={{0,1},{1,0},{2,3},{3,2},{4,5},{5,4},{6,7},{7,6},{8,9},{9,8},{10,11... | collective-permute-start | bytes 811016 | tf_op jit(solution)/shard_map/ppermute | solution.py:120
  55.9 0.7 copy-start.1
  64.4 0.8 copy-start

commit v2 on v1

v2 whole, which is shorter than its diff:
```python
import jax
import jax.numpy as jnp
from jax import lax
from jax.experimental import pallas as pl
from jax.experimental.pallas import tpu as pltpu
from jax.sharding import PartitionSpec as P

TILE = 128
SLOTS = 4
BODY = SLOTS * TILE
UNIT = BODY + 16
WIDE = 9 * TILE
F32, BF16 = jnp.float32, jnp.bfloat16


def loop_perm(f):
    pairs = []
    for i in range(32):
        z, y, c = f(i >> 2, (i >> 1) & 1, i & 1)
        pairs.append((i, (z % 8) * 4 + y * 2 + c))
    return pairs


def group_perm(f):
    pairs = []
    for i in range(8):
        x, y = f(i >> 1, i & 1)
        pairs.append((i, (x % 4) * 2 + y))
    return pairs


CORE = loop_perm(lambda z, y, c: (z, y, 1 - c))
YLO = loop_perm(lambda z, y, c: (z, 1 - y, c))
RING = loop_perm(lambda z, y, c: (z + 1 - 2 * c, y, c))
YHI = group_perm(lambda x, y: (x, 1 - y))
XNEAR = group_perm(lambda x, y: (x ^ 1, y))
XMIRROR = group_perm(lambda x, y: (3 - x, y))


def scalars(ref, base, first, count):
    marks = ref[base + BODY : base + UNIT, :].astype(F32)
    return [jnp.max(marks[s : s + 1, :]).astype(jnp.int32) for s in range(first, first + count)]


def place(dst, ref, base, row):
    for s, code in enumerate(scalars(ref, base, 0, SLOTS)):
        r = (code >= 9).astype(jnp.int32)
        c = code - 9 * r
        rows = pl.ds(pl.multiple_of(row + r * TILE, TILE), TILE)
        cols = pl.ds(pl.multiple_of(c * TILE, TILE), TILE)
        dst[rows, cols] = ref[base + s * TILE : base + (s + 1) * TILE, :]


def where_am_i():
    i = lax.axis_index("loop")
    j = lax.axis_index("group")
    return i >> 2, (i >> 1) & 1, i & 1, j >> 1, j & 1


def multiply(dense_left, dense_right, j, units):
    dense_right[...] = jnp.zeros_like(dense_right)
    for ref, base, y, c in units:
        place(dense_right, ref, base, (y * 2 + c) * 256)
    return jnp.dot(
        dense_left[j, :, : 8 * TILE], dense_right[:, : 8 * TILE], preferred_element_type=F32
    )


def round_units(refs, y, c):
    pair, beside, beside_pair = refs
    return (
        (pair, 0, y, c),
        (pair, UNIT, y, 1 - c),
        (beside, 0, 1 - y, c),
        (beside_pair, 0, 1 - y, 1 - c),
    )


def begin(*refs):
    own, rounds, left = refs[:3], refs[3:15], refs[15:17]
    dense_left, product, dense_right = refs[17:]
    z, y, c, x, h = where_am_i()
    dense_left[...] = jnp.zeros_like(dense_left)
    for k in range(8):
        xx = (x, x ^ 1, 3 - x, (3 - x) ^ 1)[k >> 1]
        place(dense_left.at[xx * 2 + (h ^ (k & 1))], left[k >> 2], (k & 3) * UNIT, 0)
    product[...] = multiply(dense_left, dense_right, z, round_units(own, y, c))
    sign = 1 - 2 * c
    for r in (1, 2):
        near, far = rounds[6 * r - 6 : 6 * r - 3], rounds[6 * r - 3 : 6 * r]
        product[...] += multiply(
            dense_left, dense_right, (z - sign * r) & 7, round_units(near, y, c)
        )
        product[...] += multiply(
            dense_left, dense_right, (z + sign * r) & 7, round_units(far, y, 1 - c)
        )


def proceed(*refs):
    near, far = refs[:3], refs[3:6]
    dense_left, before, product, dense_right = refs[6:]
    z, y, c, _, _ = where_am_i()
    sign = 1 - 2 * c
    product[...] = before[...] + multiply(
        dense_left, dense_right, (z - sign * 3) & 7, round_units(near, y, c)
    )
    product[...] += multiply(
        dense_left, dense_right, (z + sign * 3) & 7, round_units(far, y, 1 - c)
    )


def finish(unit, pair, beside, beside_pair, dense_left, before, squares, sums, dense_right, product, held, sem):
    z, y, c, _, _ = where_am_i()
    units = round_units((pair, beside, beside_pair), y, c)
    product[...] = before[...] + multiply(dense_left, dense_right, (z + 4) & 7, units)
    column = lax.broadcasted_iota(jnp.int32, (8, TILE), 0)
    total = jnp.zeros((8, TILE), F32)
    copies = []
    for s, code in enumerate(scalars(unit, 0, SLOTS, 8)):
        used = code < 16
        p = code & 15
        rows = pl.ds(pl.multiple_of((p >> 3) * TILE, TILE), TILE)
        cols = pl.ds(pl.multiple_of((p & 7) * TILE, TILE), TILE)
        tile = product[rows, cols]
        tile = jnp.where(used, tile * tile, 0.0)
        held[s] = tile
        copies.append(pltpu.make_async_copy(held.at[s], squares.at[s], sem.at[s]))
        copies[-1].start()
        part = jnp.sum(tile, axis=0, keepdims=True)
        total += jnp.where(column == (p & 7), part, 0.0)
    for k in range(32):
        sums[k] = total
    for copy in copies:
        copy.wait()


def rescale(unit, squares, sums, out, marks, inside, parts, done, sem_in, sem_out):
    ins = [pltpu.make_async_copy(sums, parts, sem_in.at[8])]
    ins.append(pltpu.make_async_copy(unit.at[pl.ds(BODY, 16)], marks, sem_in.at[9]))
    ins += [pltpu.make_async_copy(squares.at[s], inside.at[s], sem_in.at[s]) for s in range(8)]
    for copy in ins:
        copy.start()
    ins[1].wait()
    codes = scalars(marks, -BODY, SLOTS, 8)
    ins[0].wait()
    factor = 8192.0 / jnp.sum(parts[...], axis=0)
    column = lax.broadcasted_iota(jnp.int32, (8, TILE), 0)
    outs = []
    for s in range(8):
        pick = jnp.where(column == (codes[s] & 7), factor, 0.0)
        pick = jnp.sum(pick, axis=0, keepdims=True)
        ins[2 + s].wait()
        done[s] = inside[s] * pick
        outs.append(pltpu.make_async_copy(done.at[s], out.at[s], sem_out.at[s]))
        outs[-1].start()
    for copy in outs:
        copy.wait()


WHOLE = pl.BlockSpec(memory_space=pltpu.VMEM)
AWAY = pl.BlockSpec(memory_space=pl.ANY)
DENSE_LEFT = jax.ShapeDtypeStruct((8, 256, WIDE), BF16)
PRODUCT = jax.ShapeDtypeStruct((256, 1024), F32)
DENSE_RIGHT = pltpu.VMEM((1024, WIDE), BF16)
TILES = (8, TILE, TILE)


def cost(blocks):
    return pl.CostEstimate(
        flops=blocks * 2 * 256 * 1024 * 1024, bytes_accessed=blocks * 4 * 2**20, transcendentals=0
    )


def shards(tile_values, tile_coords, tile_counts, result_coords, result_counts):
    slot = jnp.arange(SLOTS, dtype=jnp.int32)
    at = tile_coords[0, 0]
    tile_code = jnp.where(slot < tile_counts[0, 0], at + (at >> 3), 8)
    slot = jnp.arange(8, dtype=jnp.int32)
    at = result_coords[0, 0]
    result_code = jnp.where(slot < result_counts[0, 0], at, at + 16)
    code = jnp.concatenate([tile_code, result_code, tile_code]).astype(BF16)
    unit = jnp.concatenate(
        [tile_values.reshape(BODY, TILE), jnp.broadcast_to(code[:, None], (16, TILE))]
    )

    def along(perm, v):
        return lax.ppermute(v, "loop", perm)

    def across(perm, v):
        return lax.ppermute(v, "group", perm)

    beside = along(YLO, unit)
    pair = jnp.concatenate([unit, along(CORE, unit)])
    beside_pair = along(CORE, beside)
    later, _ = lax.optimization_barrier((unit, beside))
    row = jnp.concatenate([later, across(YHI, later)])
    row = jnp.concatenate([row, across(XNEAR, row)])
    left = [row, across(XMIRROR, row)]

    streams = [pair, beside, beside_pair]
    right = [streams]
    for r in range(3):
        streams = [along(RING, v) for v in streams]
        right += [streams, [along(CORE, v) for v in streams]]
    last = [along(RING, v) for v in streams[:2]]
    last.append(along(CORE, last[1]))

    limit = pltpu.CompilerParams(vmem_limit_bytes=24 * 2**20)
    dense_left, product = pl.pallas_call(
        begin,
        in_specs=[WHOLE] * 17,
        out_specs=[WHOLE] * 2,
        out_shape=[DENSE_LEFT, PRODUCT],
        scratch_shapes=[DENSE_RIGHT],
        compiler_params=limit,
        cost_estimate=cost(6),
    )(*sum(right[:5], []), *left)
    product = pl.pallas_call(
        proceed,
        in_specs=[WHOLE] * 8,
        out_specs=WHOLE,
        out_shape=PRODUCT,
        scratch_shapes=[DENSE_RIGHT],
        compiler_params=limit,
        cost_estimate=cost(2),
    )(*sum(right[5:], []), dense_left, product)
    squares, sums = pl.pallas_call(
        finish,
        in_specs=[WHOLE] * 6,
        out_specs=[AWAY, WHOLE],
        out_shape=[jax.ShapeDtypeStruct(TILES, F32), jax.ShapeDtypeStruct((32, 8, TILE), F32)],
        scratch_shapes=[
            DENSE_RIGHT,
            pltpu.VMEM((256, 1024), F32),
            pltpu.VMEM(TILES, F32),
            pltpu.SemaphoreType.DMA((8,)),
        ],
        compiler_params=limit,
        cost_estimate=cost(1),
    )(unit, *last, dense_left, product)
    sums = lax.all_to_all(sums, "loop", 0, 0, tiled=True)
    out = pl.pallas_call(
        rescale,
        in_specs=[AWAY] * 3,
        out_specs=AWAY,
        out_shape=jax.ShapeDtypeStruct(TILES, F32),
        scratch_shapes=[
            pltpu.VMEM((16, TILE), BF16),
            pltpu.VMEM(TILES, F32),
            pltpu.VMEM((32, 8, TILE), F32),
            pltpu.VMEM(TILES, F32),
            pltpu.SemaphoreType.DMA((10,)),
            pltpu.SemaphoreType.DMA((8,)),
        ],
        compiler_params=limit,
    )(unit, squares, sums)
    return out[None, None]


def solution(mesh):
    placed = (
        P("loop", "group", None, None, None),
        P("loop", "group", None),
        P("loop", "group"),
        P("loop", "group", None),
        P("loop", "group"),
    )
    return jax.shard_map(
        shards,
        mesh=mesh,
        in_specs=placed,
        out_specs=P("loop", "group", None, None, None),
        check_vma=False,
    )
```

time: 82 us -> 80.8 us (0.985)
  waiting for transfers between devices: 21.6 us -> 8.44 us
  starting transfers between devices: 31.1 us -> 40.3 us
  other arithmetic: 1.04 us -> 3.26 us
  blocking collectives: 14 us -> 16.2 us
  local copies, waits for them, and re-layouts: 2.21 us -> 0.14 us
    ppermute x4 -> x3, waiting for transfers between devices: 12.3 us -> 0.01 us  [across(): return lax.ppermute(v, 'group', perm)]
    ppermute x17 -> x24, starting transfers between devices: 25.1 us -> 32.8 us  [along(): return lax.ppermute(v, 'loop', perm)]
    all_to_all x1, blocking collectives: 14 us -> 16.2 us  [shards(): sums = lax.all_to_all(sums, 'loop', 0, 0, tiled=True)]
    unnamed x9 -> x2, local copies, waits for them, and re-layouts: 2.11 us -> 0.03 us
    ppermute x4 -> x3, starting transfers between devices: 6.01 us -> 7.53 us  [across(): return lax.ppermute(v, 'group', perm)]
    another operation x0 -> x2, other arithmetic: none -> 1.32 us
    concatenate x0 -> x3, other arithmetic: none -> 1.02 us  [the longest x1 0.92 us: shards(): pair = jnp.concatenate([unit, along(CORE, unit)])]
    ppermute x17 -> x24, waiting for transfers between devices: 9.23 us -> 8.43 us  [along(): return lax.ppermute(v, 'loop', perm)]
  transfers between devices with their start and end apart: 21 -> 27, of which waited for: 8 -> 4; matrix products, arithmetic and copies ran while one was open for 0% -> 1% of each run, Pallas kernels for 0% -> 8%
where the time goes in v2:
time: 80.8 us; the launch traced here: 80.7 us
  starting transfers between devices  40.3 us (50%)
  blocking collectives  16.2 us (20%)
  Pallas kernels  10.7 us (13%)
  waiting for transfers between devices  8.44 us (10%)
  other arithmetic  3.26 us (4%)
  between operations  1.58 us (2%)
    ppermute x24, starting transfers between devices, along(): return lax.ppermute(v, 'loop', perm)  32.8 us
    all_to_all x1, blocking collectives, shards(): sums = lax.all_to_all(sums, 'loop', 0, 0, tiled=True)  16.2 us
    ppermute x24, waiting for transfers between devices, along(): return lax.ppermute(v, 'loop', perm)  8.43 us
    ppermute x3, starting transfers between devices, across(): return lax.ppermute(v, 'group', perm)  7.53 us
    pallas_call x1, Pallas kernels, shards(): pl.pallas_call(begin, in_specs=[WHOLE] * 17, out_specs=[WHOLE] * 2, out_s...  4.8 us
    pallas_call x1, Pallas kernels, shards(): pl.pallas_call(finish, in_specs=[WHOLE] * 6, out_specs=[AWAY, WHOLE], out...  2.11 us
    pallas_call x1, Pallas kernels, shards(): pl.pallas_call(rescale, in_specs=[AWAY] * 3, out_specs=AWAY, out_shape=ja...  1.94 us
    pallas_call x1, Pallas kernels, shards(): pl.pallas_call(proceed, in_specs=[WHOLE] * 8, out_specs=WHOLE, out_shape=...  1.81 us
  transfers between devices with their start and end apart: 27, of which 4 were waited for; matrix products, arithmetic and copies ran while one was open for 1% of the time, Pallas kernels for 8%

profile of v2, /device:TPU:1, one launch (start us, length us, event | category | flops | bytes accessed | tf_op | source)
XLA Modules:
  0.0 80.7 jit_solution(11268349503760661567)
XLA Ops:
  1.3 0.7 fusion
  2.0 0.7 fusion.1
  2.6 0.1 pad_maximum_fusion.3
  2.7 0.1 broadcast_in_dim.14
  2.8 0.9 %pad_maximum_fusion.2.unit = bf16[528,128]{1,0:T(8,128)(2,1)S(1)} fusion(bf16[16,128]{1,0:T(8,128)(2,1)S(1)} %broadcast_in_dim.14, bf16[512,128]{1,0:T(8,128)(2,1)} %bitcast.14), kind=kLoop, calls=%fused_computation.2 | loop fusion | flops 270336 | bytes 270336 | tf_op jit(solution)/shard_map/concatenate | solution.py:182
  3.7 2.2 %collective-permute-start.5 = (bf16[528,128]{1,0:T(8,128)(2,1)S(1)}, bf16[528,128]{1,0:T(8,128)(2,1)S(1)}, u32[]{:S(2)}, u32[]{:S(2)}) collective-permute-start(bf16[528,128]{1,0:T(8,128)(2,1)S(1)} %pad_maximum_fusion.2.unit), channel_id=1, source_target_pairs={{0,2},{1,3},{2,0},{3,1},{4,6},{5,7},{6,4},{7,5},{8,10},{9,11},{10,... | collective-permute-start | bytes 405512 | tf_op jit(solution)/shard_map/ppermute | solution.py:187
  5.9 1.2 %collective-permute-start = (bf16[528,128]{1,0:T(8,128)(2,1)S(1)}, bf16[528,128]{1,0:T(8,128)(2,1)S(1)}, u32[]{:S(2)}, u32[]{:S(2)}) collective-permute-start(bf16[528,128]{1,0:T(8,128)(2,1)S(1)} %pad_maximum_fusion.2.unit), channel_id=1, source_target_pairs={{0,1},{1,0},{2,3},{3,2},{4,5},{5,4},{6,7},{7,6},{8,9},{9,8},{10,11... | collective-permute-start | bytes 405512 | tf_op jit(solution)/shard_map/ppermute | solution.py:187
  7.1 1.2 %collective-permute-done.5.refs_1_ = bf16[528,128]{1,0:T(8,128)(2,1)S(1)} collective-permute-done((bf16[528,128]{1,0:T(8,128)(2,1)S(1)}, bf16[528,128]{1,0:T(8,128)(2,1)S(1)}, u32[]{:S(2)}, u32[]{:S(2)}) %collective-permute-start.5) | collective-permute-done | bytes 135200 | tf_op jit(solution)/shard_map/ppermute | solution.py:187
  8.3 3.7 %collective-permute-start.20 = (bf16[528,128]{1,0:T(8,128)(2,1)S(1)}, bf16[528,128]{1,0:T(8,128)(2,1)S(1)}, u32[]{:S(2)}, u32[]{:S(2)}) collective-permute-start(bf16[528,128]{1,0:T(8,128)(2,1)S(1)} %pad_maximum_fusion.2.unit), channel_id=1, source_target_pairs={{0,32},{32,0},{64,96},{96,64},{128,160},{160,128},{192,224},{224,1... | collective-permute-start | bytes 405512 | tf_op jit(solution)/shard_map/ppermute | solution.py:190
  12.0 0.0 collective-permute-done
  12.0 0.9 %pad_maximum_fusion.refs_0_ = bf16[1056,128]{1,0:T(8,128)(2,1)S(1)} fusion(bf16[528,128]{1,0:T(8,128)(2,1)S(1)} %collective-permute-done, bf16[16,128]{1,0:T(8,128)(2,1)S(1)} %broadcast_in_dim.14, bf16[512,128]{1,0:T(8,128)(2,1)} %bitcast.15), kind=kLoop, calls=%fused_computation | loop fusion | flops 811008 | bytes 540672 | tf_op jit(solution)/shard_map/concatenate | solution.py:193
  12.9 5.7 %collective-permute-start.1 = (bf16[1056,128]{1,0:T(8,128)(2,1)S(1)}, bf16[1056,128]{1,0:T(8,128)(2,1)S(1)}, u32[]{:S(2)}, u32[]{:S(2)}) collective-permute-start(bf16[1056,128]{1,0:T(8,128)(2,1)S(1)} %pad_maximum_fusion.refs_0_), channel_id=1, source_target_pairs={{0,4},{1,29},{2,6},{3,31},{4,8},{5,1},{6,10},{7,3},{8,12},{9,5},{1... | collective-permute-start | bytes 811016 | tf_op jit(solution)/shard_map/ppermute | solution.py:187
  18.6 0.0 collective-permute-start.11
  18.6 1.9 %collective-permute-start.6 = (bf16[528,128]{1,0:T(8,128)(2,1)S(1)}, bf16[528,128]{1,0:T(8,128)(2,1)S(1)}, u32[]{:S(2)}, u32[]{:S(2)}) collective-permute-start(bf16[528,128]{1,0:T(8,128)(2,1)S(1)} %collective-permute-done.5.refs_1_), channel_id=1, source_target_pairs={{0,4},{1,29},{2,6},{3,31},{4,8},{5,1},{6,10},{7,3},{8,12},{9,5},{1... | collective-permute-start | bytes 405512 | tf_op jit(solution)/shard_map/ppermute | solution.py:187
  20.5 0.0 collective-permute-done.20
  20.5 1.3 %collective-permute-start.21 = (bf16[1056,128]{1,0:T(8,128)(2,1)S(1)}, bf16[1056,128]{1,0:T(8,128)(2,1)S(1)}, u32[]{:S(2)}, u32[]{:S(2)}) collective-permute-start(bf16[1056,128]{1,0:T(8,128)(2,1)S(1)} %pad_maximum_fusion.1), channel_id=1, source_target_pairs={{0,64},{32,96},{64,0},{96,32},{128,192},{160,224},{192,128},{224,1... | collective-permute-start | bytes 811016 | tf_op jit(solution)/shard_map/ppermute | solution.py:190
  21.8 0.0 collective-permute-done.11.refs_2_
  21.8 1.6 %collective-permute-start.12 = (bf16[528,128]{1,0:T(8,128)(2,1)S(1)}, bf16[528,128]{1,0:T(8,128)(2,1)S(1)}, u32[]{:S(2)}, u32[]{:S(2)}) collective-permute-start(bf16[528,128]{1,0:T(8,128)(2,1)S(1)} %collective-permute-done.11.refs_2_), channel_id=1, source_target_pairs={{0,4},{1,29},{2,6},{3,31},{4,8},{5,1},{6,10},{7,3},{8,12},{9,5},{1... | collective-permute-start | bytes 405512 | tf_op jit(solution)/shard_map/ppermute | solution.py:187
  23.5 0.0 collective-permute-done.6.refs_4_
  23.5 3.1 %collective-permute-start.7 = (bf16[528,128]{1,0:T(8,128)(2,1)S(1)}, bf16[528,128]{1,0:T(8,128)(2,1)S(1)}, u32[]{:S(2)}, u32[]{:S(2)}) collective-permute-start(bf16[528,128]{1,0:T(8,128)(2,1)S(1)} %collective-permute-done.6.refs_4_), channel_id=1, source_target_pairs={{0,4},{1,29},{2,6},{3,31},{4,8},{5,1},{6,10},{7,3},{8,12},{9,5},{1... | collective-permute-start | bytes 405512 | tf_op jit(solution)/shard_map/ppermute | solution.py:187
  26.5 0.1 collective-permute-start.14
  26.7 0.0 collective-permute-done.12.refs_5_
  26.7 3.0 %collective-permute-start.16 = (bf16[528,128]{1,0:T(8,128)(2,1)S(1)}, bf16[528,128]{1,0:T(8,128)(2,1)S(1)}, u32[]{:S(2)}, u32[]{:S(2)}) collective-permute-start(bf16[528,128]{1,0:T(8,128)(2,1)S(1)} %collective-permute-done.12.refs_5_), channel_id=1, source_target_pairs={{0,4},{1,29},{2,6},{3,31},{4,8},{5,1},{6,10},{7,3},{8,12},{9,5},{1... | collective-permute-start | bytes 405512 | tf_op jit(solution)/shard_map/ppermute | solution.py:187
  29.7 0.0 collective-permute-done.1.refs_3_
  29.7 0.5 collective-permute-start.2
  30.3 0.0 collective-permute-done.7.refs_10_
  30.3 2.5 %collective-permute-start.18 = (bf16[528,128]{1,0:T(8,128)(2,1)S(1)}, bf16[528,128]{1,0:T(8,128)(2,1)S(1)}, u32[]{:S(2)}, u32[]{:S(2)}) collective-permute-start(bf16[528,128]{1,0:T(8,128)(2,1)S(1)} %collective-permute-done.7.refs_10_), channel_id=1, source_target_pairs={{0,1},{1,0},{2,3},{3,2},{4,5},{5,4},{6,7},{7,6},{8,9},{9,8},{10,11... | collective-permute-start | bytes 405512 | tf_op jit(solution)/shard_map/ppermute | solution.py:187
  32.8 0.0 collective-permute-done.21
  32.8 2.6 %collective-permute-start.22 = (bf16[2112,128]{1,0:T(8,128)(2,1)S(1)}, bf16[2112,128]{1,0:T(8,128)(2,1)S(1)}, u32[]{:S(2)}, u32[]{:S(2)}) collective-permute-start(bf16[2112,128]{1,0:T(8,128)(2,1)S(1)} %constant_dynamic-update-slice_fusion.refs_15_), channel_id=1, source_target_pairs={{0,192},{32,224},{64,128},{96,160},{128,64},{160,96},{192,0},{224,... | collective-permute-start | bytes 1622024 | tf_op jit(solution)/shard_map/ppermute | solution.py:190
  35.4 0.0 collective-permute-done.14.refs_7_
  35.4 0.3 collective-permute-start.13
  35.7 0.0 collective-permute-done.16.refs_11_
  35.7 0.2 collective-permute-start.15
  35.9 0.0 collective-permute-done.18.refs_13_
  35.9 0.5 collective-permute-start.8
  36.4 0.7 collective-permute-done.15.refs_8_
  37.1 0.3 collective-permute-start.19
  37.4 0.0 collective-permute-done.2.refs_9_
  37.4 0.2 collective-permute-start.17
  37.6 2.4 %collective-permute-done.8.refs_1_ = bf16[528,128]{1,0:T(8,128)(2,1)S(1)} collective-permute-done((bf16[528,128]{1,0:T(8,128)(2,1)S(1)}, bf16[528,128]{1,0:T(8,128)(2,1)S(1)}, u32[]{:S(2)}, u32[]{:S(2)}) %collective-permute-start.8) | collective-permute-done | bytes 135200 | tf_op jit(solution)/shard_map/ppermute | solution.py:187
  40.1 1.7 %collective-permute-start.3 = (bf16[1056,128]{1,0:T(8,128)(2,1)S(1)}, bf16[1056,128]{1,0:T(8,128)(2,1)S(1)}, u32[]{:S(2)}, u32[]{:S(2)}) collective-permute-start(bf16[1056,128]{1,0:T(8,128)(2,1)S(1)} %collective-permute-done.2.refs_9_), channel_id=1, source_target_pairs={{0,4},{1,29},{2,6},{3,31},{4,8},{5,1},{6,10},{7,3},{8,12},{9,5},{1... | collective-permute-start | bytes 811016 | tf_op jit(solution)/shard_map/ppermute | solution.py:187
  41.8 0.0 collective-permute-done.13.refs_6_
  41.8 0.0 collective-permute-start.23
  41.8 0.0 collective-permute-done.19.refs_14_
  41.8 1.2 %collective-permute-start.9 = (bf16[528,128]{1,0:T(8,128)(2,1)S(1)}, bf16[528,128]{1,0:T(8,128)(2,1)S(1)}, u32[]{:S(2)}, u32[]{:S(2)}) collective-permute-start(bf16[528,128]{1,0:T(8,128)(2,1)S(1)} %collective-permute-done.8.refs_1_), channel_id=1, source_target_pairs={{0,4},{1,29},{2,6},{3,31},{4,8},{5,1},{6,10},{7,3},{8,12},{9,5},{1... | collective-permute-start | bytes 405512 | tf_op jit(solution)/shard_map/ppermute | solution.py:187
  43.0 4.1 %collective-permute-done.23.refs_2_ = bf16[528,128]{1,0:T(8,128)(2,1)S(1)} collective-permute-done((bf16[528,128]{1,0:T(8,128)(2,1)S(1)}, bf16[528,128]{1,0:T(8,128)(2,1)S(1)}, u32[]{:S(2)}, u32[]{:S(2)}) %collective-permute-start.23) | collective-permute-done | bytes 135200 | tf_op jit(solution)/shard_map/ppermute | solution.py:187
  47.1 4.4 %collective-permute-start.25 = (bf16[528,128]{1,0:T(8,128)(2,1)S(1)}, bf16[528,128]{1,0:T(8,128)(2,1)S(1)}, u32[]{:S(2)}, u32[]{:S(2)}) collective-permute-start(bf16[528,128]{1,0:T(8,128)(2,1)S(1)} %collective-permute-done.8.refs_1_), channel_id=1, source_target_pairs={{0,1},{1,0},{2,3},{3,2},{4,5},{5,4},{6,7},{7,6},{8,9},{9,8},{10,11... | collective-permute-start | bytes 405512 | tf_op jit(solution)/shard_map/ppermute | solution.py:187
  51.5 0.0 collective-permute-done.9.beside
  51.5 1.4 %collective-permute-start.26 = (bf16[528,128]{1,0:T(8,128)(2,1)S(1)}, bf16[528,128]{1,0:T(8,128)(2,1)S(1)}, u32[]{:S(2)}, u32[]{:S(2)}) collective-permute-start(bf16[528,128]{1,0:T(8,128)(2,1)S(1)} %collective-permute-done.23.refs_2_), channel_id=1, source_target_pairs={{0,1},{1,0},{2,3},{3,2},{4,5},{5,4},{6,7},{7,6},{8,9},{9,8},{10,11... | collective-permute-start | bytes 405512 | tf_op jit(solution)/shard_map/ppermute | solution.py:187
  53.0 0.0 collective-permute-done.17.refs_12_
  53.0 0.0 collective-permute-start.10
  53.0 0.0 collective-permute-done.3.refs_0_
  53.0 0.5 collective-permute-start.24
  53.5 0.0 collective-permute-done.22.refs_16_
  53.5 0.0 collective-permute-start.4
  53.5 4.8 %shard_map.55 = (bf16[8,256,1152]{2,1,0:T(8,128)(2,1)S(1)}, f32[256,1024]{1,0:T(8,128)S(1)}) custom-call(bf16[1056,128]{1,0:T(8,128)(2,1)S(1)} %pad_maximum_fusion.refs_0_, bf16[528,128]{1,0:T(8,128)(2,1)S(1)} %collective-permute-done.5.refs_1_, bf16[528,128]{1,0:T(8,128)(2,1)S(1)} %collective-permute-done.11.refs_2_, ...), custom_call_target="tpu_custom_call" | custom-call | flops 3221225472 | bytes 25165824 | tf_op jit(solution)/shard_map/pallas_call | solution.py:209
  58.3 0.0 collective-permute-done.25.refs_4_
  58.3 0.0 collective-permute-done.26.refs_5_
  58.3 0.0 collective-permute-done.24.refs_3_
  58.3 1.8 %shard_map.56.before = f32[256,1024]{1,0:T(8,128)S(1)} custom-call(bf16[1056,128]{1,0:T(8,128)(2,1)S(1)} %collective-permute-done.3.refs_0_, bf16[528,128]{1,0:T(8,128)(2,1)S(1)} %collective-permute-done.8.refs_1_, bf16[528,128]{1,0:T(8,128)(2,1)S(1)} %collective-permute-done.23.refs_2_, bf16[1056,128]{1,0:T(8,128)(2,1)S(1)} %collective-permute-done.24.refs_3_, ...), custom_call_target="tpu_custom_call" | custom-call | flops 1073741824 | bytes 8388608 | tf_op jit(solution)/shard_map/pallas_call | solution.py:218
  60.2 0.0 collective-permute-done.10.beside_pair
  60.2 2.1 %shard_map.57 = (f32[8,128,128]{2,1,0:T(8,128)S(1)}, f32[32,8,128]{2,1,0:T(8,128)S(1)}) custom-call(bf16[528,128]{1,0:T(8,128)(2,1)S(1)} %pad_maximum_fusion.2.unit, bf16[1056,128]{1,0:T(8,128)(2,1)S(1)} %collective-permute-done.4.pair, bf16[528,128]{1,0:T(8,128)(2,1)S(1)} %collective-permute-done.9.beside, ...), custom_call_target="tpu_custom_call" | custom-call | flops 536870912 | bytes 4194304 | tf_op jit(solution)/shard_map/pallas_call | solution.py:227
  62.3 16.2 %all_to_all.5.sums = f32[32,8,128]{2,1,0:T(8,128)S(1)} all-to-all(f32[32,8,128]{2,1,0:T(8,128)S(1)} %get-tuple-element.14), channel_id=1, replica_groups=mesh['group'=8,'loop'=32] {'loop'}, dimensions={0} | all-to-all | bytes 262144 | tf_op jit(solution)/shard_map/all_to_all | solution.py:241
  78.6 1.9 %shard_map.58 = f32[8,128,128]{2,1,0:T(8,128)} custom-call(bf16[528,128]{1,0:T(8,128)(2,1)S(1)} %pad_maximum_fusion.2.unit, f32[8,128,128]{2,1,0:T(8,128)S(1)} %get-tuple-element.13.squares, f32[32,8,128]{2,1,0:T(8,128)S(1)} %all_to_all.5.sums), custom_call_target="tpu_custom_call" | custom-call | tf_op jit(solution)/shard_map/pallas_call | solution.py:242
  (5 shorter events, 0.1 us)
Async XLA Ops:
  3.7 4.6 %collective-permute-start.5 = (bf16[528,128]{1,0:T(8,128)(2,1)S(1)}, bf16[528,128]{1,0:T(8,128)(2,1)S(1)}, u32[]{:S(2)}, u32[]{:S(2)}) collective-permute-start(bf16[528,128]{1,0:T(8,128)(2,1)S(1)} %pad_maximum_fusion.2.unit), channel_id=1, source_target_pairs={{0,2},{1,3},{2,0},{3,1},{4,6},{5,7},{6,4},{7,5},{8,10},{9,11},{10,... | collective-permute-start | bytes 405512 | tf_op jit(solution)/shard_map/ppermute | solution.py:187
  5.9 6.1 %collective-permute-start = (bf16[528,128]{1,0:T(8,128)(2,1)S(1)}, bf16[528,128]{1,0:T(8,128)(2,1)S(1)}, u32[]{:S(2)}, u32[]{:S(2)}) collective-permute-start(bf16[528,128]{1,0:T(8,128)(2,1)S(1)} %pad_maximum_fusion.2.unit), channel_id=1, source_target_pairs={{0,1},{1,0},{2,3},{3,2},{4,5},{5,4},{6,7},{7,6},{8,9},{9,8},{10,11... | collective-permute-start | bytes 405512 | tf_op jit(solution)/shard_map/ppermute | solution.py:187
  8.3 12.2 %collective-permute-start.20 = (bf16[528,128]{1,0:T(8,128)(2,1)S(1)}, bf16[528,128]{1,0:T(8,128)(2,1)S(1)}, u32[]{:S(2)}, u32[]{:S(2)}) collective-permute-start(bf16[528,128]{1,0:T(8,128)(2,1)S(1)} %pad_maximum_fusion.2.unit), channel_id=1, source_target_pairs={{0,32},{32,0},{64,96},{96,64},{128,160},{160,128},{192,224},{224,1... | collective-permute-start | bytes 405512 | tf_op jit(solution)/shard_map/ppermute | solution.py:190
  12.9 16.8 %collective-permute-start.1 = (bf16[1056,128]{1,0:T(8,128)(2,1)S(1)}, bf16[1056,128]{1,0:T(8,128)(2,1)S(1)}, u32[]{:S(2)}, u32[]{:S(2)}) collective-permute-start(bf16[1056,128]{1,0:T(8,128)(2,1)S(1)} %pad_maximum_fusion.refs_0_), channel_id=1, source_target_pairs={{0,4},{1,29},{2,6},{3,31},{4,8},{5,1},{6,10},{7,3},{8,12},{9,5},{1... | collective-permute-start | bytes 811016 | tf_op jit(solution)/shard_map/ppermute | solution.py:187
  18.6 3.3 %collective-permute-start.11 = (bf16[528,128]{1,0:T(8,128)(2,1)S(1)}, bf16[528,128]{1,0:T(8,128)(2,1)S(1)}, u32[]{:S(2)}, u32[]{:S(2)}) collective-permute-start(bf16[528,128]{1,0:T(8,128)(2,1)S(1)} %collective-permute-done.5.refs_1_), channel_id=1, source_target_pairs={{0,1},{1,0},{2,3},{3,2},{4,5},{5,4},{6,7},{7,6},{8,9},{9,8},{10,11... | collective-permute-start | bytes 405512 | tf_op jit(solution)/shard_map/ppermute | solution.py:187
  18.6 4.9 %collective-permute-start.6 = (bf16[528,128]{1,0:T(8,128)(2,1)S(1)}, bf16[528,128]{1,0:T(8,128)(2,1)S(1)}, u32[]{:S(2)}, u32[]{:S(2)}) collective-permute-start(bf16[528,128]{1,0:T(8,128)(2,1)S(1)} %collective-permute-done.5.refs_1_), channel_id=1, source_target_pairs={{0,4},{1,29},{2,6},{3,31},{4,8},{5,1},{6,10},{7,3},{8,12},{9,5},{1... | collective-permute-start | bytes 405512 | tf_op jit(solution)/shard_map/ppermute | solution.py:187
  20.5 12.3 %collective-permute-start.21 = (bf16[1056,128]{1,0:T(8,128)(2,1)S(1)}, bf16[1056,128]{1,0:T(8,128)(2,1)S(1)}, u32[]{:S(2)}, u32[]{:S(2)}) collective-permute-start(bf16[1056,128]{1,0:T(8,128)(2,1)S(1)} %pad_maximum_fusion.1), channel_id=1, source_target_pairs={{0,64},{32,96},{64,0},{96,32},{128,192},{160,224},{192,128},{224,1... | collective-permute-start | bytes 811016 | tf_op jit(solution)/shard_map/ppermute | solution.py:190
  21.8 4.9 %collective-permute-start.12 = (bf16[528,128]{1,0:T(8,128)(2,1)S(1)}, bf16[528,128]{1,0:T(8,128)(2,1)S(1)}, u32[]{:S(2)}, u32[]{:S(2)}) collective-permute-start(bf16[528,128]{1,0:T(8,128)(2,1)S(1)} %collective-permute-done.11.refs_2_), channel_id=1, source_target_pairs={{0,4},{1,29},{2,6},{3,31},{4,8},{5,1},{6,10},{7,3},{8,12},{9,5},{1... | collective-permute-start | bytes 405512 | tf_op jit(solution)/shard_map/ppermute | solution.py:187
  23.5 6.8 %collective-permute-start.7 = (bf16[528,128]{1,0:T(8,128)(2,1)S(1)}, bf16[528,128]{1,0:T(8,128)(2,1)S(1)}, u32[]{:S(2)}, u32[]{:S(2)}) collective-permute-start(bf16[528,128]{1,0:T(8,128)(2,1)S(1)} %collective-permute-done.6.refs_4_), channel_id=1, source_target_pairs={{0,4},{1,29},{2,6},{3,31},{4,8},{5,1},{6,10},{7,3},{8,12},{9,5},{1... | collective-permute-start | bytes 405512 | tf_op jit(solution)/shard_map/ppermute | solution.py:187
  26.5 8.8 %collective-permute-start.14 = (bf16[528,128]{1,0:T(8,128)(2,1)S(1)}, bf16[528,128]{1,0:T(8,128)(2,1)S(1)}, u32[]{:S(2)}, u32[]{:S(2)}) collective-permute-start(bf16[528,128]{1,0:T(8,128)(2,1)S(1)} %collective-permute-done.6.refs_4_), channel_id=1, source_target_pairs={{0,1},{1,0},{2,3},{3,2},{4,5},{5,4},{6,7},{7,6},{8,9},{9,8},{10,11... | collective-permute-start | bytes 405512 | tf_op jit(solution)/shard_map/ppermute | solution.py:187
  26.7 9.0 %collective-permute-start.16 = (bf16[528,128]{1,0:T(8,128)(2,1)S(1)}, bf16[528,128]{1,0:T(8,128)(2,1)S(1)}, u32[]{:S(2)}, u32[]{:S(2)}) collective-permute-start(bf16[528,128]{1,0:T(8,128)(2,1)S(1)} %collective-permute-done.12.refs_5_), channel_id=1, source_target_pairs={{0,4},{1,29},{2,6},{3,31},{4,8},{5,1},{6,10},{7,3},{8,12},{9,5},{1... | collective-permute-start | bytes 405512 | tf_op jit(solution)/shard_map/ppermute | solution.py:187
  29.7 7.7 %collective-permute-start.2 = (bf16[1056,128]{1,0:T(8,128)(2,1)S(1)}, bf16[1056,128]{1,0:T(8,128)(2,1)S(1)}, u32[]{:S(2)}, u32[]{:S(2)}) collective-permute-start(bf16[1056,128]{1,0:T(8,128)(2,1)S(1)} %collective-permute-done.1.refs_3_), channel_id=1, source_target_pairs={{0,4},{1,29},{2,6},{3,31},{4,8},{5,1},{6,10},{7,3},{8,12},{9,5},{1... | collective-permute-start | bytes 811016 | tf_op jit(solution)/shard_map/ppermute | solution.py:187
  30.3 5.6 %collective-permute-start.18 = (bf16[528,128]{1,0:T(8,128)(2,1)S(1)}, bf16[528,128]{1,0:T(8,128)(2,1)S(1)}, u32[]{:S(2)}, u32[]{:S(2)}) collective-permute-start(bf16[528,128]{1,0:T(8,128)(2,1)S(1)} %collective-permute-done.7.refs_10_), channel_id=1, source_target_pairs={{0,1},{1,0},{2,3},{3,2},{4,5},{5,4},{6,7},{7,6},{8,9},{9,8},{10,11... | collective-permute-start | bytes 405512 | tf_op jit(solution)/shard_map/ppermute | solution.py:187
  32.8 20.7 %collective-permute-start.22 = (bf16[2112,128]{1,0:T(8,128)(2,1)S(1)}, bf16[2112,128]{1,0:T(8,128)(2,1)S(1)}, u32[]{:S(2)}, u32[]{:S(2)}) collective-permute-start(bf16[2112,128]{1,0:T(8,128)(2,1)S(1)} %constant_dynamic-update-slice_fusion.refs_15_), channel_id=1, source_target_pairs={{0,192},{32,224},{64,128},{96,160},{128,64},{160,96},{192,0},{224,... | collective-permute-start | bytes 1622024 | tf_op jit(solution)/shard_map/ppermute | solution.py:190
  35.4 6.4 %collective-permute-start.13 = (bf16[1056,128]{1,0:T(8,128)(2,1)S(1)}, bf16[1056,128]{1,0:T(8,128)(2,1)S(1)}, u32[]{:S(2)}, u32[]{:S(2)}) collective-permute-start(bf16[1056,128]{1,0:T(8,128)(2,1)S(1)} %collective-permute-done.1.refs_3_), channel_id=1, source_target_pairs={{0,1},{1,0},{2,3},{3,2},{4,5},{5,4},{6,7},{7,6},{8,9},{9,8},{10,11... | collective-permute-start | bytes 811016 | tf_op jit(solution)/shard_map/ppermute | solution.py:187
  35.7 1.5 %collective-permute-start.15 = (bf16[528,128]{1,0:T(8,128)(2,1)S(1)}, bf16[528,128]{1,0:T(8,128)(2,1)S(1)}, u32[]{:S(2)}, u32[]{:S(2)}) collective-permute-start(bf16[528,128]{1,0:T(8,128)(2,1)S(1)} %collective-permute-done.12.refs_5_), channel_id=1, source_target_pairs={{0,1},{1,0},{2,3},{3,2},{4,5},{5,4},{6,7},{7,6},{8,9},{9,8},{10,11... | collective-permute-start | bytes 405512 | tf_op jit(solution)/shard_map/ppermute | solution.py:187
  35.9 4.2 %collective-permute-start.8 = (bf16[528,128]{1,0:T(8,128)(2,1)S(1)}, bf16[528,128]{1,0:T(8,128)(2,1)S(1)}, u32[]{:S(2)}, u32[]{:S(2)}) collective-permute-start(bf16[528,128]{1,0:T(8,128)(2,1)S(1)} %collective-permute-done.7.refs_10_), channel_id=1, source_target_pairs={{0,4},{1,29},{2,6},{3,31},{4,8},{5,1},{6,10},{7,3},{8,12},{9,5},{1... | collective-permute-start | bytes 405512 | tf_op jit(solution)/shard_map/ppermute | solution.py:187
  37.1 4.7 %collective-permute-start.19 = (bf16[528,128]{1,0:T(8,128)(2,1)S(1)}, bf16[528,128]{1,0:T(8,128)(2,1)S(1)}, u32[]{:S(2)}, u32[]{:S(2)}) collective-permute-start(bf16[528,128]{1,0:T(8,128)(2,1)S(1)} %collective-permute-done.16.refs_11_), channel_id=1, source_target_pairs={{0,1},{1,0},{2,3},{3,2},{4,5},{5,4},{6,7},{7,6},{8,9},{9,8},{10,11... | collective-permute-start | bytes 405512 | tf_op jit(solution)/shard_map/ppermute | solution.py:187
  37.4 15.6 %collective-permute-start.17 = (bf16[1056,128]{1,0:T(8,128)(2,1)S(1)}, bf16[1056,128]{1,0:T(8,128)(2,1)S(1)}, u32[]{:S(2)}, u32[]{:S(2)}) collective-permute-start(bf16[1056,128]{1,0:T(8,128)(2,1)S(1)} %collective-permute-done.2.refs_9_), channel_id=1, source_target_pairs={{0,1},{1,0},{2,3},{3,2},{4,5},{5,4},{6,7},{7,6},{8,9},{9,8},{10,11... | collective-permute-start | bytes 811016 | tf_op jit(solution)/shard_map/ppermute | solution.py:187
  40.1 12.9 %collective-permute-start.3 = (bf16[1056,128]{1,0:T(8,128)(2,1)S(1)}, bf16[1056,128]{1,0:T(8,128)(2,1)S(1)}, u32[]{:S(2)}, u32[]{:S(2)}) collective-permute-start(bf16[1056,128]{1,0:T(8,128)(2,1)S(1)} %collective-permute-done.2.refs_9_), channel_id=1, source_target_pairs={{0,4},{1,29},{2,6},{3,31},{4,8},{5,1},{6,10},{7,3},{8,12},{9,5},{1... | collective-permute-start | bytes 811016 | tf_op jit(solution)/shard_map/ppermute | solution.py:187
  41.8 5.3 %collective-permute-start.23 = (bf16[528,128]{1,0:T(8,128)(2,1)S(1)}, bf16[528,128]{1,0:T(8,128)(2,1)S(1)}, u32[]{:S(2)}, u32[]{:S(2)}) collective-permute-start(bf16[528,128]{1,0:T(8,128)(2,1)S(1)} %collective-permute-done.16.refs_11_), channel_id=1, source_target_pairs={{0,4},{1,29},{2,6},{3,31},{4,8},{5,1},{6,10},{7,3},{8,12},{9,5},{1... | collective-permute-start | bytes 405512 | tf_op jit(solution)/shard_map/ppermute | solution.py:187
  41.8 9.7 %collective-permute-start.9 = (bf16[528,128]{1,0:T(8,128)(2,1)S(1)}, bf16[528,128]{1,0:T(8,128)(2,1)S(1)}, u32[]{:S(2)}, u32[]{:S(2)}) collective-permute-start(bf16[528,128]{1,0:T(8,128)(2,1)S(1)} %collective-permute-done.8.refs_1_), channel_id=1, source_target_pairs={{0,4},{1,29},{2,6},{3,31},{4,8},{5,1},{6,10},{7,3},{8,12},{9,5},{1... | collective-permute-start | bytes 405512 | tf_op jit(solution)/shard_map/ppermute | solution.py:187
  47.1 11.2 %collective-permute-start.25 = (bf16[528,128]{1,0:T(8,128)(2,1)S(1)}, bf16[528,128]{1,0:T(8,128)(2,1)S(1)}, u32[]{:S(2)}, u32[]{:S(2)}) collective-permute-start(bf16[528,128]{1,0:T(8,128)(2,1)S(1)} %collective-permute-done.8.refs_1_), channel_id=1, source_target_pairs={{0,1},{1,0},{2,3},{3,2},{4,5},{5,4},{6,7},{7,6},{8,9},{9,8},{10,11... | collective-permute-start | bytes 405512 | tf_op jit(solution)/shard_map/ppermute | solution.py:187
  51.5 6.8 %collective-permute-start.26 = (bf16[528,128]{1,0:T(8,128)(2,1)S(1)}, bf16[528,128]{1,0:T(8,128)(2,1)S(1)}, u32[]{:S(2)}, u32[]{:S(2)}) collective-permute-start(bf16[528,128]{1,0:T(8,128)(2,1)S(1)} %collective-permute-done.23.refs_2_), channel_id=1, source_target_pairs={{0,1},{1,0},{2,3},{3,2},{4,5},{5,4},{6,7},{7,6},{8,9},{9,8},{10,11... | collective-permute-start | bytes 405512 | tf_op jit(solution)/shard_map/ppermute | solution.py:187
  53.0 7.2 %collective-permute-start.10 = (bf16[528,128]{1,0:T(8,128)(2,1)S(1)}, bf16[528,128]{1,0:T(8,128)(2,1)S(1)}, u32[]{:S(2)}, u32[]{:S(2)}) collective-permute-start(bf16[528,128]{1,0:T(8,128)(2,1)S(1)} %collective-permute-done.9.beside), channel_id=1, source_target_pairs={{0,1},{1,0},{2,3},{3,2},{4,5},{5,4},{6,7},{7,6},{8,9},{9,8},{10,11... | collective-permute-start | bytes 405512 | tf_op jit(solution)/shard_map/ppermute | solution.py:187
  53.0 5.3 %collective-permute-start.24 = (bf16[1056,128]{1,0:T(8,128)(2,1)S(1)}, bf16[1056,128]{1,0:T(8,128)(2,1)S(1)}, u32[]{:S(2)}, u32[]{:S(2)}) collective-permute-start(bf16[1056,128]{1,0:T(8,128)(2,1)S(1)} %collective-permute-done.3.refs_0_), channel_id=1, source_target_pairs={{0,1},{1,0},{2,3},{3,2},{4,5},{5,4},{6,7},{7,6},{8,9},{9,8},{10,11... | collective-permute-start | bytes 811016 | tf_op jit(solution)/shard_map/ppermute | solution.py:187
  53.5 6.7 %collective-permute-start.4 = (bf16[1056,128]{1,0:T(8,128)(2,1)S(1)}, bf16[1056,128]{1,0:T(8,128)(2,1)S(1)}, u32[]{:S(2)}, u32[]{:S(2)}) collective-permute-start(bf16[1056,128]{1,0:T(8,128)(2,1)S(1)} %collective-permute-done.3.refs_0_), channel_id=1, source_target_pairs={{0,4},{1,29},{2,6},{3,31},{4,8},{5,1},{6,10},{7,3},{8,12},{9,5},{1... | collective-permute-start | bytes 811016 | tf_op jit(solution)/shard_map/ppermute | solution.py:187

commit v3 on v2

--- a/solution.py
+++ b/solution.py
@@ -31,6 +31,7 @@
 
 CORE = loop_perm(lambda z, y, c: (z, y, 1 - c))
 YLO = loop_perm(lambda z, y, c: (z, 1 - y, c))
+DIAGONAL = loop_perm(lambda z, y, c: (z, 1 - y, 1 - c))
 RING = loop_perm(lambda z, y, c: (z + 1 - 2 * c, y, c))
 YHI = group_perm(lambda x, y: (x, 1 - y))
 XNEAR = group_perm(lambda x, y: (x ^ 1, y))
@@ -38,12 +39,12 @@
 
 
 def scalars(ref, base, first, count):
-    marks = ref[base + BODY : base + UNIT, :].astype(F32)
+    marks = ref[base : base + 16, :].astype(F32)
     return [jnp.max(marks[s : s + 1, :]).astype(jnp.int32) for s in range(first, first + count)]
 
 
 def place(dst, ref, base, row):
-    for s, code in enumerate(scalars(ref, base, 0, SLOTS)):
+    for s, code in enumerate(scalars(ref, base + BODY, 0, SLOTS)):
         r = (code >= 9).astype(jnp.int32)
         c = code - 9 * r
         rows = pl.ds(pl.multiple_of(row + r * TILE, TILE), TILE)
@@ -67,18 +68,18 @@
 
 
 def round_units(refs, y, c):
-    pair, beside, beside_pair = refs
+    pair, beside = refs
     return (
         (pair, 0, y, c),
         (pair, UNIT, y, 1 - c),
         (beside, 0, 1 - y, c),
-        (beside_pair, 0, 1 - y, 1 - c),
+        (beside, UNIT, 1 - y, 1 - c),
     )
 
 
 def begin(*refs):
-    own, rounds, left = refs[:3], refs[3:15], refs[15:17]
-    dense_left, product, dense_right = refs[17:]
+    own, rounds, left = refs[:2], refs[2:10], refs[10:12]
+    dense_left, product, dense_right = refs[12:]
     z, y, c, x, h = where_am_i()
     dense_left[...] = jnp.zeros_like(dense_left)
     for k in range(8):
@@ -87,7 +88,7 @@
     product[...] = multiply(dense_left, dense_right, z, round_units(own, y, c))
     sign = 1 - 2 * c
     for r in (1, 2):
-        near, far = rounds[6 * r - 6 : 6 * r - 3], rounds[6 * r - 3 : 6 * r]
+        near, far = rounds[4 * r - 4 : 4 * r - 2], rounds[4 * r - 2 : 4 * r]
         product[...] += multiply(
             dense_left, dense_right, (z - sign * r) & 7, round_units(near, y, c)
         )
@@ -97,8 +98,8 @@
 
 
 def proceed(*refs):
-    near, far = refs[:3], refs[3:6]
-    dense_left, before, product, dense_right = refs[6:]
+    near, far = refs[:2], refs[2:4]
+    dense_left, before, product, dense_right = refs[4:]
     z, y, c, _, _ = where_am_i()
     sign = 1 - 2 * c
     product[...] = before[...] + multiply(
@@ -109,14 +110,14 @@
     )
 
 
-def finish(unit, pair, beside, beside_pair, dense_left, before, squares, sums, dense_right, product, held, sem):
+def finish(codes, pair, beside, dense_left, before, squares, sums, dense_right, product, held, sem):
     z, y, c, _, _ = where_am_i()
-    units = round_units((pair, beside, beside_pair), y, c)
+    units = round_units((pair, beside), y, c)
     product[...] = before[...] + multiply(dense_left, dense_right, (z + 4) & 7, units)
     column = lax.broadcasted_iota(jnp.int32, (8, TILE), 0)
     total = jnp.zeros((8, TILE), F32)
     copies = []
-    for s, code in enumerate(scalars(unit, 0, SLOTS, 8)):
+    for s, code in enumerate(scalars(codes, 0, 0, 8)):
         used = code < 16
         p = code & 15
         rows = pl.ds(pl.multiple_of((p >> 3) * TILE, TILE), TILE)
@@ -134,20 +135,20 @@
         copy.wait()
 
 
-def rescale(unit, squares, sums, out, marks, inside, parts, done, sem_in, sem_out):
+def rescale(codes, squares, sums, out, marks, inside, parts, done, sem_in, sem_out):
     ins = [pltpu.make_async_copy(sums, parts, sem_in.at[8])]
-    ins.append(pltpu.make_async_copy(unit.at[pl.ds(BODY, 16)], marks, sem_in.at[9]))
+    ins.append(pltpu.make_async_copy(codes, marks, sem_in.at[9]))
     ins += [pltpu.make_async_copy(squares.at[s], inside.at[s], sem_in.at[s]) for s in range(8)]
     for copy in ins:
         copy.start()
     ins[1].wait()
-    codes = scalars(marks, -BODY, SLOTS, 8)
+    at = scalars(marks, 0, 0, 8)
     ins[0].wait()
     factor = 8192.0 / jnp.sum(parts[...], axis=0)
     column = lax.broadcasted_iota(jnp.int32, (8, TILE), 0)
     outs = []
     for s in range(8):
-        pick = jnp.where(column == (codes[s] & 7), factor, 0.0)
+        pick = jnp.where(column == (at[s] & 7), factor, 0.0)
         pick = jnp.sum(pick, axis=0, keepdims=True)
         ins[2 + s].wait()
         done[s] = inside[s] * pick
@@ -172,13 +173,9 @@
 
 
 def shards(tile_values, tile_coords, tile_counts, result_coords, result_counts):
-    slot = jnp.arange(SLOTS, dtype=jnp.int32)
-    at = tile_coords[0, 0]
-    tile_code = jnp.where(slot < tile_counts[0, 0], at + (at >> 3), 8)
-    slot = jnp.arange(8, dtype=jnp.int32)
-    at = result_coords[0, 0]
-    result_code = jnp.where(slot < result_counts[0, 0], at, at + 16)
-    code = jnp.concatenate([tile_code, result_code, tile_code]).astype(BF16)
+    slot = jnp.arange(16, dtype=jnp.int32)
+    at = jnp.pad(tile_coords[0, 0], (0, 12))
+    code = jnp.where(slot < tile_counts[0, 0], at + (at >> 3), 8).astype(BF16)
     unit = jnp.concatenate(
         [tile_values.reshape(BODY, TILE), jnp.broadcast_to(code[:, None], (16, TILE))]
     )
@@ -189,26 +186,29 @@
     def across(perm, v):
         return lax.ppermute(v, "group", perm)
 
-    beside = along(YLO, unit)
-    pair = jnp.concatenate([unit, along(CORE, unit)])
-    beside_pair = along(CORE, beside)
-    later, _ = lax.optimization_barrier((unit, beside))
+    beside, crossed = along(YLO, unit), along(DIAGONAL, unit)
+    first = jnp.concatenate([unit, along(CORE, unit)])
+    beside, crossed, _ = lax.optimization_barrier((beside, crossed, first))
+    second = jnp.concatenate([beside, crossed])
+    later, beside_later, _ = lax.optimization_barrier((unit, result_coords, beside))
     row = jnp.concatenate([later, across(YHI, later)])
     row = jnp.concatenate([row, across(XNEAR, row)])
     left = [row, across(XMIRROR, row)]
-
-    streams = [pair, beside, beside_pair]
+    at = jnp.pad(beside_later[0, 0], (0, 8))
+    code = jnp.where(slot < result_counts[0, 0], at, at + 16).astype(BF16)
+    codes = jnp.broadcast_to(code[:, None], (16, TILE))
+
+    streams = [first, second]
     right = [streams]
     for r in range(3):
         streams = [along(RING, v) for v in streams]
         right += [streams, [along(CORE, v) for v in streams]]
-    last = [along(RING, v) for v in streams[:2]]
-    last.append(along(CORE, last[1]))
+    last = [along(RING, v) for v in streams]
 
     limit = pltpu.CompilerParams(vmem_limit_bytes=24 * 2**20)
     dense_left, product = pl.pallas_call(
         begin,
-        in_specs=[WHOLE] * 17,
+        in_specs=[WHOLE] * 12,
         out_specs=[WHOLE] * 2,
         out_shape=[DENSE_LEFT, PRODUCT],
         scratch_shapes=[DENSE_RIGHT],
@@ -217,7 +217,7 @@
     )(*sum(right[:5], []), *left)
     product = pl.pallas_call(
         proceed,
-        in_specs=[WHOLE] * 8,
+        in_specs=[WHOLE] * 6,
         out_specs=WHOLE,
         out_shape=PRODUCT,
         scratch_shapes=[DENSE_RIGHT],
@@ -226,7 +226,7 @@
     )(*sum(right[5:], []), dense_left, product)
     squares, sums = pl.pallas_call(
         finish,
-        in_specs=[WHOLE] * 6,
+        in_specs=[WHOLE] * 5,
         out_specs=[AWAY, WHOLE],
         out_shape=[jax.ShapeDtypeStruct(TILES, F32), jax.ShapeDtypeStruct((32, 8, TILE), F32)],
         scratch_shapes=[
@@ -237,7 +237,7 @@
         ],
         compiler_params=limit,
         cost_estimate=cost(1),
-    )(unit, *last, dense_left, product)
+    )(codes, *last, dense_left, product)
     sums = lax.all_to_all(sums, "loop", 0, 0, tiled=True)
     out = pl.pallas_call(
         rescale,
@@ -253,7 +253,7 @@
             pltpu.SemaphoreType.DMA((8,)),
         ],
         compiler_params=limit,
-    )(unit, squares, sums)
+    )(codes, squares, sums)
     return out[None, None]
 
 

time: 80.8 us -> 74.3 us (0.920)
  starting transfers between devices: 40.3 us -> 32.7 us
  waiting for transfers between devices: 8.44 us -> 9.72 us
    ppermute x24 -> x17, starting transfers between devices: 32.8 us -> 27.7 us  [along(): return lax.ppermute(v, 'loop', perm)]
    ppermute x3, starting transfers between devices: 7.53 us -> 5.04 us  [across(): return lax.ppermute(v, 'group', perm)]
    convert_element_type x0 -> x2, other arithmetic: none -> 1.33 us  [the longest x1 0.66 us: shards(): code = jnp.where(slot < tile_counts[0, 0], at + (at >> 3), 8).astype(BF16)]
    another operation x2 -> x0, other arithmetic: 1.32 us -> none
    ppermute x24 -> x17, waiting for transfers between devices: 8.43 us -> 9.71 us  [along(): return lax.ppermute(v, 'loop', perm)]
  transfers between devices with their start and end apart: 27 -> 20, of which waited for: 4 -> 3; matrix products, arithmetic and copies ran while one was open for 1% -> 2% of each run, Pallas kernels for 8% -> 9%
where the time goes in v3:
time: 74.3 us; the launch traced here: 74.1 us
  starting transfers between devices  32.7 us (44%)
  blocking collectives  16.1 us (22%)
  Pallas kernels  10.5 us (14%)
  waiting for transfers between devices  9.72 us (13%)
  other arithmetic  3.18 us (4%)
  between operations  1.58 us (2%)
    ppermute x17, starting transfers between devices, along(): return lax.ppermute(v, 'loop', perm)  27.7 us
    all_to_all x1, blocking collectives, shards(): sums = lax.all_to_all(sums, 'loop', 0, 0, tiled=True)  16.1 us
    ppermute x17, waiting for transfers between devices, along(): return lax.ppermute(v, 'loop', perm)  9.71 us
    ppermute x3, starting transfers between devices, across(): return lax.ppermute(v, 'group', perm)  5.04 us
    pallas_call x1, Pallas kernels, shards(): pl.pallas_call(begin, in_specs=[WHOLE] * 12, out_specs=[WHOLE] * 2, out_s...  4.8 us
    pallas_call x1, Pallas kernels, shards(): pl.pallas_call(finish, in_specs=[WHOLE] * 5, out_specs=[AWAY, WHOLE], out...  1.98 us
    pallas_call x1, Pallas kernels, shards(): pl.pallas_call(rescale, in_specs=[AWAY] * 3, out_specs=AWAY, out_shape=ja...  1.94 us
    pallas_call x1, Pallas kernels, shards(): pl.pallas_call(proceed, in_specs=[WHOLE] * 6, out_specs=WHOLE, out_shape=...  1.81 us
  transfers between devices with their start and end apart: 20, of which 3 were waited for; matrix products, arithmetic and copies ran while one was open for 2% of the time, Pallas kernels for 9%

profile of v3, /device:TPU:1, one launch (start us, length us, event | category | flops | bytes accessed | tf_op | source)
XLA Modules:
  0.0 74.1 jit_solution(11100301680328445892)
XLA Ops:
  0.7 0.7 fusion
  1.3 0.1 broadcast_in_dim.20
  1.4 0.9 %pad_maximum_fusion.2 = bf16[528,128]{1,0:T(8,128)(2,1)S(1)} fusion(bf16[16,128]{1,0:T(8,128)(2,1)S(1)} %broadcast_in_dim.20, bf16[512,128]{1,0:T(8,128)(2,1)} %bitcast.8), kind=kLoop, calls=%fused_computation.2 | loop fusion | flops 270336 | bytes 270336 | tf_op jit(solution)/shard_map/concatenate | solution.py:179
  2.3 3.3 %collective-permute-start.2 = (bf16[528,128]{1,0:T(8,128)(2,1)S(1)}, bf16[528,128]{1,0:T(8,128)(2,1)S(1)}, u32[]{:S(2)}, u32[]{:S(2)}) collective-permute-start(bf16[528,128]{1,0:T(8,128)(2,1)S(1)} %pad_maximum_fusion.2), channel_id=1, source_target_pairs={{0,1},{1,0},{2,3},{3,2},{4,5},{5,4},{6,7},{7,6},{8,9},{9,8},{10,11... | collective-permute-start | bytes 405512 | tf_op jit(solution)/shard_map/ppermute | solution.py:184
  5.6 0.0 collective-permute-start
  5.6 1.7 %collective-permute-start.1 = (bf16[528,128]{1,0:T(8,128)(2,1)S(1)}, bf16[528,128]{1,0:T(8,128)(2,1)S(1)}, u32[]{:S(2)}, u32[]{:S(2)}) collective-permute-start(bf16[528,128]{1,0:T(8,128)(2,1)S(1)} %pad_maximum_fusion.2), channel_id=1, source_target_pairs={{0,3},{1,2},{2,1},{3,0},{4,7},{5,6},{6,5},{7,4},{8,11},{9,10},{10,... | collective-permute-start | bytes 405512 | tf_op jit(solution)/shard_map/ppermute | solution.py:184
  7.4 0.0 collective-permute-done.2
  7.4 0.9 %pad_maximum_fusion.refs_0_ = bf16[1056,128]{1,0:T(8,128)(2,1)S(1)} fusion(bf16[528,128]{1,0:T(8,128)(2,1)S(1)} %collective-permute-done.2, bf16[16,128]{1,0:T(8,128)(2,1)S(1)} %broadcast_in_dim.20, bf16[512,128]{1,0:T(8,128)(2,1)} %bitcast.9), kind=kLoop, calls=%fused_computation | loop fusion | flops 811008 | bytes 540672 | tf_op jit(solution)/shard_map/concatenate | solution.py:190
  8.3 2.5 %collective-permute-done = bf16[528,128]{1,0:T(8,128)(2,1)S(1)} collective-permute-done((bf16[528,128]{1,0:T(8,128)(2,1)S(1)}, bf16[528,128]{1,0:T(8,128)(2,1)S(1)}, u32[]{:S(2)}, u32[]{:S(2)}) %collective-permute-start) | collective-permute-done | bytes 135200 | tf_op jit(solution)/shard_map/ppermute | solution.py:184
  10.8 3.1 %collective-permute-done.1 = bf16[528,128]{1,0:T(8,128)(2,1)S(1)} collective-permute-done((bf16[528,128]{1,0:T(8,128)(2,1)S(1)}, bf16[528,128]{1,0:T(8,128)(2,1)S(1)}, u32[]{:S(2)}, u32[]{:S(2)}) %collective-permute-start.1) | collective-permute-done | bytes 135200 | tf_op jit(solution)/shard_map/ppermute | solution.py:184
  13.9 1.2 %collective-permute-start.15 = (bf16[528,128]{1,0:T(8,128)(2,1)S(1)}, bf16[528,128]{1,0:T(8,128)(2,1)S(1)}, u32[]{:S(2)}, u32[]{:S(2)}) collective-permute-start(bf16[528,128]{1,0:T(8,128)(2,1)S(1)} %pad_maximum_fusion.2), channel_id=1, source_target_pairs={{0,32},{32,0},{64,96},{96,64},{128,160},{160,128},{192,224},{224,1... | collective-permute-start | bytes 405512 | tf_op jit(solution)/shard_map/ppermute | solution.py:187
  15.1 5.7 %collective-permute-start.3 = (bf16[1056,128]{1,0:T(8,128)(2,1)S(1)}, bf16[1056,128]{1,0:T(8,128)(2,1)S(1)}, u32[]{:S(2)}, u32[]{:S(2)}) collective-permute-start(bf16[1056,128]{1,0:T(8,128)(2,1)S(1)} %pad_maximum_fusion.refs_0_), channel_id=1, source_target_pairs={{0,4},{1,29},{2,6},{3,31},{4,8},{5,1},{6,10},{7,3},{8,12},{9,5},{1... | collective-permute-start | bytes 811016 | tf_op jit(solution)/shard_map/ppermute | solution.py:184
  20.7 0.8 %collective-permute-start.7 = (bf16[1056,128]{1,0:T(8,128)(2,1)S(1)}, bf16[1056,128]{1,0:T(8,128)(2,1)S(1)}, u32[]{:S(2)}, u32[]{:S(2)}) collective-permute-start(bf16[1056,128]{1,0:T(8,128)(2,1)S(1)} %constant_dynamic-update-slice_fusion.refs_1_), channel_id=1, source_target_pairs={{0,4},{1,29},{2,6},{3,31},{4,8},{5,1},{6,10},{7,3},{8,12},{9,5},{1... | collective-permute-start | bytes 811016 | tf_op jit(solution)/shard_map/ppermute | solution.py:184
  21.5 0.0 collective-permute-done.15
  21.6 1.3 %collective-permute-start.16 = (bf16[1056,128]{1,0:T(8,128)(2,1)S(1)}, bf16[1056,128]{1,0:T(8,128)(2,1)S(1)}, u32[]{:S(2)}, u32[]{:S(2)}) collective-permute-start(bf16[1056,128]{1,0:T(8,128)(2,1)S(1)} %pad_maximum_fusion.1), channel_id=1, source_target_pairs={{0,64},{32,96},{64,0},{96,32},{128,192},{160,224},{192,128},{224,1... | collective-permute-start | bytes 811016 | tf_op jit(solution)/shard_map/ppermute | solution.py:187
  22.9 4.1 %collective-permute-done.7.refs_3_ = bf16[1056,128]{1,0:T(8,128)(2,1)S(1)} collective-permute-done((bf16[1056,128]{1,0:T(8,128)(2,1)S(1)}, bf16[1056,128]{1,0:T(8,128)(2,1)S(1)}, u32[]{:S(2)}, u32[]{:S(2)}) %collective-permute-start.7) | collective-permute-done | bytes 270368 | tf_op jit(solution)/shard_map/ppermute | solution.py:184
  27.0 3.1 %collective-permute-start.8 = (bf16[1056,128]{1,0:T(8,128)(2,1)S(1)}, bf16[1056,128]{1,0:T(8,128)(2,1)S(1)}, u32[]{:S(2)}, u32[]{:S(2)}) collective-permute-start(bf16[1056,128]{1,0:T(8,128)(2,1)S(1)} %collective-permute-done.7.refs_3_), channel_id=1, source_target_pairs={{0,4},{1,29},{2,6},{3,31},{4,8},{5,1},{6,10},{7,3},{8,12},{9,5},{1... | collective-permute-start | bytes 811016 | tf_op jit(solution)/shard_map/ppermute | solution.py:184
  30.1 0.0 collective-permute-start.12
  30.1 0.0 collective-permute-done.3.refs_2_
  30.1 1.6 %collective-permute-start.4 = (bf16[1056,128]{1,0:T(8,128)(2,1)S(1)}, bf16[1056,128]{1,0:T(8,128)(2,1)S(1)}, u32[]{:S(2)}, u32[]{:S(2)}) collective-permute-start(bf16[1056,128]{1,0:T(8,128)(2,1)S(1)} %collective-permute-done.3.refs_2_), channel_id=1, source_target_pairs={{0,4},{1,29},{2,6},{3,31},{4,8},{5,1},{6,10},{7,3},{8,12},{9,5},{1... | collective-permute-start | bytes 811016 | tf_op jit(solution)/shard_map/ppermute | solution.py:184
  31.8 0.0 collective-permute-start.11
  31.8 0.0 collective-permute-done.16
  31.8 2.6 %collective-permute-start.17 = (bf16[2112,128]{1,0:T(8,128)(2,1)S(1)}, bf16[2112,128]{1,0:T(8,128)(2,1)S(1)}, u32[]{:S(2)}, u32[]{:S(2)}) collective-permute-start(bf16[2112,128]{1,0:T(8,128)(2,1)S(1)} %constant_dynamic-update-slice_fusion.2.refs_10_), channel_id=1, source_target_pairs={{0,192},{32,224},{64,128},{96,160},{128,64},{160,96},{192,0},{224,... | collective-permute-start | bytes 1622024 | tf_op jit(solution)/shard_map/ppermute | solution.py:187
  34.4 0.0 collective-permute-done.8.refs_7_
  34.4 2.3 %collective-permute-start.9 = (bf16[1056,128]{1,0:T(8,128)(2,1)S(1)}, bf16[1056,128]{1,0:T(8,128)(2,1)S(1)}, u32[]{:S(2)}, u32[]{:S(2)}) collective-permute-start(bf16[1056,128]{1,0:T(8,128)(2,1)S(1)} %collective-permute-done.8.refs_7_), channel_id=1, source_target_pairs={{0,4},{1,29},{2,6},{3,31},{4,8},{5,1},{6,10},{7,3},{8,12},{9,5},{1... | collective-permute-start | bytes 811016 | tf_op jit(solution)/shard_map/ppermute | solution.py:184
  36.6 0.0 collective-permute-done.12.refs_5_
  36.7 0.0 collective-permute-start.14
  36.7 0.0 collective-permute-done.4.refs_6_
  36.7 3.2 %collective-permute-start.5 = (bf16[1056,128]{1,0:T(8,128)(2,1)S(1)}, bf16[1056,128]{1,0:T(8,128)(2,1)S(1)}, u32[]{:S(2)}, u32[]{:S(2)}) collective-permute-start(bf16[1056,128]{1,0:T(8,128)(2,1)S(1)} %collective-permute-done.4.refs_6_), channel_id=1, source_target_pairs={{0,4},{1,29},{2,6},{3,31},{4,8},{5,1},{6,10},{7,3},{8,12},{9,5},{1... | collective-permute-start | bytes 811016 | tf_op jit(solution)/shard_map/ppermute | solution.py:184
  39.8 0.0 collective-permute-done.11.refs_4_
  39.8 0.0 collective-permute-start.13
  40.5 0.7 fusion.1
  41.2 0.0 collective-permute-done.9.refs_1_
  41.2 3.0 %collective-permute-start.19 = (bf16[1056,128]{1,0:T(8,128)(2,1)S(1)}, bf16[1056,128]{1,0:T(8,128)(2,1)S(1)}, u32[]{:S(2)}, u32[]{:S(2)}) collective-permute-start(bf16[1056,128]{1,0:T(8,128)(2,1)S(1)} %collective-permute-done.9.refs_1_), channel_id=1, source_target_pairs={{0,1},{1,0},{2,3},{3,2},{4,5},{5,4},{6,7},{7,6},{8,9},{9,8},{10,11... | collective-permute-start | bytes 811016 | tf_op jit(solution)/shard_map/ppermute | solution.py:184
  44.2 0.0 collective-permute-done.14.refs_9_
  44.2 0.0 collective-permute-start.10
  44.2 0.0 collective-permute-done.5.refs_0_
  44.2 2.9 %collective-permute-start.18 = (bf16[1056,128]{1,0:T(8,128)(2,1)S(1)}, bf16[1056,128]{1,0:T(8,128)(2,1)S(1)}, u32[]{:S(2)}, u32[]{:S(2)}) collective-permute-start(bf16[1056,128]{1,0:T(8,128)(2,1)S(1)} %collective-permute-done.5.refs_0_), channel_id=1, source_target_pairs={{0,1},{1,0},{2,3},{3,2},{4,5},{5,4},{6,7},{7,6},{8,9},{9,8},{10,11... | collective-permute-start | bytes 811016 | tf_op jit(solution)/shard_map/ppermute | solution.py:184
  47.1 0.0 collective-permute-done.13.refs_8_
  47.1 0.1 collective-permute-start.6
  47.1 0.0 collective-permute-done.17.refs_11_
  47.1 4.8 %shard_map.55 = (bf16[8,256,1152]{2,1,0:T(8,128)(2,1)S(1)}, f32[256,1024]{1,0:T(8,128)S(1)}) custom-call(bf16[1056,128]{1,0:T(8,128)(2,1)S(1)} %pad_maximum_fusion.refs_0_, bf16[1056,128]{1,0:T(8,128)(2,1)S(1)} %constant_dynamic-update-slice_fusion.refs_1_, bf16[1056,128]{1,0:T(8,128)(2,1)S(1)} %collective-permute-done.3.refs_2_, ...), custom_call_target="tpu_custom_call" | custom-call | flops 3221225472 | bytes 25165824 | tf_op jit(solution)/shard_map/pallas_call | solution.py:209
  51.9 0.0 collective-permute-done.19.refs_3_
  52.0 0.0 collective-permute-done.18.refs_2_
  52.0 1.8 %shard_map.56.before = f32[256,1024]{1,0:T(8,128)S(1)} custom-call(bf16[1056,128]{1,0:T(8,128)(2,1)S(1)} %collective-permute-done.5.refs_0_, bf16[1056,128]{1,0:T(8,128)(2,1)S(1)} %collective-permute-done.9.refs_1_, bf16[1056,128]{1,0:T(8,128)(2,1)S(1)} %collective-permute-done.18.refs_2_, bf16[1056,128]{1,0:T(8,128)(2,1)S(1)} %collective-permute-done.19.refs_3_, ...), custom_call_target="tpu_custom_call" | custom-call | flops 1073741824 | bytes 8388608 | tf_op jit(solution)/shard_map/pallas_call | solution.py:218
  53.8 0.0 collective-permute-done.10.beside
  53.8 0.0 collective-permute-done.6.pair
  53.8 0.1 broadcast_in_dim.21.codes
  53.9 2.0 %shard_map.57 = (f32[8,128,128]{2,1,0:T(8,128)S(1)}, f32[32,8,128]{2,1,0:T(8,128)S(1)}) custom-call(bf16[16,128]{1,0:T(8,128)(2,1)S(1)} %broadcast_in_dim.21.codes, bf16[1056,128]{1,0:T(8,128)(2,1)S(1)} %collective-permute-done.6.pair, bf16[1056,128]{1,0:T(8,128)(2,1)S(1)} %collective-permute-done.10.beside, ...), custom_call_target="tpu_custom_call" | custom-call | flops 536870912 | bytes 4194304 | tf_op jit(solution)/shard_map/pallas_call | solution.py:227
  55.9 16.1 %all_to_all.5.sums = f32[32,8,128]{2,1,0:T(8,128)S(1)} all-to-all(f32[32,8,128]{2,1,0:T(8,128)S(1)} %get-tuple-element.20), channel_id=1, replica_groups=mesh['group'=8,'loop'=32] {'loop'}, dimensions={0} | all-to-all | bytes 262144 | tf_op jit(solution)/shard_map/all_to_all | solution.py:241
  72.0 1.9 %shard_map.58 = f32[8,128,128]{2,1,0:T(8,128)} custom-call(bf16[16,128]{1,0:T(8,128)(2,1)S(1)} %broadcast_in_dim.21.codes, f32[8,128,128]{2,1,0:T(8,128)S(1)} %get-tuple-element.19.squares, f32[32,8,128]{2,1,0:T(8,128)S(1)} %all_to_all.5.sums), custom_call_target="tpu_custom_call" | custom-call | tf_op jit(solution)/shard_map/pallas_call | solution.py:242
  (6 shorter events, 0.1 us)
Async XLA Ops:
  2.3 5.1 %collective-permute-start.2 = (bf16[528,128]{1,0:T(8,128)(2,1)S(1)}, bf16[528,128]{1,0:T(8,128)(2,1)S(1)}, u32[]{:S(2)}, u32[]{:S(2)}) collective-permute-start(bf16[528,128]{1,0:T(8,128)(2,1)S(1)} %pad_maximum_fusion.2), channel_id=1, source_target_pairs={{0,1},{1,0},{2,3},{3,2},{4,5},{5,4},{6,7},{7,6},{8,9},{9,8},{10,11... | collective-permute-start | bytes 405512 | tf_op jit(solution)/shard_map/ppermute | solution.py:184
  5.6 5.1 %collective-permute-start = (bf16[528,128]{1,0:T(8,128)(2,1)S(1)}, bf16[528,128]{1,0:T(8,128)(2,1)S(1)}, u32[]{:S(2)}, u32[]{:S(2)}) collective-permute-start(bf16[528,128]{1,0:T(8,128)(2,1)S(1)} %pad_maximum_fusion.2), channel_id=1, source_target_pairs={{0,2},{1,3},{2,0},{3,1},{4,6},{5,7},{6,4},{7,5},{8,10},{9,11},{10,... | collective-permute-start | bytes 405512 | tf_op jit(solution)/shard_map/ppermute | solution.py:184
  5.6 8.2 %collective-permute-start.1 = (bf16[528,128]{1,0:T(8,128)(2,1)S(1)}, bf16[528,128]{1,0:T(8,128)(2,1)S(1)}, u32[]{:S(2)}, u32[]{:S(2)}) collective-permute-start(bf16[528,128]{1,0:T(8,128)(2,1)S(1)} %pad_maximum_fusion.2), channel_id=1, source_target_pairs={{0,3},{1,2},{2,1},{3,0},{4,7},{5,6},{6,5},{7,4},{8,11},{9,10},{10,... | collective-permute-start | bytes 405512 | tf_op jit(solution)/shard_map/ppermute | solution.py:184
  13.9 7.7 %collective-permute-start.15 = (bf16[528,128]{1,0:T(8,128)(2,1)S(1)}, bf16[528,128]{1,0:T(8,128)(2,1)S(1)}, u32[]{:S(2)}, u32[]{:S(2)}) collective-permute-start(bf16[528,128]{1,0:T(8,128)(2,1)S(1)} %pad_maximum_fusion.2), channel_id=1, source_target_pairs={{0,32},{32,0},{64,96},{96,64},{128,160},{160,128},{192,224},{224,1... | collective-permute-start | bytes 405512 | tf_op jit(solution)/shard_map/ppermute | solution.py:187
  15.1 15.1 %collective-permute-start.3 = (bf16[1056,128]{1,0:T(8,128)(2,1)S(1)}, bf16[1056,128]{1,0:T(8,128)(2,1)S(1)}, u32[]{:S(2)}, u32[]{:S(2)}) collective-permute-start(bf16[1056,128]{1,0:T(8,128)(2,1)S(1)} %pad_maximum_fusion.refs_0_), channel_id=1, source_target_pairs={{0,4},{1,29},{2,6},{3,31},{4,8},{5,1},{6,10},{7,3},{8,12},{9,5},{1... | collective-permute-start | bytes 811016 | tf_op jit(solution)/shard_map/ppermute | solution.py:184
  20.7 6.3 %collective-permute-start.7 = (bf16[1056,128]{1,0:T(8,128)(2,1)S(1)}, bf16[1056,128]{1,0:T(8,128)(2,1)S(1)}, u32[]{:S(2)}, u32[]{:S(2)}) collective-permute-start(bf16[1056,128]{1,0:T(8,128)(2,1)S(1)} %constant_dynamic-update-slice_fusion.refs_1_), channel_id=1, source_target_pairs={{0,4},{1,29},{2,6},{3,31},{4,8},{5,1},{6,10},{7,3},{8,12},{9,5},{1... | collective-permute-start | bytes 811016 | tf_op jit(solution)/shard_map/ppermute | solution.py:184
  21.6 10.2 %collective-permute-start.16 = (bf16[1056,128]{1,0:T(8,128)(2,1)S(1)}, bf16[1056,128]{1,0:T(8,128)(2,1)S(1)}, u32[]{:S(2)}, u32[]{:S(2)}) collective-permute-start(bf16[1056,128]{1,0:T(8,128)(2,1)S(1)} %pad_maximum_fusion.1), channel_id=1, source_target_pairs={{0,64},{32,96},{64,0},{96,32},{128,192},{160,224},{192,128},{224,1... | collective-permute-start | bytes 811016 | tf_op jit(solution)/shard_map/ppermute | solution.py:187
  27.0 7.4 %collective-permute-start.8 = (bf16[1056,128]{1,0:T(8,128)(2,1)S(1)}, bf16[1056,128]{1,0:T(8,128)(2,1)S(1)}, u32[]{:S(2)}, u32[]{:S(2)}) collective-permute-start(bf16[1056,128]{1,0:T(8,128)(2,1)S(1)} %collective-permute-done.7.refs_3_), channel_id=1, source_target_pairs={{0,4},{1,29},{2,6},{3,31},{4,8},{5,1},{6,10},{7,3},{8,12},{9,5},{1... | collective-permute-start | bytes 811016 | tf_op jit(solution)/shard_map/ppermute | solution.py:184
  30.1 6.5 %collective-permute-start.12 = (bf16[1056,128]{1,0:T(8,128)(2,1)S(1)}, bf16[1056,128]{1,0:T(8,128)(2,1)S(1)}, u32[]{:S(2)}, u32[]{:S(2)}) collective-permute-start(bf16[1056,128]{1,0:T(8,128)(2,1)S(1)} %collective-permute-done.7.refs_3_), channel_id=1, source_target_pairs={{0,1},{1,0},{2,3},{3,2},{4,5},{5,4},{6,7},{7,6},{8,9},{9,8},{10,11... | collective-permute-start | bytes 811016 | tf_op jit(solution)/shard_map/ppermute | solution.py:184
  30.1 6.5 %collective-permute-start.4 = (bf16[1056,128]{1,0:T(8,128)(2,1)S(1)}, bf16[1056,128]{1,0:T(8,128)(2,1)S(1)}, u32[]{:S(2)}, u32[]{:S(2)}) collective-permute-start(bf16[1056,128]{1,0:T(8,128)(2,1)S(1)} %collective-permute-done.3.refs_2_), channel_id=1, source_target_pairs={{0,4},{1,29},{2,6},{3,31},{4,8},{5,1},{6,10},{7,3},{8,12},{9,5},{1... | collective-permute-start | bytes 811016 | tf_op jit(solution)/shard_map/ppermute | solution.py:184
  31.8 8.1 %collective-permute-start.11 = (bf16[1056,128]{1,0:T(8,128)(2,1)S(1)}, bf16[1056,128]{1,0:T(8,128)(2,1)S(1)}, u32[]{:S(2)}, u32[]{:S(2)}) collective-permute-start(bf16[1056,128]{1,0:T(8,128)(2,1)S(1)} %collective-permute-done.3.refs_2_), channel_id=1, source_target_pairs={{0,1},{1,0},{2,3},{3,2},{4,5},{5,4},{6,7},{7,6},{8,9},{9,8},{10,11... | collective-permute-start | bytes 811016 | tf_op jit(solution)/shard_map/ppermute | solution.py:184
  31.8 15.3 %collective-permute-start.17 = (bf16[2112,128]{1,0:T(8,128)(2,1)S(1)}, bf16[2112,128]{1,0:T(8,128)(2,1)S(1)}, u32[]{:S(2)}, u32[]{:S(2)}) collective-permute-start(bf16[2112,128]{1,0:T(8,128)(2,1)S(1)} %constant_dynamic-update-slice_fusion.2.refs_10_), channel_id=1, source_target_pairs={{0,192},{32,224},{64,128},{96,160},{128,64},{160,96},{192,0},{224,... | collective-permute-start | bytes 1622024 | tf_op jit(solution)/shard_map/ppermute | solution.py:187
  34.4 6.8 %collective-permute-start.9 = (bf16[1056,128]{1,0:T(8,128)(2,1)S(1)}, bf16[1056,128]{1,0:T(8,128)(2,1)S(1)}, u32[]{:S(2)}, u32[]{:S(2)}) collective-permute-start(bf16[1056,128]{1,0:T(8,128)(2,1)S(1)} %collective-permute-done.8.refs_7_), channel_id=1, source_target_pairs={{0,4},{1,29},{2,6},{3,31},{4,8},{5,1},{6,10},{7,3},{8,12},{9,5},{1... | collective-permute-start | bytes 811016 | tf_op jit(solution)/shard_map/ppermute | solution.py:184
  36.7 7.5 %collective-permute-start.14 = (bf16[1056,128]{1,0:T(8,128)(2,1)S(1)}, bf16[1056,128]{1,0:T(8,128)(2,1)S(1)}, u32[]{:S(2)}, u32[]{:S(2)}) collective-permute-start(bf16[1056,128]{1,0:T(8,128)(2,1)S(1)} %collective-permute-done.8.refs_7_), channel_id=1, source_target_pairs={{0,1},{1,0},{2,3},{3,2},{4,5},{5,4},{6,7},{7,6},{8,9},{9,8},{10,11... | collective-permute-start | bytes 811016 | tf_op jit(solution)/shard_map/ppermute | solution.py:184
  36.7 7.5 %collective-permute-start.5 = (bf16[1056,128]{1,0:T(8,128)(2,1)S(1)}, bf16[1056,128]{1,0:T(8,128)(2,1)S(1)}, u32[]{:S(2)}, u32[]{:S(2)}) collective-permute-start(bf16[1056,128]{1,0:T(8,128)(2,1)S(1)} %collective-permute-done.4.refs_6_), channel_id=1, source_target_pairs={{0,4},{1,29},{2,6},{3,31},{4,8},{5,1},{6,10},{7,3},{8,12},{9,5},{1... | collective-permute-start | bytes 811016 | tf_op jit(solution)/shard_map/ppermute | solution.py:184
  39.8 7.2 %collective-permute-start.13 = (bf16[1056,128]{1,0:T(8,128)(2,1)S(1)}, bf16[1056,128]{1,0:T(8,128)(2,1)S(1)}, u32[]{:S(2)}, u32[]{:S(2)}) collective-permute-start(bf16[1056,128]{1,0:T(8,128)(2,1)S(1)} %collective-permute-done.4.refs_6_), channel_id=1, source_target_pairs={{0,1},{1,0},{2,3},{3,2},{4,5},{5,4},{6,7},{7,6},{8,9},{9,8},{10,11... | collective-permute-start | bytes 811016 | tf_op jit(solution)/shard_map/ppermute | solution.py:184
  41.2 10.8 %collective-permute-start.19 = (bf16[1056,128]{1,0:T(8,128)(2,1)S(1)}, bf16[1056,128]{1,0:T(8,128)(2,1)S(1)}, u32[]{:S(2)}, u32[]{:S(2)}) collective-permute-start(bf16[1056,128]{1,0:T(8,128)(2,1)S(1)} %collective-permute-done.9.refs_1_), channel_id=1, source_target_pairs={{0,1},{1,0},{2,3},{3,2},{4,5},{5,4},{6,7},{7,6},{8,9},{9,8},{10,11... | collective-permute-start | bytes 811016 | tf_op jit(solution)/shard_map/ppermute | solution.py:184
  44.2 9.6 %collective-permute-start.10 = (bf16[1056,128]{1,0:T(8,128)(2,1)S(1)}, bf16[1056,128]{1,0:T(8,128)(2,1)S(1)}, u32[]{:S(2)}, u32[]{:S(2)}) collective-permute-start(bf16[1056,128]{1,0:T(8,128)(2,1)S(1)} %collective-permute-done.9.refs_1_), channel_id=1, source_target_pairs={{0,4},{1,29},{2,6},{3,31},{4,8},{5,1},{6,10},{7,3},{8,12},{9,5},{1... | collective-permute-start | bytes 811016 | tf_op jit(solution)/shard_map/ppermute | solution.py:184
  44.2 7.8 %collective-permute-start.18 = (bf16[1056,128]{1,0:T(8,128)(2,1)S(1)}, bf16[1056,128]{1,0:T(8,128)(2,1)S(1)}, u32[]{:S(2)}, u32[]{:S(2)}) collective-permute-start(bf16[1056,128]{1,0:T(8,128)(2,1)S(1)} %collective-permute-done.5.refs_0_), channel_id=1, source_target_pairs={{0,1},{1,0},{2,3},{3,2},{4,5},{5,4},{6,7},{7,6},{8,9},{9,8},{10,11... | collective-permute-start | bytes 811016 | tf_op jit(solution)/shard_map/ppermute | solution.py:184
  47.1 6.7 %collective-permute-start.6 = (bf16[1056,128]{1,0:T(8,128)(2,1)S(1)}, bf16[1056,128]{1,0:T(8,128)(2,1)S(1)}, u32[]{:S(2)}, u32[]{:S(2)}) collective-permute-start(bf16[1056,128]{1,0:T(8,128)(2,1)S(1)} %collective-permute-done.5.refs_0_), channel_id=1, source_target_pairs={{0,4},{1,29},{2,6},{3,31},{4,8},{5,1},{6,10},{7,3},{8,12},{9,5},{1... | collective-permute-start | bytes 811016 | tf_op jit(solution)/shard_map/ppermute | solution.py:184

commit v4 on v3

--- a/solution.py
+++ b/solution.py
@@ -190,7 +190,7 @@
     first = jnp.concatenate([unit, along(CORE, unit)])
     beside, crossed, _ = lax.optimization_barrier((beside, crossed, first))
     second = jnp.concatenate([beside, crossed])
-    later, beside_later, _ = lax.optimization_barrier((unit, result_coords, beside))
+    later, beside_later, _ = lax.optimization_barrier((unit, result_coords, first))
     row = jnp.concatenate([later, across(YHI, later)])
     row = jnp.concatenate([row, across(XNEAR, row)])
     left = [row, across(XMIRROR, row)]
@@ -201,7 +201,11 @@
     streams = [first, second]
     right = [streams]
     for r in range(3):
-        streams = [along(RING, v) for v in streams]
+        ahead = along(RING, streams[0])
+        behind = streams[1]
+        if r == 0:
+            behind, _ = lax.optimization_barrier((behind, ahead))
+        streams = [ahead, along(RING, behind)]
         right += [streams, [along(CORE, v) for v in streams]]
     last = [along(RING, v) for v in streams]
 

time: 74.3 us -> 70.3 us (0.946)
  waiting for transfers between devices: 9.72 us -> 2.05 us
  starting transfers between devices: 32.7 us -> 37.7 us
  blocking collectives: 16.1 us -> 14.8 us
    ppermute x17, waiting for transfers between devices: 9.71 us -> 1.74 us  [along(): return lax.ppermute(v, 'loop', perm)]
    ppermute x17, starting transfers between devices: 27.7 us -> 30.9 us  [along(): return lax.ppermute(v, 'loop', perm)]
    ppermute x3, starting transfers between devices: 5.04 us -> 6.78 us  [across(): return lax.ppermute(v, 'group', perm)]
    all_to_all x1, blocking collectives: 16.1 us -> 14.8 us  [shards(): sums = lax.all_to_all(sums, 'loop', 0, 0, tiled=True)]
where the time goes in v4:
time: 70.3 us; the launch traced here: 70.1 us
  starting transfers between devices  37.7 us (54%)
  blocking collectives  14.8 us (21%)
  Pallas kernels  10.5 us (15%)
  other arithmetic  3.19 us (5%)
  waiting for transfers between devices  2.05 us (3%)
  between operations  1.58 us (2%)
    ppermute x17, starting transfers between devices, along(): return lax.ppermute(v, 'loop', perm)  30.9 us
    all_to_all x1, blocking collectives, shards(): sums = lax.all_to_all(sums, 'loop', 0, 0, tiled=True)  14.8 us
    ppermute x3, starting transfers between devices, across(): return lax.ppermute(v, 'group', perm)  6.78 us
    pallas_call x1, Pallas kernels, shards(): pl.pallas_call(begin, in_specs=[WHOLE] * 12, out_specs=[WHOLE] * 2, out_s...  4.8 us
    pallas_call x1, Pallas kernels, shards(): pl.pallas_call(finish, in_specs=[WHOLE] * 5, out_specs=[AWAY, WHOLE], out...  1.98 us
    pallas_call x1, Pallas kernels, shards(): pl.pallas_call(rescale, in_specs=[AWAY] * 3, out_specs=AWAY, out_shape=ja...  1.94 us
    pallas_call x1, Pallas kernels, shards(): pl.pallas_call(proceed, in_specs=[WHOLE] * 6, out_specs=WHOLE, out_shape=...  1.81 us
    ppermute x17, waiting for transfers between devices, along(): return lax.ppermute(v, 'loop', perm)  1.74 us
  transfers between devices with their start and end apart: 20, of which 3 were waited for; matrix products, arithmetic and copies ran while one was open for 2% of the time, Pallas kernels for 9%

profile of v4, /device:TPU:1, one launch (start us, length us, event | category | flops | bytes accessed | tf_op | source)
XLA Modules:
  0.0 70.1 jit_solution(1090757082180923185)
XLA Ops:
  0.7 0.7 fusion
  1.3 0.1 broadcast_in_dim.20
  1.4 0.9 %pad_maximum_fusion.2 = bf16[528,128]{1,0:T(8,128)(2,1)S(1)} fusion(bf16[16,128]{1,0:T(8,128)(2,1)S(1)} %broadcast_in_dim.20, bf16[512,128]{1,0:T(8,128)(2,1)} %bitcast.8), kind=kLoop, calls=%fused_computation.2 | loop fusion | flops 270336 | bytes 270336 | tf_op jit(solution)/shard_map/concatenate | solution.py:179
  2.3 3.3 %collective-permute-start = (bf16[528,128]{1,0:T(8,128)(2,1)S(1)}, bf16[528,128]{1,0:T(8,128)(2,1)S(1)}, u32[]{:S(2)}, u32[]{:S(2)}) collective-permute-start(bf16[528,128]{1,0:T(8,128)(2,1)S(1)} %pad_maximum_fusion.2), channel_id=1, source_target_pairs={{0,1},{1,0},{2,3},{3,2},{4,5},{5,4},{6,7},{7,6},{8,9},{9,8},{10,11... | collective-permute-start | bytes 405512 | tf_op jit(solution)/shard_map/ppermute | solution.py:184
  5.6 0.0 collective-permute-start.5
  5.6 1.7 %collective-permute-start.6 = (bf16[528,128]{1,0:T(8,128)(2,1)S(1)}, bf16[528,128]{1,0:T(8,128)(2,1)S(1)}, u32[]{:S(2)}, u32[]{:S(2)}) collective-permute-start(bf16[528,128]{1,0:T(8,128)(2,1)S(1)} %pad_maximum_fusion.2), channel_id=1, source_target_pairs={{0,3},{1,2},{2,1},{3,0},{4,7},{5,6},{6,5},{7,4},{8,11},{9,10},{10,... | collective-permute-start | bytes 405512 | tf_op jit(solution)/shard_map/ppermute | solution.py:184
  7.4 0.0 collective-permute-done
  7.4 0.9 %pad_maximum_fusion.refs_0_ = bf16[1056,128]{1,0:T(8,128)(2,1)S(1)} fusion(bf16[528,128]{1,0:T(8,128)(2,1)S(1)} %collective-permute-done, bf16[16,128]{1,0:T(8,128)(2,1)S(1)} %broadcast_in_dim.20, bf16[512,128]{1,0:T(8,128)(2,1)} %bitcast.9), kind=kLoop, calls=%fused_computation | loop fusion | flops 811008 | bytes 540672 | tf_op jit(solution)/shard_map/concatenate | solution.py:190
  8.3 3.9 %collective-permute-start.1 = (bf16[1056,128]{1,0:T(8,128)(2,1)S(1)}, bf16[1056,128]{1,0:T(8,128)(2,1)S(1)}, u32[]{:S(2)}, u32[]{:S(2)}) collective-permute-start(bf16[1056,128]{1,0:T(8,128)(2,1)S(1)} %pad_maximum_fusion.refs_0_), channel_id=1, source_target_pairs={{0,4},{1,29},{2,6},{3,31},{4,8},{5,1},{6,10},{7,3},{8,12},{9,5},{1... | collective-permute-start | bytes 811016 | tf_op jit(solution)/shard_map/ppermute | solution.py:184
  12.2 2.9 %collective-permute-start.15 = (bf16[528,128]{1,0:T(8,128)(2,1)S(1)}, bf16[528,128]{1,0:T(8,128)(2,1)S(1)}, u32[]{:S(2)}, u32[]{:S(2)}) collective-permute-start(bf16[528,128]{1,0:T(8,128)(2,1)S(1)} %pad_maximum_fusion.2), channel_id=1, source_target_pairs={{0,32},{32,0},{64,96},{96,64},{128,160},{160,128},{192,224},{224,1... | collective-permute-start | bytes 405512 | tf_op jit(solution)/shard_map/ppermute | solution.py:187
  15.1 0.0 collective-permute-done.5
  15.1 0.0 collective-permute-done.6
  15.2 0.4 collective-permute-done.1.refs_2_
  15.6 3.1 %collective-permute-start.7 = (bf16[1056,128]{1,0:T(8,128)(2,1)S(1)}, bf16[1056,128]{1,0:T(8,128)(2,1)S(1)}, u32[]{:S(2)}, u32[]{:S(2)}) collective-permute-start(bf16[1056,128]{1,0:T(8,128)(2,1)S(1)} %constant_dynamic-update-slice_fusion.refs_1_), channel_id=1, source_target_pairs={{0,4},{1,29},{2,6},{3,31},{4,8},{5,1},{6,10},{7,3},{8,12},{9,5},{1... | collective-permute-start | bytes 811016 | tf_op jit(solution)/shard_map/ppermute | solution.py:184
  18.7 0.0 collective-permute-done.15
  18.8 1.3 %collective-permute-start.16 = (bf16[1056,128]{1,0:T(8,128)(2,1)S(1)}, bf16[1056,128]{1,0:T(8,128)(2,1)S(1)}, u32[]{:S(2)}, u32[]{:S(2)}) collective-permute-start(bf16[1056,128]{1,0:T(8,128)(2,1)S(1)} %pad_maximum_fusion.1), channel_id=1, source_target_pairs={{0,64},{32,96},{64,0},{96,32},{128,192},{160,224},{192,128},{224,1... | collective-permute-start | bytes 811016 | tf_op jit(solution)/shard_map/ppermute | solution.py:187
  20.1 4.2 %collective-permute-start.2 = (bf16[1056,128]{1,0:T(8,128)(2,1)S(1)}, bf16[1056,128]{1,0:T(8,128)(2,1)S(1)}, u32[]{:S(2)}, u32[]{:S(2)}) collective-permute-start(bf16[1056,128]{1,0:T(8,128)(2,1)S(1)} %collective-permute-done.1.refs_2_), channel_id=1, source_target_pairs={{0,4},{1,29},{2,6},{3,31},{4,8},{5,1},{6,10},{7,3},{8,12},{9,5},{1... | collective-permute-start | bytes 811016 | tf_op jit(solution)/shard_map/ppermute | solution.py:184
  24.3 0.0 collective-permute-start.11
  24.3 0.0 collective-permute-done.7.refs_3_
  24.3 1.2 %collective-permute-start.8 = (bf16[1056,128]{1,0:T(8,128)(2,1)S(1)}, bf16[1056,128]{1,0:T(8,128)(2,1)S(1)}, u32[]{:S(2)}, u32[]{:S(2)}) collective-permute-start(bf16[1056,128]{1,0:T(8,128)(2,1)S(1)} %collective-permute-done.7.refs_3_), channel_id=1, source_target_pairs={{0,4},{1,29},{2,6},{3,31},{4,8},{5,1},{6,10},{7,3},{8,12},{9,5},{1... | collective-permute-start | bytes 811016 | tf_op jit(solution)/shard_map/ppermute | solution.py:184
  25.6 0.3 collective-permute-done.16
  25.9 2.6 %collective-permute-start.17 = (bf16[2112,128]{1,0:T(8,128)(2,1)S(1)}, bf16[2112,128]{1,0:T(8,128)(2,1)S(1)}, u32[]{:S(2)}, u32[]{:S(2)}) collective-permute-start(bf16[2112,128]{1,0:T(8,128)(2,1)S(1)} %constant_dynamic-update-slice_fusion.2.refs_10_), channel_id=1, source_target_pairs={{0,192},{32,224},{64,128},{96,160},{128,64},{160,96},{192,0},{224,... | collective-permute-start | bytes 1622024 | tf_op jit(solution)/shard_map/ppermute | solution.py:187
  28.5 0.0 collective-permute-start.12
  28.5 0.0 collective-permute-done.2.refs_6_
  28.5 6.3 %collective-permute-start.3 = (bf16[1056,128]{1,0:T(8,128)(2,1)S(1)}, bf16[1056,128]{1,0:T(8,128)(2,1)S(1)}, u32[]{:S(2)}, u32[]{:S(2)}) collective-permute-start(bf16[1056,128]{1,0:T(8,128)(2,1)S(1)} %collective-permute-done.2.refs_6_), channel_id=1, source_target_pairs={{0,4},{1,29},{2,6},{3,31},{4,8},{5,1},{6,10},{7,3},{8,12},{9,5},{1... | collective-permute-start | bytes 811016 | tf_op jit(solution)/shard_map/ppermute | solution.py:184
  34.8 0.0 collective-permute-done.11.refs_4_
  34.8 0.0 collective-permute-start.13
  34.8 0.0 collective-permute-done.8.refs_7_
  34.8 0.8 %collective-permute-start.9 = (bf16[1056,128]{1,0:T(8,128)(2,1)S(1)}, bf16[1056,128]{1,0:T(8,128)(2,1)S(1)}, u32[]{:S(2)}, u32[]{:S(2)}) collective-permute-start(bf16[1056,128]{1,0:T(8,128)(2,1)S(1)} %collective-permute-done.8.refs_7_), channel_id=1, source_target_pairs={{0,4},{1,29},{2,6},{3,31},{4,8},{5,1},{6,10},{7,3},{8,12},{9,5},{1... | collective-permute-start | bytes 811016 | tf_op jit(solution)/shard_map/ppermute | solution.py:184
  35.6 0.0 collective-permute-done.12.refs_5_
  35.6 0.0 collective-permute-start.14
  36.2 0.7 fusion.1
  36.9 1.3 %collective-permute-done.3.refs_0_ = bf16[1056,128]{1,0:T(8,128)(2,1)S(1)} collective-permute-done((bf16[1056,128]{1,0:T(8,128)(2,1)S(1)}, bf16[1056,128]{1,0:T(8,128)(2,1)S(1)}, u32[]{:S(2)}, u32[]{:S(2)}) %collective-permute-start.3) | collective-permute-done | bytes 270368 | tf_op jit(solution)/shard_map/ppermute | solution.py:184
  38.2 1.3 %collective-permute-start.18 = (bf16[1056,128]{1,0:T(8,128)(2,1)S(1)}, bf16[1056,128]{1,0:T(8,128)(2,1)S(1)}, u32[]{:S(2)}, u32[]{:S(2)}) collective-permute-start(bf16[1056,128]{1,0:T(8,128)(2,1)S(1)} %collective-permute-done.3.refs_0_), channel_id=1, source_target_pairs={{0,1},{1,0},{2,3},{3,2},{4,5},{5,4},{6,7},{7,6},{8,9},{9,8},{10,11... | collective-permute-start | bytes 811016 | tf_op jit(solution)/shard_map/ppermute | solution.py:184
  39.5 0.0 collective-permute-done.13.refs_8_
  39.5 2.1 %collective-permute-start.4 = (bf16[1056,128]{1,0:T(8,128)(2,1)S(1)}, bf16[1056,128]{1,0:T(8,128)(2,1)S(1)}, u32[]{:S(2)}, u32[]{:S(2)}) collective-permute-start(bf16[1056,128]{1,0:T(8,128)(2,1)S(1)} %collective-permute-done.3.refs_0_), channel_id=1, source_target_pairs={{0,4},{1,29},{2,6},{3,31},{4,8},{5,1},{6,10},{7,3},{8,12},{9,5},{1... | collective-permute-start | bytes 811016 | tf_op jit(solution)/shard_map/ppermute | solution.py:184
  41.6 0.0 collective-permute-done.9.refs_1_
  41.6 1.4 %collective-permute-start.19 = (bf16[1056,128]{1,0:T(8,128)(2,1)S(1)}, bf16[1056,128]{1,0:T(8,128)(2,1)S(1)}, u32[]{:S(2)}, u32[]{:S(2)}) collective-permute-start(bf16[1056,128]{1,0:T(8,128)(2,1)S(1)} %collective-permute-done.9.refs_1_), channel_id=1, source_target_pairs={{0,1},{1,0},{2,3},{3,2},{4,5},{5,4},{6,7},{7,6},{8,9},{9,8},{10,11... | collective-permute-start | bytes 811016 | tf_op jit(solution)/shard_map/ppermute | solution.py:184
  43.0 0.0 collective-permute-done.17.refs_11_
  43.0 1.5 %collective-permute-start.10 = (bf16[1056,128]{1,0:T(8,128)(2,1)S(1)}, bf16[1056,128]{1,0:T(8,128)(2,1)S(1)}, u32[]{:S(2)}, u32[]{:S(2)}) collective-permute-start(bf16[1056,128]{1,0:T(8,128)(2,1)S(1)} %collective-permute-done.9.refs_1_), channel_id=1, source_target_pairs={{0,4},{1,29},{2,6},{3,31},{4,8},{5,1},{6,10},{7,3},{8,12},{9,5},{1... | collective-permute-start | bytes 811016 | tf_op jit(solution)/shard_map/ppermute | solution.py:184
  44.5 0.0 collective-permute-done.14.refs_9_
  44.5 4.8 %shard_map.55 = (bf16[8,256,1152]{2,1,0:T(8,128)(2,1)S(1)}, f32[256,1024]{1,0:T(8,128)S(1)}) custom-call(bf16[1056,128]{1,0:T(8,128)(2,1)S(1)} %pad_maximum_fusion.refs_0_, bf16[1056,128]{1,0:T(8,128)(2,1)S(1)} %constant_dynamic-update-slice_fusion.refs_1_, bf16[1056,128]{1,0:T(8,128)(2,1)S(1)} %collective-permute-done.1.refs_2_, ...), custom_call_target="tpu_custom_call" | custom-call | flops 3221225472 | bytes 25165824 | tf_op jit(solution)/shard_map/pallas_call | solution.py:213
  49.3 0.0 collective-permute-done.18.refs_2_
  49.3 0.0 collective-permute-done.19.refs_3_
  49.3 1.8 %shard_map.56.before = f32[256,1024]{1,0:T(8,128)S(1)} custom-call(bf16[1056,128]{1,0:T(8,128)(2,1)S(1)} %collective-permute-done.3.refs_0_, bf16[1056,128]{1,0:T(8,128)(2,1)S(1)} %collective-permute-done.9.refs_1_, bf16[1056,128]{1,0:T(8,128)(2,1)S(1)} %collective-permute-done.18.refs_2_, bf16[1056,128]{1,0:T(8,128)(2,1)S(1)} %collective-permute-done.19.refs_3_, ...), custom_call_target="tpu_custom_call" | custom-call | flops 1073741824 | bytes 8388608 | tf_op jit(solution)/shard_map/pallas_call | solution.py:222
  51.1 0.0 collective-permute-done.4.pair
  51.1 0.0 collective-permute-done.10.beside
  51.2 0.1 broadcast_in_dim.21.codes
  51.2 2.0 %shard_map.57 = (f32[8,128,128]{2,1,0:T(8,128)S(1)}, f32[32,8,128]{2,1,0:T(8,128)S(1)}) custom-call(bf16[16,128]{1,0:T(8,128)(2,1)S(1)} %broadcast_in_dim.21.codes, bf16[1056,128]{1,0:T(8,128)(2,1)S(1)} %collective-permute-done.4.pair, bf16[1056,128]{1,0:T(8,128)(2,1)S(1)} %collective-permute-done.10.beside, ...), custom_call_target="tpu_custom_call" | custom-call | flops 536870912 | bytes 4194304 | tf_op jit(solution)/shard_map/pallas_call | solution.py:231
  53.2 14.8 %all_to_all.5.sums = f32[32,8,128]{2,1,0:T(8,128)S(1)} all-to-all(f32[32,8,128]{2,1,0:T(8,128)S(1)} %get-tuple-element.22), channel_id=1, replica_groups=mesh['group'=8,'loop'=32] {'loop'}, dimensions={0} | all-to-all | bytes 262144 | tf_op jit(solution)/shard_map/all_to_all | solution.py:245
  68.0 1.9 %shard_map.58 = f32[8,128,128]{2,1,0:T(8,128)} custom-call(bf16[16,128]{1,0:T(8,128)(2,1)S(1)} %broadcast_in_dim.21.codes, f32[8,128,128]{2,1,0:T(8,128)S(1)} %get-tuple-element.21.squares, f32[32,8,128]{2,1,0:T(8,128)S(1)} %all_to_all.5.sums), custom_call_target="tpu_custom_call" | custom-call | tf_op jit(solution)/shard_map/pallas_call | solution.py:246
  (6 shorter events, 0.1 us)
Async XLA Ops:
  2.3 5.1 %collective-permute-start = (bf16[528,128]{1,0:T(8,128)(2,1)S(1)}, bf16[528,128]{1,0:T(8,128)(2,1)S(1)}, u32[]{:S(2)}, u32[]{:S(2)}) collective-permute-start(bf16[528,128]{1,0:T(8,128)(2,1)S(1)} %pad_maximum_fusion.2), channel_id=1, source_target_pairs={{0,1},{1,0},{2,3},{3,2},{4,5},{5,4},{6,7},{7,6},{8,9},{9,8},{10,11... | collective-permute-start | bytes 405512 | tf_op jit(solution)/shard_map/ppermute | solution.py:184
  5.6 9.5 %collective-permute-start.5 = (bf16[528,128]{1,0:T(8,128)(2,1)S(1)}, bf16[528,128]{1,0:T(8,128)(2,1)S(1)}, u32[]{:S(2)}, u32[]{:S(2)}) collective-permute-start(bf16[528,128]{1,0:T(8,128)(2,1)S(1)} %pad_maximum_fusion.2), channel_id=1, source_target_pairs={{0,2},{1,3},{2,0},{3,1},{4,6},{5,7},{6,4},{7,5},{8,10},{9,11},{10,... | collective-permute-start | bytes 405512 | tf_op jit(solution)/shard_map/ppermute | solution.py:184
  5.6 9.5 %collective-permute-start.6 = (bf16[528,128]{1,0:T(8,128)(2,1)S(1)}, bf16[528,128]{1,0:T(8,128)(2,1)S(1)}, u32[]{:S(2)}, u32[]{:S(2)}) collective-permute-start(bf16[528,128]{1,0:T(8,128)(2,1)S(1)} %pad_maximum_fusion.2), channel_id=1, source_target_pairs={{0,3},{1,2},{2,1},{3,0},{4,7},{5,6},{6,5},{7,4},{8,11},{9,10},{10,... | collective-permute-start | bytes 405512 | tf_op jit(solution)/shard_map/ppermute | solution.py:184
  8.3 7.3 %collective-permute-start.1 = (bf16[1056,128]{1,0:T(8,128)(2,1)S(1)}, bf16[1056,128]{1,0:T(8,128)(2,1)S(1)}, u32[]{:S(2)}, u32[]{:S(2)}) collective-permute-start(bf16[1056,128]{1,0:T(8,128)(2,1)S(1)} %pad_maximum_fusion.refs_0_), channel_id=1, source_target_pairs={{0,4},{1,29},{2,6},{3,31},{4,8},{5,1},{6,10},{7,3},{8,12},{9,5},{1... | collective-permute-start | bytes 811016 | tf_op jit(solution)/shard_map/ppermute | solution.py:184
  12.2 6.5 %collective-permute-start.15 = (bf16[528,128]{1,0:T(8,128)(2,1)S(1)}, bf16[528,128]{1,0:T(8,128)(2,1)S(1)}, u32[]{:S(2)}, u32[]{:S(2)}) collective-permute-start(bf16[528,128]{1,0:T(8,128)(2,1)S(1)} %pad_maximum_fusion.2), channel_id=1, source_target_pairs={{0,32},{32,0},{64,96},{96,64},{128,160},{160,128},{192,224},{224,1... | collective-permute-start | bytes 405512 | tf_op jit(solution)/shard_map/ppermute | solution.py:187
  15.6 8.7 %collective-permute-start.7 = (bf16[1056,128]{1,0:T(8,128)(2,1)S(1)}, bf16[1056,128]{1,0:T(8,128)(2,1)S(1)}, u32[]{:S(2)}, u32[]{:S(2)}) collective-permute-start(bf16[1056,128]{1,0:T(8,128)(2,1)S(1)} %constant_dynamic-update-slice_fusion.refs_1_), channel_id=1, source_target_pairs={{0,4},{1,29},{2,6},{3,31},{4,8},{5,1},{6,10},{7,3},{8,12},{9,5},{1... | collective-permute-start | bytes 811016 | tf_op jit(solution)/shard_map/ppermute | solution.py:184
  18.8 7.1 %collective-permute-start.16 = (bf16[1056,128]{1,0:T(8,128)(2,1)S(1)}, bf16[1056,128]{1,0:T(8,128)(2,1)S(1)}, u32[]{:S(2)}, u32[]{:S(2)}) collective-permute-start(bf16[1056,128]{1,0:T(8,128)(2,1)S(1)} %pad_maximum_fusion.1), channel_id=1, source_target_pairs={{0,64},{32,96},{64,0},{96,32},{128,192},{160,224},{192,128},{224,1... | collective-permute-start | bytes 811016 | tf_op jit(solution)/shard_map/ppermute | solution.py:187
  20.1 8.4 %collective-permute-start.2 = (bf16[1056,128]{1,0:T(8,128)(2,1)S(1)}, bf16[1056,128]{1,0:T(8,128)(2,1)S(1)}, u32[]{:S(2)}, u32[]{:S(2)}) collective-permute-start(bf16[1056,128]{1,0:T(8,128)(2,1)S(1)} %collective-permute-done.1.refs_2_), channel_id=1, source_target_pairs={{0,4},{1,29},{2,6},{3,31},{4,8},{5,1},{6,10},{7,3},{8,12},{9,5},{1... | collective-permute-start | bytes 811016 | tf_op jit(solution)/shard_map/ppermute | solution.py:184
  24.3 10.5 %collective-permute-start.11 = (bf16[1056,128]{1,0:T(8,128)(2,1)S(1)}, bf16[1056,128]{1,0:T(8,128)(2,1)S(1)}, u32[]{:S(2)}, u32[]{:S(2)}) collective-permute-start(bf16[1056,128]{1,0:T(8,128)(2,1)S(1)} %collective-permute-done.1.refs_2_), channel_id=1, source_target_pairs={{0,1},{1,0},{2,3},{3,2},{4,5},{5,4},{6,7},{7,6},{8,9},{9,8},{10,11... | collective-permute-start | bytes 811016 | tf_op jit(solution)/shard_map/ppermute | solution.py:184
  24.3 10.5 %collective-permute-start.8 = (bf16[1056,128]{1,0:T(8,128)(2,1)S(1)}, bf16[1056,128]{1,0:T(8,128)(2,1)S(1)}, u32[]{:S(2)}, u32[]{:S(2)}) collective-permute-start(bf16[1056,128]{1,0:T(8,128)(2,1)S(1)} %collective-permute-done.7.refs_3_), channel_id=1, source_target_pairs={{0,4},{1,29},{2,6},{3,31},{4,8},{5,1},{6,10},{7,3},{8,12},{9,5},{1... | collective-permute-start | bytes 811016 | tf_op jit(solution)/shard_map/ppermute | solution.py:184
  25.9 17.0 %collective-permute-start.17 = (bf16[2112,128]{1,0:T(8,128)(2,1)S(1)}, bf16[2112,128]{1,0:T(8,128)(2,1)S(1)}, u32[]{:S(2)}, u32[]{:S(2)}) collective-permute-start(bf16[2112,128]{1,0:T(8,128)(2,1)S(1)} %constant_dynamic-update-slice_fusion.2.refs_10_), channel_id=1, source_target_pairs={{0,192},{32,224},{64,128},{96,160},{128,64},{160,96},{192,0},{224,... | collective-permute-start | bytes 1622024 | tf_op jit(solution)/shard_map/ppermute | solution.py:187
  28.5 7.1 %collective-permute-start.12 = (bf16[1056,128]{1,0:T(8,128)(2,1)S(1)}, bf16[1056,128]{1,0:T(8,128)(2,1)S(1)}, u32[]{:S(2)}, u32[]{:S(2)}) collective-permute-start(bf16[1056,128]{1,0:T(8,128)(2,1)S(1)} %collective-permute-done.7.refs_3_), channel_id=1, source_target_pairs={{0,1},{1,0},{2,3},{3,2},{4,5},{5,4},{6,7},{7,6},{8,9},{9,8},{10,11... | collective-permute-start | bytes 811016 | tf_op jit(solution)/shard_map/ppermute | solution.py:184
  28.5 9.7 %collective-permute-start.3 = (bf16[1056,128]{1,0:T(8,128)(2,1)S(1)}, bf16[1056,128]{1,0:T(8,128)(2,1)S(1)}, u32[]{:S(2)}, u32[]{:S(2)}) collective-permute-start(bf16[1056,128]{1,0:T(8,128)(2,1)S(1)} %collective-permute-done.2.refs_6_), channel_id=1, source_target_pairs={{0,4},{1,29},{2,6},{3,31},{4,8},{5,1},{6,10},{7,3},{8,12},{9,5},{1... | collective-permute-start | bytes 811016 | tf_op jit(solution)/shard_map/ppermute | solution.py:184
  34.8 4.7 %collective-permute-start.13 = (bf16[1056,128]{1,0:T(8,128)(2,1)S(1)}, bf16[1056,128]{1,0:T(8,128)(2,1)S(1)}, u32[]{:S(2)}, u32[]{:S(2)}) collective-permute-start(bf16[1056,128]{1,0:T(8,128)(2,1)S(1)} %collective-permute-done.2.refs_6_), channel_id=1, source_target_pairs={{0,1},{1,0},{2,3},{3,2},{4,5},{5,4},{6,7},{7,6},{8,9},{9,8},{10,11... | collective-permute-start | bytes 811016 | tf_op jit(solution)/shard_map/ppermute | solution.py:184
  34.8 6.8 %collective-permute-start.9 = (bf16[1056,128]{1,0:T(8,128)(2,1)S(1)}, bf16[1056,128]{1,0:T(8,128)(2,1)S(1)}, u32[]{:S(2)}, u32[]{:S(2)}) collective-permute-start(bf16[1056,128]{1,0:T(8,128)(2,1)S(1)} %collective-permute-done.8.refs_7_), channel_id=1, source_target_pairs={{0,4},{1,29},{2,6},{3,31},{4,8},{5,1},{6,10},{7,3},{8,12},{9,5},{1... | collective-permute-start | bytes 811016 | tf_op jit(solution)/shard_map/ppermute | solution.py:184
  35.6 8.9 %collective-permute-start.14 = (bf16[1056,128]{1,0:T(8,128)(2,1)S(1)}, bf16[1056,128]{1,0:T(8,128)(2,1)S(1)}, u32[]{:S(2)}, u32[]{:S(2)}) collective-permute-start(bf16[1056,128]{1,0:T(8,128)(2,1)S(1)} %collective-permute-done.8.refs_7_), channel_id=1, source_target_pairs={{0,1},{1,0},{2,3},{3,2},{4,5},{5,4},{6,7},{7,6},{8,9},{9,8},{10,11... | collective-permute-start | bytes 811016 | tf_op jit(solution)/shard_map/ppermute | solution.py:184
  38.2 11.1 %collective-permute-start.18 = (bf16[1056,128]{1,0:T(8,128)(2,1)S(1)}, bf16[1056,128]{1,0:T(8,128)(2,1)S(1)}, u32[]{:S(2)}, u32[]{:S(2)}) collective-permute-start(bf16[1056,128]{1,0:T(8,128)(2,1)S(1)} %collective-permute-done.3.refs_0_), channel_id=1, source_target_pairs={{0,1},{1,0},{2,3},{3,2},{4,5},{5,4},{6,7},{7,6},{8,9},{9,8},{10,11... | collective-permute-start | bytes 811016 | tf_op jit(solution)/shard_map/ppermute | solution.py:184
  39.5 11.6 %collective-permute-start.4 = (bf16[1056,128]{1,0:T(8,128)(2,1)S(1)}, bf16[1056,128]{1,0:T(8,128)(2,1)S(1)}, u32[]{:S(2)}, u32[]{:S(2)}) collective-permute-start(bf16[1056,128]{1,0:T(8,128)(2,1)S(1)} %collective-permute-done.3.refs_0_), channel_id=1, source_target_pairs={{0,4},{1,29},{2,6},{3,31},{4,8},{5,1},{6,10},{7,3},{8,12},{9,5},{1... | collective-permute-start | bytes 811016 | tf_op jit(solution)/shard_map/ppermute | solution.py:184
  41.6 7.7 %collective-permute-start.19 = (bf16[1056,128]{1,0:T(8,128)(2,1)S(1)}, bf16[1056,128]{1,0:T(8,128)(2,1)S(1)}, u32[]{:S(2)}, u32[]{:S(2)}) collective-permute-start(bf16[1056,128]{1,0:T(8,128)(2,1)S(1)} %collective-permute-done.9.refs_1_), channel_id=1, source_target_pairs={{0,1},{1,0},{2,3},{3,2},{4,5},{5,4},{6,7},{7,6},{8,9},{9,8},{10,11... | collective-permute-start | bytes 811016 | tf_op jit(solution)/shard_map/ppermute | solution.py:184
  43.0 8.2 %collective-permute-start.10 = (bf16[1056,128]{1,0:T(8,128)(2,1)S(1)}, bf16[1056,128]{1,0:T(8,128)(2,1)S(1)}, u32[]{:S(2)}, u32[]{:S(2)}) collective-permute-start(bf16[1056,128]{1,0:T(8,128)(2,1)S(1)} %collective-permute-done.9.refs_1_), channel_id=1, source_target_pairs={{0,4},{1,29},{2,6},{3,31},{4,8},{5,1},{6,10},{7,3},{8,12},{9,5},{1... | collective-permute-start | bytes 811016 | tf_op jit(solution)/shard_map/ppermute | solution.py:184

commit v5 on v3

--- a/solution.py
+++ b/solution.py
@@ -68,7 +68,7 @@
 
 
 def round_units(refs, y, c):
-    pair, beside = refs
+    beside, pair = refs
     return (
         (pair, 0, y, c),
         (pair, UNIT, y, 1 - c),
@@ -110,9 +110,9 @@
     )
 
 
-def finish(codes, pair, beside, dense_left, before, squares, sums, dense_right, product, held, sem):
+def finish(codes, beside, pair, dense_left, before, squares, sums, dense_right, product, held, sem):
     z, y, c, _, _ = where_am_i()
-    units = round_units((pair, beside), y, c)
+    units = round_units((beside, pair), y, c)
     product[...] = before[...] + multiply(dense_left, dense_right, (z + 4) & 7, units)
     column = lax.broadcasted_iota(jnp.int32, (8, TILE), 0)
     total = jnp.zeros((8, TILE), F32)
@@ -190,7 +190,7 @@
     first = jnp.concatenate([unit, along(CORE, unit)])
     beside, crossed, _ = lax.optimization_barrier((beside, crossed, first))
     second = jnp.concatenate([beside, crossed])
-    later, beside_later, _ = lax.optimization_barrier((unit, result_coords, beside))
+    later, beside_later, _ = lax.optimization_barrier((unit, result_coords, first))
     row = jnp.concatenate([later, across(YHI, later)])
     row = jnp.concatenate([row, across(XNEAR, row)])
     left = [row, across(XMIRROR, row)]
@@ -198,11 +198,12 @@
     code = jnp.where(slot < result_counts[0, 0], at, at + 16).astype(BF16)
     codes = jnp.broadcast_to(code[:, None], (16, TILE))
 
-    streams = [first, second]
+    streams = [second, first]
     right = [streams]
     for r in range(3):
         streams = [along(RING, v) for v in streams]
-        right += [streams, [along(CORE, v) for v in streams]]
+        other = lax.optimization_barrier(streams)
+        right += [streams, [along(CORE, v) for v in other]]
     last = [along(RING, v) for v in streams]
 
     limit = pltpu.CompilerParams(vmem_limit_bytes=24 * 2**20)

time: 74.3 us -> 74.4 us (level)
  waiting for transfers between devices: 9.72 us -> 13 us
  blocking collectives: 16.1 us -> 13.3 us
    ppermute x3, waiting for transfers between devices: 0.01 us -> 7.37 us  [across(): return lax.ppermute(v, 'group', perm)]
    ppermute x17, waiting for transfers between devices: 9.71 us -> 5.6 us  [along(): return lax.ppermute(v, 'loop', perm)]
    all_to_all x1, blocking collectives: 16.1 us -> 13.3 us  [shards(): sums = lax.all_to_all(sums, 'loop', 0, 0, tiled=True)]
    ppermute x17, starting transfers between devices: 27.7 us -> 25.6 us  [along(): return lax.ppermute(v, 'loop', perm)]
    ppermute x3, starting transfers between devices: 5.04 us -> 6.78 us  [across(): return lax.ppermute(v, 'group', perm)]
  transfers between devices with their start and end apart: 20 -> 20, of which waited for: 3 -> 4; matrix products, arithmetic and copies ran while one was open for 2% -> 2% of each run, Pallas kernels for 9% -> 9%
where the time goes in v5:
time: 74.4 us; the launch traced here: 74.2 us
  starting transfers between devices  32.4 us (44%)
  blocking collectives  13.3 us (18%)
  waiting for transfers between devices  13 us (17%)
  Pallas kernels  10.5 us (14%)
  other arithmetic  3.19 us (4%)
  between operations  1.59 us (2%)
    ppermute x17, starting transfers between devices, along(): return lax.ppermute(v, 'loop', perm)  25.6 us
    all_to_all x1, blocking collectives, shards(): sums = lax.all_to_all(sums, 'loop', 0, 0, tiled=True)  13.3 us
    ppermute x3, waiting for transfers between devices, across(): return lax.ppermute(v, 'group', perm)  7.37 us
    ppermute x3, starting transfers between devices, across(): return lax.ppermute(v, 'group', perm)  6.78 us
    ppermute x17, waiting for transfers between devices, along(): return lax.ppermute(v, 'loop', perm)  5.6 us
    pallas_call x1, Pallas kernels, shards(): pl.pallas_call(begin, in_specs=[WHOLE] * 12, out_specs=[WHOLE] * 2, out_s...  4.79 us
    pallas_call x1, Pallas kernels, shards(): pl.pallas_call(finish, in_specs=[WHOLE] * 5, out_specs=[AWAY, WHOLE], out...  1.98 us
    pallas_call x1, Pallas kernels, shards(): pl.pallas_call(rescale, in_specs=[AWAY] * 3, out_specs=AWAY, out_shape=ja...  1.94 us
  transfers between devices with their start and end apart: 20, of which 4 were waited for; matrix products, arithmetic and copies ran while one was open for 2% of the time, Pallas kernels for 9%

profile of v5, /device:TPU:1, one launch (start us, length us, event | category | flops | bytes accessed | tf_op | source)
XLA Modules:
  0.0 74.2 jit_solution(15873814904807621202)
XLA Ops:
  0.7 0.7 fusion
  1.3 0.1 broadcast_in_dim.20
  1.4 0.9 %pad_maximum_fusion.2 = bf16[528,128]{1,0:T(8,128)(2,1)S(1)} fusion(bf16[16,128]{1,0:T(8,128)(2,1)S(1)} %broadcast_in_dim.20, bf16[512,128]{1,0:T(8,128)(2,1)} %bitcast.8), kind=kLoop, calls=%fused_computation.2 | loop fusion | flops 270336 | bytes 270336 | tf_op jit(solution)/shard_map/concatenate | solution.py:179
  2.3 3.3 %collective-permute-start = (bf16[528,128]{1,0:T(8,128)(2,1)S(1)}, bf16[528,128]{1,0:T(8,128)(2,1)S(1)}, u32[]{:S(2)}, u32[]{:S(2)}) collective-permute-start(bf16[528,128]{1,0:T(8,128)(2,1)S(1)} %pad_maximum_fusion.2), channel_id=1, source_target_pairs={{0,1},{1,0},{2,3},{3,2},{4,5},{5,4},{6,7},{7,6},{8,9},{9,8},{10,11... | collective-permute-start | bytes 405512 | tf_op jit(solution)/shard_map/ppermute | solution.py:184
  5.6 0.0 collective-permute-start.1
  5.6 1.7 %collective-permute-start.2 = (bf16[528,128]{1,0:T(8,128)(2,1)S(1)}, bf16[528,128]{1,0:T(8,128)(2,1)S(1)}, u32[]{:S(2)}, u32[]{:S(2)}) collective-permute-start(bf16[528,128]{1,0:T(8,128)(2,1)S(1)} %pad_maximum_fusion.2), channel_id=1, source_target_pairs={{0,3},{1,2},{2,1},{3,0},{4,7},{5,6},{6,5},{7,4},{8,11},{9,10},{10,... | collective-permute-start | bytes 405512 | tf_op jit(solution)/shard_map/ppermute | solution.py:184
  7.4 0.0 collective-permute-done
  7.4 0.9 %pad_maximum_fusion.refs_1_ = bf16[1056,128]{1,0:T(8,128)(2,1)S(1)} fusion(bf16[528,128]{1,0:T(8,128)(2,1)S(1)} %collective-permute-done, bf16[16,128]{1,0:T(8,128)(2,1)S(1)} %broadcast_in_dim.20, bf16[512,128]{1,0:T(8,128)(2,1)} %bitcast.9), kind=kLoop, calls=%fused_computation | loop fusion | flops 811008 | bytes 540672 | tf_op jit(solution)/shard_map/concatenate | solution.py:190
  8.3 2.5 %collective-permute-done.1 = bf16[528,128]{1,0:T(8,128)(2,1)S(1)} collective-permute-done((bf16[528,128]{1,0:T(8,128)(2,1)S(1)}, bf16[528,128]{1,0:T(8,128)(2,1)S(1)}, u32[]{:S(2)}, u32[]{:S(2)}) %collective-permute-start.1) | collective-permute-done | bytes 135200 | tf_op jit(solution)/shard_map/ppermute | solution.py:184
  10.8 3.1 %collective-permute-done.2 = bf16[528,128]{1,0:T(8,128)(2,1)S(1)} collective-permute-done((bf16[528,128]{1,0:T(8,128)(2,1)S(1)}, bf16[528,128]{1,0:T(8,128)(2,1)S(1)}, u32[]{:S(2)}, u32[]{:S(2)}) %collective-permute-start.2) | collective-permute-done | bytes 135200 | tf_op jit(solution)/shard_map/ppermute | solution.py:184
  13.9 3.9 %collective-permute-start.3 = (bf16[1056,128]{1,0:T(8,128)(2,1)S(1)}, bf16[1056,128]{1,0:T(8,128)(2,1)S(1)}, u32[]{:S(2)}, u32[]{:S(2)}) collective-permute-start(bf16[1056,128]{1,0:T(8,128)(2,1)S(1)} %constant_dynamic-update-slice_fusion.refs_0_), channel_id=1, source_target_pairs={{0,4},{1,29},{2,6},{3,31},{4,8},{5,1},{6,10},{7,3},{8,12},{9,5},{1... | collective-permute-start | bytes 811016 | tf_op jit(solution)/shard_map/ppermute | solution.py:184
  17.8 0.7 collective-permute-start.7
  18.6 2.9 %collective-permute-start.15 = (bf16[528,128]{1,0:T(8,128)(2,1)S(1)}, bf16[528,128]{1,0:T(8,128)(2,1)S(1)}, u32[]{:S(2)}, u32[]{:S(2)}) collective-permute-start(bf16[528,128]{1,0:T(8,128)(2,1)S(1)} %pad_maximum_fusion.2), channel_id=1, source_target_pairs={{0,32},{32,0},{64,96},{96,64},{128,160},{160,128},{192,224},{224,1... | collective-permute-start | bytes 405512 | tf_op jit(solution)/shard_map/ppermute | solution.py:187
  21.5 0.0 collective-permute-done.3.refs_2_
  21.5 3.2 %collective-permute-start.4 = (bf16[1056,128]{1,0:T(8,128)(2,1)S(1)}, bf16[1056,128]{1,0:T(8,128)(2,1)S(1)}, u32[]{:S(2)}, u32[]{:S(2)}) collective-permute-start(bf16[1056,128]{1,0:T(8,128)(2,1)S(1)} %collective-permute-done.3.refs_2_), channel_id=1, source_target_pairs={{0,4},{1,29},{2,6},{3,31},{4,8},{5,1},{6,10},{7,3},{8,12},{9,5},{1... | collective-permute-start | bytes 811016 | tf_op jit(solution)/shard_map/ppermute | solution.py:184
  24.6 0.0 collective-permute-done.7.refs_3_
  24.6 2.6 %collective-permute-start.8 = (bf16[1056,128]{1,0:T(8,128)(2,1)S(1)}, bf16[1056,128]{1,0:T(8,128)(2,1)S(1)}, u32[]{:S(2)}, u32[]{:S(2)}) collective-permute-start(bf16[1056,128]{1,0:T(8,128)(2,1)S(1)} %collective-permute-done.7.refs_3_), channel_id=1, source_target_pairs={{0,4},{1,29},{2,6},{3,31},{4,8},{5,1},{6,10},{7,3},{8,12},{9,5},{1... | collective-permute-start | bytes 811016 | tf_op jit(solution)/shard_map/ppermute | solution.py:184
  27.2 0.0 collective-permute-done.15
  27.3 1.3 %collective-permute-start.16 = (bf16[1056,128]{1,0:T(8,128)(2,1)S(1)}, bf16[1056,128]{1,0:T(8,128)(2,1)S(1)}, u32[]{:S(2)}, u32[]{:S(2)}) collective-permute-start(bf16[1056,128]{1,0:T(8,128)(2,1)S(1)} %pad_maximum_fusion.1), channel_id=1, source_target_pairs={{0,64},{32,96},{64,0},{96,32},{128,192},{160,224},{192,128},{224,1... | collective-permute-start | bytes 811016 | tf_op jit(solution)/shard_map/ppermute | solution.py:187
  28.6 0.0 collective-permute-done.4.refs_6_
  28.6 2.5 %collective-permute-start.5 = (bf16[1056,128]{1,0:T(8,128)(2,1)S(1)}, bf16[1056,128]{1,0:T(8,128)(2,1)S(1)}, u32[]{:S(2)}, u32[]{:S(2)}) collective-permute-start(bf16[1056,128]{1,0:T(8,128)(2,1)S(1)} %collective-permute-done.4.refs_6_), channel_id=1, source_target_pairs={{0,4},{1,29},{2,6},{3,31},{4,8},{5,1},{6,10},{7,3},{8,12},{9,5},{1... | collective-permute-start | bytes 811016 | tf_op jit(solution)/shard_map/ppermute | solution.py:184
  31.2 0.0 collective-permute-done.8.refs_7_
  31.2 2.9 %collective-permute-start.9 = (bf16[1056,128]{1,0:T(8,128)(2,1)S(1)}, bf16[1056,128]{1,0:T(8,128)(2,1)S(1)}, u32[]{:S(2)}, u32[]{:S(2)}) collective-permute-start(bf16[1056,128]{1,0:T(8,128)(2,1)S(1)} %collective-permute-done.8.refs_7_), channel_id=1, source_target_pairs={{0,4},{1,29},{2,6},{3,31},{4,8},{5,1},{6,10},{7,3},{8,12},{9,5},{1... | collective-permute-start | bytes 811016 | tf_op jit(solution)/shard_map/ppermute | solution.py:184
  34.1 0.4 collective-permute-done.16
  34.5 2.6 %collective-permute-start.17 = (bf16[2112,128]{1,0:T(8,128)(2,1)S(1)}, bf16[2112,128]{1,0:T(8,128)(2,1)S(1)}, u32[]{:S(2)}, u32[]{:S(2)}) collective-permute-start(bf16[2112,128]{1,0:T(8,128)(2,1)S(1)} %constant_dynamic-update-slice_fusion.2.refs_10_), channel_id=1, source_target_pairs={{0,192},{32,224},{64,128},{96,160},{128,64},{160,96},{192,0},{224,... | collective-permute-start | bytes 1622024 | tf_op jit(solution)/shard_map/ppermute | solution.py:187
  37.0 0.0 collective-permute-start.11
  37.0 0.5 collective-permute-start.12
  37.6 0.0 collective-permute-done.5.refs_0_
  37.6 0.5 collective-permute-start.13
  38.1 0.0 collective-permute-done.9.refs_1_
  38.1 2.9 %collective-permute-start.14 = (bf16[1056,128]{1,0:T(8,128)(2,1)S(1)}, bf16[1056,128]{1,0:T(8,128)(2,1)S(1)}, u32[]{:S(2)}, u32[]{:S(2)}) collective-permute-start(bf16[1056,128]{1,0:T(8,128)(2,1)S(1)} %collective-permute-done.8.refs_7_), channel_id=1, source_target_pairs={{0,1},{1,0},{2,3},{3,2},{4,5},{5,4},{6,7},{7,6},{8,9},{9,8},{10,11... | collective-permute-start | bytes 811016 | tf_op jit(solution)/shard_map/ppermute | solution.py:184
  41.6 0.7 fusion.1
  42.3 0.0 collective-permute-done.11.refs_4_
  42.3 0.0 collective-permute-start.18
  42.3 0.0 collective-permute-done.12.refs_5_
  42.3 0.5 collective-permute-start.19
  42.8 0.0 collective-permute-done.13.refs_8_
  42.8 0.1 collective-permute-start.6
  43.0 0.0 collective-permute-done.14.refs_9_
  43.0 0.1 collective-permute-start.10
  43.1 7.0 %collective-permute-done.17.refs_11_ = bf16[2112,128]{1,0:T(8,128)(2,1)S(1)} collective-permute-done((bf16[2112,128]{1,0:T(8,128)(2,1)S(1)}, bf16[2112,128]{1,0:T(8,128)(2,1)S(1)}, u32[]{:S(2)}, u32[]{:S(2)}) %collective-permute-start.17) | collective-permute-done | bytes 540704 | tf_op jit(solution)/shard_map/ppermute | solution.py:187
  50.1 4.8 %shard_map.55 = (bf16[8,256,1152]{2,1,0:T(8,128)(2,1)S(1)}, f32[256,1024]{1,0:T(8,128)S(1)}) custom-call(bf16[1056,128]{1,0:T(8,128)(2,1)S(1)} %constant_dynamic-update-slice_fusion.refs_0_, bf16[1056,128]{1,0:T(8,128)(2,1)S(1)} %pad_maximum_fusion.refs_1_, bf16[1056,128]{1,0:T(8,128)(2,1)S(1)} %collective-permute-done.3.refs_2_, ...), custom_call_target="tpu_custom_call" | custom-call | flops 3221225472 | bytes 25165824 | tf_op jit(solution)/shard_map/pallas_call | solution.py:210
  54.9 0.0 collective-permute-done.18.refs_2_
  54.9 0.0 collective-permute-done.19.refs_3_
  54.9 1.8 %shard_map.56.before = f32[256,1024]{1,0:T(8,128)S(1)} custom-call(bf16[1056,128]{1,0:T(8,128)(2,1)S(1)} %collective-permute-done.5.refs_0_, bf16[1056,128]{1,0:T(8,128)(2,1)S(1)} %collective-permute-done.9.refs_1_, bf16[1056,128]{1,0:T(8,128)(2,1)S(1)} %collective-permute-done.18.refs_2_, bf16[1056,128]{1,0:T(8,128)(2,1)S(1)} %collective-permute-done.19.refs_3_, ...), custom_call_target="tpu_custom_call" | custom-call | flops 1073741824 | bytes 8388608 | tf_op jit(solution)/shard_map/pallas_call | solution.py:219
  56.7 0.0 collective-permute-done.6.beside
  56.7 0.0 collective-permute-done.10.pair
  56.7 0.1 broadcast_in_dim.21.codes
  56.8 2.0 %shard_map.57 = (f32[8,128,128]{2,1,0:T(8,128)S(1)}, f32[32,8,128]{2,1,0:T(8,128)S(1)}) custom-call(bf16[16,128]{1,0:T(8,128)(2,1)S(1)} %broadcast_in_dim.21.codes, bf16[1056,128]{1,0:T(8,128)(2,1)S(1)} %collective-permute-done.6.beside, bf16[1056,128]{1,0:T(8,128)(2,1)S(1)} %collective-permute-done.10.pair, ...), custom_call_target="tpu_custom_call" | custom-call | flops 536870912 | bytes 4194304 | tf_op jit(solution)/shard_map/pallas_call | solution.py:228
  58.8 13.3 %all_to_all.5.sums = f32[32,8,128]{2,1,0:T(8,128)S(1)} all-to-all(f32[32,8,128]{2,1,0:T(8,128)S(1)} %get-tuple-element.32), channel_id=1, replica_groups=mesh['group'=8,'loop'=32] {'loop'}, dimensions={0} | all-to-all | bytes 262144 | tf_op jit(solution)/shard_map/all_to_all | solution.py:242
  72.1 1.9 %shard_map.58 = f32[8,128,128]{2,1,0:T(8,128)} custom-call(bf16[16,128]{1,0:T(8,128)(2,1)S(1)} %broadcast_in_dim.21.codes, f32[8,128,128]{2,1,0:T(8,128)S(1)} %get-tuple-element.31.squares, f32[32,8,128]{2,1,0:T(8,128)S(1)} %all_to_all.5.sums), custom_call_target="tpu_custom_call" | custom-call | tf_op jit(solution)/shard_map/pallas_call | solution.py:243
  (6 shorter events, 0.1 us)
Async XLA Ops:
  2.3 5.1 %collective-permute-start = (bf16[528,128]{1,0:T(8,128)(2,1)S(1)}, bf16[528,128]{1,0:T(8,128)(2,1)S(1)}, u32[]{:S(2)}, u32[]{:S(2)}) collective-permute-start(bf16[528,128]{1,0:T(8,128)(2,1)S(1)} %pad_maximum_fusion.2), channel_id=1, source_target_pairs={{0,1},{1,0},{2,3},{3,2},{4,5},{5,4},{6,7},{7,6},{8,9},{9,8},{10,11... | collective-permute-start | bytes 405512 | tf_op jit(solution)/shard_map/ppermute | solution.py:184
  5.6 5.1 %collective-permute-start.1 = (bf16[528,128]{1,0:T(8,128)(2,1)S(1)}, bf16[528,128]{1,0:T(8,128)(2,1)S(1)}, u32[]{:S(2)}, u32[]{:S(2)}) collective-permute-start(bf16[528,128]{1,0:T(8,128)(2,1)S(1)} %pad_maximum_fusion.2), channel_id=1, source_target_pairs={{0,2},{1,3},{2,0},{3,1},{4,6},{5,7},{6,4},{7,5},{8,10},{9,11},{10,... | collective-permute-start | bytes 405512 | tf_op jit(solution)/shard_map/ppermute | solution.py:184
  5.6 8.2 %collective-permute-start.2 = (bf16[528,128]{1,0:T(8,128)(2,1)S(1)}, bf16[528,128]{1,0:T(8,128)(2,1)S(1)}, u32[]{:S(2)}, u32[]{:S(2)}) collective-permute-start(bf16[528,128]{1,0:T(8,128)(2,1)S(1)} %pad_maximum_fusion.2), channel_id=1, source_target_pairs={{0,3},{1,2},{2,1},{3,0},{4,7},{5,6},{6,5},{7,4},{8,11},{9,10},{10,... | collective-permute-start | bytes 405512 | tf_op jit(solution)/shard_map/ppermute | solution.py:184
  13.9 7.6 %collective-permute-start.3 = (bf16[1056,128]{1,0:T(8,128)(2,1)S(1)}, bf16[1056,128]{1,0:T(8,128)(2,1)S(1)}, u32[]{:S(2)}, u32[]{:S(2)}) collective-permute-start(bf16[1056,128]{1,0:T(8,128)(2,1)S(1)} %constant_dynamic-update-slice_fusion.refs_0_), channel_id=1, source_target_pairs={{0,4},{1,29},{2,6},{3,31},{4,8},{5,1},{6,10},{7,3},{8,12},{9,5},{1... | collective-permute-start | bytes 811016 | tf_op jit(solution)/shard_map/ppermute | solution.py:184
  17.8 6.8 %collective-permute-start.7 = (bf16[1056,128]{1,0:T(8,128)(2,1)S(1)}, bf16[1056,128]{1,0:T(8,128)(2,1)S(1)}, u32[]{:S(2)}, u32[]{:S(2)}) collective-permute-start(bf16[1056,128]{1,0:T(8,128)(2,1)S(1)} %pad_maximum_fusion.refs_1_), channel_id=1, source_target_pairs={{0,4},{1,29},{2,6},{3,31},{4,8},{5,1},{6,10},{7,3},{8,12},{9,5},{1... | collective-permute-start | bytes 811016 | tf_op jit(solution)/shard_map/ppermute | solution.py:184
  18.6 8.7 %collective-permute-start.15 = (bf16[528,128]{1,0:T(8,128)(2,1)S(1)}, bf16[528,128]{1,0:T(8,128)(2,1)S(1)}, u32[]{:S(2)}, u32[]{:S(2)}) collective-permute-start(bf16[528,128]{1,0:T(8,128)(2,1)S(1)} %pad_maximum_fusion.2), channel_id=1, source_target_pairs={{0,32},{32,0},{64,96},{96,64},{128,160},{160,128},{192,224},{224,1... | collective-permute-start | bytes 405512 | tf_op jit(solution)/shard_map/ppermute | solution.py:187
  21.5 7.1 %collective-permute-start.4 = (bf16[1056,128]{1,0:T(8,128)(2,1)S(1)}, bf16[1056,128]{1,0:T(8,128)(2,1)S(1)}, u32[]{:S(2)}, u32[]{:S(2)}) collective-permute-start(bf16[1056,128]{1,0:T(8,128)(2,1)S(1)} %collective-permute-done.3.refs_2_), channel_id=1, source_target_pairs={{0,4},{1,29},{2,6},{3,31},{4,8},{5,1},{6,10},{7,3},{8,12},{9,5},{1... | collective-permute-start | bytes 811016 | tf_op jit(solution)/shard_map/ppermute | solution.py:184
  24.6 6.5 %collective-permute-start.8 = (bf16[1056,128]{1,0:T(8,128)(2,1)S(1)}, bf16[1056,128]{1,0:T(8,128)(2,1)S(1)}, u32[]{:S(2)}, u32[]{:S(2)}) collective-permute-start(bf16[1056,128]{1,0:T(8,128)(2,1)S(1)} %collective-permute-done.7.refs_3_), channel_id=1, source_target_pairs={{0,4},{1,29},{2,6},{3,31},{4,8},{5,1},{6,10},{7,3},{8,12},{9,5},{1... | collective-permute-start | bytes 811016 | tf_op jit(solution)/shard_map/ppermute | solution.py:184
  27.3 7.2 %collective-permute-start.16 = (bf16[1056,128]{1,0:T(8,128)(2,1)S(1)}, bf16[1056,128]{1,0:T(8,128)(2,1)S(1)}, u32[]{:S(2)}, u32[]{:S(2)}) collective-permute-start(bf16[1056,128]{1,0:T(8,128)(2,1)S(1)} %pad_maximum_fusion.1), channel_id=1, source_target_pairs={{0,64},{32,96},{64,0},{96,32},{128,192},{160,224},{192,128},{224,1... | collective-permute-start | bytes 811016 | tf_op jit(solution)/shard_map/ppermute | solution.py:187
  28.6 8.9 %collective-permute-start.5 = (bf16[1056,128]{1,0:T(8,128)(2,1)S(1)}, bf16[1056,128]{1,0:T(8,128)(2,1)S(1)}, u32[]{:S(2)}, u32[]{:S(2)}) collective-permute-start(bf16[1056,128]{1,0:T(8,128)(2,1)S(1)} %collective-permute-done.4.refs_6_), channel_id=1, source_target_pairs={{0,4},{1,29},{2,6},{3,31},{4,8},{5,1},{6,10},{7,3},{8,12},{9,5},{1... | collective-permute-start | bytes 811016 | tf_op jit(solution)/shard_map/ppermute | solution.py:184
  31.2 6.9 %collective-permute-start.9 = (bf16[1056,128]{1,0:T(8,128)(2,1)S(1)}, bf16[1056,128]{1,0:T(8,128)(2,1)S(1)}, u32[]{:S(2)}, u32[]{:S(2)}) collective-permute-start(bf16[1056,128]{1,0:T(8,128)(2,1)S(1)} %collective-permute-done.8.refs_7_), channel_id=1, source_target_pairs={{0,4},{1,29},{2,6},{3,31},{4,8},{5,1},{6,10},{7,3},{8,12},{9,5},{1... | collective-permute-start | bytes 811016 | tf_op jit(solution)/shard_map/ppermute | solution.py:184
  34.5 15.6 %collective-permute-start.17 = (bf16[2112,128]{1,0:T(8,128)(2,1)S(1)}, bf16[2112,128]{1,0:T(8,128)(2,1)S(1)}, u32[]{:S(2)}, u32[]{:S(2)}) collective-permute-start(bf16[2112,128]{1,0:T(8,128)(2,1)S(1)} %constant_dynamic-update-slice_fusion.2.refs_10_), channel_id=1, source_target_pairs={{0,192},{32,224},{64,128},{96,160},{128,64},{160,96},{192,0},{224,... | collective-permute-start | bytes 1622024 | tf_op jit(solution)/shard_map/ppermute | solution.py:187
  37.0 5.3 %collective-permute-start.11 = (bf16[1056,128]{1,0:T(8,128)(2,1)S(1)}, bf16[1056,128]{1,0:T(8,128)(2,1)S(1)}, u32[]{:S(2)}, u32[]{:S(2)}) collective-permute-start(bf16[1056,128]{1,0:T(8,128)(2,1)S(1)} %collective-permute-done.3.refs_2_), channel_id=1, source_target_pairs={{0,1},{1,0},{2,3},{3,2},{4,5},{5,4},{6,7},{7,6},{8,9},{9,8},{10,11... | collective-permute-start | bytes 811016 | tf_op jit(solution)/shard_map/ppermute | solution.py:184
  37.0 5.3 %collective-permute-start.12 = (bf16[1056,128]{1,0:T(8,128)(2,1)S(1)}, bf16[1056,128]{1,0:T(8,128)(2,1)S(1)}, u32[]{:S(2)}, u32[]{:S(2)}) collective-permute-start(bf16[1056,128]{1,0:T(8,128)(2,1)S(1)} %collective-permute-done.7.refs_3_), channel_id=1, source_target_pairs={{0,1},{1,0},{2,3},{3,2},{4,5},{5,4},{6,7},{7,6},{8,9},{9,8},{10,11... | collective-permute-start | bytes 811016 | tf_op jit(solution)/shard_map/ppermute | solution.py:184
  37.6 5.3 %collective-permute-start.13 = (bf16[1056,128]{1,0:T(8,128)(2,1)S(1)}, bf16[1056,128]{1,0:T(8,128)(2,1)S(1)}, u32[]{:S(2)}, u32[]{:S(2)}) collective-permute-start(bf16[1056,128]{1,0:T(8,128)(2,1)S(1)} %collective-permute-done.4.refs_6_), channel_id=1, source_target_pairs={{0,1},{1,0},{2,3},{3,2},{4,5},{5,4},{6,7},{7,6},{8,9},{9,8},{10,11... | collective-permute-start | bytes 811016 | tf_op jit(solution)/shard_map/ppermute | solution.py:184
  38.1 4.9 %collective-permute-start.14 = (bf16[1056,128]{1,0:T(8,128)(2,1)S(1)}, bf16[1056,128]{1,0:T(8,128)(2,1)S(1)}, u32[]{:S(2)}, u32[]{:S(2)}) collective-permute-start(bf16[1056,128]{1,0:T(8,128)(2,1)S(1)} %collective-permute-done.8.refs_7_), channel_id=1, source_target_pairs={{0,1},{1,0},{2,3},{3,2},{4,5},{5,4},{6,7},{7,6},{8,9},{9,8},{10,11... | collective-permute-start | bytes 811016 | tf_op jit(solution)/shard_map/ppermute | solution.py:184
  42.3 12.5 %collective-permute-start.18 = (bf16[1056,128]{1,0:T(8,128)(2,1)S(1)}, bf16[1056,128]{1,0:T(8,128)(2,1)S(1)}, u32[]{:S(2)}, u32[]{:S(2)}) collective-permute-start(bf16[1056,128]{1,0:T(8,128)(2,1)S(1)} %collective-permute-done.5.refs_0_), channel_id=1, source_target_pairs={{0,1},{1,0},{2,3},{3,2},{4,5},{5,4},{6,7},{7,6},{8,9},{9,8},{10,11... | collective-permute-start | bytes 811016 | tf_op jit(solution)/shard_map/ppermute | solution.py:184
  42.3 12.5 %collective-permute-start.19 = (bf16[1056,128]{1,0:T(8,128)(2,1)S(1)}, bf16[1056,128]{1,0:T(8,128)(2,1)S(1)}, u32[]{:S(2)}, u32[]{:S(2)}) collective-permute-start(bf16[1056,128]{1,0:T(8,128)(2,1)S(1)} %collective-permute-done.9.refs_1_), channel_id=1, source_target_pairs={{0,1},{1,0},{2,3},{3,2},{4,5},{5,4},{6,7},{7,6},{8,9},{9,8},{10,11... | collective-permute-start | bytes 811016 | tf_op jit(solution)/shard_map/ppermute | solution.py:184
  42.8 13.9 %collective-permute-start.6 = (bf16[1056,128]{1,0:T(8,128)(2,1)S(1)}, bf16[1056,128]{1,0:T(8,128)(2,1)S(1)}, u32[]{:S(2)}, u32[]{:S(2)}) collective-permute-start(bf16[1056,128]{1,0:T(8,128)(2,1)S(1)} %collective-permute-done.5.refs_0_), channel_id=1, source_target_pairs={{0,4},{1,29},{2,6},{3,31},{4,8},{5,1},{6,10},{7,3},{8,12},{9,5},{1... | collective-permute-start | bytes 811016 | tf_op jit(solution)/shard_map/ppermute | solution.py:184
  43.0 13.7 %collective-permute-start.10 = (bf16[1056,128]{1,0:T(8,128)(2,1)S(1)}, bf16[1056,128]{1,0:T(8,128)(2,1)S(1)}, u32[]{:S(2)}, u32[]{:S(2)}) collective-permute-start(bf16[1056,128]{1,0:T(8,128)(2,1)S(1)} %collective-permute-done.9.refs_1_), channel_id=1, source_target_pairs={{0,4},{1,29},{2,6},{3,31},{4,8},{5,1},{6,10},{7,3},{8,12},{9,5},{1... | collective-permute-start | bytes 811016 | tf_op jit(solution)/shard_map/ppermute | solution.py:184

commit v6 on v5

--- a/solution.py
+++ b/solution.py
@@ -110,10 +110,26 @@
     )
 
 
-def finish(codes, beside, pair, dense_left, before, squares, sums, dense_right, product, held, sem):
-    z, y, c, _, _ = where_am_i()
-    units = round_units((beside, pair), y, c)
-    product[...] = before[...] + multiply(dense_left, dense_right, (z + 4) & 7, units)
+def half(ref, y, c, dense_left, dense_half):
+    z = where_am_i()[0]
+    dense_half[...] = jnp.zeros_like(dense_half)
+    place(dense_half, ref, 0, c * 256)
+    place(dense_half, ref, UNIT, (1 - c) * 256)
+    return jnp.dot(
+        dense_left[(z + 4) & 7, :, pl.ds(pl.multiple_of(y * 512, 512), 512)],
+        dense_half[:, : 8 * TILE],
+        preferred_element_type=F32,
+    )
+
+
+def add_half(beside, dense_left, before, product, dense_half):
+    _, y, c, _, _ = where_am_i()
+    product[...] = before[...] + half(beside, 1 - y, c, dense_left, dense_half)
+
+
+def finish(codes, pair, dense_left, before, squares, sums, dense_half, product, held, sem):
+    _, y, c, _, _ = where_am_i()
+    product[...] = before[...] + half(pair, y, c, dense_left, dense_half)
     column = lax.broadcasted_iota(jnp.int32, (8, TILE), 0)
     total = jnp.zeros((8, TILE), F32)
     copies = []
@@ -163,12 +179,13 @@
 DENSE_LEFT = jax.ShapeDtypeStruct((8, 256, WIDE), BF16)
 PRODUCT = jax.ShapeDtypeStruct((256, 1024), F32)
 DENSE_RIGHT = pltpu.VMEM((1024, WIDE), BF16)
+DENSE_HALF = pltpu.VMEM((512, WIDE), BF16)
 TILES = (8, TILE, TILE)
 
 
 def cost(blocks):
     return pl.CostEstimate(
-        flops=blocks * 2 * 256 * 1024 * 1024, bytes_accessed=blocks * 4 * 2**20, transcendentals=0
+        flops=blocks * 2**20, bytes_accessed=blocks * 2**16, transcendentals=0
     )
 
 
@@ -187,23 +204,34 @@
         return lax.ppermute(v, "group", perm)
 
     beside, crossed = along(YLO, unit), along(DIAGONAL, unit)
-    first = jnp.concatenate([unit, along(CORE, unit)])
+    pair = along(CORE, unit)
+    first = jnp.concatenate([unit, pair])
     beside, crossed, _ = lax.optimization_barrier((beside, crossed, first))
     second = jnp.concatenate([beside, crossed])
-    later, beside_later, _ = lax.optimization_barrier((unit, result_coords, first))
+    later, beside_later, _ = lax.optimization_barrier((unit, result_coords, pair))
     row = jnp.concatenate([later, across(YHI, later)])
-    row = jnp.concatenate([row, across(XNEAR, row)])
-    left = [row, across(XMIRROR, row)]
     at = jnp.pad(beside_later[0, 0], (0, 8))
     code = jnp.where(slot < result_counts[0, 0], at, at + 16).astype(BF16)
     codes = jnp.broadcast_to(code[:, None], (16, TILE))
 
+    def after(v, *others):
+        return lax.optimization_barrier((v, *others))
+
     streams = [second, first]
     right = [streams]
+    row = jnp.concatenate([row, across(XNEAR, row)])
     for r in range(3):
+        if r == 2:
+            streams = [after(streams[0], *right[-3])[0], streams[1]]
         streams = [along(RING, v) for v in streams]
-        other = lax.optimization_barrier(streams)
+        if r == 0:
+            streams[1], row = after(streams[1], row)
+            left = [row, across(XMIRROR, row)]
+        other = after(*streams)
+        if r == 2:
+            other = after(*other, left[1])[:2]
         right += [streams, [along(CORE, v) for v in other]]
+    streams = [after(streams[0], *right[-3])[0], streams[1]]
     last = [along(RING, v) for v in streams]
 
     limit = pltpu.CompilerParams(vmem_limit_bytes=24 * 2**20)
@@ -217,6 +245,15 @@
         cost_estimate=cost(6),
     )(*sum(right[:5], []), *left)
     product = pl.pallas_call(
+        add_half,
+        in_specs=[WHOLE] * 3,
+        out_specs=WHOLE,
+        out_shape=PRODUCT,
+        scratch_shapes=[DENSE_HALF],
+        compiler_params=limit,
+        cost_estimate=cost(1),
+    )(last[0], dense_left, product)
+    product = pl.pallas_call(
         proceed,
         in_specs=[WHOLE] * 6,
         out_specs=WHOLE,
@@ -227,18 +264,18 @@
     )(*sum(right[5:], []), dense_left, product)
     squares, sums = pl.pallas_call(
         finish,
-        in_specs=[WHOLE] * 5,
+        in_specs=[WHOLE] * 4,
         out_specs=[AWAY, WHOLE],
         out_shape=[jax.ShapeDtypeStruct(TILES, F32), jax.ShapeDtypeStruct((32, 8, TILE), F32)],
         scratch_shapes=[
-            DENSE_RIGHT,
+            DENSE_HALF,
             pltpu.VMEM((256, 1024), F32),
             pltpu.VMEM(TILES, F32),
             pltpu.SemaphoreType.DMA((8,)),
         ],
         compiler_params=limit,
         cost_estimate=cost(1),
-    )(codes, *last, dense_left, product)
+    )(codes, last[1], dense_left, product)
     sums = lax.all_to_all(sums, "loop", 0, 0, tiled=True)
     out = pl.pallas_call(
         rescale,

time: 74.4 us -> 75.1 us (level)
  blocking collectives: 13.3 us -> 14.5 us
    ppermute x3, waiting for transfers between devices: 7.37 us -> 4.35 us  [across(): return lax.ppermute(v, 'group', perm)]
    ppermute x17, waiting for transfers between devices: 5.6 us -> 8.57 us  [along(): return lax.ppermute(v, 'loop', perm)]
    ppermute x17, starting transfers between devices: 25.6 us -> 27.5 us  [along(): return lax.ppermute(v, 'loop', perm)]
    ppermute x3, starting transfers between devices: 6.78 us -> 4.96 us  [across(): return lax.ppermute(v, 'group', perm)]
    all_to_all x1, blocking collectives: 13.3 us -> 14.5 us  [shards(): sums = lax.all_to_all(sums, 'loop', 0, 0, tiled=True)]
    pallas_call x1 -> x2, Pallas kernels: 1.98 us -> 2.16 us  [the longest x1 1.54 us: shards(): pl.pallas_call(finish, in_specs=[WHOLE] * 4, out_specs=[AWAY, WHOLE], out...]
  transfers between devices with their start and end apart: 20 -> 20, of which waited for: 4 -> 8; matrix products, arithmetic and copies ran while one was open for 2% -> 1% of each run, Pallas kernels for 9% -> 10%
where the time goes in v6:
time: 75.1 us; the launch traced here: 75 us
  starting transfers between devices  32.5 us (43%)
  blocking collectives  14.5 us (19%)
  waiting for transfers between devices  12.9 us (17%)
  Pallas kernels  10.7 us (14%)
  other arithmetic  2.56 us (3%)
  between operations  1.6 us (2%)
    ppermute x17, starting transfers between devices, along(): return lax.ppermute(v, 'loop', perm)  27.5 us
    all_to_all x1, blocking collectives, shards(): sums = lax.all_to_all(sums, 'loop', 0, 0, tiled=True)  14.5 us
    ppermute x17, waiting for transfers between devices, along(): return lax.ppermute(v, 'loop', perm)  8.57 us
    ppermute x3, starting transfers between devices, across(): return lax.ppermute(v, 'group', perm)  4.96 us
    pallas_call x1, Pallas kernels, shards(): pl.pallas_call(begin, in_specs=[WHOLE] * 12, out_specs=[WHOLE] * 2, out_s...  4.8 us
    ppermute x3, waiting for transfers between devices, across(): return lax.ppermute(v, 'group', perm)  4.35 us
    pallas_call x1, Pallas kernels, shards(): pl.pallas_call(rescale, in_specs=[AWAY] * 3, out_specs=AWAY, out_shape=ja...  1.94 us
    pallas_call x1, Pallas kernels, shards(): pl.pallas_call(proceed, in_specs=[WHOLE] * 6, out_specs=WHOLE, out_shape=...  1.8 us
  transfers between devices with their start and end apart: 20, of which 8 were waited for; matrix products, arithmetic and copies ran while one was open for 1% of the time, Pallas kernels for 10%

profile of v6, /device:TPU:1, one launch (start us, length us, event | category | flops | bytes accessed | tf_op | source)
XLA Modules:
  0.0 75.0 jit_solution(16678972933030453510)
XLA Ops:
  0.7 0.7 fusion
  1.3 0.1 broadcast_in_dim.20
  1.4 0.9 %pad_maximum_fusion.3 = bf16[528,128]{1,0:T(8,128)(2,1)S(1)} fusion(bf16[16,128]{1,0:T(8,128)(2,1)S(1)} %broadcast_in_dim.20, bf16[512,128]{1,0:T(8,128)(2,1)} %bitcast.8), kind=kLoop, calls=%fused_computation.3 | loop fusion | flops 270336 | bytes 270336 | tf_op jit(solution)/shard_map/concatenate | solution.py:196
  2.3 3.3 %collective-permute-start = (bf16[528,128]{1,0:T(8,128)(2,1)S(1)}, bf16[528,128]{1,0:T(8,128)(2,1)S(1)}, u32[]{:S(2)}, u32[]{:S(2)}) collective-permute-start(bf16[528,128]{1,0:T(8,128)(2,1)S(1)} %pad_maximum_fusion.3), channel_id=1, source_target_pairs={{0,1},{1,0},{2,3},{3,2},{4,5},{5,4},{6,7},{7,6},{8,9},{9,8},{10,11... | collective-permute-start | bytes 405512 | tf_op jit(solution)/shard_map/ppermute | solution.py:201
  5.6 0.0 collective-permute-start.7
  5.6 1.7 %collective-permute-start.8 = (bf16[528,128]{1,0:T(8,128)(2,1)S(1)}, bf16[528,128]{1,0:T(8,128)(2,1)S(1)}, u32[]{:S(2)}, u32[]{:S(2)}) collective-permute-start(bf16[528,128]{1,0:T(8,128)(2,1)S(1)} %pad_maximum_fusion.3), channel_id=1, source_target_pairs={{0,3},{1,2},{2,1},{3,0},{4,7},{5,6},{6,5},{7,4},{8,11},{9,10},{10,... | collective-permute-start | bytes 405512 | tf_op jit(solution)/shard_map/ppermute | solution.py:201
  7.4 0.0 collective-permute-done
  7.4 1.2 %collective-permute-start.2 = (bf16[528,128]{1,0:T(8,128)(2,1)S(1)}, bf16[528,128]{1,0:T(8,128)(2,1)S(1)}, u32[]{:S(2)}, u32[]{:S(2)}) collective-permute-start(bf16[528,128]{1,0:T(8,128)(2,1)S(1)} %pad_maximum_fusion.3), channel_id=1, source_target_pairs={{0,32},{32,0},{64,96},{96,64},{128,160},{160,128},{192,224},{224,1... | collective-permute-start | bytes 405512 | tf_op jit(solution)/shard_map/ppermute | solution.py:204
  8.6 0.9 %pad_maximum_fusion.1.refs_1_ = bf16[1056,128]{1,0:T(8,128)(2,1)S(1)} fusion(bf16[528,128]{1,0:T(8,128)(2,1)S(1)} %collective-permute-done, bf16[16,128]{1,0:T(8,128)(2,1)S(1)} %broadcast_in_dim.20, bf16[512,128]{1,0:T(8,128)(2,1)} %bitcast.9), kind=kLoop, calls=%fused_computation.1 | loop fusion | flops 811008 | bytes 540672 | tf_op jit(solution)/shard_map/concatenate | solution.py:208
  9.5 0.0 copy-start
  9.5 1.3 %collective-permute-done.7 = bf16[528,128]{1,0:T(8,128)(2,1)S(1)} collective-permute-done((bf16[528,128]{1,0:T(8,128)(2,1)S(1)}, bf16[528,128]{1,0:T(8,128)(2,1)S(1)}, u32[]{:S(2)}, u32[]{:S(2)}) %collective-permute-start.7) | collective-permute-done | bytes 135200 | tf_op jit(solution)/shard_map/ppermute | solution.py:201
  10.8 3.6 %collective-permute-done.8 = bf16[528,128]{1,0:T(8,128)(2,1)S(1)} collective-permute-done((bf16[528,128]{1,0:T(8,128)(2,1)S(1)}, bf16[528,128]{1,0:T(8,128)(2,1)S(1)}, u32[]{:S(2)}, u32[]{:S(2)}) %collective-permute-start.8) | collective-permute-done | bytes 135200 | tf_op jit(solution)/shard_map/ppermute | solution.py:201
  14.4 3.9 %collective-permute-start.9 = (bf16[1056,128]{1,0:T(8,128)(2,1)S(1)}, bf16[1056,128]{1,0:T(8,128)(2,1)S(1)}, u32[]{:S(2)}, u32[]{:S(2)}) collective-permute-start(bf16[1056,128]{1,0:T(8,128)(2,1)S(1)} %constant_dynamic-update-slice_fusion.refs_0_), channel_id=1, source_target_pairs={{0,4},{1,29},{2,6},{3,31},{4,8},{5,1},{6,10},{7,3},{8,12},{9,5},{1... | collective-permute-start | bytes 811016 | tf_op jit(solution)/shard_map/ppermute | solution.py:201
  18.3 0.0 collective-permute-done.2
  18.3 1.3 %collective-permute-start.3 = (bf16[1056,128]{1,0:T(8,128)(2,1)S(1)}, bf16[1056,128]{1,0:T(8,128)(2,1)S(1)}, u32[]{:S(2)}, u32[]{:S(2)}) collective-permute-start(bf16[1056,128]{1,0:T(8,128)(2,1)S(1)} %pad_maximum_fusion.2), channel_id=1, source_target_pairs={{0,64},{32,96},{64,0},{96,32},{128,192},{160,224},{192,128},{224,1... | collective-permute-start | bytes 811016 | tf_op jit(solution)/shard_map/ppermute | solution.py:204
  19.6 4.6 %collective-permute-start.1 = (bf16[1056,128]{1,0:T(8,128)(2,1)S(1)}, bf16[1056,128]{1,0:T(8,128)(2,1)S(1)}, u32[]{:S(2)}, u32[]{:S(2)}) collective-permute-start(bf16[1056,128]{1,0:T(8,128)(2,1)S(1)} %pad_maximum_fusion.1.refs_1_), channel_id=1, source_target_pairs={{0,4},{1,29},{2,6},{3,31},{4,8},{5,1},{6,10},{7,3},{8,12},{9,5},{1... | collective-permute-start | bytes 811016 | tf_op jit(solution)/shard_map/ppermute | solution.py:201
  24.2 0.0 collective-permute-done.9.refs_2_
  24.2 0.7 collective-permute-start.12
  24.9 1.7 %collective-permute-done.3 = bf16[1056,128]{1,0:T(8,128)(2,1)S(1)} collective-permute-done((bf16[1056,128]{1,0:T(8,128)(2,1)S(1)}, bf16[1056,128]{1,0:T(8,128)(2,1)S(1)}, u32[]{:S(2)}, u32[]{:S(2)}) %collective-permute-start.3) | collective-permute-done | bytes 270368 | tf_op jit(solution)/shard_map/ppermute | solution.py:204
  26.6 1.0 %collective-permute-done.1.refs_3_ = bf16[1056,128]{1,0:T(8,128)(2,1)S(1)} collective-permute-done((bf16[1056,128]{1,0:T(8,128)(2,1)S(1)}, bf16[1056,128]{1,0:T(8,128)(2,1)S(1)}, u32[]{:S(2)}, u32[]{:S(2)}) %collective-permute-start.1) | collective-permute-done | bytes 270368 | tf_op jit(solution)/shard_map/ppermute | solution.py:201
  27.6 2.5 %collective-permute-start.10 = (bf16[1056,128]{1,0:T(8,128)(2,1)S(1)}, bf16[1056,128]{1,0:T(8,128)(2,1)S(1)}, u32[]{:S(2)}, u32[]{:S(2)}) collective-permute-start(bf16[1056,128]{1,0:T(8,128)(2,1)S(1)} %collective-permute-done.9.refs_2_), channel_id=1, source_target_pairs={{0,1},{1,0},{2,3},{3,2},{4,5},{5,4},{6,7},{7,6},{8,9},{9,8},{10,11... | collective-permute-start | bytes 811016 | tf_op jit(solution)/shard_map/ppermute | solution.py:201
  30.1 0.0 collective-permute-start.11
  30.1 2.0 %collective-permute-start.4 = (bf16[1056,128]{1,0:T(8,128)(2,1)S(1)}, bf16[1056,128]{1,0:T(8,128)(2,1)S(1)}, u32[]{:S(2)}, u32[]{:S(2)}) collective-permute-start(bf16[1056,128]{1,0:T(8,128)(2,1)S(1)} %collective-permute-done.1.refs_3_), channel_id=1, source_target_pairs={{0,4},{1,29},{2,6},{3,31},{4,8},{5,1},{6,10},{7,3},{8,12},{9,5},{1... | collective-permute-start | bytes 811016 | tf_op jit(solution)/shard_map/ppermute | solution.py:201
  32.1 2.5 %collective-permute-start.15 = (bf16[2112,128]{1,0:T(8,128)(2,1)S(1)}, bf16[2112,128]{1,0:T(8,128)(2,1)S(1)}, u32[]{:S(2)}, u32[]{:S(2)}) collective-permute-start(bf16[2112,128]{1,0:T(8,128)(2,1)S(1)} %pad_maximum_fusion.refs_10_), channel_id=1, source_target_pairs={{0,192},{32,224},{64,128},{96,160},{128,64},{160,96},{192,0},{224,... | collective-permute-start | bytes 1622024 | tf_op jit(solution)/shard_map/ppermute | solution.py:204
  34.6 0.0 collective-permute-done.12.refs_6_
  34.6 0.0 collective-permute-done.10.refs_4_
  34.6 0.0 collective-permute-done.11.refs_5_
  34.6 0.8 %collective-permute-start.16 = (bf16[1056,128]{1,0:T(8,128)(2,1)S(1)}, bf16[1056,128]{1,0:T(8,128)(2,1)S(1)}, u32[]{:S(2)}, u32[]{:S(2)}) collective-permute-start(bf16[1056,128]{1,0:T(8,128)(2,1)S(1)} %collective-permute-done.12.refs_6_), channel_id=1, source_target_pairs={{0,4},{1,29},{2,6},{3,31},{4,8},{5,1},{6,10},{7,3},{8,12},{9,5},{1... | collective-permute-start | bytes 811016 | tf_op jit(solution)/shard_map/ppermute | solution.py:201
  35.4 0.3 collective-permute-done.4.refs_7_
  35.7 2.6 %collective-permute-start.13 = (bf16[1056,128]{1,0:T(8,128)(2,1)S(1)}, bf16[1056,128]{1,0:T(8,128)(2,1)S(1)}, u32[]{:S(2)}, u32[]{:S(2)}) collective-permute-start(bf16[1056,128]{1,0:T(8,128)(2,1)S(1)} %collective-permute-done.12.refs_6_), channel_id=1, source_target_pairs={{0,1},{1,0},{2,3},{3,2},{4,5},{5,4},{6,7},{7,6},{8,9},{9,8},{10,11... | collective-permute-start | bytes 811016 | tf_op jit(solution)/shard_map/ppermute | solution.py:201
  38.2 0.0 collective-permute-start.14
  38.2 1.2 %collective-permute-start.5 = (bf16[1056,128]{1,0:T(8,128)(2,1)S(1)}, bf16[1056,128]{1,0:T(8,128)(2,1)S(1)}, u32[]{:S(2)}, u32[]{:S(2)}) collective-permute-start(bf16[1056,128]{1,0:T(8,128)(2,1)S(1)} %collective-permute-done.4.refs_7_), channel_id=1, source_target_pairs={{0,4},{1,29},{2,6},{3,31},{4,8},{5,1},{6,10},{7,3},{8,12},{9,5},{1... | collective-permute-start | bytes 811016 | tf_op jit(solution)/shard_map/ppermute | solution.py:201
  39.4 0.8 %collective-permute-done.16.refs_0_ = bf16[1056,128]{1,0:T(8,128)(2,1)S(1)} collective-permute-done((bf16[1056,128]{1,0:T(8,128)(2,1)S(1)}, bf16[1056,128]{1,0:T(8,128)(2,1)S(1)}, u32[]{:S(2)}, u32[]{:S(2)}) %collective-permute-start.16) | collective-permute-done | bytes 270368 | tf_op jit(solution)/shard_map/ppermute | solution.py:201
  40.3 0.0 collective-permute-done.13.refs_8_
  40.3 0.0 collective-permute-done.14.refs_9_
  40.3 1.9 %collective-permute-start.19 = (bf16[1056,128]{1,0:T(8,128)(2,1)S(1)}, bf16[1056,128]{1,0:T(8,128)(2,1)S(1)}, u32[]{:S(2)}, u32[]{:S(2)}) collective-permute-start(bf16[1056,128]{1,0:T(8,128)(2,1)S(1)} %collective-permute-done.16.refs_0_), channel_id=1, source_target_pairs={{0,4},{1,29},{2,6},{3,31},{4,8},{5,1},{6,10},{7,3},{8,12},{9,5},{1... | collective-permute-start | bytes 811016 | tf_op jit(solution)/shard_map/ppermute | solution.py:201
  42.2 1.6 %collective-permute-done.5.refs_1_ = bf16[1056,128]{1,0:T(8,128)(2,1)S(1)} collective-permute-done((bf16[1056,128]{1,0:T(8,128)(2,1)S(1)}, bf16[1056,128]{1,0:T(8,128)(2,1)S(1)}, u32[]{:S(2)}, u32[]{:S(2)}) %collective-permute-start.5) | collective-permute-done | bytes 270368 | tf_op jit(solution)/shard_map/ppermute | solution.py:201
  43.9 2.7 %collective-permute-done.15.refs_11_ = bf16[2112,128]{1,0:T(8,128)(2,1)S(1)} collective-permute-done((bf16[2112,128]{1,0:T(8,128)(2,1)S(1)}, bf16[2112,128]{1,0:T(8,128)(2,1)S(1)}, u32[]{:S(2)}, u32[]{:S(2)}) %collective-permute-start.15) | collective-permute-done | bytes 540704 | tf_op jit(solution)/shard_map/ppermute | solution.py:204
  46.5 0.0 collective-permute-start.17
  46.5 0.5 collective-permute-start.18
  47.0 1.7 %collective-permute-start.6 = (bf16[1056,128]{1,0:T(8,128)(2,1)S(1)}, bf16[1056,128]{1,0:T(8,128)(2,1)S(1)}, u32[]{:S(2)}, u32[]{:S(2)}) collective-permute-start(bf16[1056,128]{1,0:T(8,128)(2,1)S(1)} %collective-permute-done.5.refs_1_), channel_id=1, source_target_pairs={{0,4},{1,29},{2,6},{3,31},{4,8},{5,1},{6,10},{7,3},{8,12},{9,5},{1... | collective-permute-start | bytes 811016 | tf_op jit(solution)/shard_map/ppermute | solution.py:201
  49.4 0.0 copy-done
  49.4 4.8 %shard_map.55 = (bf16[8,256,1152]{2,1,0:T(8,128)(2,1)S(1)}, f32[256,1024]{1,0:T(8,128)S(1)}) custom-call(bf16[1056,128]{1,0:T(8,128)(2,1)S(1)} %constant_dynamic-update-slice_fusion.refs_0_, bf16[1056,128]{1,0:T(8,128)(2,1)S(1)} %pad_maximum_fusion.1.refs_1_, bf16[1056,128]{1,0:T(8,128)(2,1)S(1)} %collective-permute-done.9.refs_2_, ...), custom_call_target="tpu_custom_call" | custom-call | flops 6291456 | bytes 393216 | tf_op jit(solution)/shard_map/pallas_call | solution.py:238
  54.2 0.0 collective-permute-done.19.beside
  54.2 0.6 shard_map.56.refs_5_
  54.9 0.0 collective-permute-done.17.refs_2_
  54.9 0.0 collective-permute-done.18.refs_3_
  54.9 1.8 %shard_map.57.before = f32[256,1024]{1,0:T(8,128)S(1)} custom-call(bf16[1056,128]{1,0:T(8,128)(2,1)S(1)} %collective-permute-done.16.refs_0_, bf16[1056,128]{1,0:T(8,128)(2,1)S(1)} %collective-permute-done.5.refs_1_, bf16[1056,128]{1,0:T(8,128)(2,1)S(1)} %collective-permute-done.17.refs_2_, bf16[1056,128]{1,0:T(8,128)(2,1)S(1)} %collective-permute-done.18.refs_3_, ...), custom_call_target="tpu_custom_call" | custom-call | flops 2097152 | bytes 131072 | tf_op jit(solution)/shard_map/pallas_call | solution.py:256
  56.7 0.0 collective-permute-done.6.pair
  56.7 0.1 broadcast_in_dim.21.codes
  56.8 1.5 %shard_map.58 = (f32[8,128,128]{2,1,0:T(8,128)S(1)}, f32[32,8,128]{2,1,0:T(8,128)S(1)}) custom-call(bf16[16,128]{1,0:T(8,128)(2,1)S(1)} %broadcast_in_dim.21.codes, bf16[1056,128]{1,0:T(8,128)(2,1)S(1)} %collective-permute-done.6.pair, bf16[8,256,1152]{2,1,0:T(8,128)(2,1)S(1)} %get-tuple-element.35.dense_left.refs_4_, f32[256,1024]{1,0:T(8,128)S(1)} %shard_map.57.before), custom_call_target="tpu_custom_call" | custom-call | flops 1048576 | bytes 65536 | tf_op jit(solution)/shard_map/pallas_call | solution.py:265
  58.3 14.5 %all_to_all.5.sums = f32[32,8,128]{2,1,0:T(8,128)S(1)} all-to-all(f32[32,8,128]{2,1,0:T(8,128)S(1)} %get-tuple-element.44), channel_id=1, replica_groups=mesh['group'=8,'loop'=32] {'loop'}, dimensions={0} | all-to-all | bytes 262144 | tf_op jit(solution)/shard_map/all_to_all | solution.py:279
  72.9 1.9 %shard_map.59 = f32[8,128,128]{2,1,0:T(8,128)} custom-call(bf16[16,128]{1,0:T(8,128)(2,1)S(1)} %broadcast_in_dim.21.codes, f32[8,128,128]{2,1,0:T(8,128)S(1)} %get-tuple-element.43.squares, f32[32,8,128]{2,1,0:T(8,128)S(1)} %all_to_all.5.sums), custom_call_target="tpu_custom_call" | custom-call | tf_op jit(solution)/shard_map/pallas_call | solution.py:280
  (5 shorter events, 0.1 us)
Async XLA Ops:
  2.3 5.1 %collective-permute-start = (bf16[528,128]{1,0:T(8,128)(2,1)S(1)}, bf16[528,128]{1,0:T(8,128)(2,1)S(1)}, u32[]{:S(2)}, u32[]{:S(2)}) collective-permute-start(bf16[528,128]{1,0:T(8,128)(2,1)S(1)} %pad_maximum_fusion.3), channel_id=1, source_target_pairs={{0,1},{1,0},{2,3},{3,2},{4,5},{5,4},{6,7},{7,6},{8,9},{9,8},{10,11... | collective-permute-start | bytes 405512 | tf_op jit(solution)/shard_map/ppermute | solution.py:201
  5.6 5.1 %collective-permute-start.7 = (bf16[528,128]{1,0:T(8,128)(2,1)S(1)}, bf16[528,128]{1,0:T(8,128)(2,1)S(1)}, u32[]{:S(2)}, u32[]{:S(2)}) collective-permute-start(bf16[528,128]{1,0:T(8,128)(2,1)S(1)} %pad_maximum_fusion.3), channel_id=1, source_target_pairs={{0,2},{1,3},{2,0},{3,1},{4,6},{5,7},{6,4},{7,5},{8,10},{9,11},{10,... | collective-permute-start | bytes 405512 | tf_op jit(solution)/shard_map/ppermute | solution.py:201
  5.6 8.7 %collective-permute-start.8 = (bf16[528,128]{1,0:T(8,128)(2,1)S(1)}, bf16[528,128]{1,0:T(8,128)(2,1)S(1)}, u32[]{:S(2)}, u32[]{:S(2)}) collective-permute-start(bf16[528,128]{1,0:T(8,128)(2,1)S(1)} %pad_maximum_fusion.3), channel_id=1, source_target_pairs={{0,3},{1,2},{2,1},{3,0},{4,7},{5,6},{6,5},{7,4},{8,11},{9,10},{10,... | collective-permute-start | bytes 405512 | tf_op jit(solution)/shard_map/ppermute | solution.py:201
  7.4 10.9 %collective-permute-start.2 = (bf16[528,128]{1,0:T(8,128)(2,1)S(1)}, bf16[528,128]{1,0:T(8,128)(2,1)S(1)}, u32[]{:S(2)}, u32[]{:S(2)}) collective-permute-start(bf16[528,128]{1,0:T(8,128)(2,1)S(1)} %pad_maximum_fusion.3), channel_id=1, source_target_pairs={{0,32},{32,0},{64,96},{96,64},{128,160},{160,128},{192,224},{224,1... | collective-permute-start | bytes 405512 | tf_op jit(solution)/shard_map/ppermute | solution.py:204
  9.5 39.9 %copy-start = (s32[1,1,8]{2,1,0:T(1,128)S(1)}, s32[1,1,8]{2,1,0:T(1,128)}, u32[]{:S(2)}) copy-start(s32[1,1,8]{2,1,0:T(1,128)} %param.8) | copy-start | bytes 100
  14.4 9.8 %collective-permute-start.9 = (bf16[1056,128]{1,0:T(8,128)(2,1)S(1)}, bf16[1056,128]{1,0:T(8,128)(2,1)S(1)}, u32[]{:S(2)}, u32[]{:S(2)}) collective-permute-start(bf16[1056,128]{1,0:T(8,128)(2,1)S(1)} %constant_dynamic-update-slice_fusion.refs_0_), channel_id=1, source_target_pairs={{0,4},{1,29},{2,6},{3,31},{4,8},{5,1},{6,10},{7,3},{8,12},{9,5},{1... | collective-permute-start | bytes 811016 | tf_op jit(solution)/shard_map/ppermute | solution.py:201
  18.3 8.3 %collective-permute-start.3 = (bf16[1056,128]{1,0:T(8,128)(2,1)S(1)}, bf16[1056,128]{1,0:T(8,128)(2,1)S(1)}, u32[]{:S(2)}, u32[]{:S(2)}) collective-permute-start(bf16[1056,128]{1,0:T(8,128)(2,1)S(1)} %pad_maximum_fusion.2), channel_id=1, source_target_pairs={{0,64},{32,96},{64,0},{96,32},{128,192},{160,224},{192,128},{224,1... | collective-permute-start | bytes 811016 | tf_op jit(solution)/shard_map/ppermute | solution.py:204
  19.6 8.0 %collective-permute-start.1 = (bf16[1056,128]{1,0:T(8,128)(2,1)S(1)}, bf16[1056,128]{1,0:T(8,128)(2,1)S(1)}, u32[]{:S(2)}, u32[]{:S(2)}) collective-permute-start(bf16[1056,128]{1,0:T(8,128)(2,1)S(1)} %pad_maximum_fusion.1.refs_1_), channel_id=1, source_target_pairs={{0,4},{1,29},{2,6},{3,31},{4,8},{5,1},{6,10},{7,3},{8,12},{9,5},{1... | collective-permute-start | bytes 811016 | tf_op jit(solution)/shard_map/ppermute | solution.py:201
  24.2 10.4 %collective-permute-start.12 = (bf16[1056,128]{1,0:T(8,128)(2,1)S(1)}, bf16[1056,128]{1,0:T(8,128)(2,1)S(1)}, u32[]{:S(2)}, u32[]{:S(2)}) collective-permute-start(bf16[1056,128]{1,0:T(8,128)(2,1)S(1)} %collective-permute-done.9.refs_2_), channel_id=1, source_target_pairs={{0,4},{1,29},{2,6},{3,31},{4,8},{5,1},{6,10},{7,3},{8,12},{9,5},{1... | collective-permute-start | bytes 811016 | tf_op jit(solution)/shard_map/ppermute | solution.py:201
  27.6 7.0 %collective-permute-start.10 = (bf16[1056,128]{1,0:T(8,128)(2,1)S(1)}, bf16[1056,128]{1,0:T(8,128)(2,1)S(1)}, u32[]{:S(2)}, u32[]{:S(2)}) collective-permute-start(bf16[1056,128]{1,0:T(8,128)(2,1)S(1)} %collective-permute-done.9.refs_2_), channel_id=1, source_target_pairs={{0,1},{1,0},{2,3},{3,2},{4,5},{5,4},{6,7},{7,6},{8,9},{9,8},{10,11... | collective-permute-start | bytes 811016 | tf_op jit(solution)/shard_map/ppermute | solution.py:201
  30.1 4.5 %collective-permute-start.11 = (bf16[1056,128]{1,0:T(8,128)(2,1)S(1)}, bf16[1056,128]{1,0:T(8,128)(2,1)S(1)}, u32[]{:S(2)}, u32[]{:S(2)}) collective-permute-start(bf16[1056,128]{1,0:T(8,128)(2,1)S(1)} %collective-permute-done.1.refs_3_), channel_id=1, source_target_pairs={{0,1},{1,0},{2,3},{3,2},{4,5},{5,4},{6,7},{7,6},{8,9},{9,8},{10,11... | collective-permute-start | bytes 811016 | tf_op jit(solution)/shard_map/ppermute | solution.py:201
  30.1 5.6 %collective-permute-start.4 = (bf16[1056,128]{1,0:T(8,128)(2,1)S(1)}, bf16[1056,128]{1,0:T(8,128)(2,1)S(1)}, u32[]{:S(2)}, u32[]{:S(2)}) collective-permute-start(bf16[1056,128]{1,0:T(8,128)(2,1)S(1)} %collective-permute-done.1.refs_3_), channel_id=1, source_target_pairs={{0,4},{1,29},{2,6},{3,31},{4,8},{5,1},{6,10},{7,3},{8,12},{9,5},{1... | collective-permute-start | bytes 811016 | tf_op jit(solution)/shard_map/ppermute | solution.py:201
  32.1 14.4 %collective-permute-start.15 = (bf16[2112,128]{1,0:T(8,128)(2,1)S(1)}, bf16[2112,128]{1,0:T(8,128)(2,1)S(1)}, u32[]{:S(2)}, u32[]{:S(2)}) collective-permute-start(bf16[2112,128]{1,0:T(8,128)(2,1)S(1)} %pad_maximum_fusion.refs_10_), channel_id=1, source_target_pairs={{0,192},{32,224},{64,128},{96,160},{128,64},{160,96},{192,0},{224,... | collective-permute-start | bytes 1622024 | tf_op jit(solution)/shard_map/ppermute | solution.py:204
  34.6 5.7 %collective-permute-start.16 = (bf16[1056,128]{1,0:T(8,128)(2,1)S(1)}, bf16[1056,128]{1,0:T(8,128)(2,1)S(1)}, u32[]{:S(2)}, u32[]{:S(2)}) collective-permute-start(bf16[1056,128]{1,0:T(8,128)(2,1)S(1)} %collective-permute-done.12.refs_6_), channel_id=1, source_target_pairs={{0,4},{1,29},{2,6},{3,31},{4,8},{5,1},{6,10},{7,3},{8,12},{9,5},{1... | collective-permute-start | bytes 811016 | tf_op jit(solution)/shard_map/ppermute | solution.py:201
  35.7 4.6 %collective-permute-start.13 = (bf16[1056,128]{1,0:T(8,128)(2,1)S(1)}, bf16[1056,128]{1,0:T(8,128)(2,1)S(1)}, u32[]{:S(2)}, u32[]{:S(2)}) collective-permute-start(bf16[1056,128]{1,0:T(8,128)(2,1)S(1)} %collective-permute-done.12.refs_6_), channel_id=1, source_target_pairs={{0,1},{1,0},{2,3},{3,2},{4,5},{5,4},{6,7},{7,6},{8,9},{9,8},{10,11... | collective-permute-start | bytes 811016 | tf_op jit(solution)/shard_map/ppermute | solution.py:201
  38.2 2.1 %collective-permute-start.14 = (bf16[1056,128]{1,0:T(8,128)(2,1)S(1)}, bf16[1056,128]{1,0:T(8,128)(2,1)S(1)}, u32[]{:S(2)}, u32[]{:S(2)}) collective-permute-start(bf16[1056,128]{1,0:T(8,128)(2,1)S(1)} %collective-permute-done.4.refs_7_), channel_id=1, source_target_pairs={{0,1},{1,0},{2,3},{3,2},{4,5},{5,4},{6,7},{7,6},{8,9},{9,8},{10,11... | collective-permute-start | bytes 811016 | tf_op jit(solution)/shard_map/ppermute | solution.py:201
  38.2 5.6 %collective-permute-start.5 = (bf16[1056,128]{1,0:T(8,128)(2,1)S(1)}, bf16[1056,128]{1,0:T(8,128)(2,1)S(1)}, u32[]{:S(2)}, u32[]{:S(2)}) collective-permute-start(bf16[1056,128]{1,0:T(8,128)(2,1)S(1)} %collective-permute-done.4.refs_7_), channel_id=1, source_target_pairs={{0,4},{1,29},{2,6},{3,31},{4,8},{5,1},{6,10},{7,3},{8,12},{9,5},{1... | collective-permute-start | bytes 811016 | tf_op jit(solution)/shard_map/ppermute | solution.py:201
  40.3 13.9 %collective-permute-start.19 = (bf16[1056,128]{1,0:T(8,128)(2,1)S(1)}, bf16[1056,128]{1,0:T(8,128)(2,1)S(1)}, u32[]{:S(2)}, u32[]{:S(2)}) collective-permute-start(bf16[1056,128]{1,0:T(8,128)(2,1)S(1)} %collective-permute-done.16.refs_0_), channel_id=1, source_target_pairs={{0,4},{1,29},{2,6},{3,31},{4,8},{5,1},{6,10},{7,3},{8,12},{9,5},{1... | collective-permute-start | bytes 811016 | tf_op jit(solution)/shard_map/ppermute | solution.py:201
  46.5 8.3 %collective-permute-start.17 = (bf16[1056,128]{1,0:T(8,128)(2,1)S(1)}, bf16[1056,128]{1,0:T(8,128)(2,1)S(1)}, u32[]{:S(2)}, u32[]{:S(2)}) collective-permute-start(bf16[1056,128]{1,0:T(8,128)(2,1)S(1)} %collective-permute-done.16.refs_0_), channel_id=1, source_target_pairs={{0,1},{1,0},{2,3},{3,2},{4,5},{5,4},{6,7},{7,6},{8,9},{9,8},{10,11... | collective-permute-start | bytes 811016 | tf_op jit(solution)/shard_map/ppermute | solution.py:201
  46.5 8.3 %collective-permute-start.18 = (bf16[1056,128]{1,0:T(8,128)(2,1)S(1)}, bf16[1056,128]{1,0:T(8,128)(2,1)S(1)}, u32[]{:S(2)}, u32[]{:S(2)}) collective-permute-start(bf16[1056,128]{1,0:T(8,128)(2,1)S(1)} %collective-permute-done.5.refs_1_), channel_id=1, source_target_pairs={{0,1},{1,0},{2,3},{3,2},{4,5},{5,4},{6,7},{7,6},{8,9},{9,8},{10,11... | collective-permute-start | bytes 811016 | tf_op jit(solution)/shard_map/ppermute | solution.py:201
  47.0 9.6 %collective-permute-start.6 = (bf16[1056,128]{1,0:T(8,128)(2,1)S(1)}, bf16[1056,128]{1,0:T(8,128)(2,1)S(1)}, u32[]{:S(2)}, u32[]{:S(2)}) collective-permute-start(bf16[1056,128]{1,0:T(8,128)(2,1)S(1)} %collective-permute-done.5.refs_1_), channel_id=1, source_target_pairs={{0,4},{1,29},{2,6},{3,31},{4,8},{5,1},{6,10},{7,3},{8,12},{9,5},{1... | collective-permute-start | bytes 811016 | tf_op jit(solution)/shard_map/ppermute | solution.py:201

commit v7 on v6

--- a/solution.py
+++ b/solution.py
@@ -68,7 +68,7 @@
 
 
 def round_units(refs, y, c):
-    beside, pair = refs
+    pair, beside = refs
     return (
         (pair, 0, y, c),
         (pair, UNIT, y, 1 - c),
@@ -122,14 +122,14 @@
     )
 
 
-def add_half(beside, dense_left, before, product, dense_half):
+def add_half(pair, dense_left, before, product, dense_half):
+    _, y, c, _, _ = where_am_i()
+    product[...] = before[...] + half(pair, y, c, dense_left, dense_half)
+
+
+def finish(codes, beside, dense_left, before, squares, sums, dense_half, product, held, sem):
     _, y, c, _, _ = where_am_i()
     product[...] = before[...] + half(beside, 1 - y, c, dense_left, dense_half)
-
-
-def finish(codes, pair, dense_left, before, squares, sums, dense_half, product, held, sem):
-    _, y, c, _, _ = where_am_i()
-    product[...] = before[...] + half(pair, y, c, dense_left, dense_half)
     column = lax.broadcasted_iota(jnp.int32, (8, TILE), 0)
     total = jnp.zeros((8, TILE), F32)
     copies = []
@@ -208,7 +208,7 @@
     first = jnp.concatenate([unit, pair])
     beside, crossed, _ = lax.optimization_barrier((beside, crossed, first))
     second = jnp.concatenate([beside, crossed])
-    later, beside_later, _ = lax.optimization_barrier((unit, result_coords, pair))
+    later, beside_later, _ = lax.optimization_barrier((unit, result_coords, first))
     row = jnp.concatenate([later, across(YHI, later)])
     at = jnp.pad(beside_later[0, 0], (0, 8))
     code = jnp.where(slot < result_counts[0, 0], at, at + 16).astype(BF16)
@@ -217,21 +217,19 @@
     def after(v, *others):
         return lax.optimization_barrier((v, *others))
 
-    streams = [second, first]
+    streams = [first, second]
     right = [streams]
     row = jnp.concatenate([row, across(XNEAR, row)])
+    left = [row, across(XMIRROR, row)]
     for r in range(3):
         if r == 2:
-            streams = [after(streams[0], *right[-3])[0], streams[1]]
-        streams = [along(RING, v) for v in streams]
-        if r == 0:
-            streams[1], row = after(streams[1], row)
-            left = [row, across(XMIRROR, row)]
+            streams = [streams[0], after(streams[1], *right[-3])[0]]
+        ahead = along(RING, streams[0])
+        behind = after(streams[1], ahead)[0] if r == 0 else streams[1]
+        streams = [ahead, along(RING, behind)]
         other = after(*streams)
-        if r == 2:
-            other = after(*other, left[1])[:2]
         right += [streams, [along(CORE, v) for v in other]]
-    streams = [after(streams[0], *right[-3])[0], streams[1]]
+    streams = [streams[0], after(streams[1], *right[-3])[0]]
     last = [along(RING, v) for v in streams]
 
     limit = pltpu.CompilerParams(vmem_limit_bytes=24 * 2**20)

time: 75.1 us -> 74 us (0.985)
  waiting for transfers between devices: 12.9 us -> 4.95 us
  starting transfers between devices: 32.5 us -> 38 us
    ppermute x17, starting transfers between devices: 27.5 us -> 32.9 us  [along(): return lax.ppermute(v, 'loop', perm)]
    ppermute x17, waiting for transfers between devices: 8.57 us -> 4.48 us  [along(): return lax.ppermute(v, 'loop', perm)]
    ppermute x3, waiting for transfers between devices: 4.35 us -> 0.47 us  [across(): return lax.ppermute(v, 'group', perm)]
  transfers between devices with their start and end apart: 20 -> 20, of which waited for: 8 -> 4; matrix products, arithmetic and copies ran while one was open for 1% -> 2% of each run, Pallas kernels for 10% -> 10%
where the time goes in v7:
time: 74 us; the launch traced here: 73.8 us
  starting transfers between devices  38 us (51%)
  blocking collectives  15.1 us (20%)
  Pallas kernels  10.7 us (14%)
  waiting for transfers between devices  4.95 us (7%)
  other arithmetic  3.19 us (4%)
  between operations  1.58 us (2%)
    ppermute x17, starting transfers between devices, along(): return lax.ppermute(v, 'loop', perm)  32.9 us
    all_to_all x1, blocking collectives, shards(): sums = lax.all_to_all(sums, 'loop', 0, 0, tiled=True)  15.1 us
    ppermute x3, starting transfers between devices, across(): return lax.ppermute(v, 'group', perm)  5.08 us
    pallas_call x1, Pallas kernels, shards(): pl.pallas_call(begin, in_specs=[WHOLE] * 12, out_specs=[WHOLE] * 2, out_s...  4.8 us
    ppermute x17, waiting for transfers between devices, along(): return lax.ppermute(v, 'loop', perm)  4.48 us
    pallas_call x1, Pallas kernels, shards(): pl.pallas_call(rescale, in_specs=[AWAY] * 3, out_specs=AWAY, out_shape=ja...  1.94 us
    pallas_call x1, Pallas kernels, shards(): pl.pallas_call(proceed, in_specs=[WHOLE] * 6, out_specs=WHOLE, out_shape=...  1.8 us
    pallas_call x1, Pallas kernels, shards(): pl.pallas_call(finish, in_specs=[WHOLE] * 4, out_specs=[AWAY, WHOLE], out...  1.55 us
  transfers between devices with their start and end apart: 20, of which 4 were waited for; matrix products, arithmetic and copies ran while one was open for 2% of the time, Pallas kernels for 10%

profile of v7, /device:TPU:1, one launch (start us, length us, event | category | flops | bytes accessed | tf_op | source)
XLA Modules:
  0.0 73.8 jit_solution(11878758789968324589)
XLA Ops:
  0.7 0.7 fusion
  1.3 0.1 broadcast_in_dim.20
  1.4 0.9 %pad_maximum_fusion.2 = bf16[528,128]{1,0:T(8,128)(2,1)S(1)} fusion(bf16[16,128]{1,0:T(8,128)(2,1)S(1)} %broadcast_in_dim.20, bf16[512,128]{1,0:T(8,128)(2,1)} %bitcast.8), kind=kLoop, calls=%fused_computation.2 | loop fusion | flops 270336 | bytes 270336 | tf_op jit(solution)/shard_map/concatenate | solution.py:196
  2.3 3.3 %collective-permute-start = (bf16[528,128]{1,0:T(8,128)(2,1)S(1)}, bf16[528,128]{1,0:T(8,128)(2,1)S(1)}, u32[]{:S(2)}, u32[]{:S(2)}) collective-permute-start(bf16[528,128]{1,0:T(8,128)(2,1)S(1)} %pad_maximum_fusion.2), channel_id=1, source_target_pairs={{0,1},{1,0},{2,3},{3,2},{4,5},{5,4},{6,7},{7,6},{8,9},{9,8},{10,11... | collective-permute-start | bytes 405512 | tf_op jit(solution)/shard_map/ppermute | solution.py:201
  5.6 0.0 collective-permute-start.1
  5.6 1.7 %collective-permute-start.2 = (bf16[528,128]{1,0:T(8,128)(2,1)S(1)}, bf16[528,128]{1,0:T(8,128)(2,1)S(1)}, u32[]{:S(2)}, u32[]{:S(2)}) collective-permute-start(bf16[528,128]{1,0:T(8,128)(2,1)S(1)} %pad_maximum_fusion.2), channel_id=1, source_target_pairs={{0,3},{1,2},{2,1},{3,0},{4,7},{5,6},{6,5},{7,4},{8,11},{9,10},{10,... | collective-permute-start | bytes 405512 | tf_op jit(solution)/shard_map/ppermute | solution.py:201
  7.4 0.0 collective-permute-done
  7.4 0.9 %pad_maximum_fusion.refs_0_ = bf16[1056,128]{1,0:T(8,128)(2,1)S(1)} fusion(bf16[528,128]{1,0:T(8,128)(2,1)S(1)} %collective-permute-done, bf16[16,128]{1,0:T(8,128)(2,1)S(1)} %broadcast_in_dim.20, bf16[512,128]{1,0:T(8,128)(2,1)} %bitcast.9), kind=kLoop, calls=%fused_computation | loop fusion | flops 811008 | bytes 540672 | tf_op jit(solution)/shard_map/concatenate | solution.py:208
  8.3 3.9 %collective-permute-start.3 = (bf16[1056,128]{1,0:T(8,128)(2,1)S(1)}, bf16[1056,128]{1,0:T(8,128)(2,1)S(1)}, u32[]{:S(2)}, u32[]{:S(2)}) collective-permute-start(bf16[1056,128]{1,0:T(8,128)(2,1)S(1)} %pad_maximum_fusion.refs_0_), channel_id=1, source_target_pairs={{0,4},{1,29},{2,6},{3,31},{4,8},{5,1},{6,10},{7,3},{8,12},{9,5},{1... | collective-permute-start | bytes 811016 | tf_op jit(solution)/shard_map/ppermute | solution.py:201
  12.2 0.0 collective-permute-done.1
  12.2 1.9 %collective-permute-done.2 = bf16[528,128]{1,0:T(8,128)(2,1)S(1)} collective-permute-done((bf16[528,128]{1,0:T(8,128)(2,1)S(1)}, bf16[528,128]{1,0:T(8,128)(2,1)S(1)}, u32[]{:S(2)}, u32[]{:S(2)}) %collective-permute-start.2) | collective-permute-done | bytes 135200 | tf_op jit(solution)/shard_map/ppermute | solution.py:201
  14.2 1.0 %collective-permute-start.13 = (bf16[528,128]{1,0:T(8,128)(2,1)S(1)}, bf16[528,128]{1,0:T(8,128)(2,1)S(1)}, u32[]{:S(2)}, u32[]{:S(2)}) collective-permute-start(bf16[528,128]{1,0:T(8,128)(2,1)S(1)} %pad_maximum_fusion.2), channel_id=1, source_target_pairs={{0,32},{32,0},{64,96},{96,64},{128,160},{160,128},{192,224},{224,1... | collective-permute-start | bytes 405512 | tf_op jit(solution)/shard_map/ppermute | solution.py:204
  15.2 0.4 collective-permute-done.3.refs_2_
  15.6 5.4 %collective-permute-start.4 = (bf16[1056,128]{1,0:T(8,128)(2,1)S(1)}, bf16[1056,128]{1,0:T(8,128)(2,1)S(1)}, u32[]{:S(2)}, u32[]{:S(2)}) collective-permute-start(bf16[1056,128]{1,0:T(8,128)(2,1)S(1)} %constant_dynamic-update-slice_fusion.refs_1_), channel_id=1, source_target_pairs={{0,4},{1,29},{2,6},{3,31},{4,8},{5,1},{6,10},{7,3},{8,12},{9,5},{1... | collective-permute-start | bytes 811016 | tf_op jit(solution)/shard_map/ppermute | solution.py:201
  21.0 0.0 collective-permute-done.13
  21.1 1.3 %collective-permute-start.14 = (bf16[1056,128]{1,0:T(8,128)(2,1)S(1)}, bf16[1056,128]{1,0:T(8,128)(2,1)S(1)}, u32[]{:S(2)}, u32[]{:S(2)}) collective-permute-start(bf16[1056,128]{1,0:T(8,128)(2,1)S(1)} %pad_maximum_fusion.1), channel_id=1, source_target_pairs={{0,64},{32,96},{64,0},{96,32},{128,192},{160,224},{192,128},{224,1... | collective-permute-start | bytes 811016 | tf_op jit(solution)/shard_map/ppermute | solution.py:204
  22.4 3.8 %collective-permute-start.9 = (bf16[1056,128]{1,0:T(8,128)(2,1)S(1)}, bf16[1056,128]{1,0:T(8,128)(2,1)S(1)}, u32[]{:S(2)}, u32[]{:S(2)}) collective-permute-start(bf16[1056,128]{1,0:T(8,128)(2,1)S(1)} %collective-permute-done.3.refs_2_), channel_id=1, source_target_pairs={{0,4},{1,29},{2,6},{3,31},{4,8},{5,1},{6,10},{7,3},{8,12},{9,5},{1... | collective-permute-start | bytes 811016 | tf_op jit(solution)/shard_map/ppermute | solution.py:201
  26.2 0.0 collective-permute-done.4.refs_3_
  26.2 0.0 collective-permute-start.6
  26.2 0.5 collective-permute-start.7
  26.7 1.3 %collective-permute-start.5 = (bf16[1056,128]{1,0:T(8,128)(2,1)S(1)}, bf16[1056,128]{1,0:T(8,128)(2,1)S(1)}, u32[]{:S(2)}, u32[]{:S(2)}) collective-permute-start(bf16[1056,128]{1,0:T(8,128)(2,1)S(1)} %collective-permute-done.4.refs_3_), channel_id=1, source_target_pairs={{0,4},{1,29},{2,6},{3,31},{4,8},{5,1},{6,10},{7,3},{8,12},{9,5},{1... | collective-permute-start | bytes 811016 | tf_op jit(solution)/shard_map/ppermute | solution.py:201
  28.1 0.5 collective-permute-done.14
  28.6 2.8 %collective-permute-start.15 = (bf16[2112,128]{1,0:T(8,128)(2,1)S(1)}, bf16[2112,128]{1,0:T(8,128)(2,1)S(1)}, u32[]{:S(2)}, u32[]{:S(2)}) collective-permute-start(bf16[2112,128]{1,0:T(8,128)(2,1)S(1)} %constant_dynamic-update-slice_fusion.2.refs_10_), channel_id=1, source_target_pairs={{0,192},{32,224},{64,128},{96,160},{128,64},{160,96},{192,0},{224,... | collective-permute-start | bytes 1622024 | tf_op jit(solution)/shard_map/ppermute | solution.py:204
  31.4 0.0 collective-permute-done.9.refs_6_
  31.4 3.5 %collective-permute-start.16 = (bf16[1056,128]{1,0:T(8,128)(2,1)S(1)}, bf16[1056,128]{1,0:T(8,128)(2,1)S(1)}, u32[]{:S(2)}, u32[]{:S(2)}) collective-permute-start(bf16[1056,128]{1,0:T(8,128)(2,1)S(1)} %collective-permute-done.9.refs_6_), channel_id=1, source_target_pairs={{0,4},{1,29},{2,6},{3,31},{4,8},{5,1},{6,10},{7,3},{8,12},{9,5},{1... | collective-permute-start | bytes 811016 | tf_op jit(solution)/shard_map/ppermute | solution.py:201
  34.9 0.0 collective-permute-done.5.refs_7_
  34.9 0.0 collective-permute-done.6.refs_4_
  34.9 0.0 collective-permute-done.7.refs_5_
  34.9 0.8 %collective-permute-start.8 = (bf16[1056,128]{1,0:T(8,128)(2,1)S(1)}, bf16[1056,128]{1,0:T(8,128)(2,1)S(1)}, u32[]{:S(2)}, u32[]{:S(2)}) collective-permute-start(bf16[1056,128]{1,0:T(8,128)(2,1)S(1)} %collective-permute-done.5.refs_7_), channel_id=1, source_target_pairs={{0,4},{1,29},{2,6},{3,31},{4,8},{5,1},{6,10},{7,3},{8,12},{9,5},{1... | collective-permute-start | bytes 811016 | tf_op jit(solution)/shard_map/ppermute | solution.py:201
  35.7 0.0 collective-permute-start.10
  35.7 0.5 collective-permute-start.11
  36.2 2.1 %collective-permute-done.16.refs_0_ = bf16[1056,128]{1,0:T(8,128)(2,1)S(1)} collective-permute-done((bf16[1056,128]{1,0:T(8,128)(2,1)S(1)}, bf16[1056,128]{1,0:T(8,128)(2,1)S(1)}, u32[]{:S(2)}, u32[]{:S(2)}) %collective-permute-start.16) | collective-permute-done | bytes 270368 | tf_op jit(solution)/shard_map/ppermute | solution.py:201
  38.3 3.4 %collective-permute-start.19 = (bf16[1056,128]{1,0:T(8,128)(2,1)S(1)}, bf16[1056,128]{1,0:T(8,128)(2,1)S(1)}, u32[]{:S(2)}, u32[]{:S(2)}) collective-permute-start(bf16[1056,128]{1,0:T(8,128)(2,1)S(1)} %collective-permute-done.16.refs_0_), channel_id=1, source_target_pairs={{0,4},{1,29},{2,6},{3,31},{4,8},{5,1},{6,10},{7,3},{8,12},{9,5},{1... | collective-permute-start | bytes 811016 | tf_op jit(solution)/shard_map/ppermute | solution.py:201
  41.7 0.0 collective-permute-done.8.refs_1_
  41.7 2.6 %collective-permute-start.17 = (bf16[1056,128]{1,0:T(8,128)(2,1)S(1)}, bf16[1056,128]{1,0:T(8,128)(2,1)S(1)}, u32[]{:S(2)}, u32[]{:S(2)}) collective-permute-start(bf16[1056,128]{1,0:T(8,128)(2,1)S(1)} %collective-permute-done.16.refs_0_), channel_id=1, source_target_pairs={{0,1},{1,0},{2,3},{3,2},{4,5},{5,4},{6,7},{7,6},{8,9},{9,8},{10,11... | collective-permute-start | bytes 811016 | tf_op jit(solution)/shard_map/ppermute | solution.py:201
  44.3 0.0 collective-permute-done.10.refs_8_
  44.3 0.0 collective-permute-start.18
  44.3 0.0 collective-permute-done.11.refs_9_
  44.3 2.0 %collective-permute-start.12 = (bf16[1056,128]{1,0:T(8,128)(2,1)S(1)}, bf16[1056,128]{1,0:T(8,128)(2,1)S(1)}, u32[]{:S(2)}, u32[]{:S(2)}) collective-permute-start(bf16[1056,128]{1,0:T(8,128)(2,1)S(1)} %collective-permute-done.8.refs_1_), channel_id=1, source_target_pairs={{0,4},{1,29},{2,6},{3,31},{4,8},{5,1},{6,10},{7,3},{8,12},{9,5},{1... | collective-permute-start | bytes 811016 | tf_op jit(solution)/shard_map/ppermute | solution.py:201
  47.0 0.7 fusion.1
  47.7 0.0 collective-permute-done.15.refs_11_
  47.7 4.8 %shard_map.55 = (bf16[8,256,1152]{2,1,0:T(8,128)(2,1)S(1)}, f32[256,1024]{1,0:T(8,128)S(1)}) custom-call(bf16[1056,128]{1,0:T(8,128)(2,1)S(1)} %pad_maximum_fusion.refs_0_, bf16[1056,128]{1,0:T(8,128)(2,1)S(1)} %constant_dynamic-update-slice_fusion.refs_1_, bf16[1056,128]{1,0:T(8,128)(2,1)S(1)} %collective-permute-done.3.refs_2_, ...), custom_call_target="tpu_custom_call" | custom-call | flops 6291456 | bytes 393216 | tf_op jit(solution)/shard_map/pallas_call | solution.py:236
  52.5 0.0 collective-permute-done.19.pair
  52.5 0.6 shard_map.56.refs_5_
  53.1 0.0 collective-permute-done.17.refs_2_
  53.1 0.0 collective-permute-done.18.refs_3_
  53.1 1.8 %shard_map.57.before = f32[256,1024]{1,0:T(8,128)S(1)} custom-call(bf16[1056,128]{1,0:T(8,128)(2,1)S(1)} %collective-permute-done.16.refs_0_, bf16[1056,128]{1,0:T(8,128)(2,1)S(1)} %collective-permute-done.8.refs_1_, bf16[1056,128]{1,0:T(8,128)(2,1)S(1)} %collective-permute-done.17.refs_2_, bf16[1056,128]{1,0:T(8,128)(2,1)S(1)} %collective-permute-done.18.refs_3_, ...), custom_call_target="tpu_custom_call" | custom-call | flops 2097152 | bytes 131072 | tf_op jit(solution)/shard_map/pallas_call | solution.py:254
  54.9 0.0 collective-permute-done.12.beside
  54.9 0.1 broadcast_in_dim.21.codes
  55.0 1.5 %shard_map.58 = (f32[8,128,128]{2,1,0:T(8,128)S(1)}, f32[32,8,128]{2,1,0:T(8,128)S(1)}) custom-call(bf16[16,128]{1,0:T(8,128)(2,1)S(1)} %broadcast_in_dim.21.codes, bf16[1056,128]{1,0:T(8,128)(2,1)S(1)} %collective-permute-done.12.beside, bf16[8,256,1152]{2,1,0:T(8,128)(2,1)S(1)} %get-tuple-element.33.dense_left.refs_4_, f32[256,1024]{1,0:T(8,128)S(1)} %shard_map.57.before), custom_call_target="tpu_custom_call" | custom-call | flops 1048576 | bytes 65536 | tf_op jit(solution)/shard_map/pallas_call | solution.py:263
  56.6 15.1 %all_to_all.5.sums = f32[32,8,128]{2,1,0:T(8,128)S(1)} all-to-all(f32[32,8,128]{2,1,0:T(8,128)S(1)} %get-tuple-element.38), channel_id=1, replica_groups=mesh['group'=8,'loop'=32] {'loop'}, dimensions={0} | all-to-all | bytes 262144 | tf_op jit(solution)/shard_map/all_to_all | solution.py:277
  71.7 1.9 %shard_map.59 = f32[8,128,128]{2,1,0:T(8,128)} custom-call(bf16[16,128]{1,0:T(8,128)(2,1)S(1)} %broadcast_in_dim.21.codes, f32[8,128,128]{2,1,0:T(8,128)S(1)} %get-tuple-element.37.squares, f32[32,8,128]{2,1,0:T(8,128)S(1)} %all_to_all.5.sums), custom_call_target="tpu_custom_call" | custom-call | tf_op jit(solution)/shard_map/pallas_call | solution.py:278
  (6 shorter events, 0.1 us)
Async XLA Ops:
  2.3 5.1 %collective-permute-start = (bf16[528,128]{1,0:T(8,128)(2,1)S(1)}, bf16[528,128]{1,0:T(8,128)(2,1)S(1)}, u32[]{:S(2)}, u32[]{:S(2)}) collective-permute-start(bf16[528,128]{1,0:T(8,128)(2,1)S(1)} %pad_maximum_fusion.2), channel_id=1, source_target_pairs={{0,1},{1,0},{2,3},{3,2},{4,5},{5,4},{6,7},{7,6},{8,9},{9,8},{10,11... | collective-permute-start | bytes 405512 | tf_op jit(solution)/shard_map/ppermute | solution.py:201
  5.6 6.6 %collective-permute-start.1 = (bf16[528,128]{1,0:T(8,128)(2,1)S(1)}, bf16[528,128]{1,0:T(8,128)(2,1)S(1)}, u32[]{:S(2)}, u32[]{:S(2)}) collective-permute-start(bf16[528,128]{1,0:T(8,128)(2,1)S(1)} %pad_maximum_fusion.2), channel_id=1, source_target_pairs={{0,2},{1,3},{2,0},{3,1},{4,6},{5,7},{6,4},{7,5},{8,10},{9,11},{10,... | collective-permute-start | bytes 405512 | tf_op jit(solution)/shard_map/ppermute | solution.py:201
  5.6 8.5 %collective-permute-start.2 = (bf16[528,128]{1,0:T(8,128)(2,1)S(1)}, bf16[528,128]{1,0:T(8,128)(2,1)S(1)}, u32[]{:S(2)}, u32[]{:S(2)}) collective-permute-start(bf16[528,128]{1,0:T(8,128)(2,1)S(1)} %pad_maximum_fusion.2), channel_id=1, source_target_pairs={{0,3},{1,2},{2,1},{3,0},{4,7},{5,6},{6,5},{7,4},{8,11},{9,10},{10,... | collective-permute-start | bytes 405512 | tf_op jit(solution)/shard_map/ppermute | solution.py:201
  8.3 7.3 %collective-permute-start.3 = (bf16[1056,128]{1,0:T(8,128)(2,1)S(1)}, bf16[1056,128]{1,0:T(8,128)(2,1)S(1)}, u32[]{:S(2)}, u32[]{:S(2)}) collective-permute-start(bf16[1056,128]{1,0:T(8,128)(2,1)S(1)} %pad_maximum_fusion.refs_0_), channel_id=1, source_target_pairs={{0,4},{1,29},{2,6},{3,31},{4,8},{5,1},{6,10},{7,3},{8,12},{9,5},{1... | collective-permute-start | bytes 811016 | tf_op jit(solution)/shard_map/ppermute | solution.py:201
  14.2 6.9 %collective-permute-start.13 = (bf16[528,128]{1,0:T(8,128)(2,1)S(1)}, bf16[528,128]{1,0:T(8,128)(2,1)S(1)}, u32[]{:S(2)}, u32[]{:S(2)}) collective-permute-start(bf16[528,128]{1,0:T(8,128)(2,1)S(1)} %pad_maximum_fusion.2), channel_id=1, source_target_pairs={{0,32},{32,0},{64,96},{96,64},{128,160},{160,128},{192,224},{224,1... | collective-permute-start | bytes 405512 | tf_op jit(solution)/shard_map/ppermute | solution.py:204
  15.6 10.6 %collective-permute-start.4 = (bf16[1056,128]{1,0:T(8,128)(2,1)S(1)}, bf16[1056,128]{1,0:T(8,128)(2,1)S(1)}, u32[]{:S(2)}, u32[]{:S(2)}) collective-permute-start(bf16[1056,128]{1,0:T(8,128)(2,1)S(1)} %constant_dynamic-update-slice_fusion.refs_1_), channel_id=1, source_target_pairs={{0,4},{1,29},{2,6},{3,31},{4,8},{5,1},{6,10},{7,3},{8,12},{9,5},{1... | collective-permute-start | bytes 811016 | tf_op jit(solution)/shard_map/ppermute | solution.py:201
  21.1 7.5 %collective-permute-start.14 = (bf16[1056,128]{1,0:T(8,128)(2,1)S(1)}, bf16[1056,128]{1,0:T(8,128)(2,1)S(1)}, u32[]{:S(2)}, u32[]{:S(2)}) collective-permute-start(bf16[1056,128]{1,0:T(8,128)(2,1)S(1)} %pad_maximum_fusion.1), channel_id=1, source_target_pairs={{0,64},{32,96},{64,0},{96,32},{128,192},{160,224},{192,128},{224,1... | collective-permute-start | bytes 811016 | tf_op jit(solution)/shard_map/ppermute | solution.py:204
  22.4 9.0 %collective-permute-start.9 = (bf16[1056,128]{1,0:T(8,128)(2,1)S(1)}, bf16[1056,128]{1,0:T(8,128)(2,1)S(1)}, u32[]{:S(2)}, u32[]{:S(2)}) collective-permute-start(bf16[1056,128]{1,0:T(8,128)(2,1)S(1)} %collective-permute-done.3.refs_2_), channel_id=1, source_target_pairs={{0,4},{1,29},{2,6},{3,31},{4,8},{5,1},{6,10},{7,3},{8,12},{9,5},{1... | collective-permute-start | bytes 811016 | tf_op jit(solution)/shard_map/ppermute | solution.py:201
  26.2 8.6 %collective-permute-start.6 = (bf16[1056,128]{1,0:T(8,128)(2,1)S(1)}, bf16[1056,128]{1,0:T(8,128)(2,1)S(1)}, u32[]{:S(2)}, u32[]{:S(2)}) collective-permute-start(bf16[1056,128]{1,0:T(8,128)(2,1)S(1)} %collective-permute-done.3.refs_2_), channel_id=1, source_target_pairs={{0,1},{1,0},{2,3},{3,2},{4,5},{5,4},{6,7},{7,6},{8,9},{9,8},{10,11... | collective-permute-start | bytes 811016 | tf_op jit(solution)/shard_map/ppermute | solution.py:201
  26.2 8.6 %collective-permute-start.7 = (bf16[1056,128]{1,0:T(8,128)(2,1)S(1)}, bf16[1056,128]{1,0:T(8,128)(2,1)S(1)}, u32[]{:S(2)}, u32[]{:S(2)}) collective-permute-start(bf16[1056,128]{1,0:T(8,128)(2,1)S(1)} %collective-permute-done.4.refs_3_), channel_id=1, source_target_pairs={{0,1},{1,0},{2,3},{3,2},{4,5},{5,4},{6,7},{7,6},{8,9},{9,8},{10,11... | collective-permute-start | bytes 811016 | tf_op jit(solution)/shard_map/ppermute | solution.py:201
  26.7 8.1 %collective-permute-start.5 = (bf16[1056,128]{1,0:T(8,128)(2,1)S(1)}, bf16[1056,128]{1,0:T(8,128)(2,1)S(1)}, u32[]{:S(2)}, u32[]{:S(2)}) collective-permute-start(bf16[1056,128]{1,0:T(8,128)(2,1)S(1)} %collective-permute-done.4.refs_3_), channel_id=1, source_target_pairs={{0,4},{1,29},{2,6},{3,31},{4,8},{5,1},{6,10},{7,3},{8,12},{9,5},{1... | collective-permute-start | bytes 811016 | tf_op jit(solution)/shard_map/ppermute | solution.py:201
  28.6 19.1 %collective-permute-start.15 = (bf16[2112,128]{1,0:T(8,128)(2,1)S(1)}, bf16[2112,128]{1,0:T(8,128)(2,1)S(1)}, u32[]{:S(2)}, u32[]{:S(2)}) collective-permute-start(bf16[2112,128]{1,0:T(8,128)(2,1)S(1)} %constant_dynamic-update-slice_fusion.2.refs_10_), channel_id=1, source_target_pairs={{0,192},{32,224},{64,128},{96,160},{128,64},{160,96},{192,0},{224,... | collective-permute-start | bytes 1622024 | tf_op jit(solution)/shard_map/ppermute | solution.py:204
  31.4 6.9 %collective-permute-start.16 = (bf16[1056,128]{1,0:T(8,128)(2,1)S(1)}, bf16[1056,128]{1,0:T(8,128)(2,1)S(1)}, u32[]{:S(2)}, u32[]{:S(2)}) collective-permute-start(bf16[1056,128]{1,0:T(8,128)(2,1)S(1)} %collective-permute-done.9.refs_6_), channel_id=1, source_target_pairs={{0,4},{1,29},{2,6},{3,31},{4,8},{5,1},{6,10},{7,3},{8,12},{9,5},{1... | collective-permute-start | bytes 811016 | tf_op jit(solution)/shard_map/ppermute | solution.py:201
  34.9 6.8 %collective-permute-start.8 = (bf16[1056,128]{1,0:T(8,128)(2,1)S(1)}, bf16[1056,128]{1,0:T(8,128)(2,1)S(1)}, u32[]{:S(2)}, u32[]{:S(2)}) collective-permute-start(bf16[1056,128]{1,0:T(8,128)(2,1)S(1)} %collective-permute-done.5.refs_7_), channel_id=1, source_target_pairs={{0,4},{1,29},{2,6},{3,31},{4,8},{5,1},{6,10},{7,3},{8,12},{9,5},{1... | collective-permute-start | bytes 811016 | tf_op jit(solution)/shard_map/ppermute | solution.py:201
  35.7 8.6 %collective-permute-start.10 = (bf16[1056,128]{1,0:T(8,128)(2,1)S(1)}, bf16[1056,128]{1,0:T(8,128)(2,1)S(1)}, u32[]{:S(2)}, u32[]{:S(2)}) collective-permute-start(bf16[1056,128]{1,0:T(8,128)(2,1)S(1)} %collective-permute-done.9.refs_6_), channel_id=1, source_target_pairs={{0,1},{1,0},{2,3},{3,2},{4,5},{5,4},{6,7},{7,6},{8,9},{9,8},{10,11... | collective-permute-start | bytes 811016 | tf_op jit(solution)/shard_map/ppermute | solution.py:201
  35.7 8.6 %collective-permute-start.11 = (bf16[1056,128]{1,0:T(8,128)(2,1)S(1)}, bf16[1056,128]{1,0:T(8,128)(2,1)S(1)}, u32[]{:S(2)}, u32[]{:S(2)}) collective-permute-start(bf16[1056,128]{1,0:T(8,128)(2,1)S(1)} %collective-permute-done.5.refs_7_), channel_id=1, source_target_pairs={{0,1},{1,0},{2,3},{3,2},{4,5},{5,4},{6,7},{7,6},{8,9},{9,8},{10,11... | collective-permute-start | bytes 811016 | tf_op jit(solution)/shard_map/ppermute | solution.py:201
  38.3 14.2 %collective-permute-start.19 = (bf16[1056,128]{1,0:T(8,128)(2,1)S(1)}, bf16[1056,128]{1,0:T(8,128)(2,1)S(1)}, u32[]{:S(2)}, u32[]{:S(2)}) collective-permute-start(bf16[1056,128]{1,0:T(8,128)(2,1)S(1)} %collective-permute-done.16.refs_0_), channel_id=1, source_target_pairs={{0,4},{1,29},{2,6},{3,31},{4,8},{5,1},{6,10},{7,3},{8,12},{9,5},{1... | collective-permute-start | bytes 811016 | tf_op jit(solution)/shard_map/ppermute | solution.py:201
  41.7 11.4 %collective-permute-start.17 = (bf16[1056,128]{1,0:T(8,128)(2,1)S(1)}, bf16[1056,128]{1,0:T(8,128)(2,1)S(1)}, u32[]{:S(2)}, u32[]{:S(2)}) collective-permute-start(bf16[1056,128]{1,0:T(8,128)(2,1)S(1)} %collective-permute-done.16.refs_0_), channel_id=1, source_target_pairs={{0,1},{1,0},{2,3},{3,2},{4,5},{5,4},{6,7},{7,6},{8,9},{9,8},{10,11... | collective-permute-start | bytes 811016 | tf_op jit(solution)/shard_map/ppermute | solution.py:201
  44.3 8.8 %collective-permute-start.18 = (bf16[1056,128]{1,0:T(8,128)(2,1)S(1)}, bf16[1056,128]{1,0:T(8,128)(2,1)S(1)}, u32[]{:S(2)}, u32[]{:S(2)}) collective-permute-start(bf16[1056,128]{1,0:T(8,128)(2,1)S(1)} %collective-permute-done.8.refs_1_), channel_id=1, source_target_pairs={{0,1},{1,0},{2,3},{3,2},{4,5},{5,4},{6,7},{7,6},{8,9},{9,8},{10,11... | collective-permute-start | bytes 811016 | tf_op jit(solution)/shard_map/ppermute | solution.py:201
  44.3 10.6 %collective-permute-start.12 = (bf16[1056,128]{1,0:T(8,128)(2,1)S(1)}, bf16[1056,128]{1,0:T(8,128)(2,1)S(1)}, u32[]{:S(2)}, u32[]{:S(2)}) collective-permute-start(bf16[1056,128]{1,0:T(8,128)(2,1)S(1)} %collective-permute-done.8.refs_1_), channel_id=1, source_target_pairs={{0,4},{1,29},{2,6},{3,31},{4,8},{5,1},{6,10},{7,3},{8,12},{9,5},{1... | collective-permute-start | bytes 811016 | tf_op jit(solution)/shard_map/ppermute | solution.py:201

commit v8 on v7

--- a/solution.py
+++ b/solution.py
@@ -185,7 +185,7 @@
 
 def cost(blocks):
     return pl.CostEstimate(
-        flops=blocks * 2**20, bytes_accessed=blocks * 2**16, transcendentals=0
+        flops=blocks * 2 * 256 * 1024 * 1024, bytes_accessed=blocks * 4 * 2**20, transcendentals=0
     )
 
 
@@ -222,14 +222,11 @@
     row = jnp.concatenate([row, across(XNEAR, row)])
     left = [row, across(XMIRROR, row)]
     for r in range(3):
-        if r == 2:
-            streams = [streams[0], after(streams[1], *right[-3])[0]]
         ahead = along(RING, streams[0])
         behind = after(streams[1], ahead)[0] if r == 0 else streams[1]
         streams = [ahead, along(RING, behind)]
-        other = after(*streams)
+        other = streams
         right += [streams, [along(CORE, v) for v in other]]
-    streams = [streams[0], after(streams[1], *right[-3])[0]]
     last = [along(RING, v) for v in streams]
 
     limit = pltpu.CompilerParams(vmem_limit_bytes=24 * 2**20)

time: 74 us -> 70.4 us (0.951)
  waiting for transfers between devices: 4.95 us -> 2.05 us
    ppermute x17, waiting for transfers between devices: 4.48 us -> 1.74 us  [along(): return lax.ppermute(v, 'loop', perm)]
    ppermute x17, starting transfers between devices: 32.9 us -> 30.9 us  [along(): return lax.ppermute(v, 'loop', perm)]
    ppermute x3, starting transfers between devices: 5.08 us -> 6.78 us  [across(): return lax.ppermute(v, 'group', perm)]
  transfers between devices with their start and end apart: 20 -> 20, of which waited for: 4 -> 3; matrix products, arithmetic and copies ran while one was open for 2% -> 2% of each run, Pallas kernels for 10% -> 10%
where the time goes in v8:
time: 70.4 us; the launch traced here: 70.3 us
  starting transfers between devices  37.7 us (54%)
  blocking collectives  14.8 us (21%)
  Pallas kernels  10.7 us (15%)
  other arithmetic  3.19 us (5%)
  waiting for transfers between devices  2.05 us (3%)
  between operations  1.59 us (2%)
    ppermute x17, starting transfers between devices, along(): return lax.ppermute(v, 'loop', perm)  30.9 us
    all_to_all x1, blocking collectives, shards(): sums = lax.all_to_all(sums, 'loop', 0, 0, tiled=True)  14.8 us
    ppermute x3, starting transfers between devices, across(): return lax.ppermute(v, 'group', perm)  6.78 us
    pallas_call x1, Pallas kernels, shards(): pl.pallas_call(begin, in_specs=[WHOLE] * 12, out_specs=[WHOLE] * 2, out_s...  4.8 us
    pallas_call x1, Pallas kernels, shards(): pl.pallas_call(rescale, in_specs=[AWAY] * 3, out_specs=AWAY, out_shape=ja...  1.94 us
    pallas_call x1, Pallas kernels, shards(): pl.pallas_call(proceed, in_specs=[WHOLE] * 6, out_specs=WHOLE, out_shape=...  1.8 us
    ppermute x17, waiting for transfers between devices, along(): return lax.ppermute(v, 'loop', perm)  1.74 us
    pallas_call x1, Pallas kernels, shards(): pl.pallas_call(finish, in_specs=[WHOLE] * 4, out_specs=[AWAY, WHOLE], out...  1.55 us
  transfers between devices with their start and end apart: 20, of which 3 were waited for; matrix products, arithmetic and copies ran while one was open for 2% of the time, Pallas kernels for 10%

profile of v8, /device:TPU:1, one launch (start us, length us, event | category | flops | bytes accessed | tf_op | source)
XLA Modules:
  0.0 70.3 jit_solution(11775483346470332538)
XLA Ops:
  0.7 0.7 fusion
  1.3 0.1 broadcast_in_dim.20
  1.4 0.9 %pad_maximum_fusion.2 = bf16[528,128]{1,0:T(8,128)(2,1)S(1)} fusion(bf16[16,128]{1,0:T(8,128)(2,1)S(1)} %broadcast_in_dim.20, bf16[512,128]{1,0:T(8,128)(2,1)} %bitcast.8), kind=kLoop, calls=%fused_computation.2 | loop fusion | flops 270336 | bytes 270336 | tf_op jit(solution)/shard_map/concatenate | solution.py:196
  2.3 3.3 %collective-permute-start = (bf16[528,128]{1,0:T(8,128)(2,1)S(1)}, bf16[528,128]{1,0:T(8,128)(2,1)S(1)}, u32[]{:S(2)}, u32[]{:S(2)}) collective-permute-start(bf16[528,128]{1,0:T(8,128)(2,1)S(1)} %pad_maximum_fusion.2), channel_id=1, source_target_pairs={{0,1},{1,0},{2,3},{3,2},{4,5},{5,4},{6,7},{7,6},{8,9},{9,8},{10,11... | collective-permute-start | bytes 405512 | tf_op jit(solution)/shard_map/ppermute | solution.py:201
  5.6 0.0 collective-permute-start.1
  5.6 1.7 %collective-permute-start.2 = (bf16[528,128]{1,0:T(8,128)(2,1)S(1)}, bf16[528,128]{1,0:T(8,128)(2,1)S(1)}, u32[]{:S(2)}, u32[]{:S(2)}) collective-permute-start(bf16[528,128]{1,0:T(8,128)(2,1)S(1)} %pad_maximum_fusion.2), channel_id=1, source_target_pairs={{0,3},{1,2},{2,1},{3,0},{4,7},{5,6},{6,5},{7,4},{8,11},{9,10},{10,... | collective-permute-start | bytes 405512 | tf_op jit(solution)/shard_map/ppermute | solution.py:201
  7.4 0.0 collective-permute-done
  7.4 0.9 %pad_maximum_fusion.refs_0_ = bf16[1056,128]{1,0:T(8,128)(2,1)S(1)} fusion(bf16[528,128]{1,0:T(8,128)(2,1)S(1)} %collective-permute-done, bf16[16,128]{1,0:T(8,128)(2,1)S(1)} %broadcast_in_dim.20, bf16[512,128]{1,0:T(8,128)(2,1)} %bitcast.9), kind=kLoop, calls=%fused_computation | loop fusion | flops 811008 | bytes 540672 | tf_op jit(solution)/shard_map/concatenate | solution.py:208
  8.3 3.9 %collective-permute-start.3 = (bf16[1056,128]{1,0:T(8,128)(2,1)S(1)}, bf16[1056,128]{1,0:T(8,128)(2,1)S(1)}, u32[]{:S(2)}, u32[]{:S(2)}) collective-permute-start(bf16[1056,128]{1,0:T(8,128)(2,1)S(1)} %pad_maximum_fusion.refs_0_), channel_id=1, source_target_pairs={{0,4},{1,29},{2,6},{3,31},{4,8},{5,1},{6,10},{7,3},{8,12},{9,5},{1... | collective-permute-start | bytes 811016 | tf_op jit(solution)/shard_map/ppermute | solution.py:201
  12.2 2.9 %collective-permute-start.13 = (bf16[528,128]{1,0:T(8,128)(2,1)S(1)}, bf16[528,128]{1,0:T(8,128)(2,1)S(1)}, u32[]{:S(2)}, u32[]{:S(2)}) collective-permute-start(bf16[528,128]{1,0:T(8,128)(2,1)S(1)} %pad_maximum_fusion.2), channel_id=1, source_target_pairs={{0,32},{32,0},{64,96},{96,64},{128,160},{160,128},{192,224},{224,1... | collective-permute-start | bytes 405512 | tf_op jit(solution)/shard_map/ppermute | solution.py:204
  15.1 0.0 collective-permute-done.1
  15.1 0.0 collective-permute-done.2
  15.2 0.4 collective-permute-done.3.refs_2_
  15.6 3.1 %collective-permute-start.4 = (bf16[1056,128]{1,0:T(8,128)(2,1)S(1)}, bf16[1056,128]{1,0:T(8,128)(2,1)S(1)}, u32[]{:S(2)}, u32[]{:S(2)}) collective-permute-start(bf16[1056,128]{1,0:T(8,128)(2,1)S(1)} %constant_dynamic-update-slice_fusion.refs_1_), channel_id=1, source_target_pairs={{0,4},{1,29},{2,6},{3,31},{4,8},{5,1},{6,10},{7,3},{8,12},{9,5},{1... | collective-permute-start | bytes 811016 | tf_op jit(solution)/shard_map/ppermute | solution.py:201
  18.7 0.0 collective-permute-done.13
  18.8 1.3 %collective-permute-start.14 = (bf16[1056,128]{1,0:T(8,128)(2,1)S(1)}, bf16[1056,128]{1,0:T(8,128)(2,1)S(1)}, u32[]{:S(2)}, u32[]{:S(2)}) collective-permute-start(bf16[1056,128]{1,0:T(8,128)(2,1)S(1)} %pad_maximum_fusion.1), channel_id=1, source_target_pairs={{0,64},{32,96},{64,0},{96,32},{128,192},{160,224},{192,128},{224,1... | collective-permute-start | bytes 811016 | tf_op jit(solution)/shard_map/ppermute | solution.py:204
  20.1 4.2 %collective-permute-start.10 = (bf16[1056,128]{1,0:T(8,128)(2,1)S(1)}, bf16[1056,128]{1,0:T(8,128)(2,1)S(1)}, u32[]{:S(2)}, u32[]{:S(2)}) collective-permute-start(bf16[1056,128]{1,0:T(8,128)(2,1)S(1)} %collective-permute-done.3.refs_2_), channel_id=1, source_target_pairs={{0,4},{1,29},{2,6},{3,31},{4,8},{5,1},{6,10},{7,3},{8,12},{9,5},{1... | collective-permute-start | bytes 811016 | tf_op jit(solution)/shard_map/ppermute | solution.py:201
  24.3 0.0 collective-permute-start.8
  24.3 0.0 collective-permute-done.4.refs_3_
  24.3 1.2 %collective-permute-start.5 = (bf16[1056,128]{1,0:T(8,128)(2,1)S(1)}, bf16[1056,128]{1,0:T(8,128)(2,1)S(1)}, u32[]{:S(2)}, u32[]{:S(2)}) collective-permute-start(bf16[1056,128]{1,0:T(8,128)(2,1)S(1)} %collective-permute-done.4.refs_3_), channel_id=1, source_target_pairs={{0,4},{1,29},{2,6},{3,31},{4,8},{5,1},{6,10},{7,3},{8,12},{9,5},{1... | collective-permute-start | bytes 811016 | tf_op jit(solution)/shard_map/ppermute | solution.py:201
  25.6 0.3 collective-permute-done.14
  25.9 2.6 %collective-permute-start.15 = (bf16[2112,128]{1,0:T(8,128)(2,1)S(1)}, bf16[2112,128]{1,0:T(8,128)(2,1)S(1)}, u32[]{:S(2)}, u32[]{:S(2)}) collective-permute-start(bf16[2112,128]{1,0:T(8,128)(2,1)S(1)} %constant_dynamic-update-slice_fusion.2.refs_10_), channel_id=1, source_target_pairs={{0,192},{32,224},{64,128},{96,160},{128,64},{160,96},{192,0},{224,... | collective-permute-start | bytes 1622024 | tf_op jit(solution)/shard_map/ppermute | solution.py:204
  28.5 0.0 collective-permute-start.9
  28.5 0.0 collective-permute-done.10.refs_6_
  28.5 6.3 %collective-permute-start.16 = (bf16[1056,128]{1,0:T(8,128)(2,1)S(1)}, bf16[1056,128]{1,0:T(8,128)(2,1)S(1)}, u32[]{:S(2)}, u32[]{:S(2)}) collective-permute-start(bf16[1056,128]{1,0:T(8,128)(2,1)S(1)} %collective-permute-done.10.refs_6_), channel_id=1, source_target_pairs={{0,4},{1,29},{2,6},{3,31},{4,8},{5,1},{6,10},{7,3},{8,12},{9,5},{1... | collective-permute-start | bytes 811016 | tf_op jit(solution)/shard_map/ppermute | solution.py:201
  34.8 0.0 collective-permute-done.8.refs_4_
  34.8 0.0 collective-permute-start.11
  34.8 0.0 collective-permute-done.5.refs_7_
  34.8 0.8 %collective-permute-start.6 = (bf16[1056,128]{1,0:T(8,128)(2,1)S(1)}, bf16[1056,128]{1,0:T(8,128)(2,1)S(1)}, u32[]{:S(2)}, u32[]{:S(2)}) collective-permute-start(bf16[1056,128]{1,0:T(8,128)(2,1)S(1)} %collective-permute-done.5.refs_7_), channel_id=1, source_target_pairs={{0,4},{1,29},{2,6},{3,31},{4,8},{5,1},{6,10},{7,3},{8,12},{9,5},{1... | collective-permute-start | bytes 811016 | tf_op jit(solution)/shard_map/ppermute | solution.py:201
  35.6 0.0 collective-permute-done.9.refs_5_
  35.6 0.0 collective-permute-start.12
  36.2 0.7 fusion.1
  36.9 1.3 %collective-permute-done.16.refs_0_ = bf16[1056,128]{1,0:T(8,128)(2,1)S(1)} collective-permute-done((bf16[1056,128]{1,0:T(8,128)(2,1)S(1)}, bf16[1056,128]{1,0:T(8,128)(2,1)S(1)}, u32[]{:S(2)}, u32[]{:S(2)}) %collective-permute-start.16) | collective-permute-done | bytes 270368 | tf_op jit(solution)/shard_map/ppermute | solution.py:201
  38.2 3.4 %collective-permute-start.19 = (bf16[1056,128]{1,0:T(8,128)(2,1)S(1)}, bf16[1056,128]{1,0:T(8,128)(2,1)S(1)}, u32[]{:S(2)}, u32[]{:S(2)}) collective-permute-start(bf16[1056,128]{1,0:T(8,128)(2,1)S(1)} %collective-permute-done.16.refs_0_), channel_id=1, source_target_pairs={{0,4},{1,29},{2,6},{3,31},{4,8},{5,1},{6,10},{7,3},{8,12},{9,5},{1... | collective-permute-start | bytes 811016 | tf_op jit(solution)/shard_map/ppermute | solution.py:201
  41.6 0.0 collective-permute-done.11.refs_8_
  41.6 0.0 collective-permute-start.17
  41.6 0.0 collective-permute-done.6.refs_1_
  41.6 1.4 %collective-permute-start.18 = (bf16[1056,128]{1,0:T(8,128)(2,1)S(1)}, bf16[1056,128]{1,0:T(8,128)(2,1)S(1)}, u32[]{:S(2)}, u32[]{:S(2)}) collective-permute-start(bf16[1056,128]{1,0:T(8,128)(2,1)S(1)} %collective-permute-done.6.refs_1_), channel_id=1, source_target_pairs={{0,1},{1,0},{2,3},{3,2},{4,5},{5,4},{6,7},{7,6},{8,9},{9,8},{10,11... | collective-permute-start | bytes 811016 | tf_op jit(solution)/shard_map/ppermute | solution.py:201
  43.0 0.0 collective-permute-done.15.refs_11_
  43.0 1.5 %collective-permute-start.7 = (bf16[1056,128]{1,0:T(8,128)(2,1)S(1)}, bf16[1056,128]{1,0:T(8,128)(2,1)S(1)}, u32[]{:S(2)}, u32[]{:S(2)}) collective-permute-start(bf16[1056,128]{1,0:T(8,128)(2,1)S(1)} %collective-permute-done.6.refs_1_), channel_id=1, source_target_pairs={{0,4},{1,29},{2,6},{3,31},{4,8},{5,1},{6,10},{7,3},{8,12},{9,5},{1... | collective-permute-start | bytes 811016 | tf_op jit(solution)/shard_map/ppermute | solution.py:201
  44.5 0.0 collective-permute-done.12.refs_9_
  44.5 4.8 %shard_map.55 = (bf16[8,256,1152]{2,1,0:T(8,128)(2,1)S(1)}, f32[256,1024]{1,0:T(8,128)S(1)}) custom-call(bf16[1056,128]{1,0:T(8,128)(2,1)S(1)} %pad_maximum_fusion.refs_0_, bf16[1056,128]{1,0:T(8,128)(2,1)S(1)} %constant_dynamic-update-slice_fusion.refs_1_, bf16[1056,128]{1,0:T(8,128)(2,1)S(1)} %collective-permute-done.3.refs_2_, ...), custom_call_target="tpu_custom_call" | custom-call | flops 3221225472 | bytes 25165824 | tf_op jit(solution)/shard_map/pallas_call | solution.py:233
  49.3 0.0 collective-permute-done.19.pair
  49.3 0.6 shard_map.56.refs_5_
  49.9 0.0 collective-permute-done.17.refs_2_
  49.9 0.0 collective-permute-done.18.refs_3_
  49.9 1.8 %shard_map.57.before = f32[256,1024]{1,0:T(8,128)S(1)} custom-call(bf16[1056,128]{1,0:T(8,128)(2,1)S(1)} %collective-permute-done.16.refs_0_, bf16[1056,128]{1,0:T(8,128)(2,1)S(1)} %collective-permute-done.6.refs_1_, bf16[1056,128]{1,0:T(8,128)(2,1)S(1)} %collective-permute-done.17.refs_2_, bf16[1056,128]{1,0:T(8,128)(2,1)S(1)} %collective-permute-done.18.refs_3_, ...), custom_call_target="tpu_custom_call" | custom-call | flops 1073741824 | bytes 8388608 | tf_op jit(solution)/shard_map/pallas_call | solution.py:251
  51.8 0.0 collective-permute-done.7.beside
  51.8 0.1 broadcast_in_dim.21.codes
  51.8 1.5 %shard_map.58 = (f32[8,128,128]{2,1,0:T(8,128)S(1)}, f32[32,8,128]{2,1,0:T(8,128)S(1)}) custom-call(bf16[16,128]{1,0:T(8,128)(2,1)S(1)} %broadcast_in_dim.21.codes, bf16[1056,128]{1,0:T(8,128)(2,1)S(1)} %collective-permute-done.7.beside, bf16[8,256,1152]{2,1,0:T(8,128)(2,1)S(1)} %get-tuple-element.19.dense_left.refs_4_, f32[256,1024]{1,0:T(8,128)S(1)} %shard_map.57.before), custom_call_target="tpu_custom_call" | custom-call | flops 536870912 | bytes 4194304 | tf_op jit(solution)/shard_map/pallas_call | solution.py:260
  53.4 14.8 %all_to_all.5.sums = f32[32,8,128]{2,1,0:T(8,128)S(1)} all-to-all(f32[32,8,128]{2,1,0:T(8,128)S(1)} %get-tuple-element.22), channel_id=1, replica_groups=mesh['group'=8,'loop'=32] {'loop'}, dimensions={0} | all-to-all | bytes 262144 | tf_op jit(solution)/shard_map/all_to_all | solution.py:274
  68.2 1.9 %shard_map.59 = f32[8,128,128]{2,1,0:T(8,128)} custom-call(bf16[16,128]{1,0:T(8,128)(2,1)S(1)} %broadcast_in_dim.21.codes, f32[8,128,128]{2,1,0:T(8,128)S(1)} %get-tuple-element.21.squares, f32[32,8,128]{2,1,0:T(8,128)S(1)} %all_to_all.5.sums), custom_call_target="tpu_custom_call" | custom-call | tf_op jit(solution)/shard_map/pallas_call | solution.py:275
  (6 shorter events, 0.1 us)
Async XLA Ops:
  2.3 5.1 %collective-permute-start = (bf16[528,128]{1,0:T(8,128)(2,1)S(1)}, bf16[528,128]{1,0:T(8,128)(2,1)S(1)}, u32[]{:S(2)}, u32[]{:S(2)}) collective-permute-start(bf16[528,128]{1,0:T(8,128)(2,1)S(1)} %pad_maximum_fusion.2), channel_id=1, source_target_pairs={{0,1},{1,0},{2,3},{3,2},{4,5},{5,4},{6,7},{7,6},{8,9},{9,8},{10,11... | collective-permute-start | bytes 405512 | tf_op jit(solution)/shard_map/ppermute | solution.py:201
  5.6 9.5 %collective-permute-start.1 = (bf16[528,128]{1,0:T(8,128)(2,1)S(1)}, bf16[528,128]{1,0:T(8,128)(2,1)S(1)}, u32[]{:S(2)}, u32[]{:S(2)}) collective-permute-start(bf16[528,128]{1,0:T(8,128)(2,1)S(1)} %pad_maximum_fusion.2), channel_id=1, source_target_pairs={{0,2},{1,3},{2,0},{3,1},{4,6},{5,7},{6,4},{7,5},{8,10},{9,11},{10,... | collective-permute-start | bytes 405512 | tf_op jit(solution)/shard_map/ppermute | solution.py:201
  5.6 9.5 %collective-permute-start.2 = (bf16[528,128]{1,0:T(8,128)(2,1)S(1)}, bf16[528,128]{1,0:T(8,128)(2,1)S(1)}, u32[]{:S(2)}, u32[]{:S(2)}) collective-permute-start(bf16[528,128]{1,0:T(8,128)(2,1)S(1)} %pad_maximum_fusion.2), channel_id=1, source_target_pairs={{0,3},{1,2},{2,1},{3,0},{4,7},{5,6},{6,5},{7,4},{8,11},{9,10},{10,... | collective-permute-start | bytes 405512 | tf_op jit(solution)/shard_map/ppermute | solution.py:201
  8.3 7.3 %collective-permute-start.3 = (bf16[1056,128]{1,0:T(8,128)(2,1)S(1)}, bf16[1056,128]{1,0:T(8,128)(2,1)S(1)}, u32[]{:S(2)}, u32[]{:S(2)}) collective-permute-start(bf16[1056,128]{1,0:T(8,128)(2,1)S(1)} %pad_maximum_fusion.refs_0_), channel_id=1, source_target_pairs={{0,4},{1,29},{2,6},{3,31},{4,8},{5,1},{6,10},{7,3},{8,12},{9,5},{1... | collective-permute-start | bytes 811016 | tf_op jit(solution)/shard_map/ppermute | solution.py:201
  12.2 6.5 %collective-permute-start.13 = (bf16[528,128]{1,0:T(8,128)(2,1)S(1)}, bf16[528,128]{1,0:T(8,128)(2,1)S(1)}, u32[]{:S(2)}, u32[]{:S(2)}) collective-permute-start(bf16[528,128]{1,0:T(8,128)(2,1)S(1)} %pad_maximum_fusion.2), channel_id=1, source_target_pairs={{0,32},{32,0},{64,96},{96,64},{128,160},{160,128},{192,224},{224,1... | collective-permute-start | bytes 405512 | tf_op jit(solution)/shard_map/ppermute | solution.py:204
  15.6 8.7 %collective-permute-start.4 = (bf16[1056,128]{1,0:T(8,128)(2,1)S(1)}, bf16[1056,128]{1,0:T(8,128)(2,1)S(1)}, u32[]{:S(2)}, u32[]{:S(2)}) collective-permute-start(bf16[1056,128]{1,0:T(8,128)(2,1)S(1)} %constant_dynamic-update-slice_fusion.refs_1_), channel_id=1, source_target_pairs={{0,4},{1,29},{2,6},{3,31},{4,8},{5,1},{6,10},{7,3},{8,12},{9,5},{1... | collective-permute-start | bytes 811016 | tf_op jit(solution)/shard_map/ppermute | solution.py:201
  18.8 7.1 %collective-permute-start.14 = (bf16[1056,128]{1,0:T(8,128)(2,1)S(1)}, bf16[1056,128]{1,0:T(8,128)(2,1)S(1)}, u32[]{:S(2)}, u32[]{:S(2)}) collective-permute-start(bf16[1056,128]{1,0:T(8,128)(2,1)S(1)} %pad_maximum_fusion.1), channel_id=1, source_target_pairs={{0,64},{32,96},{64,0},{96,32},{128,192},{160,224},{192,128},{224,1... | collective-permute-start | bytes 811016 | tf_op jit(solution)/shard_map/ppermute | solution.py:204
  20.1 8.4 %collective-permute-start.10 = (bf16[1056,128]{1,0:T(8,128)(2,1)S(1)}, bf16[1056,128]{1,0:T(8,128)(2,1)S(1)}, u32[]{:S(2)}, u32[]{:S(2)}) collective-permute-start(bf16[1056,128]{1,0:T(8,128)(2,1)S(1)} %collective-permute-done.3.refs_2_), channel_id=1, source_target_pairs={{0,4},{1,29},{2,6},{3,31},{4,8},{5,1},{6,10},{7,3},{8,12},{9,5},{1... | collective-permute-start | bytes 811016 | tf_op jit(solution)/shard_map/ppermute | solution.py:201
  24.3 10.5 %collective-permute-start.8 = (bf16[1056,128]{1,0:T(8,128)(2,1)S(1)}, bf16[1056,128]{1,0:T(8,128)(2,1)S(1)}, u32[]{:S(2)}, u32[]{:S(2)}) collective-permute-start(bf16[1056,128]{1,0:T(8,128)(2,1)S(1)} %collective-permute-done.3.refs_2_), channel_id=1, source_target_pairs={{0,1},{1,0},{2,3},{3,2},{4,5},{5,4},{6,7},{7,6},{8,9},{9,8},{10,11... | collective-permute-start | bytes 811016 | tf_op jit(solution)/shard_map/ppermute | solution.py:201
  24.3 10.5 %collective-permute-start.5 = (bf16[1056,128]{1,0:T(8,128)(2,1)S(1)}, bf16[1056,128]{1,0:T(8,128)(2,1)S(1)}, u32[]{:S(2)}, u32[]{:S(2)}) collective-permute-start(bf16[1056,128]{1,0:T(8,128)(2,1)S(1)} %collective-permute-done.4.refs_3_), channel_id=1, source_target_pairs={{0,4},{1,29},{2,6},{3,31},{4,8},{5,1},{6,10},{7,3},{8,12},{9,5},{1... | collective-permute-start | bytes 811016 | tf_op jit(solution)/shard_map/ppermute | solution.py:201
  25.9 17.0 %collective-permute-start.15 = (bf16[2112,128]{1,0:T(8,128)(2,1)S(1)}, bf16[2112,128]{1,0:T(8,128)(2,1)S(1)}, u32[]{:S(2)}, u32[]{:S(2)}) collective-permute-start(bf16[2112,128]{1,0:T(8,128)(2,1)S(1)} %constant_dynamic-update-slice_fusion.2.refs_10_), channel_id=1, source_target_pairs={{0,192},{32,224},{64,128},{96,160},{128,64},{160,96},{192,0},{224,... | collective-permute-start | bytes 1622024 | tf_op jit(solution)/shard_map/ppermute | solution.py:204
  28.5 7.1 %collective-permute-start.9 = (bf16[1056,128]{1,0:T(8,128)(2,1)S(1)}, bf16[1056,128]{1,0:T(8,128)(2,1)S(1)}, u32[]{:S(2)}, u32[]{:S(2)}) collective-permute-start(bf16[1056,128]{1,0:T(8,128)(2,1)S(1)} %collective-permute-done.4.refs_3_), channel_id=1, source_target_pairs={{0,1},{1,0},{2,3},{3,2},{4,5},{5,4},{6,7},{7,6},{8,9},{9,8},{10,11... | collective-permute-start | bytes 811016 | tf_op jit(solution)/shard_map/ppermute | solution.py:201
  28.5 9.7 %collective-permute-start.16 = (bf16[1056,128]{1,0:T(8,128)(2,1)S(1)}, bf16[1056,128]{1,0:T(8,128)(2,1)S(1)}, u32[]{:S(2)}, u32[]{:S(2)}) collective-permute-start(bf16[1056,128]{1,0:T(8,128)(2,1)S(1)} %collective-permute-done.10.refs_6_), channel_id=1, source_target_pairs={{0,4},{1,29},{2,6},{3,31},{4,8},{5,1},{6,10},{7,3},{8,12},{9,5},{1... | collective-permute-start | bytes 811016 | tf_op jit(solution)/shard_map/ppermute | solution.py:201
  34.8 6.8 %collective-permute-start.11 = (bf16[1056,128]{1,0:T(8,128)(2,1)S(1)}, bf16[1056,128]{1,0:T(8,128)(2,1)S(1)}, u32[]{:S(2)}, u32[]{:S(2)}) collective-permute-start(bf16[1056,128]{1,0:T(8,128)(2,1)S(1)} %collective-permute-done.10.refs_6_), channel_id=1, source_target_pairs={{0,1},{1,0},{2,3},{3,2},{4,5},{5,4},{6,7},{7,6},{8,9},{9,8},{10,11... | collective-permute-start | bytes 811016 | tf_op jit(solution)/shard_map/ppermute | solution.py:201
  34.8 6.8 %collective-permute-start.6 = (bf16[1056,128]{1,0:T(8,128)(2,1)S(1)}, bf16[1056,128]{1,0:T(8,128)(2,1)S(1)}, u32[]{:S(2)}, u32[]{:S(2)}) collective-permute-start(bf16[1056,128]{1,0:T(8,128)(2,1)S(1)} %collective-permute-done.5.refs_7_), channel_id=1, source_target_pairs={{0,4},{1,29},{2,6},{3,31},{4,8},{5,1},{6,10},{7,3},{8,12},{9,5},{1... | collective-permute-start | bytes 811016 | tf_op jit(solution)/shard_map/ppermute | solution.py:201
  35.6 8.9 %collective-permute-start.12 = (bf16[1056,128]{1,0:T(8,128)(2,1)S(1)}, bf16[1056,128]{1,0:T(8,128)(2,1)S(1)}, u32[]{:S(2)}, u32[]{:S(2)}) collective-permute-start(bf16[1056,128]{1,0:T(8,128)(2,1)S(1)} %collective-permute-done.5.refs_7_), channel_id=1, source_target_pairs={{0,1},{1,0},{2,3},{3,2},{4,5},{5,4},{6,7},{7,6},{8,9},{9,8},{10,11... | collective-permute-start | bytes 811016 | tf_op jit(solution)/shard_map/ppermute | solution.py:201
  38.2 11.1 %collective-permute-start.19 = (bf16[1056,128]{1,0:T(8,128)(2,1)S(1)}, bf16[1056,128]{1,0:T(8,128)(2,1)S(1)}, u32[]{:S(2)}, u32[]{:S(2)}) collective-permute-start(bf16[1056,128]{1,0:T(8,128)(2,1)S(1)} %collective-permute-done.16.refs_0_), channel_id=1, source_target_pairs={{0,4},{1,29},{2,6},{3,31},{4,8},{5,1},{6,10},{7,3},{8,12},{9,5},{1... | collective-permute-start | bytes 811016 | tf_op jit(solution)/shard_map/ppermute | solution.py:201
  41.6 8.3 %collective-permute-start.17 = (bf16[1056,128]{1,0:T(8,128)(2,1)S(1)}, bf16[1056,128]{1,0:T(8,128)(2,1)S(1)}, u32[]{:S(2)}, u32[]{:S(2)}) collective-permute-start(bf16[1056,128]{1,0:T(8,128)(2,1)S(1)} %collective-permute-done.16.refs_0_), channel_id=1, source_target_pairs={{0,1},{1,0},{2,3},{3,2},{4,5},{5,4},{6,7},{7,6},{8,9},{9,8},{10,11... | collective-permute-start | bytes 811016 | tf_op jit(solution)/shard_map/ppermute | solution.py:201
  41.6 8.3 %collective-permute-start.18 = (bf16[1056,128]{1,0:T(8,128)(2,1)S(1)}, bf16[1056,128]{1,0:T(8,128)(2,1)S(1)}, u32[]{:S(2)}, u32[]{:S(2)}) collective-permute-start(bf16[1056,128]{1,0:T(8,128)(2,1)S(1)} %collective-permute-done.6.refs_1_), channel_id=1, source_target_pairs={{0,1},{1,0},{2,3},{3,2},{4,5},{5,4},{6,7},{7,6},{8,9},{9,8},{10,11... | collective-permute-start | bytes 811016 | tf_op jit(solution)/shard_map/ppermute | solution.py:201
  43.0 8.8 %collective-permute-start.7 = (bf16[1056,128]{1,0:T(8,128)(2,1)S(1)}, bf16[1056,128]{1,0:T(8,128)(2,1)S(1)}, u32[]{:S(2)}, u32[]{:S(2)}) collective-permute-start(bf16[1056,128]{1,0:T(8,128)(2,1)S(1)} %collective-permute-done.6.refs_1_), channel_id=1, source_target_pairs={{0,4},{1,29},{2,6},{3,31},{4,8},{5,1},{6,10},{7,3},{8,12},{9,5},{1... | collective-permute-start | bytes 811016 | tf_op jit(solution)/shard_map/ppermute | solution.py:201

commit v9 on v8

--- a/solution.py
+++ b/solution.py
@@ -58,13 +58,15 @@
     return i >> 2, (i >> 1) & 1, i & 1, j >> 1, j & 1
 
 
-def multiply(dense_left, dense_right, j, units):
-    dense_right[...] = jnp.zeros_like(dense_right)
-    for ref, base, y, c in units:
-        place(dense_right, ref, base, (y * 2 + c) * 256)
-    return jnp.dot(
-        dense_left[j, :, : 8 * TILE], dense_right[:, : 8 * TILE], preferred_element_type=F32
-    )
+def multiply(dense_left, jobs, buffers):
+    for k, (j, units) in enumerate(jobs):
+        dense_right = buffers[k % len(buffers)]
+        dense_right[...] = jnp.zeros_like(dense_right)
+        for ref, base, y, c in units:
+            place(dense_right, ref, base, (y * 2 + c) * 256)
+        yield jnp.dot(
+            dense_left[j, :, : 8 * TILE], dense_right[:, : 8 * TILE], preferred_element_type=F32
+        )
 
 
 def round_units(refs, y, c):
@@ -79,35 +81,33 @@
 
 def begin(*refs):
     own, rounds, left = refs[:2], refs[2:10], refs[10:12]
-    dense_left, product, dense_right = refs[12:]
+    dense_left, product, *dense_right = refs[12:]
     z, y, c, x, h = where_am_i()
     dense_left[...] = jnp.zeros_like(dense_left)
     for k in range(8):
         xx = (x, x ^ 1, 3 - x, (3 - x) ^ 1)[k >> 1]
         place(dense_left.at[xx * 2 + (h ^ (k & 1))], left[k >> 2], (k & 3) * UNIT, 0)
-    product[...] = multiply(dense_left, dense_right, z, round_units(own, y, c))
     sign = 1 - 2 * c
+    jobs = [(z, round_units(own, y, c))]
     for r in (1, 2):
         near, far = rounds[4 * r - 4 : 4 * r - 2], rounds[4 * r - 2 : 4 * r]
-        product[...] += multiply(
-            dense_left, dense_right, (z - sign * r) & 7, round_units(near, y, c)
-        )
-        product[...] += multiply(
-            dense_left, dense_right, (z + sign * r) & 7, round_units(far, y, 1 - c)
-        )
+        jobs.append(((z - sign * r) & 7, round_units(near, y, c)))
+        jobs.append(((z + sign * r) & 7, round_units(far, y, 1 - c)))
+    for k, part in enumerate(multiply(dense_left, jobs, dense_right)):
+        product[...] = part if k == 0 else product[...] + part
 
 
 def proceed(*refs):
     near, far = refs[:2], refs[2:4]
-    dense_left, before, product, dense_right = refs[4:]
+    dense_left, before, product, *dense_right = refs[4:]
     z, y, c, _, _ = where_am_i()
     sign = 1 - 2 * c
-    product[...] = before[...] + multiply(
-        dense_left, dense_right, (z - sign * 3) & 7, round_units(near, y, c)
-    )
-    product[...] += multiply(
-        dense_left, dense_right, (z + sign * 3) & 7, round_units(far, y, 1 - c)
-    )
+    jobs = [
+        ((z - sign * 3) & 7, round_units(near, y, c)),
+        ((z + sign * 3) & 7, round_units(far, y, 1 - c)),
+    ]
+    for k, part in enumerate(multiply(dense_left, jobs, dense_right)):
+        product[...] = (before if k == 0 else product)[...] + part
 
 
 def half(ref, y, c, dense_left, dense_half):
@@ -235,7 +235,7 @@
         in_specs=[WHOLE] * 12,
         out_specs=[WHOLE] * 2,
         out_shape=[DENSE_LEFT, PRODUCT],
-        scratch_shapes=[DENSE_RIGHT],
+        scratch_shapes=[DENSE_RIGHT] * 2,
         compiler_params=limit,
         cost_estimate=cost(6),
     )(*sum(right[:5], []), *left)
@@ -253,7 +253,7 @@
         in_specs=[WHOLE] * 6,
         out_specs=WHOLE,
         out_shape=PRODUCT,
-        scratch_shapes=[DENSE_RIGHT],
+        scratch_shapes=[DENSE_RIGHT] * 2,
         compiler_params=limit,
         cost_estimate=cost(2),
     )(*sum(right[5:], []), dense_left, product)

time: 70.4 us -> 70.2 us (level)
  no operation moved by 1% of the time
where the time goes in v9:
time: 70.2 us; the launch traced here: 70 us
  starting transfers between devices  37.7 us (54%)
  blocking collectives  14.8 us (21%)
  Pallas kernels  10.4 us (15%)
  other arithmetic  3.19 us (5%)
  waiting for transfers between devices  2.05 us (3%)
  between operations  1.59 us (2%)
    ppermute x17, starting transfers between devices, along(): return lax.ppermute(v, 'loop', perm)  30.9 us
    all_to_all x1, blocking collectives, shards(): sums = lax.all_to_all(sums, 'loop', 0, 0, tiled=True)  14.8 us
    ppermute x3, starting transfers between devices, across(): return lax.ppermute(v, 'group', perm)  6.78 us
    pallas_call x1, Pallas kernels, shards(): pl.pallas_call(begin, in_specs=[WHOLE] * 12, out_specs=[WHOLE] * 2, out_s...  4.58 us
    pallas_call x1, Pallas kernels, shards(): pl.pallas_call(rescale, in_specs=[AWAY] * 3, out_specs=AWAY, out_shape=ja...  1.94 us
    pallas_call x1, Pallas kernels, shards(): pl.pallas_call(proceed, in_specs=[WHOLE] * 6, out_specs=WHOLE, out_shape=...  1.76 us
    ppermute x17, waiting for transfers between devices, along(): return lax.ppermute(v, 'loop', perm)  1.74 us
    pallas_call x1, Pallas kernels, shards(): pl.pallas_call(finish, in_specs=[WHOLE] * 4, out_specs=[AWAY, WHOLE], out...  1.55 us
  transfers between devices with their start and end apart: 20, of which 3 were waited for; matrix products, arithmetic and copies ran while one was open for 2% of the time, Pallas kernels for 10%

profile of v9, /device:TPU:1, one launch (start us, length us, event | category | flops | bytes accessed | tf_op | source)
XLA Modules:
  0.0 70.0 jit_solution(1647453783574389926)
XLA Ops:
  0.7 0.7 fusion
  1.3 0.1 broadcast_in_dim.20
  1.4 0.9 %pad_maximum_fusion.2 = bf16[528,128]{1,0:T(8,128)(2,1)S(1)} fusion(bf16[16,128]{1,0:T(8,128)(2,1)S(1)} %broadcast_in_dim.20, bf16[512,128]{1,0:T(8,128)(2,1)} %bitcast.8), kind=kLoop, calls=%fused_computation.2 | loop fusion | flops 270336 | bytes 270336 | tf_op jit(solution)/shard_map/concatenate | solution.py:196
  2.3 3.3 %collective-permute-start = (bf16[528,128]{1,0:T(8,128)(2,1)S(1)}, bf16[528,128]{1,0:T(8,128)(2,1)S(1)}, u32[]{:S(2)}, u32[]{:S(2)}) collective-permute-start(bf16[528,128]{1,0:T(8,128)(2,1)S(1)} %pad_maximum_fusion.2), channel_id=1, source_target_pairs={{0,1},{1,0},{2,3},{3,2},{4,5},{5,4},{6,7},{7,6},{8,9},{9,8},{10,11... | collective-permute-start | bytes 405512 | tf_op jit(solution)/shard_map/ppermute | solution.py:201
  5.6 0.0 collective-permute-start.1
  5.6 1.7 %collective-permute-start.2 = (bf16[528,128]{1,0:T(8,128)(2,1)S(1)}, bf16[528,128]{1,0:T(8,128)(2,1)S(1)}, u32[]{:S(2)}, u32[]{:S(2)}) collective-permute-start(bf16[528,128]{1,0:T(8,128)(2,1)S(1)} %pad_maximum_fusion.2), channel_id=1, source_target_pairs={{0,3},{1,2},{2,1},{3,0},{4,7},{5,6},{6,5},{7,4},{8,11},{9,10},{10,... | collective-permute-start | bytes 405512 | tf_op jit(solution)/shard_map/ppermute | solution.py:201
  7.4 0.0 collective-permute-done
  7.4 0.9 %pad_maximum_fusion.refs_0_ = bf16[1056,128]{1,0:T(8,128)(2,1)S(1)} fusion(bf16[528,128]{1,0:T(8,128)(2,1)S(1)} %collective-permute-done, bf16[16,128]{1,0:T(8,128)(2,1)S(1)} %broadcast_in_dim.20, bf16[512,128]{1,0:T(8,128)(2,1)} %bitcast.9), kind=kLoop, calls=%fused_computation | loop fusion | flops 811008 | bytes 540672 | tf_op jit(solution)/shard_map/concatenate | solution.py:208
  8.3 3.9 %collective-permute-start.3 = (bf16[1056,128]{1,0:T(8,128)(2,1)S(1)}, bf16[1056,128]{1,0:T(8,128)(2,1)S(1)}, u32[]{:S(2)}, u32[]{:S(2)}) collective-permute-start(bf16[1056,128]{1,0:T(8,128)(2,1)S(1)} %pad_maximum_fusion.refs_0_), channel_id=1, source_target_pairs={{0,4},{1,29},{2,6},{3,31},{4,8},{5,1},{6,10},{7,3},{8,12},{9,5},{1... | collective-permute-start | bytes 811016 | tf_op jit(solution)/shard_map/ppermute | solution.py:201
  12.2 2.9 %collective-permute-start.13 = (bf16[528,128]{1,0:T(8,128)(2,1)S(1)}, bf16[528,128]{1,0:T(8,128)(2,1)S(1)}, u32[]{:S(2)}, u32[]{:S(2)}) collective-permute-start(bf16[528,128]{1,0:T(8,128)(2,1)S(1)} %pad_maximum_fusion.2), channel_id=1, source_target_pairs={{0,32},{32,0},{64,96},{96,64},{128,160},{160,128},{192,224},{224,1... | collective-permute-start | bytes 405512 | tf_op jit(solution)/shard_map/ppermute | solution.py:204
  15.1 0.0 collective-permute-done.1
  15.1 0.0 collective-permute-done.2
  15.2 0.4 collective-permute-done.3.refs_2_
  15.6 3.1 %collective-permute-start.4 = (bf16[1056,128]{1,0:T(8,128)(2,1)S(1)}, bf16[1056,128]{1,0:T(8,128)(2,1)S(1)}, u32[]{:S(2)}, u32[]{:S(2)}) collective-permute-start(bf16[1056,128]{1,0:T(8,128)(2,1)S(1)} %constant_dynamic-update-slice_fusion.refs_1_), channel_id=1, source_target_pairs={{0,4},{1,29},{2,6},{3,31},{4,8},{5,1},{6,10},{7,3},{8,12},{9,5},{1... | collective-permute-start | bytes 811016 | tf_op jit(solution)/shard_map/ppermute | solution.py:201
  18.7 0.0 collective-permute-done.13
  18.8 1.3 %collective-permute-start.14 = (bf16[1056,128]{1,0:T(8,128)(2,1)S(1)}, bf16[1056,128]{1,0:T(8,128)(2,1)S(1)}, u32[]{:S(2)}, u32[]{:S(2)}) collective-permute-start(bf16[1056,128]{1,0:T(8,128)(2,1)S(1)} %pad_maximum_fusion.1), channel_id=1, source_target_pairs={{0,64},{32,96},{64,0},{96,32},{128,192},{160,224},{192,128},{224,1... | collective-permute-start | bytes 811016 | tf_op jit(solution)/shard_map/ppermute | solution.py:204
  20.1 4.2 %collective-permute-start.10 = (bf16[1056,128]{1,0:T(8,128)(2,1)S(1)}, bf16[1056,128]{1,0:T(8,128)(2,1)S(1)}, u32[]{:S(2)}, u32[]{:S(2)}) collective-permute-start(bf16[1056,128]{1,0:T(8,128)(2,1)S(1)} %collective-permute-done.3.refs_2_), channel_id=1, source_target_pairs={{0,4},{1,29},{2,6},{3,31},{4,8},{5,1},{6,10},{7,3},{8,12},{9,5},{1... | collective-permute-start | bytes 811016 | tf_op jit(solution)/shard_map/ppermute | solution.py:201
  24.3 0.0 collective-permute-start.8
  24.3 0.0 collective-permute-done.4.refs_3_
  24.3 1.2 %collective-permute-start.5 = (bf16[1056,128]{1,0:T(8,128)(2,1)S(1)}, bf16[1056,128]{1,0:T(8,128)(2,1)S(1)}, u32[]{:S(2)}, u32[]{:S(2)}) collective-permute-start(bf16[1056,128]{1,0:T(8,128)(2,1)S(1)} %collective-permute-done.4.refs_3_), channel_id=1, source_target_pairs={{0,4},{1,29},{2,6},{3,31},{4,8},{5,1},{6,10},{7,3},{8,12},{9,5},{1... | collective-permute-start | bytes 811016 | tf_op jit(solution)/shard_map/ppermute | solution.py:201
  25.6 0.3 collective-permute-done.14
  25.9 2.6 %collective-permute-start.15 = (bf16[2112,128]{1,0:T(8,128)(2,1)S(1)}, bf16[2112,128]{1,0:T(8,128)(2,1)S(1)}, u32[]{:S(2)}, u32[]{:S(2)}) collective-permute-start(bf16[2112,128]{1,0:T(8,128)(2,1)S(1)} %constant_dynamic-update-slice_fusion.2.refs_10_), channel_id=1, source_target_pairs={{0,192},{32,224},{64,128},{96,160},{128,64},{160,96},{192,0},{224,... | collective-permute-start | bytes 1622024 | tf_op jit(solution)/shard_map/ppermute | solution.py:204
  28.5 0.0 collective-permute-start.9
  28.5 0.0 collective-permute-done.10.refs_6_
  28.5 6.3 %collective-permute-start.16 = (bf16[1056,128]{1,0:T(8,128)(2,1)S(1)}, bf16[1056,128]{1,0:T(8,128)(2,1)S(1)}, u32[]{:S(2)}, u32[]{:S(2)}) collective-permute-start(bf16[1056,128]{1,0:T(8,128)(2,1)S(1)} %collective-permute-done.10.refs_6_), channel_id=1, source_target_pairs={{0,4},{1,29},{2,6},{3,31},{4,8},{5,1},{6,10},{7,3},{8,12},{9,5},{1... | collective-permute-start | bytes 811016 | tf_op jit(solution)/shard_map/ppermute | solution.py:201
  34.8 0.0 collective-permute-done.8.refs_4_
  34.8 0.0 collective-permute-start.11
  34.8 0.0 collective-permute-done.5.refs_7_
  34.8 0.8 %collective-permute-start.6 = (bf16[1056,128]{1,0:T(8,128)(2,1)S(1)}, bf16[1056,128]{1,0:T(8,128)(2,1)S(1)}, u32[]{:S(2)}, u32[]{:S(2)}) collective-permute-start(bf16[1056,128]{1,0:T(8,128)(2,1)S(1)} %collective-permute-done.5.refs_7_), channel_id=1, source_target_pairs={{0,4},{1,29},{2,6},{3,31},{4,8},{5,1},{6,10},{7,3},{8,12},{9,5},{1... | collective-permute-start | bytes 811016 | tf_op jit(solution)/shard_map/ppermute | solution.py:201
  35.6 0.0 collective-permute-done.9.refs_5_
  35.6 0.0 collective-permute-start.12
  36.2 0.7 fusion.1
  36.9 1.3 %collective-permute-done.16.refs_0_ = bf16[1056,128]{1,0:T(8,128)(2,1)S(1)} collective-permute-done((bf16[1056,128]{1,0:T(8,128)(2,1)S(1)}, bf16[1056,128]{1,0:T(8,128)(2,1)S(1)}, u32[]{:S(2)}, u32[]{:S(2)}) %collective-permute-start.16) | collective-permute-done | bytes 270368 | tf_op jit(solution)/shard_map/ppermute | solution.py:201
  38.2 3.4 %collective-permute-start.19 = (bf16[1056,128]{1,0:T(8,128)(2,1)S(1)}, bf16[1056,128]{1,0:T(8,128)(2,1)S(1)}, u32[]{:S(2)}, u32[]{:S(2)}) collective-permute-start(bf16[1056,128]{1,0:T(8,128)(2,1)S(1)} %collective-permute-done.16.refs_0_), channel_id=1, source_target_pairs={{0,4},{1,29},{2,6},{3,31},{4,8},{5,1},{6,10},{7,3},{8,12},{9,5},{1... | collective-permute-start | bytes 811016 | tf_op jit(solution)/shard_map/ppermute | solution.py:201
  41.6 0.0 collective-permute-done.11.refs_8_
  41.6 0.0 collective-permute-start.17
  41.6 0.0 collective-permute-done.6.refs_1_
  41.6 1.4 %collective-permute-start.18 = (bf16[1056,128]{1,0:T(8,128)(2,1)S(1)}, bf16[1056,128]{1,0:T(8,128)(2,1)S(1)}, u32[]{:S(2)}, u32[]{:S(2)}) collective-permute-start(bf16[1056,128]{1,0:T(8,128)(2,1)S(1)} %collective-permute-done.6.refs_1_), channel_id=1, source_target_pairs={{0,1},{1,0},{2,3},{3,2},{4,5},{5,4},{6,7},{7,6},{8,9},{9,8},{10,11... | collective-permute-start | bytes 811016 | tf_op jit(solution)/shard_map/ppermute | solution.py:201
  43.0 0.0 collective-permute-done.15.refs_11_
  43.0 1.5 %collective-permute-start.7 = (bf16[1056,128]{1,0:T(8,128)(2,1)S(1)}, bf16[1056,128]{1,0:T(8,128)(2,1)S(1)}, u32[]{:S(2)}, u32[]{:S(2)}) collective-permute-start(bf16[1056,128]{1,0:T(8,128)(2,1)S(1)} %collective-permute-done.6.refs_1_), channel_id=1, source_target_pairs={{0,4},{1,29},{2,6},{3,31},{4,8},{5,1},{6,10},{7,3},{8,12},{9,5},{1... | collective-permute-start | bytes 811016 | tf_op jit(solution)/shard_map/ppermute | solution.py:201
  44.5 0.0 collective-permute-done.12.refs_9_
  44.5 4.6 %shard_map.55 = (bf16[8,256,1152]{2,1,0:T(8,128)(2,1)S(1)}, f32[256,1024]{1,0:T(8,128)S(1)}) custom-call(bf16[1056,128]{1,0:T(8,128)(2,1)S(1)} %pad_maximum_fusion.refs_0_, bf16[1056,128]{1,0:T(8,128)(2,1)S(1)} %constant_dynamic-update-slice_fusion.refs_1_, bf16[1056,128]{1,0:T(8,128)(2,1)S(1)} %collective-permute-done.3.refs_2_, ...), custom_call_target="tpu_custom_call" | custom-call | flops 3221225472 | bytes 25165824 | tf_op jit(solution)/shard_map/pallas_call | solution.py:233
  49.1 0.0 collective-permute-done.19.pair
  49.1 0.6 shard_map.56.refs_5_
  49.7 0.0 collective-permute-done.17.refs_2_
  49.7 0.0 collective-permute-done.18.refs_3_
  49.7 1.8 %shard_map.57.before = f32[256,1024]{1,0:T(8,128)S(1)} custom-call(bf16[1056,128]{1,0:T(8,128)(2,1)S(1)} %collective-permute-done.16.refs_0_, bf16[1056,128]{1,0:T(8,128)(2,1)S(1)} %collective-permute-done.6.refs_1_, bf16[1056,128]{1,0:T(8,128)(2,1)S(1)} %collective-permute-done.17.refs_2_, bf16[1056,128]{1,0:T(8,128)(2,1)S(1)} %collective-permute-done.18.refs_3_, ...), custom_call_target="tpu_custom_call" | custom-call | flops 1073741824 | bytes 8388608 | tf_op jit(solution)/shard_map/pallas_call | solution.py:251
  51.5 0.0 collective-permute-done.7.beside
  51.5 0.1 broadcast_in_dim.21.codes
  51.6 1.5 %shard_map.58 = (f32[8,128,128]{2,1,0:T(8,128)S(1)}, f32[32,8,128]{2,1,0:T(8,128)S(1)}) custom-call(bf16[16,128]{1,0:T(8,128)(2,1)S(1)} %broadcast_in_dim.21.codes, bf16[1056,128]{1,0:T(8,128)(2,1)S(1)} %collective-permute-done.7.beside, bf16[8,256,1152]{2,1,0:T(8,128)(2,1)S(1)} %get-tuple-element.19.dense_left.refs_4_, f32[256,1024]{1,0:T(8,128)S(1)} %shard_map.57.before), custom_call_target="tpu_custom_call" | custom-call | flops 536870912 | bytes 4194304 | tf_op jit(solution)/shard_map/pallas_call | solution.py:260
  53.1 14.8 %all_to_all.5.sums = f32[32,8,128]{2,1,0:T(8,128)S(1)} all-to-all(f32[32,8,128]{2,1,0:T(8,128)S(1)} %get-tuple-element.22), channel_id=1, replica_groups=mesh['group'=8,'loop'=32] {'loop'}, dimensions={0} | all-to-all | bytes 262144 | tf_op jit(solution)/shard_map/all_to_all | solution.py:274
  67.9 1.9 %shard_map.59 = f32[8,128,128]{2,1,0:T(8,128)} custom-call(bf16[16,128]{1,0:T(8,128)(2,1)S(1)} %broadcast_in_dim.21.codes, f32[8,128,128]{2,1,0:T(8,128)S(1)} %get-tuple-element.21.squares, f32[32,8,128]{2,1,0:T(8,128)S(1)} %all_to_all.5.sums), custom_call_target="tpu_custom_call" | custom-call | tf_op jit(solution)/shard_map/pallas_call | solution.py:275
  (6 shorter events, 0.1 us)
Async XLA Ops:
  2.3 5.1 %collective-permute-start = (bf16[528,128]{1,0:T(8,128)(2,1)S(1)}, bf16[528,128]{1,0:T(8,128)(2,1)S(1)}, u32[]{:S(2)}, u32[]{:S(2)}) collective-permute-start(bf16[528,128]{1,0:T(8,128)(2,1)S(1)} %pad_maximum_fusion.2), channel_id=1, source_target_pairs={{0,1},{1,0},{2,3},{3,2},{4,5},{5,4},{6,7},{7,6},{8,9},{9,8},{10,11... | collective-permute-start | bytes 405512 | tf_op jit(solution)/shard_map/ppermute | solution.py:201
  5.6 9.5 %collective-permute-start.1 = (bf16[528,128]{1,0:T(8,128)(2,1)S(1)}, bf16[528,128]{1,0:T(8,128)(2,1)S(1)}, u32[]{:S(2)}, u32[]{:S(2)}) collective-permute-start(bf16[528,128]{1,0:T(8,128)(2,1)S(1)} %pad_maximum_fusion.2), channel_id=1, source_target_pairs={{0,2},{1,3},{2,0},{3,1},{4,6},{5,7},{6,4},{7,5},{8,10},{9,11},{10,... | collective-permute-start | bytes 405512 | tf_op jit(solution)/shard_map/ppermute | solution.py:201
  5.6 9.5 %collective-permute-start.2 = (bf16[528,128]{1,0:T(8,128)(2,1)S(1)}, bf16[528,128]{1,0:T(8,128)(2,1)S(1)}, u32[]{:S(2)}, u32[]{:S(2)}) collective-permute-start(bf16[528,128]{1,0:T(8,128)(2,1)S(1)} %pad_maximum_fusion.2), channel_id=1, source_target_pairs={{0,3},{1,2},{2,1},{3,0},{4,7},{5,6},{6,5},{7,4},{8,11},{9,10},{10,... | collective-permute-start | bytes 405512 | tf_op jit(solution)/shard_map/ppermute | solution.py:201
  8.3 7.3 %collective-permute-start.3 = (bf16[1056,128]{1,0:T(8,128)(2,1)S(1)}, bf16[1056,128]{1,0:T(8,128)(2,1)S(1)}, u32[]{:S(2)}, u32[]{:S(2)}) collective-permute-start(bf16[1056,128]{1,0:T(8,128)(2,1)S(1)} %pad_maximum_fusion.refs_0_), channel_id=1, source_target_pairs={{0,4},{1,29},{2,6},{3,31},{4,8},{5,1},{6,10},{7,3},{8,12},{9,5},{1... | collective-permute-start | bytes 811016 | tf_op jit(solution)/shard_map/ppermute | solution.py:201
  12.2 6.5 %collective-permute-start.13 = (bf16[528,128]{1,0:T(8,128)(2,1)S(1)}, bf16[528,128]{1,0:T(8,128)(2,1)S(1)}, u32[]{:S(2)}, u32[]{:S(2)}) collective-permute-start(bf16[528,128]{1,0:T(8,128)(2,1)S(1)} %pad_maximum_fusion.2), channel_id=1, source_target_pairs={{0,32},{32,0},{64,96},{96,64},{128,160},{160,128},{192,224},{224,1... | collective-permute-start | bytes 405512 | tf_op jit(solution)/shard_map/ppermute | solution.py:204
  15.6 8.7 %collective-permute-start.4 = (bf16[1056,128]{1,0:T(8,128)(2,1)S(1)}, bf16[1056,128]{1,0:T(8,128)(2,1)S(1)}, u32[]{:S(2)}, u32[]{:S(2)}) collective-permute-start(bf16[1056,128]{1,0:T(8,128)(2,1)S(1)} %constant_dynamic-update-slice_fusion.refs_1_), channel_id=1, source_target_pairs={{0,4},{1,29},{2,6},{3,31},{4,8},{5,1},{6,10},{7,3},{8,12},{9,5},{1... | collective-permute-start | bytes 811016 | tf_op jit(solution)/shard_map/ppermute | solution.py:201
  18.8 7.1 %collective-permute-start.14 = (bf16[1056,128]{1,0:T(8,128)(2,1)S(1)}, bf16[1056,128]{1,0:T(8,128)(2,1)S(1)}, u32[]{:S(2)}, u32[]{:S(2)}) collective-permute-start(bf16[1056,128]{1,0:T(8,128)(2,1)S(1)} %pad_maximum_fusion.1), channel_id=1, source_target_pairs={{0,64},{32,96},{64,0},{96,32},{128,192},{160,224},{192,128},{224,1... | collective-permute-start | bytes 811016 | tf_op jit(solution)/shard_map/ppermute | solution.py:204
  20.1 8.4 %collective-permute-start.10 = (bf16[1056,128]{1,0:T(8,128)(2,1)S(1)}, bf16[1056,128]{1,0:T(8,128)(2,1)S(1)}, u32[]{:S(2)}, u32[]{:S(2)}) collective-permute-start(bf16[1056,128]{1,0:T(8,128)(2,1)S(1)} %collective-permute-done.3.refs_2_), channel_id=1, source_target_pairs={{0,4},{1,29},{2,6},{3,31},{4,8},{5,1},{6,10},{7,3},{8,12},{9,5},{1... | collective-permute-start | bytes 811016 | tf_op jit(solution)/shard_map/ppermute | solution.py:201
  24.3 10.5 %collective-permute-start.8 = (bf16[1056,128]{1,0:T(8,128)(2,1)S(1)}, bf16[1056,128]{1,0:T(8,128)(2,1)S(1)}, u32[]{:S(2)}, u32[]{:S(2)}) collective-permute-start(bf16[1056,128]{1,0:T(8,128)(2,1)S(1)} %collective-permute-done.3.refs_2_), channel_id=1, source_target_pairs={{0,1},{1,0},{2,3},{3,2},{4,5},{5,4},{6,7},{7,6},{8,9},{9,8},{10,11... | collective-permute-start | bytes 811016 | tf_op jit(solution)/shard_map/ppermute | solution.py:201
  24.3 10.5 %collective-permute-start.5 = (bf16[1056,128]{1,0:T(8,128)(2,1)S(1)}, bf16[1056,128]{1,0:T(8,128)(2,1)S(1)}, u32[]{:S(2)}, u32[]{:S(2)}) collective-permute-start(bf16[1056,128]{1,0:T(8,128)(2,1)S(1)} %collective-permute-done.4.refs_3_), channel_id=1, source_target_pairs={{0,4},{1,29},{2,6},{3,31},{4,8},{5,1},{6,10},{7,3},{8,12},{9,5},{1... | collective-permute-start | bytes 811016 | tf_op jit(solution)/shard_map/ppermute | solution.py:201
  25.9 17.0 %collective-permute-start.15 = (bf16[2112,128]{1,0:T(8,128)(2,1)S(1)}, bf16[2112,128]{1,0:T(8,128)(2,1)S(1)}, u32[]{:S(2)}, u32[]{:S(2)}) collective-permute-start(bf16[2112,128]{1,0:T(8,128)(2,1)S(1)} %constant_dynamic-update-slice_fusion.2.refs_10_), channel_id=1, source_target_pairs={{0,192},{32,224},{64,128},{96,160},{128,64},{160,96},{192,0},{224,... | collective-permute-start | bytes 1622024 | tf_op jit(solution)/shard_map/ppermute | solution.py:204
  28.5 7.1 %collective-permute-start.9 = (bf16[1056,128]{1,0:T(8,128)(2,1)S(1)}, bf16[1056,128]{1,0:T(8,128)(2,1)S(1)}, u32[]{:S(2)}, u32[]{:S(2)}) collective-permute-start(bf16[1056,128]{1,0:T(8,128)(2,1)S(1)} %collective-permute-done.4.refs_3_), channel_id=1, source_target_pairs={{0,1},{1,0},{2,3},{3,2},{4,5},{5,4},{6,7},{7,6},{8,9},{9,8},{10,11... | collective-permute-start | bytes 811016 | tf_op jit(solution)/shard_map/ppermute | solution.py:201
  28.5 9.7 %collective-permute-start.16 = (bf16[1056,128]{1,0:T(8,128)(2,1)S(1)}, bf16[1056,128]{1,0:T(8,128)(2,1)S(1)}, u32[]{:S(2)}, u32[]{:S(2)}) collective-permute-start(bf16[1056,128]{1,0:T(8,128)(2,1)S(1)} %collective-permute-done.10.refs_6_), channel_id=1, source_target_pairs={{0,4},{1,29},{2,6},{3,31},{4,8},{5,1},{6,10},{7,3},{8,12},{9,5},{1... | collective-permute-start | bytes 811016 | tf_op jit(solution)/shard_map/ppermute | solution.py:201
  34.8 6.8 %collective-permute-start.11 = (bf16[1056,128]{1,0:T(8,128)(2,1)S(1)}, bf16[1056,128]{1,0:T(8,128)(2,1)S(1)}, u32[]{:S(2)}, u32[]{:S(2)}) collective-permute-start(bf16[1056,128]{1,0:T(8,128)(2,1)S(1)} %collective-permute-done.10.refs_6_), channel_id=1, source_target_pairs={{0,1},{1,0},{2,3},{3,2},{4,5},{5,4},{6,7},{7,6},{8,9},{9,8},{10,11... | collective-permute-start | bytes 811016 | tf_op jit(solution)/shard_map/ppermute | solution.py:201
  34.8 6.8 %collective-permute-start.6 = (bf16[1056,128]{1,0:T(8,128)(2,1)S(1)}, bf16[1056,128]{1,0:T(8,128)(2,1)S(1)}, u32[]{:S(2)}, u32[]{:S(2)}) collective-permute-start(bf16[1056,128]{1,0:T(8,128)(2,1)S(1)} %collective-permute-done.5.refs_7_), channel_id=1, source_target_pairs={{0,4},{1,29},{2,6},{3,31},{4,8},{5,1},{6,10},{7,3},{8,12},{9,5},{1... | collective-permute-start | bytes 811016 | tf_op jit(solution)/shard_map/ppermute | solution.py:201
  35.6 8.9 %collective-permute-start.12 = (bf16[1056,128]{1,0:T(8,128)(2,1)S(1)}, bf16[1056,128]{1,0:T(8,128)(2,1)S(1)}, u32[]{:S(2)}, u32[]{:S(2)}) collective-permute-start(bf16[1056,128]{1,0:T(8,128)(2,1)S(1)} %collective-permute-done.5.refs_7_), channel_id=1, source_target_pairs={{0,1},{1,0},{2,3},{3,2},{4,5},{5,4},{6,7},{7,6},{8,9},{9,8},{10,11... | collective-permute-start | bytes 811016 | tf_op jit(solution)/shard_map/ppermute | solution.py:201
  38.2 10.9 %collective-permute-start.19 = (bf16[1056,128]{1,0:T(8,128)(2,1)S(1)}, bf16[1056,128]{1,0:T(8,128)(2,1)S(1)}, u32[]{:S(2)}, u32[]{:S(2)}) collective-permute-start(bf16[1056,128]{1,0:T(8,128)(2,1)S(1)} %collective-permute-done.16.refs_0_), channel_id=1, source_target_pairs={{0,4},{1,29},{2,6},{3,31},{4,8},{5,1},{6,10},{7,3},{8,12},{9,5},{1... | collective-permute-start | bytes 811016 | tf_op jit(solution)/shard_map/ppermute | solution.py:201
  41.6 8.1 %collective-permute-start.17 = (bf16[1056,128]{1,0:T(8,128)(2,1)S(1)}, bf16[1056,128]{1,0:T(8,128)(2,1)S(1)}, u32[]{:S(2)}, u32[]{:S(2)}) collective-permute-start(bf16[1056,128]{1,0:T(8,128)(2,1)S(1)} %collective-permute-done.16.refs_0_), channel_id=1, source_target_pairs={{0,1},{1,0},{2,3},{3,2},{4,5},{5,4},{6,7},{7,6},{8,9},{9,8},{10,11... | collective-permute-start | bytes 811016 | tf_op jit(solution)/shard_map/ppermute | solution.py:201
  41.6 8.1 %collective-permute-start.18 = (bf16[1056,128]{1,0:T(8,128)(2,1)S(1)}, bf16[1056,128]{1,0:T(8,128)(2,1)S(1)}, u32[]{:S(2)}, u32[]{:S(2)}) collective-permute-start(bf16[1056,128]{1,0:T(8,128)(2,1)S(1)} %collective-permute-done.6.refs_1_), channel_id=1, source_target_pairs={{0,1},{1,0},{2,3},{3,2},{4,5},{5,4},{6,7},{7,6},{8,9},{9,8},{10,11... | collective-permute-start | bytes 811016 | tf_op jit(solution)/shard_map/ppermute | solution.py:201
  43.0 8.5 %collective-permute-start.7 = (bf16[1056,128]{1,0:T(8,128)(2,1)S(1)}, bf16[1056,128]{1,0:T(8,128)(2,1)S(1)}, u32[]{:S(2)}, u32[]{:S(2)}) collective-permute-start(bf16[1056,128]{1,0:T(8,128)(2,1)S(1)} %collective-permute-done.6.refs_1_), channel_id=1, source_target_pairs={{0,4},{1,29},{2,6},{3,31},{4,8},{5,1},{6,10},{7,3},{8,12},{9,5},{1... | collective-permute-start | bytes 811016 | tf_op jit(solution)/shard_map/ppermute | solution.py:201

commit v10 on v9

--- a/solution.py
+++ b/solution.py
@@ -197,6 +197,8 @@
         [tile_values.reshape(BODY, TILE), jnp.broadcast_to(code[:, None], (16, TILE))]
     )
 
+    unit = lax.optimization_barrier(unit)
+
     def along(perm, v):
         return lax.ppermute(v, "loop", perm)
 

time: 70.2 us -> 70.2 us (level)
  other arithmetic: 3.19 us -> 2.4 us
    concatenate x1, other arithmetic: 0.92 us -> 0.02 us  [shards(): first = jnp.concatenate([unit, pair])]
  transfers between devices with their start and end apart: 20 -> 20, of which waited for: 3 -> 3; matrix products, arithmetic and copies ran while one was open for 2% -> 1% of each run, Pallas kernels for 10% -> 10%
where the time goes in v10:
time: 70.2 us; the launch traced here: 70.1 us
  starting transfers between devices  38.3 us (55%)
  blocking collectives  14.8 us (21%)
  Pallas kernels  10.4 us (15%)
  waiting for transfers between devices  2.41 us (3%)
  other arithmetic  2.4 us (3%)
  between operations  1.6 us (2%)
    ppermute x17, starting transfers between devices, along(): return lax.ppermute(v, 'loop', perm)  31.2 us
    all_to_all x1, blocking collectives, shards(): sums = lax.all_to_all(sums, 'loop', 0, 0, tiled=True)  14.8 us
    ppermute x3, starting transfers between devices, across(): return lax.ppermute(v, 'group', perm)  7.09 us
    pallas_call x1, Pallas kernels, shards(): pl.pallas_call(begin, in_specs=[WHOLE] * 12, out_specs=[WHOLE] * 2, out_s...  4.58 us
    pallas_call x1, Pallas kernels, shards(): pl.pallas_call(rescale, in_specs=[AWAY] * 3, out_specs=AWAY, out_shape=ja...  1.94 us
    pallas_call x1, Pallas kernels, shards(): pl.pallas_call(proceed, in_specs=[WHOLE] * 6, out_specs=WHOLE, out_shape=...  1.76 us
    ppermute x17, waiting for transfers between devices, along(): return lax.ppermute(v, 'loop', perm)  1.74 us
    pallas_call x1, Pallas kernels, shards(): pl.pallas_call(finish, in_specs=[WHOLE] * 4, out_specs=[AWAY, WHOLE], out...  1.55 us
  transfers between devices with their start and end apart: 20, of which 3 were waited for; matrix products, arithmetic and copies ran while one was open for 1% of the time, Pallas kernels for 10%

profile of v10, /device:TPU:1, one launch (start us, length us, event | category | flops | bytes accessed | tf_op | source)
XLA Modules:
  0.0 70.1 jit_solution(3919238161524030298)
XLA Ops:
  0.7 0.7 fusion
  1.3 1.0 %pad_maximum_fusion.2 = bf16[528,128]{1,0:T(8,128)(2,1)S(1)} fusion(bf16[512,128]{1,0:T(8,128)(2,1)} %bitcast.8, bf16[528]{0:T(1024)(128)(2,1)S(1)} %pad.15.clone), kind=kLoop, calls=%fused_computation.2 | loop fusion | flops 270336 | bytes 267296 | tf_op jit(solution)/shard_map/concatenate | solution.py:196
  2.4 3.3 %collective-permute-start = (bf16[528,128]{1,0:T(8,128)(2,1)S(1)}, bf16[528,128]{1,0:T(8,128)(2,1)S(1)}, u32[]{:S(2)}, u32[]{:S(2)}) collective-permute-start(bf16[528,128]{1,0:T(8,128)(2,1)S(1)} %pad_maximum_fusion.2), channel_id=1, source_target_pairs={{0,1},{1,0},{2,3},{3,2},{4,5},{5,4},{6,7},{7,6},{8,9},{9,8},{10,11... | collective-permute-start | bytes 405512 | tf_op jit(solution)/shard_map/ppermute | solution.py:203
  5.7 0.0 collective-permute-start.1
  5.7 1.7 %collective-permute-start.2 = (bf16[528,128]{1,0:T(8,128)(2,1)S(1)}, bf16[528,128]{1,0:T(8,128)(2,1)S(1)}, u32[]{:S(2)}, u32[]{:S(2)}) collective-permute-start(bf16[528,128]{1,0:T(8,128)(2,1)S(1)} %pad_maximum_fusion.2), channel_id=1, source_target_pairs={{0,3},{1,2},{2,1},{3,0},{4,7},{5,6},{6,5},{7,4},{8,11},{9,10},{10,... | collective-permute-start | bytes 405512 | tf_op jit(solution)/shard_map/ppermute | solution.py:203
  7.4 0.0 collective-permute-done
  7.5 3.9 %collective-permute-start.3 = (bf16[1056,128]{1,0:T(8,128)(2,1)S(1)}, bf16[1056,128]{1,0:T(8,128)(2,1)S(1)}, u32[]{:S(2)}, u32[]{:S(2)}) collective-permute-start(bf16[1056,128]{1,0:T(8,128)(2,1)S(1)} %pad_maximum_fusion.refs_0_), channel_id=1, source_target_pairs={{0,4},{1,29},{2,6},{3,31},{4,8},{5,1},{6,10},{7,3},{8,12},{9,5},{1... | collective-permute-start | bytes 811016 | tf_op jit(solution)/shard_map/ppermute | solution.py:203
  11.4 2.9 %collective-permute-start.13 = (bf16[528,128]{1,0:T(8,128)(2,1)S(1)}, bf16[528,128]{1,0:T(8,128)(2,1)S(1)}, u32[]{:S(2)}, u32[]{:S(2)}) collective-permute-start(bf16[528,128]{1,0:T(8,128)(2,1)S(1)} %pad_maximum_fusion.2), channel_id=1, source_target_pairs={{0,32},{32,0},{64,96},{96,64},{128,160},{160,128},{192,224},{224,1... | collective-permute-start | bytes 405512 | tf_op jit(solution)/shard_map/ppermute | solution.py:206
  14.3 0.0 collective-permute-done.1
  14.3 0.0 collective-permute-done.2
  14.3 0.4 collective-permute-done.3.refs_2_
  14.8 3.6 %collective-permute-start.4 = (bf16[1056,128]{1,0:T(8,128)(2,1)S(1)}, bf16[1056,128]{1,0:T(8,128)(2,1)S(1)}, u32[]{:S(2)}, u32[]{:S(2)}) collective-permute-start(bf16[1056,128]{1,0:T(8,128)(2,1)S(1)} %constant_dynamic-update-slice_fusion.refs_1_), channel_id=1, source_target_pairs={{0,4},{1,29},{2,6},{3,31},{4,8},{5,1},{6,10},{7,3},{8,12},{9,5},{1... | collective-permute-start | bytes 811016 | tf_op jit(solution)/shard_map/ppermute | solution.py:203
  18.4 0.0 collective-permute-done.13
  18.4 1.3 %collective-permute-start.14 = (bf16[1056,128]{1,0:T(8,128)(2,1)S(1)}, bf16[1056,128]{1,0:T(8,128)(2,1)S(1)}, u32[]{:S(2)}, u32[]{:S(2)}) collective-permute-start(bf16[1056,128]{1,0:T(8,128)(2,1)S(1)} %pad_maximum_fusion.1), channel_id=1, source_target_pairs={{0,64},{32,96},{64,0},{96,32},{128,192},{160,224},{192,128},{224,1... | collective-permute-start | bytes 811016 | tf_op jit(solution)/shard_map/ppermute | solution.py:206
  19.7 4.6 %collective-permute-start.10 = (bf16[1056,128]{1,0:T(8,128)(2,1)S(1)}, bf16[1056,128]{1,0:T(8,128)(2,1)S(1)}, u32[]{:S(2)}, u32[]{:S(2)}) collective-permute-start(bf16[1056,128]{1,0:T(8,128)(2,1)S(1)} %collective-permute-done.3.refs_2_), channel_id=1, source_target_pairs={{0,4},{1,29},{2,6},{3,31},{4,8},{5,1},{6,10},{7,3},{8,12},{9,5},{1... | collective-permute-start | bytes 811016 | tf_op jit(solution)/shard_map/ppermute | solution.py:203
  24.4 0.0 collective-permute-start.8
  24.4 0.0 collective-permute-done.4.refs_3_
  24.4 1.2 %collective-permute-start.5 = (bf16[1056,128]{1,0:T(8,128)(2,1)S(1)}, bf16[1056,128]{1,0:T(8,128)(2,1)S(1)}, u32[]{:S(2)}, u32[]{:S(2)}) collective-permute-start(bf16[1056,128]{1,0:T(8,128)(2,1)S(1)} %collective-permute-done.4.refs_3_), channel_id=1, source_target_pairs={{0,4},{1,29},{2,6},{3,31},{4,8},{5,1},{6,10},{7,3},{8,12},{9,5},{1... | collective-permute-start | bytes 811016 | tf_op jit(solution)/shard_map/ppermute | solution.py:203
  25.6 0.7 collective-permute-done.14
  26.3 2.9 %collective-permute-start.15 = (bf16[2112,128]{1,0:T(8,128)(2,1)S(1)}, bf16[2112,128]{1,0:T(8,128)(2,1)S(1)}, u32[]{:S(2)}, u32[]{:S(2)}) collective-permute-start(bf16[2112,128]{1,0:T(8,128)(2,1)S(1)} %constant_dynamic-update-slice_fusion.2.refs_10_), channel_id=1, source_target_pairs={{0,192},{32,224},{64,128},{96,160},{128,64},{160,96},{192,0},{224,... | collective-permute-start | bytes 1622024 | tf_op jit(solution)/shard_map/ppermute | solution.py:206
  29.2 0.3 collective-permute-start.9
  29.5 0.0 collective-permute-done.10.refs_6_
  29.5 5.3 %collective-permute-start.16 = (bf16[1056,128]{1,0:T(8,128)(2,1)S(1)}, bf16[1056,128]{1,0:T(8,128)(2,1)S(1)}, u32[]{:S(2)}, u32[]{:S(2)}) collective-permute-start(bf16[1056,128]{1,0:T(8,128)(2,1)S(1)} %collective-permute-done.10.refs_6_), channel_id=1, source_target_pairs={{0,4},{1,29},{2,6},{3,31},{4,8},{5,1},{6,10},{7,3},{8,12},{9,5},{1... | collective-permute-start | bytes 811016 | tf_op jit(solution)/shard_map/ppermute | solution.py:203
  34.8 0.0 collective-permute-done.8.refs_4_
  34.8 0.0 collective-permute-start.11
  34.8 0.0 collective-permute-done.5.refs_7_
  34.8 0.8 %collective-permute-start.6 = (bf16[1056,128]{1,0:T(8,128)(2,1)S(1)}, bf16[1056,128]{1,0:T(8,128)(2,1)S(1)}, u32[]{:S(2)}, u32[]{:S(2)}) collective-permute-start(bf16[1056,128]{1,0:T(8,128)(2,1)S(1)} %collective-permute-done.5.refs_7_), channel_id=1, source_target_pairs={{0,4},{1,29},{2,6},{3,31},{4,8},{5,1},{6,10},{7,3},{8,12},{9,5},{1... | collective-permute-start | bytes 811016 | tf_op jit(solution)/shard_map/ppermute | solution.py:203
  35.6 0.0 collective-permute-done.9.refs_5_
  35.6 0.0 collective-permute-start.12
  36.3 0.7 fusion.1
  37.0 1.3 %collective-permute-done.16.refs_0_ = bf16[1056,128]{1,0:T(8,128)(2,1)S(1)} collective-permute-done((bf16[1056,128]{1,0:T(8,128)(2,1)S(1)}, bf16[1056,128]{1,0:T(8,128)(2,1)S(1)}, u32[]{:S(2)}, u32[]{:S(2)}) %collective-permute-start.16) | collective-permute-done | bytes 270368 | tf_op jit(solution)/shard_map/ppermute | solution.py:203
  38.2 3.4 %collective-permute-start.19 = (bf16[1056,128]{1,0:T(8,128)(2,1)S(1)}, bf16[1056,128]{1,0:T(8,128)(2,1)S(1)}, u32[]{:S(2)}, u32[]{:S(2)}) collective-permute-start(bf16[1056,128]{1,0:T(8,128)(2,1)S(1)} %collective-permute-done.16.refs_0_), channel_id=1, source_target_pairs={{0,4},{1,29},{2,6},{3,31},{4,8},{5,1},{6,10},{7,3},{8,12},{9,5},{1... | collective-permute-start | bytes 811016 | tf_op jit(solution)/shard_map/ppermute | solution.py:203
  41.6 0.0 collective-permute-done.11.refs_8_
  41.6 0.0 collective-permute-start.17
  41.6 0.0 collective-permute-done.6.refs_1_
  41.7 1.4 %collective-permute-start.18 = (bf16[1056,128]{1,0:T(8,128)(2,1)S(1)}, bf16[1056,128]{1,0:T(8,128)(2,1)S(1)}, u32[]{:S(2)}, u32[]{:S(2)}) collective-permute-start(bf16[1056,128]{1,0:T(8,128)(2,1)S(1)} %collective-permute-done.6.refs_1_), channel_id=1, source_target_pairs={{0,1},{1,0},{2,3},{3,2},{4,5},{5,4},{6,7},{7,6},{8,9},{9,8},{10,11... | collective-permute-start | bytes 811016 | tf_op jit(solution)/shard_map/ppermute | solution.py:203
  43.0 0.0 collective-permute-done.15.refs_11_
  43.0 1.5 %collective-permute-start.7 = (bf16[1056,128]{1,0:T(8,128)(2,1)S(1)}, bf16[1056,128]{1,0:T(8,128)(2,1)S(1)}, u32[]{:S(2)}, u32[]{:S(2)}) collective-permute-start(bf16[1056,128]{1,0:T(8,128)(2,1)S(1)} %collective-permute-done.6.refs_1_), channel_id=1, source_target_pairs={{0,4},{1,29},{2,6},{3,31},{4,8},{5,1},{6,10},{7,3},{8,12},{9,5},{1... | collective-permute-start | bytes 811016 | tf_op jit(solution)/shard_map/ppermute | solution.py:203
  44.5 0.0 collective-permute-done.12.refs_9_
  44.5 4.6 %shard_map.55 = (bf16[8,256,1152]{2,1,0:T(8,128)(2,1)S(1)}, f32[256,1024]{1,0:T(8,128)S(1)}) custom-call(bf16[1056,128]{1,0:T(8,128)(2,1)S(1)} %pad_maximum_fusion.refs_0_, bf16[1056,128]{1,0:T(8,128)(2,1)S(1)} %constant_dynamic-update-slice_fusion.refs_1_, bf16[1056,128]{1,0:T(8,128)(2,1)S(1)} %collective-permute-done.3.refs_2_, ...), custom_call_target="tpu_custom_call" | custom-call | flops 3221225472 | bytes 25165824 | tf_op jit(solution)/shard_map/pallas_call | solution.py:235
  49.1 0.0 collective-permute-done.19.pair
  49.1 0.6 shard_map.56.refs_5_
  49.8 0.0 collective-permute-done.17.refs_2_
  49.8 0.0 collective-permute-done.18.refs_3_
  49.8 1.8 %shard_map.57.before = f32[256,1024]{1,0:T(8,128)S(1)} custom-call(bf16[1056,128]{1,0:T(8,128)(2,1)S(1)} %collective-permute-done.16.refs_0_, bf16[1056,128]{1,0:T(8,128)(2,1)S(1)} %collective-permute-done.6.refs_1_, bf16[1056,128]{1,0:T(8,128)(2,1)S(1)} %collective-permute-done.17.refs_2_, bf16[1056,128]{1,0:T(8,128)(2,1)S(1)} %collective-permute-done.18.refs_3_, ...), custom_call_target="tpu_custom_call" | custom-call | flops 1073741824 | bytes 8388608 | tf_op jit(solution)/shard_map/pallas_call | solution.py:253
  51.6 0.0 collective-permute-done.7.beside
  51.6 0.1 broadcast_in_dim.21.codes
  51.6 1.5 %shard_map.58 = (f32[8,128,128]{2,1,0:T(8,128)S(1)}, f32[32,8,128]{2,1,0:T(8,128)S(1)}) custom-call(bf16[16,128]{1,0:T(8,128)(2,1)S(1)} %broadcast_in_dim.21.codes, bf16[1056,128]{1,0:T(8,128)(2,1)S(1)} %collective-permute-done.7.beside, bf16[8,256,1152]{2,1,0:T(8,128)(2,1)S(1)} %get-tuple-element.19.dense_left.refs_4_, f32[256,1024]{1,0:T(8,128)S(1)} %shard_map.57.before), custom_call_target="tpu_custom_call" | custom-call | flops 536870912 | bytes 4194304 | tf_op jit(solution)/shard_map/pallas_call | solution.py:262
  53.2 14.8 %all_to_all.5.sums = f32[32,8,128]{2,1,0:T(8,128)S(1)} all-to-all(f32[32,8,128]{2,1,0:T(8,128)S(1)} %get-tuple-element.22), channel_id=1, replica_groups=mesh['group'=8,'loop'=32] {'loop'}, dimensions={0} | all-to-all | bytes 262144 | tf_op jit(solution)/shard_map/all_to_all | solution.py:276
  68.0 1.9 %shard_map.59 = f32[8,128,128]{2,1,0:T(8,128)} custom-call(bf16[16,128]{1,0:T(8,128)(2,1)S(1)} %broadcast_in_dim.21.codes, f32[8,128,128]{2,1,0:T(8,128)S(1)} %get-tuple-element.21.squares, f32[32,8,128]{2,1,0:T(8,128)S(1)} %all_to_all.5.sums), custom_call_target="tpu_custom_call" | custom-call | tf_op jit(solution)/shard_map/pallas_call | solution.py:277
  (8 shorter events, 0.1 us)
Async XLA Ops:
  2.4 5.1 %collective-permute-start = (bf16[528,128]{1,0:T(8,128)(2,1)S(1)}, bf16[528,128]{1,0:T(8,128)(2,1)S(1)}, u32[]{:S(2)}, u32[]{:S(2)}) collective-permute-start(bf16[528,128]{1,0:T(8,128)(2,1)S(1)} %pad_maximum_fusion.2), channel_id=1, source_target_pairs={{0,1},{1,0},{2,3},{3,2},{4,5},{5,4},{6,7},{7,6},{8,9},{9,8},{10,11... | collective-permute-start | bytes 405512 | tf_op jit(solution)/shard_map/ppermute | solution.py:203
  5.7 8.6 %collective-permute-start.1 = (bf16[528,128]{1,0:T(8,128)(2,1)S(1)}, bf16[528,128]{1,0:T(8,128)(2,1)S(1)}, u32[]{:S(2)}, u32[]{:S(2)}) collective-permute-start(bf16[528,128]{1,0:T(8,128)(2,1)S(1)} %pad_maximum_fusion.2), channel_id=1, source_target_pairs={{0,2},{1,3},{2,0},{3,1},{4,6},{5,7},{6,4},{7,5},{8,10},{9,11},{10,... | collective-permute-start | bytes 405512 | tf_op jit(solution)/shard_map/ppermute | solution.py:203
  5.7 8.6 %collective-permute-start.2 = (bf16[528,128]{1,0:T(8,128)(2,1)S(1)}, bf16[528,128]{1,0:T(8,128)(2,1)S(1)}, u32[]{:S(2)}, u32[]{:S(2)}) collective-permute-start(bf16[528,128]{1,0:T(8,128)(2,1)S(1)} %pad_maximum_fusion.2), channel_id=1, source_target_pairs={{0,3},{1,2},{2,1},{3,0},{4,7},{5,6},{6,5},{7,4},{8,11},{9,10},{10,... | collective-permute-start | bytes 405512 | tf_op jit(solution)/shard_map/ppermute | solution.py:203
  7.5 7.3 %collective-permute-start.3 = (bf16[1056,128]{1,0:T(8,128)(2,1)S(1)}, bf16[1056,128]{1,0:T(8,128)(2,1)S(1)}, u32[]{:S(2)}, u32[]{:S(2)}) collective-permute-start(bf16[1056,128]{1,0:T(8,128)(2,1)S(1)} %pad_maximum_fusion.refs_0_), channel_id=1, source_target_pairs={{0,4},{1,29},{2,6},{3,31},{4,8},{5,1},{6,10},{7,3},{8,12},{9,5},{1... | collective-permute-start | bytes 811016 | tf_op jit(solution)/shard_map/ppermute | solution.py:203
  11.4 7.0 %collective-permute-start.13 = (bf16[528,128]{1,0:T(8,128)(2,1)S(1)}, bf16[528,128]{1,0:T(8,128)(2,1)S(1)}, u32[]{:S(2)}, u32[]{:S(2)}) collective-permute-start(bf16[528,128]{1,0:T(8,128)(2,1)S(1)} %pad_maximum_fusion.2), channel_id=1, source_target_pairs={{0,32},{32,0},{64,96},{96,64},{128,160},{160,128},{192,224},{224,1... | collective-permute-start | bytes 405512 | tf_op jit(solution)/shard_map/ppermute | solution.py:206
  14.8 9.6 %collective-permute-start.4 = (bf16[1056,128]{1,0:T(8,128)(2,1)S(1)}, bf16[1056,128]{1,0:T(8,128)(2,1)S(1)}, u32[]{:S(2)}, u32[]{:S(2)}) collective-permute-start(bf16[1056,128]{1,0:T(8,128)(2,1)S(1)} %constant_dynamic-update-slice_fusion.refs_1_), channel_id=1, source_target_pairs={{0,4},{1,29},{2,6},{3,31},{4,8},{5,1},{6,10},{7,3},{8,12},{9,5},{1... | collective-permute-start | bytes 811016 | tf_op jit(solution)/shard_map/ppermute | solution.py:203
  18.4 7.9 %collective-permute-start.14 = (bf16[1056,128]{1,0:T(8,128)(2,1)S(1)}, bf16[1056,128]{1,0:T(8,128)(2,1)S(1)}, u32[]{:S(2)}, u32[]{:S(2)}) collective-permute-start(bf16[1056,128]{1,0:T(8,128)(2,1)S(1)} %pad_maximum_fusion.1), channel_id=1, source_target_pairs={{0,64},{32,96},{64,0},{96,32},{128,192},{160,224},{192,128},{224,1... | collective-permute-start | bytes 811016 | tf_op jit(solution)/shard_map/ppermute | solution.py:206
  19.7 9.8 %collective-permute-start.10 = (bf16[1056,128]{1,0:T(8,128)(2,1)S(1)}, bf16[1056,128]{1,0:T(8,128)(2,1)S(1)}, u32[]{:S(2)}, u32[]{:S(2)}) collective-permute-start(bf16[1056,128]{1,0:T(8,128)(2,1)S(1)} %collective-permute-done.3.refs_2_), channel_id=1, source_target_pairs={{0,4},{1,29},{2,6},{3,31},{4,8},{5,1},{6,10},{7,3},{8,12},{9,5},{1... | collective-permute-start | bytes 811016 | tf_op jit(solution)/shard_map/ppermute | solution.py:203
  24.4 10.5 %collective-permute-start.8 = (bf16[1056,128]{1,0:T(8,128)(2,1)S(1)}, bf16[1056,128]{1,0:T(8,128)(2,1)S(1)}, u32[]{:S(2)}, u32[]{:S(2)}) collective-permute-start(bf16[1056,128]{1,0:T(8,128)(2,1)S(1)} %collective-permute-done.3.refs_2_), channel_id=1, source_target_pairs={{0,1},{1,0},{2,3},{3,2},{4,5},{5,4},{6,7},{7,6},{8,9},{9,8},{10,11... | collective-permute-start | bytes 811016 | tf_op jit(solution)/shard_map/ppermute | solution.py:203
  24.4 10.5 %collective-permute-start.5 = (bf16[1056,128]{1,0:T(8,128)(2,1)S(1)}, bf16[1056,128]{1,0:T(8,128)(2,1)S(1)}, u32[]{:S(2)}, u32[]{:S(2)}) collective-permute-start(bf16[1056,128]{1,0:T(8,128)(2,1)S(1)} %collective-permute-done.4.refs_3_), channel_id=1, source_target_pairs={{0,4},{1,29},{2,6},{3,31},{4,8},{5,1},{6,10},{7,3},{8,12},{9,5},{1... | collective-permute-start | bytes 811016 | tf_op jit(solution)/shard_map/ppermute | solution.py:203
  26.3 16.7 %collective-permute-start.15 = (bf16[2112,128]{1,0:T(8,128)(2,1)S(1)}, bf16[2112,128]{1,0:T(8,128)(2,1)S(1)}, u32[]{:S(2)}, u32[]{:S(2)}) collective-permute-start(bf16[2112,128]{1,0:T(8,128)(2,1)S(1)} %constant_dynamic-update-slice_fusion.2.refs_10_), channel_id=1, source_target_pairs={{0,192},{32,224},{64,128},{96,160},{128,64},{160,96},{192,0},{224,... | collective-permute-start | bytes 1622024 | tf_op jit(solution)/shard_map/ppermute | solution.py:206
  29.2 6.4 %collective-permute-start.9 = (bf16[1056,128]{1,0:T(8,128)(2,1)S(1)}, bf16[1056,128]{1,0:T(8,128)(2,1)S(1)}, u32[]{:S(2)}, u32[]{:S(2)}) collective-permute-start(bf16[1056,128]{1,0:T(8,128)(2,1)S(1)} %collective-permute-done.4.refs_3_), channel_id=1, source_target_pairs={{0,1},{1,0},{2,3},{3,2},{4,5},{5,4},{6,7},{7,6},{8,9},{9,8},{10,11... | collective-permute-start | bytes 811016 | tf_op jit(solution)/shard_map/ppermute | solution.py:203
  29.5 8.7 %collective-permute-start.16 = (bf16[1056,128]{1,0:T(8,128)(2,1)S(1)}, bf16[1056,128]{1,0:T(8,128)(2,1)S(1)}, u32[]{:S(2)}, u32[]{:S(2)}) collective-permute-start(bf16[1056,128]{1,0:T(8,128)(2,1)S(1)} %collective-permute-done.10.refs_6_), channel_id=1, source_target_pairs={{0,4},{1,29},{2,6},{3,31},{4,8},{5,1},{6,10},{7,3},{8,12},{9,5},{1... | collective-permute-start | bytes 811016 | tf_op jit(solution)/shard_map/ppermute | solution.py:203
  34.8 6.8 %collective-permute-start.11 = (bf16[1056,128]{1,0:T(8,128)(2,1)S(1)}, bf16[1056,128]{1,0:T(8,128)(2,1)S(1)}, u32[]{:S(2)}, u32[]{:S(2)}) collective-permute-start(bf16[1056,128]{1,0:T(8,128)(2,1)S(1)} %collective-permute-done.10.refs_6_), channel_id=1, source_target_pairs={{0,1},{1,0},{2,3},{3,2},{4,5},{5,4},{6,7},{7,6},{8,9},{9,8},{10,11... | collective-permute-start | bytes 811016 | tf_op jit(solution)/shard_map/ppermute | solution.py:203
  34.8 6.8 %collective-permute-start.6 = (bf16[1056,128]{1,0:T(8,128)(2,1)S(1)}, bf16[1056,128]{1,0:T(8,128)(2,1)S(1)}, u32[]{:S(2)}, u32[]{:S(2)}) collective-permute-start(bf16[1056,128]{1,0:T(8,128)(2,1)S(1)} %collective-permute-done.5.refs_7_), channel_id=1, source_target_pairs={{0,4},{1,29},{2,6},{3,31},{4,8},{5,1},{6,10},{7,3},{8,12},{9,5},{1... | collective-permute-start | bytes 811016 | tf_op jit(solution)/shard_map/ppermute | solution.py:203
  35.6 8.9 %collective-permute-start.12 = (bf16[1056,128]{1,0:T(8,128)(2,1)S(1)}, bf16[1056,128]{1,0:T(8,128)(2,1)S(1)}, u32[]{:S(2)}, u32[]{:S(2)}) collective-permute-start(bf16[1056,128]{1,0:T(8,128)(2,1)S(1)} %collective-permute-done.5.refs_7_), channel_id=1, source_target_pairs={{0,1},{1,0},{2,3},{3,2},{4,5},{5,4},{6,7},{7,6},{8,9},{9,8},{10,11... | collective-permute-start | bytes 811016 | tf_op jit(solution)/shard_map/ppermute | solution.py:203
  38.2 10.9 %collective-permute-start.19 = (bf16[1056,128]{1,0:T(8,128)(2,1)S(1)}, bf16[1056,128]{1,0:T(8,128)(2,1)S(1)}, u32[]{:S(2)}, u32[]{:S(2)}) collective-permute-start(bf16[1056,128]{1,0:T(8,128)(2,1)S(1)} %collective-permute-done.16.refs_0_), channel_id=1, source_target_pairs={{0,4},{1,29},{2,6},{3,31},{4,8},{5,1},{6,10},{7,3},{8,12},{9,5},{1... | collective-permute-start | bytes 811016 | tf_op jit(solution)/shard_map/ppermute | solution.py:203
  41.6 8.1 %collective-permute-start.17 = (bf16[1056,128]{1,0:T(8,128)(2,1)S(1)}, bf16[1056,128]{1,0:T(8,128)(2,1)S(1)}, u32[]{:S(2)}, u32[]{:S(2)}) collective-permute-start(bf16[1056,128]{1,0:T(8,128)(2,1)S(1)} %collective-permute-done.16.refs_0_), channel_id=1, source_target_pairs={{0,1},{1,0},{2,3},{3,2},{4,5},{5,4},{6,7},{7,6},{8,9},{9,8},{10,11... | collective-permute-start | bytes 811016 | tf_op jit(solution)/shard_map/ppermute | solution.py:203
  41.7 8.1 %collective-permute-start.18 = (bf16[1056,128]{1,0:T(8,128)(2,1)S(1)}, bf16[1056,128]{1,0:T(8,128)(2,1)S(1)}, u32[]{:S(2)}, u32[]{:S(2)}) collective-permute-start(bf16[1056,128]{1,0:T(8,128)(2,1)S(1)} %collective-permute-done.6.refs_1_), channel_id=1, source_target_pairs={{0,1},{1,0},{2,3},{3,2},{4,5},{5,4},{6,7},{7,6},{8,9},{9,8},{10,11... | collective-permute-start | bytes 811016 | tf_op jit(solution)/shard_map/ppermute | solution.py:203
  43.0 8.5 %collective-permute-start.7 = (bf16[1056,128]{1,0:T(8,128)(2,1)S(1)}, bf16[1056,128]{1,0:T(8,128)(2,1)S(1)}, u32[]{:S(2)}, u32[]{:S(2)}) collective-permute-start(bf16[1056,128]{1,0:T(8,128)(2,1)S(1)} %collective-permute-done.6.refs_1_), channel_id=1, source_target_pairs={{0,4},{1,29},{2,6},{3,31},{4,8},{5,1},{6,10},{7,3},{8,12},{9,5},{1... | collective-permute-start | bytes 811016 | tf_op jit(solution)/shard_map/ppermute | solution.py:203

commit v11 on v10

--- a/solution.py
+++ b/solution.py
@@ -227,7 +227,7 @@
         ahead = along(RING, streams[0])
         behind = after(streams[1], ahead)[0] if r == 0 else streams[1]
         streams = [ahead, along(RING, behind)]
-        other = streams
+        other = after(*streams) if r < 2 else streams
         right += [streams, [along(CORE, v) for v in other]]
     last = [along(RING, v) for v in streams]
 

time: 70.2 us -> 73.8 us (1.051)
  waiting for transfers between devices: 2.41 us -> 4.92 us
    ppermute x17, starting transfers between devices: 31.2 us -> 34.5 us  [along(): return lax.ppermute(v, 'loop', perm)]
    ppermute x3, starting transfers between devices: 7.09 us -> 4.51 us  [across(): return lax.ppermute(v, 'group', perm)]
    ppermute x3, waiting for transfers between devices: 0.67 us -> 2.95 us  [across(): return lax.ppermute(v, 'group', perm)]
  transfers between devices with their start and end apart: 20 -> 20, of which waited for: 3 -> 4; matrix products, arithmetic and copies ran while one was open for 1% -> 1% of each run, Pallas kernels for 10% -> 9%
where the time goes in v11:
time: 73.8 us; the launch traced here: 73.7 us
  starting transfers between devices  39 us (53%)
  blocking collectives  15.2 us (21%)
  Pallas kernels  10.4 us (14%)
  waiting for transfers between devices  4.92 us (7%)
  other arithmetic  2.4 us (3%)
  between operations  1.6 us (2%)
    ppermute x17, starting transfers between devices, along(): return lax.ppermute(v, 'loop', perm)  34.5 us
    all_to_all x1, blocking collectives, shards(): sums = lax.all_to_all(sums, 'loop', 0, 0, tiled=True)  15.2 us
    pallas_call x1, Pallas kernels, shards(): pl.pallas_call(begin, in_specs=[WHOLE] * 12, out_specs=[WHOLE] * 2, out_s...  4.59 us
    ppermute x3, starting transfers between devices, across(): return lax.ppermute(v, 'group', perm)  4.51 us
    ppermute x3, waiting for transfers between devices, across(): return lax.ppermute(v, 'group', perm)  2.95 us
    ppermute x17, waiting for transfers between devices, along(): return lax.ppermute(v, 'loop', perm)  1.97 us
    pallas_call x1, Pallas kernels, shards(): pl.pallas_call(rescale, in_specs=[AWAY] * 3, out_specs=AWAY, out_shape=ja...  1.94 us
    pallas_call x1, Pallas kernels, shards(): pl.pallas_call(proceed, in_specs=[WHOLE] * 6, out_specs=WHOLE, out_shape=...  1.76 us
  transfers between devices with their start and end apart: 20, of which 4 were waited for; matrix products, arithmetic and copies ran while one was open for 1% of the time, Pallas kernels for 9%

profile of v11, /device:TPU:1, one launch (start us, length us, event | category | flops | bytes accessed | tf_op | source)
XLA Modules:
  0.0 73.7 jit_solution(8689161584103962658)
XLA Ops:
  0.7 0.7 fusion
  1.3 1.0 %pad_maximum_fusion.2 = bf16[528,128]{1,0:T(8,128)(2,1)S(1)} fusion(bf16[512,128]{1,0:T(8,128)(2,1)} %bitcast.8, bf16[528]{0:T(1024)(128)(2,1)S(1)} %pad.15.clone), kind=kLoop, calls=%fused_computation.2 | loop fusion | flops 270336 | bytes 267296 | tf_op jit(solution)/shard_map/concatenate | solution.py:196
  2.4 3.3 %collective-permute-start = (bf16[528,128]{1,0:T(8,128)(2,1)S(1)}, bf16[528,128]{1,0:T(8,128)(2,1)S(1)}, u32[]{:S(2)}, u32[]{:S(2)}) collective-permute-start(bf16[528,128]{1,0:T(8,128)(2,1)S(1)} %pad_maximum_fusion.2), channel_id=1, source_target_pairs={{0,1},{1,0},{2,3},{3,2},{4,5},{5,4},{6,7},{7,6},{8,9},{9,8},{10,11... | collective-permute-start | bytes 405512 | tf_op jit(solution)/shard_map/ppermute | solution.py:203
  5.7 0.0 collective-permute-start.1
  5.7 1.7 %collective-permute-start.2 = (bf16[528,128]{1,0:T(8,128)(2,1)S(1)}, bf16[528,128]{1,0:T(8,128)(2,1)S(1)}, u32[]{:S(2)}, u32[]{:S(2)}) collective-permute-start(bf16[528,128]{1,0:T(8,128)(2,1)S(1)} %pad_maximum_fusion.2), channel_id=1, source_target_pairs={{0,3},{1,2},{2,1},{3,0},{4,7},{5,6},{6,5},{7,4},{8,11},{9,10},{10,... | collective-permute-start | bytes 405512 | tf_op jit(solution)/shard_map/ppermute | solution.py:203
  7.4 0.0 collective-permute-done
  7.5 1.3 %collective-permute-start.13 = (bf16[528,128]{1,0:T(8,128)(2,1)S(1)}, bf16[528,128]{1,0:T(8,128)(2,1)S(1)}, u32[]{:S(2)}, u32[]{:S(2)}) collective-permute-start(bf16[528,128]{1,0:T(8,128)(2,1)S(1)} %pad_maximum_fusion.2), channel_id=1, source_target_pairs={{0,32},{32,0},{64,96},{96,64},{128,160},{160,128},{192,224},{224,1... | collective-permute-start | bytes 405512 | tf_op jit(solution)/shard_map/ppermute | solution.py:206
  8.7 5.6 %collective-permute-start.3 = (bf16[1056,128]{1,0:T(8,128)(2,1)S(1)}, bf16[1056,128]{1,0:T(8,128)(2,1)S(1)}, u32[]{:S(2)}, u32[]{:S(2)}) collective-permute-start(bf16[1056,128]{1,0:T(8,128)(2,1)S(1)} %pad_maximum_fusion.refs_0_), channel_id=1, source_target_pairs={{0,4},{1,29},{2,6},{3,31},{4,8},{5,1},{6,10},{7,3},{8,12},{9,5},{1... | collective-permute-start | bytes 811016 | tf_op jit(solution)/shard_map/ppermute | solution.py:203
  14.3 0.0 collective-permute-done.1
  14.3 0.1 collective-permute-done.2
  14.4 2.9 %collective-permute-done.13 = bf16[528,128]{1,0:T(8,128)(2,1)S(1)} collective-permute-done((bf16[528,128]{1,0:T(8,128)(2,1)S(1)}, bf16[528,128]{1,0:T(8,128)(2,1)S(1)}, u32[]{:S(2)}, u32[]{:S(2)}) %collective-permute-start.13) | collective-permute-done | bytes 135200 | tf_op jit(solution)/shard_map/ppermute | solution.py:206
  17.4 1.3 %collective-permute-start.14 = (bf16[1056,128]{1,0:T(8,128)(2,1)S(1)}, bf16[1056,128]{1,0:T(8,128)(2,1)S(1)}, u32[]{:S(2)}, u32[]{:S(2)}) collective-permute-start(bf16[1056,128]{1,0:T(8,128)(2,1)S(1)} %pad_maximum_fusion.1), channel_id=1, source_target_pairs={{0,64},{32,96},{64,0},{96,32},{128,192},{160,224},{192,128},{224,1... | collective-permute-start | bytes 811016 | tf_op jit(solution)/shard_map/ppermute | solution.py:206
  18.7 0.0 collective-permute-done.3.refs_2_
  18.7 5.7 %collective-permute-start.4 = (bf16[1056,128]{1,0:T(8,128)(2,1)S(1)}, bf16[1056,128]{1,0:T(8,128)(2,1)S(1)}, u32[]{:S(2)}, u32[]{:S(2)}) collective-permute-start(bf16[1056,128]{1,0:T(8,128)(2,1)S(1)} %constant_dynamic-update-slice_fusion.refs_1_), channel_id=1, source_target_pairs={{0,4},{1,29},{2,6},{3,31},{4,8},{5,1},{6,10},{7,3},{8,12},{9,5},{1... | collective-permute-start | bytes 811016 | tf_op jit(solution)/shard_map/ppermute | solution.py:203
  24.4 0.8 %collective-permute-start.10 = (bf16[1056,128]{1,0:T(8,128)(2,1)S(1)}, bf16[1056,128]{1,0:T(8,128)(2,1)S(1)}, u32[]{:S(2)}, u32[]{:S(2)}) collective-permute-start(bf16[1056,128]{1,0:T(8,128)(2,1)S(1)} %collective-permute-done.3.refs_2_), channel_id=1, source_target_pairs={{0,4},{1,29},{2,6},{3,31},{4,8},{5,1},{6,10},{7,3},{8,12},{9,5},{1... | collective-permute-start | bytes 811016 | tf_op jit(solution)/shard_map/ppermute | solution.py:203
  25.2 0.0 collective-permute-done.14
  25.2 1.9 %collective-permute-start.15 = (bf16[2112,128]{1,0:T(8,128)(2,1)S(1)}, bf16[2112,128]{1,0:T(8,128)(2,1)S(1)}, u32[]{:S(2)}, u32[]{:S(2)}) collective-permute-start(bf16[2112,128]{1,0:T(8,128)(2,1)S(1)} %constant_dynamic-update-slice_fusion.2.refs_10_), channel_id=1, source_target_pairs={{0,192},{32,224},{64,128},{96,160},{128,64},{160,96},{192,0},{224,... | collective-permute-start | bytes 1622024 | tf_op jit(solution)/shard_map/ppermute | solution.py:206
  27.2 0.6 collective-permute-done.4.refs_3_
  27.8 5.0 %collective-permute-start.5 = (bf16[1056,128]{1,0:T(8,128)(2,1)S(1)}, bf16[1056,128]{1,0:T(8,128)(2,1)S(1)}, u32[]{:S(2)}, u32[]{:S(2)}) collective-permute-start(bf16[1056,128]{1,0:T(8,128)(2,1)S(1)} %collective-permute-done.4.refs_3_), channel_id=1, source_target_pairs={{0,4},{1,29},{2,6},{3,31},{4,8},{5,1},{6,10},{7,3},{8,12},{9,5},{1... | collective-permute-start | bytes 811016 | tf_op jit(solution)/shard_map/ppermute | solution.py:203
  32.8 0.0 collective-permute-start.8
  32.8 0.5 collective-permute-start.9
  33.3 0.0 collective-permute-done.10.refs_6_
  33.3 1.6 %collective-permute-start.16 = (bf16[1056,128]{1,0:T(8,128)(2,1)S(1)}, bf16[1056,128]{1,0:T(8,128)(2,1)S(1)}, u32[]{:S(2)}, u32[]{:S(2)}) collective-permute-start(bf16[1056,128]{1,0:T(8,128)(2,1)S(1)} %collective-permute-done.10.refs_6_), channel_id=1, source_target_pairs={{0,4},{1,29},{2,6},{3,31},{4,8},{5,1},{6,10},{7,3},{8,12},{9,5},{1... | collective-permute-start | bytes 811016 | tf_op jit(solution)/shard_map/ppermute | solution.py:203
  34.9 1.3 %collective-permute-done.5.refs_7_ = bf16[1056,128]{1,0:T(8,128)(2,1)S(1)} collective-permute-done((bf16[1056,128]{1,0:T(8,128)(2,1)S(1)}, bf16[1056,128]{1,0:T(8,128)(2,1)S(1)}, u32[]{:S(2)}, u32[]{:S(2)}) %collective-permute-start.5) | collective-permute-done | bytes 270368 | tf_op jit(solution)/shard_map/ppermute | solution.py:203
  36.2 3.4 %collective-permute-start.6 = (bf16[1056,128]{1,0:T(8,128)(2,1)S(1)}, bf16[1056,128]{1,0:T(8,128)(2,1)S(1)}, u32[]{:S(2)}, u32[]{:S(2)}) collective-permute-start(bf16[1056,128]{1,0:T(8,128)(2,1)S(1)} %collective-permute-done.5.refs_7_), channel_id=1, source_target_pairs={{0,4},{1,29},{2,6},{3,31},{4,8},{5,1},{6,10},{7,3},{8,12},{9,5},{1... | collective-permute-start | bytes 811016 | tf_op jit(solution)/shard_map/ppermute | solution.py:203
  39.6 0.0 collective-permute-done.8.refs_4_
  39.6 0.0 collective-permute-start.11
  39.6 0.0 collective-permute-done.9.refs_5_
  39.6 0.5 collective-permute-start.12
  40.8 0.7 fusion.1
  41.4 0.0 collective-permute-done.16.refs_0_
  41.4 2.5 %collective-permute-start.19 = (bf16[1056,128]{1,0:T(8,128)(2,1)S(1)}, bf16[1056,128]{1,0:T(8,128)(2,1)S(1)}, u32[]{:S(2)}, u32[]{:S(2)}) collective-permute-start(bf16[1056,128]{1,0:T(8,128)(2,1)S(1)} %collective-permute-done.16.refs_0_), channel_id=1, source_target_pairs={{0,4},{1,29},{2,6},{3,31},{4,8},{5,1},{6,10},{7,3},{8,12},{9,5},{1... | collective-permute-start | bytes 811016 | tf_op jit(solution)/shard_map/ppermute | solution.py:203
  43.9 0.0 collective-permute-done.15.refs_11_
  43.9 0.0 collective-permute-start.17
  43.9 0.0 collective-permute-done.6.refs_1_
  43.9 3.3 %collective-permute-start.18 = (bf16[1056,128]{1,0:T(8,128)(2,1)S(1)}, bf16[1056,128]{1,0:T(8,128)(2,1)S(1)}, u32[]{:S(2)}, u32[]{:S(2)}) collective-permute-start(bf16[1056,128]{1,0:T(8,128)(2,1)S(1)} %collective-permute-done.6.refs_1_), channel_id=1, source_target_pairs={{0,1},{1,0},{2,3},{3,2},{4,5},{5,4},{6,7},{7,6},{8,9},{9,8},{10,11... | collective-permute-start | bytes 811016 | tf_op jit(solution)/shard_map/ppermute | solution.py:203
  47.2 0.0 collective-permute-done.11.refs_8_
  47.2 0.5 collective-permute-start.7
  47.7 0.0 collective-permute-done.12.refs_9_
  47.8 4.6 %shard_map.55 = (bf16[8,256,1152]{2,1,0:T(8,128)(2,1)S(1)}, f32[256,1024]{1,0:T(8,128)S(1)}) custom-call(bf16[1056,128]{1,0:T(8,128)(2,1)S(1)} %pad_maximum_fusion.refs_0_, bf16[1056,128]{1,0:T(8,128)(2,1)S(1)} %constant_dynamic-update-slice_fusion.refs_1_, bf16[1056,128]{1,0:T(8,128)(2,1)S(1)} %collective-permute-done.3.refs_2_, ...), custom_call_target="tpu_custom_call" | custom-call | flops 3221225472 | bytes 25165824 | tf_op jit(solution)/shard_map/pallas_call | solution.py:235
  52.3 0.0 collective-permute-done.19.pair
  52.4 0.6 shard_map.56.refs_5_
  53.0 0.0 collective-permute-done.17.refs_2_
  53.0 0.0 collective-permute-done.18.refs_3_
  53.0 1.8 %shard_map.57.before = f32[256,1024]{1,0:T(8,128)S(1)} custom-call(bf16[1056,128]{1,0:T(8,128)(2,1)S(1)} %collective-permute-done.16.refs_0_, bf16[1056,128]{1,0:T(8,128)(2,1)S(1)} %collective-permute-done.6.refs_1_, bf16[1056,128]{1,0:T(8,128)(2,1)S(1)} %collective-permute-done.17.refs_2_, bf16[1056,128]{1,0:T(8,128)(2,1)S(1)} %collective-permute-done.18.refs_3_, ...), custom_call_target="tpu_custom_call" | custom-call | flops 1073741824 | bytes 8388608 | tf_op jit(solution)/shard_map/pallas_call | solution.py:253
  54.8 0.0 collective-permute-done.7.beside
  54.8 0.1 broadcast_in_dim.21.codes
  54.8 1.5 %shard_map.58 = (f32[8,128,128]{2,1,0:T(8,128)S(1)}, f32[32,8,128]{2,1,0:T(8,128)S(1)}) custom-call(bf16[16,128]{1,0:T(8,128)(2,1)S(1)} %broadcast_in_dim.21.codes, bf16[1056,128]{1,0:T(8,128)(2,1)S(1)} %collective-permute-done.7.beside, bf16[8,256,1152]{2,1,0:T(8,128)(2,1)S(1)} %get-tuple-element.27.dense_left.refs_4_, f32[256,1024]{1,0:T(8,128)S(1)} %shard_map.57.before), custom_call_target="tpu_custom_call" | custom-call | flops 536870912 | bytes 4194304 | tf_op jit(solution)/shard_map/pallas_call | solution.py:262
  56.4 15.2 %all_to_all.5.sums = f32[32,8,128]{2,1,0:T(8,128)S(1)} all-to-all(f32[32,8,128]{2,1,0:T(8,128)S(1)} %get-tuple-element.30), channel_id=1, replica_groups=mesh['group'=8,'loop'=32] {'loop'}, dimensions={0} | all-to-all | bytes 262144 | tf_op jit(solution)/shard_map/all_to_all | solution.py:276
  71.6 1.9 %shard_map.59 = f32[8,128,128]{2,1,0:T(8,128)} custom-call(bf16[16,128]{1,0:T(8,128)(2,1)S(1)} %broadcast_in_dim.21.codes, f32[8,128,128]{2,1,0:T(8,128)S(1)} %get-tuple-element.29.squares, f32[32,8,128]{2,1,0:T(8,128)S(1)} %all_to_all.5.sums), custom_call_target="tpu_custom_call" | custom-call | tf_op jit(solution)/shard_map/pallas_call | solution.py:277
  (8 shorter events, 0.1 us)
Async XLA Ops:
  2.4 5.1 %collective-permute-start = (bf16[528,128]{1,0:T(8,128)(2,1)S(1)}, bf16[528,128]{1,0:T(8,128)(2,1)S(1)}, u32[]{:S(2)}, u32[]{:S(2)}) collective-permute-start(bf16[528,128]{1,0:T(8,128)(2,1)S(1)} %pad_maximum_fusion.2), channel_id=1, source_target_pairs={{0,1},{1,0},{2,3},{3,2},{4,5},{5,4},{6,7},{7,6},{8,9},{9,8},{10,11... | collective-permute-start | bytes 405512 | tf_op jit(solution)/shard_map/ppermute | solution.py:203
  5.7 8.6 %collective-permute-start.1 = (bf16[528,128]{1,0:T(8,128)(2,1)S(1)}, bf16[528,128]{1,0:T(8,128)(2,1)S(1)}, u32[]{:S(2)}, u32[]{:S(2)}) collective-permute-start(bf16[528,128]{1,0:T(8,128)(2,1)S(1)} %pad_maximum_fusion.2), channel_id=1, source_target_pairs={{0,2},{1,3},{2,0},{3,1},{4,6},{5,7},{6,4},{7,5},{8,10},{9,11},{10,... | collective-permute-start | bytes 405512 | tf_op jit(solution)/shard_map/ppermute | solution.py:203
  5.7 8.7 %collective-permute-start.2 = (bf16[528,128]{1,0:T(8,128)(2,1)S(1)}, bf16[528,128]{1,0:T(8,128)(2,1)S(1)}, u32[]{:S(2)}, u32[]{:S(2)}) collective-permute-start(bf16[528,128]{1,0:T(8,128)(2,1)S(1)} %pad_maximum_fusion.2), channel_id=1, source_target_pairs={{0,3},{1,2},{2,1},{3,0},{4,7},{5,6},{6,5},{7,4},{8,11},{9,10},{10,... | collective-permute-start | bytes 405512 | tf_op jit(solution)/shard_map/ppermute | solution.py:203
  7.5 9.9 %collective-permute-start.13 = (bf16[528,128]{1,0:T(8,128)(2,1)S(1)}, bf16[528,128]{1,0:T(8,128)(2,1)S(1)}, u32[]{:S(2)}, u32[]{:S(2)}) collective-permute-start(bf16[528,128]{1,0:T(8,128)(2,1)S(1)} %pad_maximum_fusion.2), channel_id=1, source_target_pairs={{0,32},{32,0},{64,96},{96,64},{128,160},{160,128},{192,224},{224,1... | collective-permute-start | bytes 405512 | tf_op jit(solution)/shard_map/ppermute | solution.py:206
  8.7 10.0 %collective-permute-start.3 = (bf16[1056,128]{1,0:T(8,128)(2,1)S(1)}, bf16[1056,128]{1,0:T(8,128)(2,1)S(1)}, u32[]{:S(2)}, u32[]{:S(2)}) collective-permute-start(bf16[1056,128]{1,0:T(8,128)(2,1)S(1)} %pad_maximum_fusion.refs_0_), channel_id=1, source_target_pairs={{0,4},{1,29},{2,6},{3,31},{4,8},{5,1},{6,10},{7,3},{8,12},{9,5},{1... | collective-permute-start | bytes 811016 | tf_op jit(solution)/shard_map/ppermute | solution.py:203
  17.4 7.8 %collective-permute-start.14 = (bf16[1056,128]{1,0:T(8,128)(2,1)S(1)}, bf16[1056,128]{1,0:T(8,128)(2,1)S(1)}, u32[]{:S(2)}, u32[]{:S(2)}) collective-permute-start(bf16[1056,128]{1,0:T(8,128)(2,1)S(1)} %pad_maximum_fusion.1), channel_id=1, source_target_pairs={{0,64},{32,96},{64,0},{96,32},{128,192},{160,224},{192,128},{224,1... | collective-permute-start | bytes 811016 | tf_op jit(solution)/shard_map/ppermute | solution.py:206
  18.7 9.1 %collective-permute-start.4 = (bf16[1056,128]{1,0:T(8,128)(2,1)S(1)}, bf16[1056,128]{1,0:T(8,128)(2,1)S(1)}, u32[]{:S(2)}, u32[]{:S(2)}) collective-permute-start(bf16[1056,128]{1,0:T(8,128)(2,1)S(1)} %constant_dynamic-update-slice_fusion.refs_1_), channel_id=1, source_target_pairs={{0,4},{1,29},{2,6},{3,31},{4,8},{5,1},{6,10},{7,3},{8,12},{9,5},{1... | collective-permute-start | bytes 811016 | tf_op jit(solution)/shard_map/ppermute | solution.py:203
  24.4 8.9 %collective-permute-start.10 = (bf16[1056,128]{1,0:T(8,128)(2,1)S(1)}, bf16[1056,128]{1,0:T(8,128)(2,1)S(1)}, u32[]{:S(2)}, u32[]{:S(2)}) collective-permute-start(bf16[1056,128]{1,0:T(8,128)(2,1)S(1)} %collective-permute-done.3.refs_2_), channel_id=1, source_target_pairs={{0,4},{1,29},{2,6},{3,31},{4,8},{5,1},{6,10},{7,3},{8,12},{9,5},{1... | collective-permute-start | bytes 811016 | tf_op jit(solution)/shard_map/ppermute | solution.py:203
  25.2 18.7 %collective-permute-start.15 = (bf16[2112,128]{1,0:T(8,128)(2,1)S(1)}, bf16[2112,128]{1,0:T(8,128)(2,1)S(1)}, u32[]{:S(2)}, u32[]{:S(2)}) collective-permute-start(bf16[2112,128]{1,0:T(8,128)(2,1)S(1)} %constant_dynamic-update-slice_fusion.2.refs_10_), channel_id=1, source_target_pairs={{0,192},{32,224},{64,128},{96,160},{128,64},{160,96},{192,0},{224,... | collective-permute-start | bytes 1622024 | tf_op jit(solution)/shard_map/ppermute | solution.py:206
  27.8 8.4 %collective-permute-start.5 = (bf16[1056,128]{1,0:T(8,128)(2,1)S(1)}, bf16[1056,128]{1,0:T(8,128)(2,1)S(1)}, u32[]{:S(2)}, u32[]{:S(2)}) collective-permute-start(bf16[1056,128]{1,0:T(8,128)(2,1)S(1)} %collective-permute-done.4.refs_3_), channel_id=1, source_target_pairs={{0,4},{1,29},{2,6},{3,31},{4,8},{5,1},{6,10},{7,3},{8,12},{9,5},{1... | collective-permute-start | bytes 811016 | tf_op jit(solution)/shard_map/ppermute | solution.py:203
  32.8 6.8 %collective-permute-start.8 = (bf16[1056,128]{1,0:T(8,128)(2,1)S(1)}, bf16[1056,128]{1,0:T(8,128)(2,1)S(1)}, u32[]{:S(2)}, u32[]{:S(2)}) collective-permute-start(bf16[1056,128]{1,0:T(8,128)(2,1)S(1)} %collective-permute-done.3.refs_2_), channel_id=1, source_target_pairs={{0,1},{1,0},{2,3},{3,2},{4,5},{5,4},{6,7},{7,6},{8,9},{9,8},{10,11... | collective-permute-start | bytes 811016 | tf_op jit(solution)/shard_map/ppermute | solution.py:203
  32.8 6.8 %collective-permute-start.9 = (bf16[1056,128]{1,0:T(8,128)(2,1)S(1)}, bf16[1056,128]{1,0:T(8,128)(2,1)S(1)}, u32[]{:S(2)}, u32[]{:S(2)}) collective-permute-start(bf16[1056,128]{1,0:T(8,128)(2,1)S(1)} %collective-permute-done.4.refs_3_), channel_id=1, source_target_pairs={{0,1},{1,0},{2,3},{3,2},{4,5},{5,4},{6,7},{7,6},{8,9},{9,8},{10,11... | collective-permute-start | bytes 811016 | tf_op jit(solution)/shard_map/ppermute | solution.py:203
  33.3 8.1 %collective-permute-start.16 = (bf16[1056,128]{1,0:T(8,128)(2,1)S(1)}, bf16[1056,128]{1,0:T(8,128)(2,1)S(1)}, u32[]{:S(2)}, u32[]{:S(2)}) collective-permute-start(bf16[1056,128]{1,0:T(8,128)(2,1)S(1)} %collective-permute-done.10.refs_6_), channel_id=1, source_target_pairs={{0,4},{1,29},{2,6},{3,31},{4,8},{5,1},{6,10},{7,3},{8,12},{9,5},{1... | collective-permute-start | bytes 811016 | tf_op jit(solution)/shard_map/ppermute | solution.py:203
  36.2 7.7 %collective-permute-start.6 = (bf16[1056,128]{1,0:T(8,128)(2,1)S(1)}, bf16[1056,128]{1,0:T(8,128)(2,1)S(1)}, u32[]{:S(2)}, u32[]{:S(2)}) collective-permute-start(bf16[1056,128]{1,0:T(8,128)(2,1)S(1)} %collective-permute-done.5.refs_7_), channel_id=1, source_target_pairs={{0,4},{1,29},{2,6},{3,31},{4,8},{5,1},{6,10},{7,3},{8,12},{9,5},{1... | collective-permute-start | bytes 811016 | tf_op jit(solution)/shard_map/ppermute | solution.py:203
  39.6 7.6 %collective-permute-start.11 = (bf16[1056,128]{1,0:T(8,128)(2,1)S(1)}, bf16[1056,128]{1,0:T(8,128)(2,1)S(1)}, u32[]{:S(2)}, u32[]{:S(2)}) collective-permute-start(bf16[1056,128]{1,0:T(8,128)(2,1)S(1)} %collective-permute-done.10.refs_6_), channel_id=1, source_target_pairs={{0,1},{1,0},{2,3},{3,2},{4,5},{5,4},{6,7},{7,6},{8,9},{9,8},{10,11... | collective-permute-start | bytes 811016 | tf_op jit(solution)/shard_map/ppermute | solution.py:203
  39.6 8.2 %collective-permute-start.12 = (bf16[1056,128]{1,0:T(8,128)(2,1)S(1)}, bf16[1056,128]{1,0:T(8,128)(2,1)S(1)}, u32[]{:S(2)}, u32[]{:S(2)}) collective-permute-start(bf16[1056,128]{1,0:T(8,128)(2,1)S(1)} %collective-permute-done.5.refs_7_), channel_id=1, source_target_pairs={{0,1},{1,0},{2,3},{3,2},{4,5},{5,4},{6,7},{7,6},{8,9},{9,8},{10,11... | collective-permute-start | bytes 811016 | tf_op jit(solution)/shard_map/ppermute | solution.py:203
  41.4 10.9 %collective-permute-start.19 = (bf16[1056,128]{1,0:T(8,128)(2,1)S(1)}, bf16[1056,128]{1,0:T(8,128)(2,1)S(1)}, u32[]{:S(2)}, u32[]{:S(2)}) collective-permute-start(bf16[1056,128]{1,0:T(8,128)(2,1)S(1)} %collective-permute-done.16.refs_0_), channel_id=1, source_target_pairs={{0,4},{1,29},{2,6},{3,31},{4,8},{5,1},{6,10},{7,3},{8,12},{9,5},{1... | collective-permute-start | bytes 811016 | tf_op jit(solution)/shard_map/ppermute | solution.py:203
  43.9 9.1 %collective-permute-start.17 = (bf16[1056,128]{1,0:T(8,128)(2,1)S(1)}, bf16[1056,128]{1,0:T(8,128)(2,1)S(1)}, u32[]{:S(2)}, u32[]{:S(2)}) collective-permute-start(bf16[1056,128]{1,0:T(8,128)(2,1)S(1)} %collective-permute-done.16.refs_0_), channel_id=1, source_target_pairs={{0,1},{1,0},{2,3},{3,2},{4,5},{5,4},{6,7},{7,6},{8,9},{9,8},{10,11... | collective-permute-start | bytes 811016 | tf_op jit(solution)/shard_map/ppermute | solution.py:203
  43.9 9.1 %collective-permute-start.18 = (bf16[1056,128]{1,0:T(8,128)(2,1)S(1)}, bf16[1056,128]{1,0:T(8,128)(2,1)S(1)}, u32[]{:S(2)}, u32[]{:S(2)}) collective-permute-start(bf16[1056,128]{1,0:T(8,128)(2,1)S(1)} %collective-permute-done.6.refs_1_), channel_id=1, source_target_pairs={{0,1},{1,0},{2,3},{3,2},{4,5},{5,4},{6,7},{7,6},{8,9},{9,8},{10,11... | collective-permute-start | bytes 811016 | tf_op jit(solution)/shard_map/ppermute | solution.py:203
  47.2 7.6 %collective-permute-start.7 = (bf16[1056,128]{1,0:T(8,128)(2,1)S(1)}, bf16[1056,128]{1,0:T(8,128)(2,1)S(1)}, u32[]{:S(2)}, u32[]{:S(2)}) collective-permute-start(bf16[1056,128]{1,0:T(8,128)(2,1)S(1)} %collective-permute-done.6.refs_1_), channel_id=1, source_target_pairs={{0,4},{1,29},{2,6},{3,31},{4,8},{5,1},{6,10},{7,3},{8,12},{9,5},{1... | collective-permute-start | bytes 811016 | tf_op jit(solution)/shard_map/ppermute | solution.py:203

commit v12 on v9

--- a/solution.py
+++ b/solution.py
@@ -77,6 +77,26 @@
         (beside, 0, 1 - y, c),
         (beside, UNIT, 1 - y, 1 - c),
     )
+
+
+def pack(values, coords, counts, unit, at, count, sem):
+    copies = [
+        pltpu.make_async_copy(coords, at, sem.at[0]),
+        pltpu.make_async_copy(counts, count, sem.at[1]),
+        pltpu.make_async_copy(values, unit.at[pl.ds(0, BODY)], sem.at[2]),
+    ]
+    for copy in copies:
+        copy.start()
+    copies[0].wait()
+    copies[1].wait()
+    row = lax.broadcasted_iota(jnp.int32, (16, TILE), 0)
+    marks = jnp.full((16, TILE), 8, jnp.int32)
+    for s in range(SLOTS):
+        p = at[0, s]
+        code = jnp.where(s < count[0, 0], p + (p >> 3), 8)
+        marks = jnp.where(row == s, code, marks)
+    unit[BODY:UNIT, :] = marks.astype(F32).astype(BF16)
+    copies[2].wait()
 
 
 def begin(*refs):
@@ -191,11 +211,18 @@
 
 def shards(tile_values, tile_coords, tile_counts, result_coords, result_counts):
     slot = jnp.arange(16, dtype=jnp.int32)
-    at = jnp.pad(tile_coords[0, 0], (0, 12))
-    code = jnp.where(slot < tile_counts[0, 0], at + (at >> 3), 8).astype(BF16)
-    unit = jnp.concatenate(
-        [tile_values.reshape(BODY, TILE), jnp.broadcast_to(code[:, None], (16, TILE))]
-    )
+    unit = pl.pallas_call(
+        pack,
+        in_specs=[AWAY] * 3,
+        out_specs=WHOLE,
+        out_shape=jax.ShapeDtypeStruct((UNIT, TILE), BF16),
+        scratch_shapes=[
+            pltpu.SMEM((1, SLOTS), jnp.int32),
+            pltpu.SMEM((1, 1), jnp.int32),
+            pltpu.SemaphoreType.DMA((3,)),
+        ],
+        compiler_params=pltpu.CompilerParams(vmem_limit_bytes=60 * 2**20),
+    )(tile_values.reshape(BODY, TILE), tile_coords.reshape(1, SLOTS), tile_counts)
 
     def along(perm, v):
         return lax.ppermute(v, "loop", perm)

time: 70.2 us -> 71.3 us (1.016)
  Pallas kernels: 10.4 us -> 12 us
  local copies, waits for them, and re-layouts: 0.24 us -> 1.07 us
    pallas_call x0 -> x1, Pallas kernels: none -> 1.59 us  [shards(): pl.pallas_call(pack, in_specs=[AWAY] * 3, out_specs=WHOLE, out_shape=jax....]
    concatenate x1 -> x0, other arithmetic: 0.91 us -> none  [shards(): jnp.concatenate([tile_values.reshape(BODY, TILE), jnp.broadcast_to(code[:...]
    concatenate x1, other arithmetic: 0.02 us -> 0.92 us  [shards(): row = jnp.concatenate([later, across(YHI, later)])]
    unnamed x3, local copies, waits for them, and re-layouts: 0.04 us -> 0.94 us
  transfers between devices with their start and end apart: 20 -> 20, of which waited for: 3 -> 3; matrix products, arithmetic and copies ran while one was open for 2% -> 5% of each run, Pallas kernels for 10% -> 10%
where the time goes in v12:
time: 71.3 us; the launch traced here: 71.1 us
  starting transfers between devices  37.1 us (52%)
  blocking collectives  14.8 us (21%)
  Pallas kernels  12 us (17%)
  other arithmetic  2.54 us (4%)
  waiting for transfers between devices  1.95 us (3%)
  between operations  1.6 us (2%)
  local copies, waits for them, and re-layouts  1.07 us (2%)
    ppermute x17, starting transfers between devices, along(): return lax.ppermute(v, 'loop', perm)  31 us
    all_to_all x1, blocking collectives, shards(): sums = lax.all_to_all(sums, 'loop', 0, 0, tiled=True)  14.8 us
    ppermute x3, starting transfers between devices, across(): return lax.ppermute(v, 'group', perm)  6.11 us
    pallas_call x1, Pallas kernels, shards(): pl.pallas_call(begin, in_specs=[WHOLE] * 12, out_specs=[WHOLE] * 2, out_s...  4.58 us
    pallas_call x1, Pallas kernels, shards(): pl.pallas_call(rescale, in_specs=[AWAY] * 3, out_specs=AWAY, out_shape=ja...  1.94 us
    ppermute x17, waiting for transfers between devices, along(): return lax.ppermute(v, 'loop', perm)  1.94 us
    pallas_call x1, Pallas kernels, shards(): pl.pallas_call(proceed, in_specs=[WHOLE] * 6, out_specs=WHOLE, out_shape=...  1.77 us
    pallas_call x1, Pallas kernels, shards(): pl.pallas_call(pack, in_specs=[AWAY] * 3, out_specs=WHOLE, out_shape=jax....  1.59 us
  transfers between devices with their start and end apart: 20, of which 3 were waited for; matrix products, arithmetic and copies ran while one was open for 5% of the time, Pallas kernels for 10%

profile of v12, /device:TPU:1, one launch (start us, length us, event | category | flops | bytes accessed | tf_op | source)
XLA Modules:
  0.0 71.1 jit_solution(13023084757346930832)
XLA Ops:
  0.7 1.6 %shard_map.55 = bf16[528,128]{1,0:T(8,128)(2,1)} custom-call(bf16[512,128]{1,0:T(8,128)(2,1)} %bitcast.6, s32[1,4]{1,0:T(1,128)} %bitcast.7, s32[1,1]{1,0:T(1,128)S(6)} %copy.9.counts), custom_call_target="tpu_custom_call" | custom-call | tf_op jit(solution)/shard_map/pallas_call | solution.py:214
  2.2 3.3 %collective-permute-start = (bf16[528,128]{1,0:T(8,128)(2,1)}, bf16[528,128]{1,0:T(8,128)(2,1)S(1)}, u32[]{:S(2)}, u32[]{:S(2)}) collective-permute-start(bf16[528,128]{1,0:T(8,128)(2,1)} %shard_map.55), channel_id=1, source_target_pairs={{0,1},{1,0},{2,3},{3,2},{4,5},{5,4},{6,7},{7,6},{8,9},{9,8},{10,11... | collective-permute-start | bytes 405512 | tf_op jit(solution)/shard_map/ppermute | solution.py:228
  5.6 0.0 collective-permute-start.1
  5.6 1.7 %collective-permute-start.2 = (bf16[528,128]{1,0:T(8,128)(2,1)}, bf16[528,128]{1,0:T(8,128)(2,1)S(1)}, u32[]{:S(2)}, u32[]{:S(2)}) collective-permute-start(bf16[528,128]{1,0:T(8,128)(2,1)} %shard_map.55), channel_id=1, source_target_pairs={{0,3},{1,2},{2,1},{3,0},{4,7},{5,6},{6,5},{7,4},{8,11},{9,10},{10,... | collective-permute-start | bytes 405512 | tf_op jit(solution)/shard_map/ppermute | solution.py:228
  7.3 0.0 collective-permute-done
  7.3 1.0 %pad_maximum_fusion.refs_0_ = bf16[1056,128]{1,0:T(8,128)(2,1)S(1)} fusion(bf16[528,128]{1,0:T(8,128)(2,1)S(1)} %collective-permute-done, bf16[528,128]{1,0:T(8,128)(2,1)} %shard_map.55), kind=kLoop, calls=%fused_computation | loop fusion | flops 540672 | bytes 540672 | tf_op jit(solution)/shard_map/concatenate | solution.py:235
  8.3 3.9 %collective-permute-start.3 = (bf16[1056,128]{1,0:T(8,128)(2,1)S(1)}, bf16[1056,128]{1,0:T(8,128)(2,1)S(1)}, u32[]{:S(2)}, u32[]{:S(2)}) collective-permute-start(bf16[1056,128]{1,0:T(8,128)(2,1)S(1)} %pad_maximum_fusion.refs_0_), channel_id=1, source_target_pairs={{0,4},{1,29},{2,6},{3,31},{4,8},{5,1},{6,10},{7,3},{8,12},{9,5},{1... | collective-permute-start | bytes 811016 | tf_op jit(solution)/shard_map/ppermute | solution.py:228
  12.2 2.9 %collective-permute-start.13 = (bf16[528,128]{1,0:T(8,128)(2,1)}, bf16[528,128]{1,0:T(8,128)(2,1)S(1)}, u32[]{:S(2)}, u32[]{:S(2)}) collective-permute-start(bf16[528,128]{1,0:T(8,128)(2,1)} %shard_map.55), channel_id=1, source_target_pairs={{0,32},{32,0},{64,96},{96,64},{128,160},{160,128},{192,224},{224,1... | collective-permute-start | bytes 405512 | tf_op jit(solution)/shard_map/ppermute | solution.py:231
  15.1 0.0 collective-permute-done.1
  15.1 0.0 collective-permute-done.2
  15.1 0.4 collective-permute-done.3.refs_2_
  15.6 3.1 %collective-permute-start.4 = (bf16[1056,128]{1,0:T(8,128)(2,1)S(1)}, bf16[1056,128]{1,0:T(8,128)(2,1)S(1)}, u32[]{:S(2)}, u32[]{:S(2)}) collective-permute-start(bf16[1056,128]{1,0:T(8,128)(2,1)S(1)} %constant_dynamic-update-slice_fusion.refs_1_), channel_id=1, source_target_pairs={{0,4},{1,29},{2,6},{3,31},{4,8},{5,1},{6,10},{7,3},{8,12},{9,5},{1... | collective-permute-start | bytes 811016 | tf_op jit(solution)/shard_map/ppermute | solution.py:228
  18.7 0.0 collective-permute-done.13
  18.7 0.9 %pad_maximum_fusion.1 = bf16[1056,128]{1,0:T(8,128)(2,1)S(1)} fusion(bf16[528,128]{1,0:T(8,128)(2,1)S(1)} %collective-permute-done.13, bf16[528,128]{1,0:T(8,128)(2,1)} %shard_map.55), kind=kLoop, calls=%fused_computation.1 | loop fusion | flops 540672 | bytes 540672 | tf_op jit(solution)/shard_map/concatenate | solution.py:239
  19.6 1.3 %collective-permute-start.14 = (bf16[1056,128]{1,0:T(8,128)(2,1)S(1)}, bf16[1056,128]{1,0:T(8,128)(2,1)S(1)}, u32[]{:S(2)}, u32[]{:S(2)}) collective-permute-start(bf16[1056,128]{1,0:T(8,128)(2,1)S(1)} %pad_maximum_fusion.1), channel_id=1, source_target_pairs={{0,64},{32,96},{64,0},{96,32},{128,192},{160,224},{192,128},{224,1... | collective-permute-start | bytes 811016 | tf_op jit(solution)/shard_map/ppermute | solution.py:231
  20.9 0.9 %constant_dynamic-update-slice_fusion.4 = bf16[2112,128]{1,0:T(8,128)(2,1)S(1)} fusion(bf16[528,128]{1,0:T(8,128)(2,1)} %shard_map.55), kind=kLoop, calls=%fused_computation.6 | loop fusion | bytes 270336
  21.9 4.4 %collective-permute-start.10 = (bf16[1056,128]{1,0:T(8,128)(2,1)S(1)}, bf16[1056,128]{1,0:T(8,128)(2,1)S(1)}, u32[]{:S(2)}, u32[]{:S(2)}) collective-permute-start(bf16[1056,128]{1,0:T(8,128)(2,1)S(1)} %collective-permute-done.3.refs_2_), channel_id=1, source_target_pairs={{0,4},{1,29},{2,6},{3,31},{4,8},{5,1},{6,10},{7,3},{8,12},{9,5},{1... | collective-permute-start | bytes 811016 | tf_op jit(solution)/shard_map/ppermute | solution.py:228
  26.3 0.0 collective-permute-start.8
  26.3 0.0 collective-permute-done.4.refs_3_
  26.3 1.2 %collective-permute-start.5 = (bf16[1056,128]{1,0:T(8,128)(2,1)S(1)}, bf16[1056,128]{1,0:T(8,128)(2,1)S(1)}, u32[]{:S(2)}, u32[]{:S(2)}) collective-permute-start(bf16[1056,128]{1,0:T(8,128)(2,1)S(1)} %collective-permute-done.4.refs_3_), channel_id=1, source_target_pairs={{0,4},{1,29},{2,6},{3,31},{4,8},{5,1},{6,10},{7,3},{8,12},{9,5},{1... | collective-permute-start | bytes 811016 | tf_op jit(solution)/shard_map/ppermute | solution.py:228
  27.5 0.0 collective-permute-done.14
  27.6 1.9 %collective-permute-start.15 = (bf16[2112,128]{1,0:T(8,128)(2,1)S(1)}, bf16[2112,128]{1,0:T(8,128)(2,1)S(1)}, u32[]{:S(2)}, u32[]{:S(2)}) collective-permute-start(bf16[2112,128]{1,0:T(8,128)(2,1)S(1)} %constant_dynamic-update-slice_fusion.2.refs_10_), channel_id=1, source_target_pairs={{0,192},{32,224},{64,128},{96,160},{128,64},{160,96},{192,0},{224,... | collective-permute-start | bytes 1622024 | tf_op jit(solution)/shard_map/ppermute | solution.py:231
  29.5 0.0 collective-permute-start.9
  29.5 0.2 collective-permute-done.10.refs_6_
  29.7 6.1 %collective-permute-start.16 = (bf16[1056,128]{1,0:T(8,128)(2,1)S(1)}, bf16[1056,128]{1,0:T(8,128)(2,1)S(1)}, u32[]{:S(2)}, u32[]{:S(2)}) collective-permute-start(bf16[1056,128]{1,0:T(8,128)(2,1)S(1)} %collective-permute-done.10.refs_6_), channel_id=1, source_target_pairs={{0,4},{1,29},{2,6},{3,31},{4,8},{5,1},{6,10},{7,3},{8,12},{9,5},{1... | collective-permute-start | bytes 811016 | tf_op jit(solution)/shard_map/ppermute | solution.py:228
  35.8 0.0 collective-permute-done.8.refs_4_
  35.8 0.0 collective-permute-start.11
  35.8 0.0 collective-permute-done.5.refs_7_
  35.8 0.8 %collective-permute-start.6 = (bf16[1056,128]{1,0:T(8,128)(2,1)S(1)}, bf16[1056,128]{1,0:T(8,128)(2,1)S(1)}, u32[]{:S(2)}, u32[]{:S(2)}) collective-permute-start(bf16[1056,128]{1,0:T(8,128)(2,1)S(1)} %collective-permute-done.5.refs_7_), channel_id=1, source_target_pairs={{0,4},{1,29},{2,6},{3,31},{4,8},{5,1},{6,10},{7,3},{8,12},{9,5},{1... | collective-permute-start | bytes 811016 | tf_op jit(solution)/shard_map/ppermute | solution.py:228
  36.6 0.0 collective-permute-done.9.refs_5_
  36.6 0.0 collective-permute-start.12
  37.3 0.7 fusion
  38.0 1.3 %collective-permute-done.16.refs_0_ = bf16[1056,128]{1,0:T(8,128)(2,1)S(1)} collective-permute-done((bf16[1056,128]{1,0:T(8,128)(2,1)S(1)}, bf16[1056,128]{1,0:T(8,128)(2,1)S(1)}, u32[]{:S(2)}, u32[]{:S(2)}) %collective-permute-start.16) | collective-permute-done | bytes 270368 | tf_op jit(solution)/shard_map/ppermute | solution.py:228
  39.2 3.4 %collective-permute-start.19 = (bf16[1056,128]{1,0:T(8,128)(2,1)S(1)}, bf16[1056,128]{1,0:T(8,128)(2,1)S(1)}, u32[]{:S(2)}, u32[]{:S(2)}) collective-permute-start(bf16[1056,128]{1,0:T(8,128)(2,1)S(1)} %collective-permute-done.16.refs_0_), channel_id=1, source_target_pairs={{0,4},{1,29},{2,6},{3,31},{4,8},{5,1},{6,10},{7,3},{8,12},{9,5},{1... | collective-permute-start | bytes 811016 | tf_op jit(solution)/shard_map/ppermute | solution.py:228
  42.6 0.0 collective-permute-done.11.refs_8_
  42.6 0.0 collective-permute-start.17
  42.6 0.0 collective-permute-done.6.refs_1_
  42.6 1.4 %collective-permute-start.18 = (bf16[1056,128]{1,0:T(8,128)(2,1)S(1)}, bf16[1056,128]{1,0:T(8,128)(2,1)S(1)}, u32[]{:S(2)}, u32[]{:S(2)}) collective-permute-start(bf16[1056,128]{1,0:T(8,128)(2,1)S(1)} %collective-permute-done.6.refs_1_), channel_id=1, source_target_pairs={{0,1},{1,0},{2,3},{3,2},{4,5},{5,4},{6,7},{7,6},{8,9},{9,8},{10,11... | collective-permute-start | bytes 811016 | tf_op jit(solution)/shard_map/ppermute | solution.py:228
  44.0 0.0 collective-permute-done.15.refs_11_
  44.0 1.5 %collective-permute-start.7 = (bf16[1056,128]{1,0:T(8,128)(2,1)S(1)}, bf16[1056,128]{1,0:T(8,128)(2,1)S(1)}, u32[]{:S(2)}, u32[]{:S(2)}) collective-permute-start(bf16[1056,128]{1,0:T(8,128)(2,1)S(1)} %collective-permute-done.6.refs_1_), channel_id=1, source_target_pairs={{0,4},{1,29},{2,6},{3,31},{4,8},{5,1},{6,10},{7,3},{8,12},{9,5},{1... | collective-permute-start | bytes 811016 | tf_op jit(solution)/shard_map/ppermute | solution.py:228
  45.5 0.0 collective-permute-done.12.refs_9_
  45.5 4.6 %shard_map.56 = (bf16[8,256,1152]{2,1,0:T(8,128)(2,1)S(1)}, f32[256,1024]{1,0:T(8,128)S(1)}) custom-call(bf16[1056,128]{1,0:T(8,128)(2,1)S(1)} %pad_maximum_fusion.refs_0_, bf16[1056,128]{1,0:T(8,128)(2,1)S(1)} %constant_dynamic-update-slice_fusion.refs_1_, bf16[1056,128]{1,0:T(8,128)(2,1)S(1)} %collective-permute-done.3.refs_2_, ...), custom_call_target="tpu_custom_call" | custom-call | flops 3221225472 | bytes 25165824 | tf_op jit(solution)/shard_map/pallas_call | solution.py:260
  50.1 0.0 collective-permute-done.19.pair
  50.1 0.6 shard_map.57.refs_5_
  50.8 0.0 collective-permute-done.17.refs_2_
  50.8 0.0 collective-permute-done.18.refs_3_
  50.8 1.8 %shard_map.58.before = f32[256,1024]{1,0:T(8,128)S(1)} custom-call(bf16[1056,128]{1,0:T(8,128)(2,1)S(1)} %collective-permute-done.16.refs_0_, bf16[1056,128]{1,0:T(8,128)(2,1)S(1)} %collective-permute-done.6.refs_1_, bf16[1056,128]{1,0:T(8,128)(2,1)S(1)} %collective-permute-done.17.refs_2_, bf16[1056,128]{1,0:T(8,128)(2,1)S(1)} %collective-permute-done.18.refs_3_, ...), custom_call_target="tpu_custom_call" | custom-call | flops 1073741824 | bytes 8388608 | tf_op jit(solution)/shard_map/pallas_call | solution.py:278
  52.5 0.0 collective-permute-done.7.beside
  52.6 0.1 broadcast_in_dim.4.codes
  52.6 1.5 %shard_map.59 = (f32[8,128,128]{2,1,0:T(8,128)S(1)}, f32[32,8,128]{2,1,0:T(8,128)S(1)}) custom-call(bf16[16,128]{1,0:T(8,128)(2,1)S(1)} %broadcast_in_dim.4.codes, bf16[1056,128]{1,0:T(8,128)(2,1)S(1)} %collective-permute-done.7.beside, bf16[8,256,1152]{2,1,0:T(8,128)(2,1)S(1)} %get-tuple-element.19.dense_left.refs_4_, f32[256,1024]{1,0:T(8,128)S(1)} %shard_map.58.before), custom_call_target="tpu_custom_call" | custom-call | flops 536870912 | bytes 4194304 | tf_op jit(solution)/shard_map/pallas_call | solution.py:287
  54.2 14.8 %all_to_all.5.sums = f32[32,8,128]{2,1,0:T(8,128)S(1)} all-to-all(f32[32,8,128]{2,1,0:T(8,128)S(1)} %get-tuple-element.22), channel_id=1, replica_groups=mesh['group'=8,'loop'=32] {'loop'}, dimensions={0} | all-to-all | bytes 262144 | tf_op jit(solution)/shard_map/all_to_all | solution.py:301
  69.0 1.9 %shard_map.60 = f32[8,128,128]{2,1,0:T(8,128)} custom-call(bf16[16,128]{1,0:T(8,128)(2,1)S(1)} %broadcast_in_dim.4.codes, f32[8,128,128]{2,1,0:T(8,128)S(1)} %get-tuple-element.21.squares, f32[32,8,128]{2,1,0:T(8,128)S(1)} %all_to_all.5.sums), custom_call_target="tpu_custom_call" | custom-call | tf_op jit(solution)/shard_map/pallas_call | solution.py:302
  (4 shorter events, 0.1 us)
Async XLA Ops:
  2.2 5.1 %collective-permute-start = (bf16[528,128]{1,0:T(8,128)(2,1)}, bf16[528,128]{1,0:T(8,128)(2,1)S(1)}, u32[]{:S(2)}, u32[]{:S(2)}) collective-permute-start(bf16[528,128]{1,0:T(8,128)(2,1)} %shard_map.55), channel_id=1, source_target_pairs={{0,1},{1,0},{2,3},{3,2},{4,5},{5,4},{6,7},{7,6},{8,9},{9,8},{10,11... | collective-permute-start | bytes 405512 | tf_op jit(solution)/shard_map/ppermute | solution.py:228
  5.6 9.5 %collective-permute-start.1 = (bf16[528,128]{1,0:T(8,128)(2,1)}, bf16[528,128]{1,0:T(8,128)(2,1)S(1)}, u32[]{:S(2)}, u32[]{:S(2)}) collective-permute-start(bf16[528,128]{1,0:T(8,128)(2,1)} %shard_map.55), channel_id=1, source_target_pairs={{0,2},{1,3},{2,0},{3,1},{4,6},{5,7},{6,4},{7,5},{8,10},{9,11},{10,... | collective-permute-start | bytes 405512 | tf_op jit(solution)/shard_map/ppermute | solution.py:228
  5.6 9.5 %collective-permute-start.2 = (bf16[528,128]{1,0:T(8,128)(2,1)}, bf16[528,128]{1,0:T(8,128)(2,1)S(1)}, u32[]{:S(2)}, u32[]{:S(2)}) collective-permute-start(bf16[528,128]{1,0:T(8,128)(2,1)} %shard_map.55), channel_id=1, source_target_pairs={{0,3},{1,2},{2,1},{3,0},{4,7},{5,6},{6,5},{7,4},{8,11},{9,10},{10,... | collective-permute-start | bytes 405512 | tf_op jit(solution)/shard_map/ppermute | solution.py:228
  8.3 7.3 %collective-permute-start.3 = (bf16[1056,128]{1,0:T(8,128)(2,1)S(1)}, bf16[1056,128]{1,0:T(8,128)(2,1)S(1)}, u32[]{:S(2)}, u32[]{:S(2)}) collective-permute-start(bf16[1056,128]{1,0:T(8,128)(2,1)S(1)} %pad_maximum_fusion.refs_0_), channel_id=1, source_target_pairs={{0,4},{1,29},{2,6},{3,31},{4,8},{5,1},{6,10},{7,3},{8,12},{9,5},{1... | collective-permute-start | bytes 811016 | tf_op jit(solution)/shard_map/ppermute | solution.py:228
  12.2 6.5 %collective-permute-start.13 = (bf16[528,128]{1,0:T(8,128)(2,1)}, bf16[528,128]{1,0:T(8,128)(2,1)S(1)}, u32[]{:S(2)}, u32[]{:S(2)}) collective-permute-start(bf16[528,128]{1,0:T(8,128)(2,1)} %shard_map.55), channel_id=1, source_target_pairs={{0,32},{32,0},{64,96},{96,64},{128,160},{160,128},{192,224},{224,1... | collective-permute-start | bytes 405512 | tf_op jit(solution)/shard_map/ppermute | solution.py:231
  15.6 10.7 %collective-permute-start.4 = (bf16[1056,128]{1,0:T(8,128)(2,1)S(1)}, bf16[1056,128]{1,0:T(8,128)(2,1)S(1)}, u32[]{:S(2)}, u32[]{:S(2)}) collective-permute-start(bf16[1056,128]{1,0:T(8,128)(2,1)S(1)} %constant_dynamic-update-slice_fusion.refs_1_), channel_id=1, source_target_pairs={{0,4},{1,29},{2,6},{3,31},{4,8},{5,1},{6,10},{7,3},{8,12},{9,5},{1... | collective-permute-start | bytes 811016 | tf_op jit(solution)/shard_map/ppermute | solution.py:228
  19.6 7.9 %collective-permute-start.14 = (bf16[1056,128]{1,0:T(8,128)(2,1)S(1)}, bf16[1056,128]{1,0:T(8,128)(2,1)S(1)}, u32[]{:S(2)}, u32[]{:S(2)}) collective-permute-start(bf16[1056,128]{1,0:T(8,128)(2,1)S(1)} %pad_maximum_fusion.1), channel_id=1, source_target_pairs={{0,64},{32,96},{64,0},{96,32},{128,192},{160,224},{192,128},{224,1... | collective-permute-start | bytes 811016 | tf_op jit(solution)/shard_map/ppermute | solution.py:231
  21.9 7.8 %collective-permute-start.10 = (bf16[1056,128]{1,0:T(8,128)(2,1)S(1)}, bf16[1056,128]{1,0:T(8,128)(2,1)S(1)}, u32[]{:S(2)}, u32[]{:S(2)}) collective-permute-start(bf16[1056,128]{1,0:T(8,128)(2,1)S(1)} %collective-permute-done.3.refs_2_), channel_id=1, source_target_pairs={{0,4},{1,29},{2,6},{3,31},{4,8},{5,1},{6,10},{7,3},{8,12},{9,5},{1... | collective-permute-start | bytes 811016 | tf_op jit(solution)/shard_map/ppermute | solution.py:228
  26.3 9.6 %collective-permute-start.8 = (bf16[1056,128]{1,0:T(8,128)(2,1)S(1)}, bf16[1056,128]{1,0:T(8,128)(2,1)S(1)}, u32[]{:S(2)}, u32[]{:S(2)}) collective-permute-start(bf16[1056,128]{1,0:T(8,128)(2,1)S(1)} %collective-permute-done.3.refs_2_), channel_id=1, source_target_pairs={{0,1},{1,0},{2,3},{3,2},{4,5},{5,4},{6,7},{7,6},{8,9},{9,8},{10,11... | collective-permute-start | bytes 811016 | tf_op jit(solution)/shard_map/ppermute | solution.py:228
  26.3 9.6 %collective-permute-start.5 = (bf16[1056,128]{1,0:T(8,128)(2,1)S(1)}, bf16[1056,128]{1,0:T(8,128)(2,1)S(1)}, u32[]{:S(2)}, u32[]{:S(2)}) collective-permute-start(bf16[1056,128]{1,0:T(8,128)(2,1)S(1)} %collective-permute-done.4.refs_3_), channel_id=1, source_target_pairs={{0,4},{1,29},{2,6},{3,31},{4,8},{5,1},{6,10},{7,3},{8,12},{9,5},{1... | collective-permute-start | bytes 811016 | tf_op jit(solution)/shard_map/ppermute | solution.py:228
  27.6 16.4 %collective-permute-start.15 = (bf16[2112,128]{1,0:T(8,128)(2,1)S(1)}, bf16[2112,128]{1,0:T(8,128)(2,1)S(1)}, u32[]{:S(2)}, u32[]{:S(2)}) collective-permute-start(bf16[2112,128]{1,0:T(8,128)(2,1)S(1)} %constant_dynamic-update-slice_fusion.2.refs_10_), channel_id=1, source_target_pairs={{0,192},{32,224},{64,128},{96,160},{128,64},{160,96},{192,0},{224,... | collective-permute-start | bytes 1622024 | tf_op jit(solution)/shard_map/ppermute | solution.py:231
  29.5 7.2 %collective-permute-start.9 = (bf16[1056,128]{1,0:T(8,128)(2,1)S(1)}, bf16[1056,128]{1,0:T(8,128)(2,1)S(1)}, u32[]{:S(2)}, u32[]{:S(2)}) collective-permute-start(bf16[1056,128]{1,0:T(8,128)(2,1)S(1)} %collective-permute-done.4.refs_3_), channel_id=1, source_target_pairs={{0,1},{1,0},{2,3},{3,2},{4,5},{5,4},{6,7},{7,6},{8,9},{9,8},{10,11... | collective-permute-start | bytes 811016 | tf_op jit(solution)/shard_map/ppermute | solution.py:228
  29.7 9.6 %collective-permute-start.16 = (bf16[1056,128]{1,0:T(8,128)(2,1)S(1)}, bf16[1056,128]{1,0:T(8,128)(2,1)S(1)}, u32[]{:S(2)}, u32[]{:S(2)}) collective-permute-start(bf16[1056,128]{1,0:T(8,128)(2,1)S(1)} %collective-permute-done.10.refs_6_), channel_id=1, source_target_pairs={{0,4},{1,29},{2,6},{3,31},{4,8},{5,1},{6,10},{7,3},{8,12},{9,5},{1... | collective-permute-start | bytes 811016 | tf_op jit(solution)/shard_map/ppermute | solution.py:228
  35.8 6.8 %collective-permute-start.11 = (bf16[1056,128]{1,0:T(8,128)(2,1)S(1)}, bf16[1056,128]{1,0:T(8,128)(2,1)S(1)}, u32[]{:S(2)}, u32[]{:S(2)}) collective-permute-start(bf16[1056,128]{1,0:T(8,128)(2,1)S(1)} %collective-permute-done.10.refs_6_), channel_id=1, source_target_pairs={{0,1},{1,0},{2,3},{3,2},{4,5},{5,4},{6,7},{7,6},{8,9},{9,8},{10,11... | collective-permute-start | bytes 811016 | tf_op jit(solution)/shard_map/ppermute | solution.py:228
  35.8 6.8 %collective-permute-start.6 = (bf16[1056,128]{1,0:T(8,128)(2,1)S(1)}, bf16[1056,128]{1,0:T(8,128)(2,1)S(1)}, u32[]{:S(2)}, u32[]{:S(2)}) collective-permute-start(bf16[1056,128]{1,0:T(8,128)(2,1)S(1)} %collective-permute-done.5.refs_7_), channel_id=1, source_target_pairs={{0,4},{1,29},{2,6},{3,31},{4,8},{5,1},{6,10},{7,3},{8,12},{9,5},{1... | collective-permute-start | bytes 811016 | tf_op jit(solution)/shard_map/ppermute | solution.py:228
  36.6 8.9 %collective-permute-start.12 = (bf16[1056,128]{1,0:T(8,128)(2,1)S(1)}, bf16[1056,128]{1,0:T(8,128)(2,1)S(1)}, u32[]{:S(2)}, u32[]{:S(2)}) collective-permute-start(bf16[1056,128]{1,0:T(8,128)(2,1)S(1)} %collective-permute-done.5.refs_7_), channel_id=1, source_target_pairs={{0,1},{1,0},{2,3},{3,2},{4,5},{5,4},{6,7},{7,6},{8,9},{9,8},{10,11... | collective-permute-start | bytes 811016 | tf_op jit(solution)/shard_map/ppermute | solution.py:228
  39.2 10.9 %collective-permute-start.19 = (bf16[1056,128]{1,0:T(8,128)(2,1)S(1)}, bf16[1056,128]{1,0:T(8,128)(2,1)S(1)}, u32[]{:S(2)}, u32[]{:S(2)}) collective-permute-start(bf16[1056,128]{1,0:T(8,128)(2,1)S(1)} %collective-permute-done.16.refs_0_), channel_id=1, source_target_pairs={{0,4},{1,29},{2,6},{3,31},{4,8},{5,1},{6,10},{7,3},{8,12},{9,5},{1... | collective-permute-start | bytes 811016 | tf_op jit(solution)/shard_map/ppermute | solution.py:228
  42.6 8.1 %collective-permute-start.17 = (bf16[1056,128]{1,0:T(8,128)(2,1)S(1)}, bf16[1056,128]{1,0:T(8,128)(2,1)S(1)}, u32[]{:S(2)}, u32[]{:S(2)}) collective-permute-start(bf16[1056,128]{1,0:T(8,128)(2,1)S(1)} %collective-permute-done.16.refs_0_), channel_id=1, source_target_pairs={{0,1},{1,0},{2,3},{3,2},{4,5},{5,4},{6,7},{7,6},{8,9},{9,8},{10,11... | collective-permute-start | bytes 811016 | tf_op jit(solution)/shard_map/ppermute | solution.py:228
  42.6 8.1 %collective-permute-start.18 = (bf16[1056,128]{1,0:T(8,128)(2,1)S(1)}, bf16[1056,128]{1,0:T(8,128)(2,1)S(1)}, u32[]{:S(2)}, u32[]{:S(2)}) collective-permute-start(bf16[1056,128]{1,0:T(8,128)(2,1)S(1)} %collective-permute-done.6.refs_1_), channel_id=1, source_target_pairs={{0,1},{1,0},{2,3},{3,2},{4,5},{5,4},{6,7},{7,6},{8,9},{9,8},{10,11... | collective-permute-start | bytes 811016 | tf_op jit(solution)/shard_map/ppermute | solution.py:228
  44.0 8.5 %collective-permute-start.7 = (bf16[1056,128]{1,0:T(8,128)(2,1)S(1)}, bf16[1056,128]{1,0:T(8,128)(2,1)S(1)}, u32[]{:S(2)}, u32[]{:S(2)}) collective-permute-start(bf16[1056,128]{1,0:T(8,128)(2,1)S(1)} %collective-permute-done.6.refs_1_), channel_id=1, source_target_pairs={{0,4},{1,29},{2,6},{3,31},{4,8},{5,1},{6,10},{7,3},{8,12},{9,5},{1... | collective-permute-start | bytes 811016 | tf_op jit(solution)/shard_map/ppermute | solution.py:228
